TPU v7x, 32 devices: a whole 2x2x4 slice. The times are simulated.
32 devices in a mesh: batch: 2 (over x), seq: 4 (over y, core), head: 4 (over z).
Axes of the slice: x: 2, y: 2, z: 4, core: 2. Of those that a mesh axis runs over, the one named last changes fastest.
Arguments:
- tokens: bfloat16 [2, 4, 512, 768], P(None, 'batch', 'seq'), may hold values from -6 to 6
- spatial: bfloat16 [4, 512, 768], P('batch', 'seq'), may hold values from -6 to 6
- positions: int32 [4, 512], P('batch', 'seq'), may hold values from 0 to 511, each once within a row
- boxes: int32 [2, 4, 512], P(None, 'batch', 'seq'), may hold values from 0 to 127
- query_key_value_weight: bfloat16 [2, 3, 768, 768], P(None, None, None, 'head'), may hold values from -0.21875 to 0.21875
- w_spatial: bfloat16 [2, 768, 768], P(None, None, 'head'), may hold values from -0.21875 to 0.21875
- rel_tables: float32 [2, 3, 12, 128], P(None, None, 'head'), may hold values from -3 to 3
- exit_matrix: bfloat16 [2, 768, 768], P(None, 'head'), may hold values from -1.75 to 1.75
- ln_gains: float32 [2, 2, 768], replicated, may hold values from 0.1 to 1.9
- ln_shifts: float32 [2, 2, 768], replicated, may hold values from -2 to 2
- up_weight: bfloat16 [2, 768, 3072], P(None, None, 'head'), may hold values from -0.21875 to 0.21875
- hidden_bias: float32 [2, 3072], P(None, 'head'), may hold values from -3 to 3
- shrink_projection_array: bfloat16 [2, 3072, 768], P(None, 'head'), may hold values from -0.109375 to 0.109375
- b_down: float32 [2, 768], replicated, may hold values from -2 to 2
- cotangent: bfloat16 [2, 4, 512, 768], P(None, 'batch', 'seq'), may hold values from -6 to 6
Outputs:
- output: bfloat16 [2, 4, 512, 768], P(None, 'batch', 'seq')
- grad_tokens: float32 [2, 4, 512, 768], P(None, 'batch', 'seq')
- grad_spatial: float32 [4, 512, 768], P('batch', 'seq')
- grad_qkv: float32 [2, 3, 768, 768], P(None, None, None, 'head')
- grad_spatial_w: float32 [2, 768, 768], P(None, None, 'head')
- grad_tables: float32 [2, 3, 12, 128], P(None, None, 'head')
- output_weight_gradient: float32 [2, 768, 768], P(None, 'head')
- grad_gains: float32 [2, 2, 768], P(None, None, 'head')
- grad_shifts: float32 [2, 2, 768], P(None, None, 'head')
- grad_up: float32 [2, 768, 3072], P(None, None, 'head')
- grad_b_up: float32 [2, 3072], P(None, 'head')
- grad_down: float32 [2, 3072, 768], P(None, 'head')
- grad_b_down: float32 [2, 768], P(None, 'head')
Inputs may be any that keep to these rules, and one draw needn't show every extreme that they name: `positions`: each page's row holds every reading position from 0 to 511 once.
All inputs are finite; a program needn't handle non-finite values.
Results may differ from a plain program's by a relative error of at most 0.02.
Values may be sent and summed in bfloat16 or wider, within the bound.
No kernel may reach another device: no remote copies, remote signals or barrier semaphores. Data moves between devices by JAX's collectives and lax.ppermute only.
A program may use at most 128 MiB of HBM per device.

v0:
```python
import jax
import jax.numpy as jnp
from jax import lax
from jax.sharding import PartitionSpec as P

DH = 64
NBUCK = 128
HALF = 64


EPSILON = 1e-05


def norm_rows(row_data, gain_row, shift_row):
    centre = row_data - jnp.mean(row_data, axis=-1, keepdims=True)
    spread = jnp.mean(centre * centre, axis=-1, keepdims=True)
    return centre * lax.rsqrt(spread + EPSILON) * gain_row + shift_row


def softmax_rows(scores):
    return jax.nn.softmax(scores, axis=-1)


def gelu_exact(upper_half):
    return jax.nn.gelu(upper_half, approximate=False)


def bucket(query_place, key_place):
    return jnp.clip(key_place[None, :] - query_place[:, None], -HALF, HALF - 1) + HALF


def chosen_rows(index_table):
    levels = lax.broadcasted_iota(jnp.int32, (1, 1, NBUCK), 2)
    return (index_table[:, :, None] == levels).astype(jnp.bfloat16)


def shards(
    tokens,
    spatial,
    positions,
    boxes,
    query_key_value_weight,
    w_spatial,
    rel_tables,
    exit_matrix,
    ln_gains,
    ln_shifts,
    up_weight,
    hidden_bias,
    shrink_projection_array,
    b_down,
    cotangent,
):
    score_scale = DH ** (-0.5)
    local_heads = rel_tables.shape[2]
    local_rows = tokens.shape[2]
    model_width = tokens.shape[3]
    key_places, key_boxes = (
        lax.all_gather(positions, "seq", axis=1, tiled=True),
        lax.all_gather(boxes, "seq", axis=2, tiled=True),
    )
    leading_scale_factor = ln_gains[:, 0][:, None, :]
    shift_first = ln_shifts[:, 0][:, None, :]
    gain_second = ln_gains[:, 1][:, None, :]
    shift_second = ln_shifts[:, 1][:, None, :]
    relation_grid_fine = rel_tables.astype(jnp.bfloat16)
    relation_grid_remainder = (rel_tables - relation_grid_fine.astype(jnp.float32)).astype(
        jnp.bfloat16
    )

    def page_pass(page_item):
        token_page_rows, page_spatial, page_places, page_boxes, page_cot, all_places, all_boxes = (
            page_item
        )
        projected_rows = jnp.einsum(
            "snd,skde->skne",
            token_page_rows,
            query_key_value_weight,
            preferred_element_type=jnp.float32,
        ).astype(jnp.bfloat16)
        spatial_qk = jnp.einsum(
            "nd,kde->kne", page_spatial, w_spatial, preferred_element_type=jnp.float32
        ).astype(jnp.bfloat16)
        every_lookup_vector, spatial_keys = (
            lax.all_gather(projected_rows[:, 1:], "seq", axis=2, tiled=True),
            lax.all_gather(spatial_qk[1], "seq", axis=0, tiled=True),
        )
        length = spatial_keys.shape[0]
        queries = projected_rows[:, 0].reshape(2, local_rows, local_heads, DH)
        keys = every_lookup_vector[:, 0].reshape(2, length, local_heads, DH)
        values = every_lookup_vector[:, 1].reshape(2, length, local_heads, DH)
        spatial_q = spatial_qk[0].reshape(local_rows, local_heads, DH)
        spatial_k = spatial_keys.reshape(length, local_heads, DH)
        indices = (
            bucket(page_places, all_places),
            bucket(page_boxes[0], all_boxes[0]),
            bucket(page_boxes[1], all_boxes[1]),
        )
        bias_sum = jnp.zeros((2, local_heads, local_rows, length), jnp.float32)
        for kind_index in range(3):
            picked = chosen_rows(indices[kind_index])
            bias_sum = bias_sum + jnp.einsum(
                "ijr,shr->shij",
                picked,
                relation_grid_fine[:, kind_index],
                preferred_element_type=jnp.float32,
            )
            bias_sum = bias_sum + jnp.einsum(
                "ijr,shr->shij",
                picked,
                relation_grid_remainder[:, kind_index],
                preferred_element_type=jnp.float32,
            )
        plain_part = jnp.einsum(
            "sihd,sjhd->shij", queries, keys, preferred_element_type=jnp.float32
        )
        shared_part = jnp.einsum(
            "ihd,jhd->hij", spatial_q, spatial_k, preferred_element_type=jnp.float32
        )
        scores = (plain_part + shared_part[None]) * score_scale + bias_sum
        soft, soft_back = jax.vjp(softmax_rows, scores)
        soft_low = soft.astype(jnp.bfloat16)
        attended_values = jnp.einsum(
            "shij,sjhd->sihd", soft_low, values, preferred_element_type=jnp.float32
        )
        attended_values = attended_values.reshape(2, local_rows, -1).astype(jnp.bfloat16)
        mixed = lax.psum(
            jnp.einsum(
                "lxr,lrg->xg", attended_values, exit_matrix, preferred_element_type=jnp.float32
            ).astype(jnp.bfloat16),
            "head",
        ).astype(jnp.float32)
        normalized_rows, first_back = jax.vjp(
            norm_rows,
            token_page_rows.astype(jnp.float32) + mixed[None],
            leading_scale_factor,
            shift_first,
        )
        normed_low = normalized_rows.astype(jnp.bfloat16)
        upper_half = (
            jnp.einsum("snd,sdf->snf", normed_low, up_weight, preferred_element_type=jnp.float32)
            + hidden_bias[:, None, :]
        )
        nonzero_neurons, gelu_back = jax.vjp(gelu_exact, upper_half)
        nonzero_neurons_coarse = nonzero_neurons.astype(jnp.bfloat16)
        reduced_input = lax.psum(
            jnp.einsum(
                "her,hrk->hek",
                nonzero_neurons_coarse,
                shrink_projection_array,
                preferred_element_type=jnp.float32,
            ).astype(jnp.bfloat16),
            "head",
        ).astype(jnp.float32)
        final, second_back = jax.vjp(
            norm_rows,
            normalized_rows + reduced_input + b_down[:, None, :],
            gain_second,
            shift_second,
        )
        d_second, d_gain_two, d_shift_two = second_back(page_cot.astype(jnp.float32))
        grad_of_coarse_copy = d_second.astype(jnp.bfloat16)
        grad_down = jnp.einsum(
            "ejc,ejo->eco",
            nonzero_neurons_coarse,
            grad_of_coarse_copy,
            preferred_element_type=jnp.float32,
        )
        d_active = jnp.einsum(
            "snd,sfd->snf",
            grad_of_coarse_copy,
            shrink_projection_array,
            preferred_element_type=jnp.float32,
        )
        d_upper = gelu_back(d_active)[0].astype(jnp.bfloat16)
        grad_up = jnp.einsum(
            "snd,snf->sdf", normed_low, d_upper, preferred_element_type=jnp.float32
        )
        grad_b_up = jnp.sum(d_upper.astype(jnp.float32), axis=1)
        hidden_terms = jnp.einsum(
            "snf,sdf->snd", d_upper, up_weight, preferred_element_type=jnp.float32
        )
        d_normed = d_second + lax.psum(hidden_terms.astype(jnp.bfloat16), "head").astype(
            jnp.float32
        )
        d_first, d_gain_one, d_shift_one = first_back(d_normed)
        blended_cotangent = (d_first[0] + d_first[1]).astype(jnp.bfloat16)
        output_weight_gradient = jnp.einsum(
            "rfu,fg->rug", attended_values, blended_cotangent, preferred_element_type=jnp.float32
        )
        d_att = jnp.einsum(
            "hi,oyi->ohy", blended_cotangent, exit_matrix, preferred_element_type=jnp.float32
        ).astype(jnp.bfloat16)
        d_att = d_att.reshape(2, local_rows, local_heads, DH)
        content_cotangent = jnp.einsum(
            "shij,sihd->sjhd", soft_low, d_att, preferred_element_type=jnp.float32
        )
        d_soft = jnp.einsum("sihd,sjhd->shij", d_att, values, preferred_element_type=jnp.float32)
        d_scores = soft_back(d_soft)[0].astype(jnp.bfloat16)
        grad_tables = jnp.stack(
            [
                jnp.einsum(
                    "shij,ijr->shr",
                    d_scores,
                    chosen_rows(indices[kind_index]),
                    preferred_element_type=jnp.float32,
                )
                for kind_index in range(3)
            ],
            axis=1,
        )
        d_queries = (
            jnp.einsum("shij,sjhd->sihd", d_scores, keys, preferred_element_type=jnp.float32)
            * score_scale
        ).astype(jnp.bfloat16)
        d_keys = (
            jnp.einsum("shij,sihd->sjhd", d_scores, queries, preferred_element_type=jnp.float32)
            * score_scale
        )
        d_spatial_q = (
            jnp.einsum("shij,jhd->ihd", d_scores, spatial_k, preferred_element_type=jnp.float32)
            * score_scale
        ).astype(jnp.bfloat16)
        d_spatial_k = (
            jnp.einsum("shij,ihd->jhd", d_scores, spatial_q, preferred_element_type=jnp.float32)
            * score_scale
        )
        key_terms = jnp.stack(
            [d_keys.reshape(2, length, -1), content_cotangent.reshape(2, length, -1)], axis=1
        )
        own_keys, own_spatial = (
            lax.psum_scatter(
                key_terms.astype(jnp.bfloat16), "seq", scatter_dimension=2, tiled=True
            ).astype(jnp.float32),
            lax.psum_scatter(
                d_spatial_k.reshape(length, -1).astype(jnp.bfloat16),
                "seq",
                scatter_dimension=0,
                tiled=True,
            ).astype(jnp.float32),
        )
        d_project = jnp.concatenate(
            [d_queries.reshape(2, 1, local_rows, -1), own_keys.astype(jnp.bfloat16)], axis=1
        )
        layout_pair_cotangent = jnp.stack(
            [d_spatial_q.reshape(local_rows, -1), own_spatial.astype(jnp.bfloat16)]
        )
        grad_qkv = jnp.einsum(
            "snd,skne->skde", token_page_rows, d_project, preferred_element_type=jnp.float32
        )
        grad_spatial_w = jnp.einsum(
            "nd,kne->kde", page_spatial, layout_pair_cotangent, preferred_element_type=jnp.float32
        )
        input_terms = jnp.einsum(
            "skne,skde->snd", d_project, query_key_value_weight, preferred_element_type=jnp.float32
        )
        spatial_terms = jnp.einsum(
            "kne,kde->nd", layout_pair_cotangent, w_spatial, preferred_element_type=jnp.float32
        )
        d_inputs, d_spatial = (
            lax.psum(input_terms.astype(jnp.bfloat16), "head").astype(jnp.float32),
            lax.psum(spatial_terms.astype(jnp.bfloat16), "head").astype(jnp.float32),
        )
        page_grads = (
            grad_qkv,
            grad_spatial_w,
            grad_tables,
            output_weight_gradient,
            jnp.concatenate([d_gain_one, d_gain_two], axis=1),
            jnp.concatenate([d_shift_one, d_shift_two], axis=1),
            grad_up,
            grad_b_up,
            grad_down,
            jnp.sum(d_second, axis=1),
        )
        return ((final.astype(jnp.bfloat16), d_first + d_inputs, d_spatial), page_grads)

    shapes = [
        list(weight_arg.shape)
        for weight_arg in (
            query_key_value_weight,
            w_spatial,
            rel_tables,
            exit_matrix,
            ln_gains,
            ln_shifts,
            up_weight,
            hidden_bias,
            shrink_projection_array,
            b_down,
        )
    ]
    zero_grads = tuple((jnp.zeros(tuple(grad_shape), jnp.float32) for grad_shape in shapes))

    def page_step(totals, page_item):
        page_outputs, page_grads = page_pass(page_item)
        return (tuple(jax.tree.map(jnp.add, totals, tuple(page_grads))), page_outputs)

    page_items = (
        jnp.moveaxis(tokens, 1, 0),
        spatial,
        positions,
        jnp.moveaxis(boxes, 1, 0),
        jnp.moveaxis(cotangent, 1, 0),
        key_places,
        jnp.moveaxis(key_boxes, 1, 0),
    )
    totals, page_outputs = lax.scan(page_step, zero_grads, page_items)
    totals = (
        lax.psum_scatter(totals[0], ("batch", "seq"), scatter_dimension=2, tiled=True),
        lax.psum_scatter(totals[1], ("batch", "seq"), scatter_dimension=1, tiled=True),
        lax.psum_scatter(totals[2], ("batch", "seq"), scatter_dimension=3, tiled=True),
        lax.psum_scatter(totals[3], ("batch", "seq"), scatter_dimension=2, tiled=True),
        lax.psum_scatter(totals[4], ("batch", "seq"), scatter_dimension=2, tiled=True),
        lax.psum_scatter(totals[5], ("batch", "seq"), scatter_dimension=2, tiled=True),
        lax.psum_scatter(totals[6], ("batch", "seq"), scatter_dimension=1, tiled=True),
        lax.psum_scatter(totals[7], ("batch", "seq"), scatter_dimension=1, tiled=True),
        lax.psum_scatter(totals[8], ("batch", "seq"), scatter_dimension=2, tiled=True),
        lax.psum_scatter(totals[9], ("batch", "seq"), scatter_dimension=1, tiled=True),
    )
    summed = (
        lax.all_gather(totals[0].astype(jnp.bfloat16), ("batch", "seq"), axis=2, tiled=True).astype(
            jnp.float32
        ),
        lax.all_gather(totals[1].astype(jnp.bfloat16), ("batch", "seq"), axis=1, tiled=True).astype(
            jnp.float32
        ),
        lax.all_gather(totals[2].astype(jnp.bfloat16), ("batch", "seq"), axis=3, tiled=True).astype(
            jnp.float32
        ),
        lax.all_gather(totals[3].astype(jnp.bfloat16), ("batch", "seq"), axis=2, tiled=True).astype(
            jnp.float32
        ),
        lax.all_gather(totals[4].astype(jnp.bfloat16), ("batch", "seq"), axis=2, tiled=True).astype(
            jnp.float32
        ),
        lax.all_gather(totals[5].astype(jnp.bfloat16), ("batch", "seq"), axis=2, tiled=True).astype(
            jnp.float32
        ),
        lax.all_gather(totals[6].astype(jnp.bfloat16), ("batch", "seq"), axis=1, tiled=True).astype(
            jnp.float32
        ),
        lax.all_gather(totals[7].astype(jnp.bfloat16), ("batch", "seq"), axis=1, tiled=True).astype(
            jnp.float32
        ),
        lax.all_gather(totals[8].astype(jnp.bfloat16), ("batch", "seq"), axis=2, tiled=True).astype(
            jnp.float32
        ),
        lax.all_gather(totals[9].astype(jnp.bfloat16), ("batch", "seq"), axis=1, tiled=True).astype(
            jnp.float32
        ),
    )
    head_index = lax.axis_index("head")
    head_part = model_width // lax.axis_size("head")
    grad_gains = lax.dynamic_slice_in_dim(summed[4], head_index * head_part, head_part, 2)
    grad_shifts = lax.dynamic_slice_in_dim(summed[5], head_index * head_part, head_part, 2)
    grad_b_down = lax.dynamic_slice_in_dim(summed[9], head_index * head_part, head_part, 1)
    output = jnp.moveaxis(page_outputs[0], 0, 1)
    grad_tokens = jnp.moveaxis(page_outputs[1], 0, 1)
    return (
        output,
        grad_tokens,
        page_outputs[2],
        summed[0],
        summed[1],
        summed[2],
        summed[3],
        grad_gains,
        grad_shifts,
        summed[6],
        summed[7],
        summed[8],
        grad_b_down,
    )


def solution(mesh):
    return jax.shard_map(
        shards,
        mesh=mesh,
        in_specs=(
            P(None, "batch", "seq", None),
            P("batch", "seq", None),
            P("batch", "seq"),
            P(None, "batch", "seq"),
            P(None, None, None, "head"),
            P(None, None, "head"),
            P(None, None, "head", None),
            P(None, "head", None),
            P(),
            P(),
            P(None, None, "head"),
            P(None, "head"),
            P(None, "head", None),
            P(),
            P(None, "batch", "seq", None),
        ),
        out_specs=(
            P(None, "batch", "seq", None),
            P(None, "batch", "seq", None),
            P("batch", "seq", None),
            P(None, None, None, "head"),
            P(None, None, "head"),
            P(None, None, "head", None),
            P(None, "head", None),
            P(None, None, "head"),
            P(None, None, "head"),
            P(None, None, "head"),
            P(None, "head"),
            P(None, "head", None),
            P(None, "head"),
        ),
        check_vma=False,
    )
```

profile of v0, /device:TPU:0, one launch (start us, length us, event | category | flops | bytes accessed | tf_op | source)
XLA Modules:
  0.0 1436.4 jit_solution(5557703927232834037)
XLA Ops:
  30.3 857.0 %while.35 = (s32[]{:T(128)}, f32[2,3,768,192]{2,3,1,0:T(8,128)}, f32[2,768,192]{1,2,0:T(8,128)}, f32[2,3,3,128]{3,2,0,1:T(4,128)}, f32[2,192,768]{2,1,0:T(8,128)...) while((s32[]{:T(128)}, f32[2,3,768,192]{2,3,1,0:T(8,128)}, ...), condition=%wide.region_26.27_spmd.clone, body=%wide.region_0.26_spmd.clone.sunk | while | flops 4362024448 | bytes 250891168 | solution.py:308
  31.8 18.5 %fusion.334 = f32[128,512,2,3]{1,3,2,0:T(4,128)} fusion(s32[128,512]{1,0:T(8,128)S(1)} %clamp_add_fusion.6, bf16[2,3,3,128]{3,2,0,1:T(4,128)(2,1)} %get-tuple-element.845), kind=kOutput, calls=%fused_computation.4.clone.3 | convolution fusion | flops 109051904 | bytes 1837056 | tf_op jit(solution)/shard_map/while/body/eval_jaxpr/ijr,shr->shij/dot_general | solution.py:108
  50.3 18.5 %fusion.335 = f32[128,512,2,3]{1,3,2,0:T(4,128)} fusion(s32[128,512]{1,0:T(8,128)S(1)} %clamp_add_fusion.6, bf16[2,3,3,128]{3,2,0,1:T(4,128)(2,1)} %get-tuple-element.844), kind=kOutput, calls=%fused_computation.5.clone.1 | convolution fusion | flops 109051904 | bytes 1837056 | tf_op jit(solution)/shard_map/while/body/eval_jaxpr/ijr,shr->shij/dot_general | solution.py:102
  68.9 18.5 %fusion.336 = f32[128,512,2,3]{1,3,2,0:T(4,128)} fusion(s32[128,512]{1,0:T(8,128)S(1)} %clamp_add_fusion.7, bf16[2,3,3,128]{3,2,0,1:T(4,128)(2,1)} %get-tuple-element.845), kind=kOutput, calls=%fused_computation.9.clone.3 | convolution fusion | flops 109051904 | bytes 1837056 | tf_op jit(solution)/shard_map/while/body/eval_jaxpr/ijr,shr->shij/dot_general | solution.py:108
  87.4 18.5 %fusion.337 = f32[128,512,2,3]{1,3,2,0:T(4,128)} fusion(s32[128,512]{1,0:T(8,128)S(1)} %clamp_add_fusion.7, bf16[2,3,3,128]{3,2,0,1:T(4,128)(2,1)} %get-tuple-element.844), kind=kOutput, calls=%fused_computation.10.clone.1 | convolution fusion | flops 109051904 | bytes 1837056 | tf_op jit(solution)/shard_map/while/body/eval_jaxpr/ijr,shr->shij/dot_general | solution.py:102
  107.3 18.5 %fusion.339 = f32[128,512,2,3]{1,3,2,0:T(4,128)} fusion(s32[128,512]{1,0:T(8,128)S(1)} %clamp_add_fusion.8, bf16[2,3,3,128]{3,2,0,1:T(4,128)(2,1)} %get-tuple-element.845), kind=kOutput, calls=%fused_computation.14.clone.3 | convolution fusion | flops 109051904 | bytes 1837056 | tf_op jit(solution)/shard_map/while/body/eval_jaxpr/ijr,shr->shij/dot_general | solution.py:108
  125.8 18.5 %fusion.340 = f32[128,512,2,3]{1,3,2,0:T(4,128)} fusion(s32[128,512]{1,0:T(8,128)S(1)} %clamp_add_fusion.8, bf16[2,3,3,128]{3,2,0,1:T(4,128)(2,1)} %get-tuple-element.844), kind=kOutput, calls=%fused_computation.15.clone.1 | convolution fusion | flops 109051904 | bytes 1837056 | tf_op jit(solution)/shard_map/while/body/eval_jaxpr/ijr,shr->shij/dot_general | solution.py:102
  162.2 10.5 fusion.344
  175.2 35.5 %all-reduce.8.cloned.1.call-done = bf16[128,768]{1,0:T(8,128)(2,1)} async-done(((bf16[128,768]{1,0:T(8,128)(2,1)}), bf16[128,768]{1,0:T(8,128)(2,1)}) %all-reduce.8.cloned.1.call-update) | async-done | bytes 196624 | tf_op jit(solution)/shard_map/while/body/eval_jaxpr/psum | solution.py:127
  222.6 35.6 %all-reduce.10.cloned.1.call-done = bf16[2,128,768]{2,1,0:T(8,128)(2,1)} async-done(((bf16[2,128,768]{2,1,0:T(8,128)(2,1)}), bf16[2,128,768]{2,1,0:T(8,128)(2,1)}) %all-reduce.10.cloned.1.call-update) | async-done | bytes 393232 | tf_op jit(solution)/shard_map/while/body/eval_jaxpr/psum | solution.py:146
  278.9 25.0 %all-reduce.12.cloned.1.call-done = bf16[2,128,768]{2,1,0:T(8,128)(2,1)} async-done(((bf16[2,128,768]{2,1,0:T(8,128)(2,1)}), bf16[2,128,768]{2,1,0:T(8,128)(2,1)}) %all-reduce.12.cloned.1.call-update) | async-done | bytes 393232 | tf_op jit(solution)/shard_map/while/body/eval_jaxpr/psum | solution.py:183
  310.8 21.8 %fusion.360 = f32[2,1,3,128]{3,2,0,1:T(4,128)} fusion(s32[128,512]{1,0:T(8,128)S(1)} %copy-done.42, bf16[2,3,128,512]{3,2,1,0:T(8,128)(2,1)S(1)} %get-tuple-element.737), kind=kOutput, calls=%fused_computation.70.clone.2 | convolution fusion | flops 109051904 | bytes 1051648 | tf_op jit(solution)/shard_map/while/body/eval_jaxpr/shij,ijr->shr/dot_general | solution.py:202
  332.6 21.8 %fusion.361 = f32[2,1,3,128]{3,2,0,1:T(4,128)} fusion(s32[128,512]{1,0:T(8,128)S(1)} %copy-done.44, bf16[2,3,128,512]{3,2,1,0:T(8,128)(2,1)S(1)} %get-tuple-element.737), kind=kOutput, calls=%fused_computation.71.clone.1 | convolution fusion | flops 109051904 | bytes 1051648 | tf_op jit(solution)/shard_map/while/body/eval_jaxpr/shij,ijr->shr/dot_general | solution.py:202
  361.9 22.5 %fusion.362 = f32[2,1,3,128]{3,2,0,1:T(4,128)} fusion(s32[128,512]{1,0:T(8,128)} %copy-done.40, bf16[2,3,128,512]{3,2,1,0:T(8,128)(2,1)S(1)} %copy-done.7), kind=kOutput, calls=%fused_computation.72.clone.1 | convolution fusion | flops 109051904 | bytes 1051648 | tf_op jit(solution)/shard_map/while/body/eval_jaxpr/shij,ijr->shr/dot_general | solution.py:202
  394.9 12.7 reduce-scatter.59.cloned.1.call-done
  417.5 34.7 %all-reduce.14.cloned.1.call-done = (bf16[2,128,768]{2,1,0:T(8,128)(2,1)}, bf16[1,128,768]{2,1,0:T(8,128)(2,1)}) async-done(((bf16[2,128,768]{2,1,0:T(8,128)(2,1)}, bf16[1,128,768]{2,1,0:T(8,128)(2,1)}), (bf16[2,128,768]{2,1,0:T(8,128)(2,1)}, bf16[1,128,768]{2,1,0:T(8,128)(2,1)})) %all-reduce.14.cloned.1.call-update) | async-done | bytes 589840 | tf_op jit(solution)/shard_map/while/body/eval_jaxpr/psum | solution.py:261
  456.5 18.5 %fusion.334 = f32[128,512,2,3]{1,3,2,0:T(4,128)} fusion(s32[128,512]{1,0:T(8,128)S(1)} %clamp_add_fusion.6, bf16[2,3,3,128]{3,2,0,1:T(4,128)(2,1)} %get-tuple-element.845), kind=kOutput, calls=%fused_computation.4.clone.3 | convolution fusion | flops 109051904 | bytes 1837056 | tf_op jit(solution)/shard_map/while/body/eval_jaxpr/ijr,shr->shij/dot_general | solution.py:108
  475.0 18.5 %fusion.335 = f32[128,512,2,3]{1,3,2,0:T(4,128)} fusion(s32[128,512]{1,0:T(8,128)S(1)} %clamp_add_fusion.6, bf16[2,3,3,128]{3,2,0,1:T(4,128)(2,1)} %get-tuple-element.844), kind=kOutput, calls=%fused_computation.5.clone.1 | convolution fusion | flops 109051904 | bytes 1837056 | tf_op jit(solution)/shard_map/while/body/eval_jaxpr/ijr,shr->shij/dot_general | solution.py:102
  493.6 18.5 %fusion.336 = f32[128,512,2,3]{1,3,2,0:T(4,128)} fusion(s32[128,512]{1,0:T(8,128)S(1)} %clamp_add_fusion.7, bf16[2,3,3,128]{3,2,0,1:T(4,128)(2,1)} %get-tuple-element.845), kind=kOutput, calls=%fused_computation.9.clone.3 | convolution fusion | flops 109051904 | bytes 1837056 | tf_op jit(solution)/shard_map/while/body/eval_jaxpr/ijr,shr->shij/dot_general | solution.py:108
  512.1 18.5 %fusion.337 = f32[128,512,2,3]{1,3,2,0:T(4,128)} fusion(s32[128,512]{1,0:T(8,128)S(1)} %clamp_add_fusion.7, bf16[2,3,3,128]{3,2,0,1:T(4,128)(2,1)} %get-tuple-element.844), kind=kOutput, calls=%fused_computation.10.clone.1 | convolution fusion | flops 109051904 | bytes 1837056 | tf_op jit(solution)/shard_map/while/body/eval_jaxpr/ijr,shr->shij/dot_general | solution.py:102
  532.0 18.5 %fusion.339 = f32[128,512,2,3]{1,3,2,0:T(4,128)} fusion(s32[128,512]{1,0:T(8,128)S(1)} %clamp_add_fusion.8, bf16[2,3,3,128]{3,2,0,1:T(4,128)(2,1)} %get-tuple-element.845), kind=kOutput, calls=%fused_computation.14.clone.3 | convolution fusion | flops 109051904 | bytes 1837056 | tf_op jit(solution)/shard_map/while/body/eval_jaxpr/ijr,shr->shij/dot_general | solution.py:108
  550.5 18.5 %fusion.340 = f32[128,512,2,3]{1,3,2,0:T(4,128)} fusion(s32[128,512]{1,0:T(8,128)S(1)} %clamp_add_fusion.8, bf16[2,3,3,128]{3,2,0,1:T(4,128)(2,1)} %get-tuple-element.844), kind=kOutput, calls=%fused_computation.15.clone.1 | convolution fusion | flops 109051904 | bytes 1837056 | tf_op jit(solution)/shard_map/while/body/eval_jaxpr/ijr,shr->shij/dot_general | solution.py:102
  586.9 10.5 fusion.344
  599.9 34.6 %all-reduce.8.cloned.1.call-done = bf16[128,768]{1,0:T(8,128)(2,1)} async-done(((bf16[128,768]{1,0:T(8,128)(2,1)}), bf16[128,768]{1,0:T(8,128)(2,1)}) %all-reduce.8.cloned.1.call-update) | async-done | bytes 196624 | tf_op jit(solution)/shard_map/while/body/eval_jaxpr/psum | solution.py:127
  646.4 35.6 %all-reduce.10.cloned.1.call-done = bf16[2,128,768]{2,1,0:T(8,128)(2,1)} async-done(((bf16[2,128,768]{2,1,0:T(8,128)(2,1)}), bf16[2,128,768]{2,1,0:T(8,128)(2,1)}) %all-reduce.10.cloned.1.call-update) | async-done | bytes 393232 | tf_op jit(solution)/shard_map/while/body/eval_jaxpr/psum | solution.py:146
  705.9 21.8 %all-reduce.12.cloned.1.call-done = bf16[2,128,768]{2,1,0:T(8,128)(2,1)} async-done(((bf16[2,128,768]{2,1,0:T(8,128)(2,1)}), bf16[2,128,768]{2,1,0:T(8,128)(2,1)}) %all-reduce.12.cloned.1.call-update) | async-done | bytes 393232 | tf_op jit(solution)/shard_map/while/body/eval_jaxpr/psum | solution.py:183
  734.7 21.8 %fusion.360 = f32[2,1,3,128]{3,2,0,1:T(4,128)} fusion(s32[128,512]{1,0:T(8,128)S(1)} %copy-done.42, bf16[2,3,128,512]{3,2,1,0:T(8,128)(2,1)S(1)} %get-tuple-element.737), kind=kOutput, calls=%fused_computation.70.clone.2 | convolution fusion | flops 109051904 | bytes 1051648 | tf_op jit(solution)/shard_map/while/body/eval_jaxpr/shij,ijr->shr/dot_general | solution.py:202
  756.4 21.8 %fusion.361 = f32[2,1,3,128]{3,2,0,1:T(4,128)} fusion(s32[128,512]{1,0:T(8,128)S(1)} %copy-done.44, bf16[2,3,128,512]{3,2,1,0:T(8,128)(2,1)S(1)} %get-tuple-element.737), kind=kOutput, calls=%fused_computation.71.clone.1 | convolution fusion | flops 109051904 | bytes 1051648 | tf_op jit(solution)/shard_map/while/body/eval_jaxpr/shij,ijr->shr/dot_general | solution.py:202
  785.7 22.5 %fusion.362 = f32[2,1,3,128]{3,2,0,1:T(4,128)} fusion(s32[128,512]{1,0:T(8,128)} %copy-done.40, bf16[2,3,128,512]{3,2,1,0:T(8,128)(2,1)S(1)} %copy-done.7), kind=kOutput, calls=%fused_computation.72.clone.1 | convolution fusion | flops 109051904 | bytes 1051648 | tf_op jit(solution)/shard_map/while/body/eval_jaxpr/shij,ijr->shr/dot_general | solution.py:202
  820.2 11.1 reduce-scatter.59.cloned.1.call-done
  843.8 32.3 %all-reduce.14.cloned.1.call-done = (bf16[2,128,768]{2,1,0:T(8,128)(2,1)}, bf16[1,128,768]{2,1,0:T(8,128)(2,1)}) async-done(((bf16[2,128,768]{2,1,0:T(8,128)(2,1)}, bf16[1,128,768]{2,1,0:T(8,128)(2,1)}), (bf16[2,128,768]{2,1,0:T(8,128)(2,1)}, bf16[1,128,768]{2,1,0:T(8,128)(2,1)})) %all-reduce.14.cloned.1.call-update) | async-done | bytes 589840 | tf_op jit(solution)/shard_map/while/body/eval_jaxpr/psum | solution.py:261
  931.8 18.0 %reduce-scatter.41.cloned.1.call-done = f32[96,1152]{1,0:T(8,128)} async-done(((f32[768,1152]{1,0:T(8,128)}), f32[96,1152]{1,0:T(8,128)}) %reduce-scatter.41.cloned.1.call-update) | async-done | bytes 442384
  952.5 54.9 %reduce-scatter.55.cloned.1.call-done = f32[96,1536]{1,0:T(8,128)} async-done(((f32[768,1536]{1,0:T(8,128)}), f32[96,1536]{1,0:T(8,128)}) %reduce-scatter.55.cloned.1.call-update) | async-done | bytes 589840
  1009.8 55.8 %reduce-scatter.39.cloned.1.call-done = f32[2,96,768]{2,1,0:T(8,128)} async-done(((f32[2,768,768]{2,1,0:T(8,128)}), f32[2,96,768]{2,1,0:T(8,128)}) %reduce-scatter.39.cloned.1.call-update) | async-done | bytes 589840 | tf_op jit(solution)/shard_map/reduce_scatter | solution.py:316
  1067.4 35.1 %reduce-scatter.57.cloned.1.call-done = f32[96,2]{1,0:T(8,128)} async-done(((f32[768,2]{1,0:T(8,128)}), f32[96,2]{1,0:T(8,128)}) %reduce-scatter.57.cloned.1.call-update) | async-done | bytes 784
  1112.1 27.3 %reduce-scatter.53.cloned.1.call-done = f32[96,2]{1,0:T(8,128)} async-done(((f32[768,2]{1,0:T(8,128)}), f32[96,2]{1,0:T(8,128)}) %reduce-scatter.53.cloned.1.call-update) | async-done | bytes 784
  1150.3 25.4 %reduce-scatter.45.cloned.1.call-done = f32[16,18]{1,0:T(8,128)} async-done(((f32[128,18]{1,0:T(8,128)}), f32[16,18]{1,0:T(8,128)}) %reduce-scatter.45.cloned.1.call-update) | async-done | bytes 1168
  1186.7 26.1 %reduce-scatter.49.cloned.1.call-done = f32[96,4]{1,0:T(8,128)} async-done(((f32[768,4]{1,0:T(8,128)}), f32[96,4]{1,0:T(8,128)}) %reduce-scatter.49.cloned.1.call-update) | async-done | bytes 1552
  1214.0 9.5 all_gather.48
  1224.3 25.7 %reduce-scatter.51.cloned.1.call-done = f32[96,4]{1,0:T(8,128)} async-done(((f32[768,4]{1,0:T(8,128)}), f32[96,4]{1,0:T(8,128)}) %reduce-scatter.51.cloned.1.call-update) | async-done | bytes 1552
  1251.1 9.5 all_gather.49
  1261.4 29.2 %reduce-scatter.43.cloned.1.call-done = f32[96,384]{1,0:T(8,128)} async-done(((f32[768,384]{1,0:T(8,128)}), f32[96,384]{1,0:T(8,128)}) %reduce-scatter.43.cloned.1.call-update) | async-done | bytes 147472
  1291.9 10.6 all_gather.45
  1304.3 26.2 %reduce-scatter.47.cloned.1.call-done = f32[96,384]{1,0:T(8,128)} async-done(((f32[768,384]{1,0:T(8,128)}), f32[96,384]{1,0:T(8,128)}) %reduce-scatter.47.cloned.1.call-update) | async-done | bytes 147472
  1331.9 10.3 all_gather.47
  1344.1 17.9 %all-gather.10.cloned.1.call-done = bf16[2,3,768,192]{3,0,1,2:T(2,128)(2,1)} async-done(((bf16[2,3,96,192]{3,0,1,2:T(2,128)(2,1)}), bf16[2,3,768,192]{3,0,1,2:T(2,128)(2,1)}) %all-gather.10.cloned.1.call-update) | async-done | bytes 1769488 | tf_op jit(solution)/shard_map/all_gather | solution.py:322
  1369.1 23.7 %all-gather.14.cloned.1.call-done = bf16[2,768,768]{1,0,2:T(2,128)(2,1)} async-done(((bf16[2,768,96]{1,0,2:T(2,128)(2,1)}), bf16[2,768,768]{1,0,2:T(2,128)(2,1)}) %all-gather.14.cloned.1.call-update) | async-done | bytes 2359312 | tf_op jit(solution)/shard_map/all_gather | solution.py:346
  1400.4 23.9 %all-gather.12.cloned.1.call-done = bf16[2,768,768]{2,1,0:T(8,128)(2,1)} async-done(((bf16[2,96,768]{2,1,0:T(8,128)(2,1)}), bf16[2,768,768]{2,1,0:T(8,128)(2,1)}) %all-gather.12.cloned.1.call-update) | async-done | bytes 2359312 | tf_op jit(solution)/shard_map/all_gather | solution.py:340
  (548 shorter events, 327.3 us)
Async XLA Ops:
  8.0 22.2 %copy-start.2 = (bf16[2,3,768,192]{2,3,1,0:T(8,128)(2,1)S(1)}, bf16[2,3,768,192]{2,3,1,0:T(8,128)(2,1)}, u32[]{:S(2)}) copy-start(bf16[2,3,768,192]{2,3,1,0:T(8,128)(2,1)} %param.21) | copy-start | bytes 5308420
  30.3 180.5 %all-reduce.8.cloned.1.call-start = ((), (), s32[]{:S(2)}) async-start(), calls=%async_computation.25 | async-start | bytes 393216 | tf_op jit(solution)/shard_map/while/body/eval_jaxpr/psum | solution.py:127
  175.2 83.0 %all-reduce.10.cloned.1.call-start = ((), (), s32[]{:S(2)}) async-start(), calls=%async_computation.26 | async-start | bytes 786432 | tf_op jit(solution)/shard_map/while/body/eval_jaxpr/psum | solution.py:146
  221.3 82.6 %all-reduce.12.cloned.1.call-start = ((), (), s32[]{:S(2)}) async-start(), calls=%async_computation.27 | async-start | bytes 786432 | tf_op jit(solution)/shard_map/while/body/eval_jaxpr/psum | solution.py:183
  267.0 124.8 %reduce-scatter.61.cloned.1.call-start = ((), (), s32[]{:S(2)}) async-start(), calls=%async_computation.29 | async-start | bytes 327680 | tf_op jit(solution)/shard_map/while
  275.0 28.9 %copy-start.1 = (f32[2,128,768]{2,1,0:T(8,128)S(1)}, f32[2,128,768]{2,1,0:T(8,128)}, u32[]{:S(2)}) copy-start(f32[2,128,768]{2,1,0:T(8,128)} %copy-done) | copy-start | bytes 2359300 | tf_op jit(solution)/shard_map/while
  310.0 22.6 %copy-start.6 = (bf16[2,3,128,512]{3,2,1,0:T(8,128)(2,1)}, bf16[2,3,128,512]{3,2,1,0:T(8,128)(2,1)S(1)}, u32[]{:S(2)}) copy-start(bf16[2,3,128,512]{3,2,1,0:T(8,128)(2,1)S(1)} %get-tuple-element.737) | copy-start | bytes 2359300 | tf_op jit(solution)/shard_map/while
  310.1 44.3 %copy-start.10 = (bf16[3,128,512]{2,1,0:T(8,128)(2,1)}, bf16[3,128,512]{2,1,0:T(8,128)(2,1)S(1)}, u32[]{:S(2)}) copy-start(bf16[3,128,512]{2,1,0:T(8,128)(2,1)S(1)} %get-tuple-element.738) | copy-start | bytes 1179652 | tf_op jit(solution)/shard_map/while
  310.8 21.8 %copy-start.44 = (s32[128,512]{1,0:T(8,128)S(1)}, s32[128,512]{1,0:T(8,128)}, u32[]{:S(2)}) copy-start(s32[128,512]{1,0:T(8,128)} %copy-done.43) | copy-start | bytes 786436 | tf_op jit(solution)/shard_map/while
  332.6 21.8 %copy-start.38 = (bf16[1,128,192]{1,2,0:T(8,128)(2,1)S(1)}, bf16[1,128,192]{1,2,0:T(8,128)(2,1)}, u32[]{:S(2)}) copy-start(bf16[1,128,192]{1,2,0:T(8,128)(2,1)} %copy-done.37) | copy-start | bytes 147460 | tf_op jit(solution)/shard_map/while
  332.6 22.9 %copy-start.28 = (bf16[2,3,64,512]{3,2,1,0:T(8,128)(2,1)S(1)}, bf16[2,3,64,512]{3,2,1,0:T(8,128)(2,1)}, u32[]{:S(2)}) copy-start(bf16[2,3,64,512]{3,2,1,0:T(8,128)(2,1)} %convolution_convert_fusion.14) | copy-start | bytes 1179652 | tf_op jit(solution)/shard_map/while
  355.5 52.1 %reduce-scatter.59.cloned.1.call-start = ((), (), s32[]{:S(2)}) async-start(), calls=%async_computation.28 | async-start | bytes 983040 | tf_op jit(solution)/shard_map/while
  361.9 25.3 %copy-start.51 = (f32[2,1,768]{2,1,0:T(1,128)S(1)}, f32[2,1,768]{2,1,0:T(1,128)}, u32[]{:S(2)}) copy-start(f32[2,1,768]{2,1,0:T(1,128)} %reshape.314) | copy-start | bytes 18436 | tf_op jit(solution)/shard_map/while
  361.9 26.7 %copy-start.11 = (bf16[3,128,512]{2,1,0:T(8,128)(2,1)S(1)}, bf16[3,128,512]{2,1,0:T(8,128)(2,1)}, u32[]{:S(2)}) copy-start(bf16[3,128,512]{2,1,0:T(8,128)(2,1)} %copy-done.10) | copy-start | bytes 1179652 | tf_op jit(solution)/shard_map/while
  361.9 26.7 %copy-start.24 = (bf16[1,512,192]{1,2,0:T(8,128)(2,1)S(1)}, bf16[1,512,192]{1,2,0:T(8,128)(2,1)}, u32[]{:S(2)}) copy-start(bf16[1,512,192]{1,2,0:T(8,128)(2,1)} %copy-done.23) | copy-start | bytes 589828 | tf_op jit(solution)/shard_map/while
  361.9 27.5 %copy-start.9 = (bf16[2,1,512,192]{2,3,1,0:T(8,128)(2,1)S(1)}, bf16[2,1,512,192]{2,3,1,0:T(8,128)(2,1)}, u32[]{:S(2)}) copy-start(bf16[2,1,512,192]{2,3,1,0:T(8,128)(2,1)} %copy-done.8) | copy-start | bytes 1179652 | tf_op jit(solution)/shard_map/while
  384.5 67.7 %all-reduce.14.cloned.1.call-start = ((), (), s32[]{:S(2)}) async-start(), calls=%async_computation.30 | async-start | bytes 1179648 | tf_op jit(solution)/shard_map/while/body/eval_jaxpr/psum | solution.py:261
  390.5 20.0 %copy-start.3 = (bf16[2,3,768,192]{2,3,1,0:T(8,128)(2,1)S(1)}, bf16[2,3,768,192]{2,3,1,0:T(8,128)(2,1)}, u32[]{:S(2)}) copy-start(bf16[2,3,768,192]{2,3,1,0:T(8,128)(2,1)} %get-tuple-element.918) | copy-start | bytes 5308420 | tf_op jit(solution)/shard_map/while
  455.0 179.6 %all-reduce.8.cloned.1.call-start = ((), (), s32[]{:S(2)}) async-start(), calls=%async_computation.25 | async-start | bytes 393216 | tf_op jit(solution)/shard_map/while/body/eval_jaxpr/psum | solution.py:127
  599.9 82.1 %all-reduce.10.cloned.1.call-start = ((), (), s32[]{:S(2)}) async-start(), calls=%async_computation.26 | async-start | bytes 786432 | tf_op jit(solution)/shard_map/while/body/eval_jaxpr/psum | solution.py:146
  645.1 82.6 %all-reduce.12.cloned.1.call-start = ((), (), s32[]{:S(2)}) async-start(), calls=%async_computation.27 | async-start | bytes 786432 | tf_op jit(solution)/shard_map/while/body/eval_jaxpr/psum | solution.py:183
  690.8 126.4 %reduce-scatter.61.cloned.1.call-start = ((), (), s32[]{:S(2)}) async-start(), calls=%async_computation.29 | async-start | bytes 327680 | tf_op jit(solution)/shard_map/while
  700.4 27.3 %copy-start.1 = (f32[2,128,768]{2,1,0:T(8,128)S(1)}, f32[2,128,768]{2,1,0:T(8,128)}, u32[]{:S(2)}) copy-start(f32[2,128,768]{2,1,0:T(8,128)} %copy-done) | copy-start | bytes 2359300 | tf_op jit(solution)/shard_map/while
  733.9 22.6 %copy-start.6 = (bf16[2,3,128,512]{3,2,1,0:T(8,128)(2,1)}, bf16[2,3,128,512]{3,2,1,0:T(8,128)(2,1)S(1)}, u32[]{:S(2)}) copy-start(bf16[2,3,128,512]{3,2,1,0:T(8,128)(2,1)S(1)} %get-tuple-element.737) | copy-start | bytes 2359300 | tf_op jit(solution)/shard_map/while
  733.9 44.3 %copy-start.10 = (bf16[3,128,512]{2,1,0:T(8,128)(2,1)}, bf16[3,128,512]{2,1,0:T(8,128)(2,1)S(1)}, u32[]{:S(2)}) copy-start(bf16[3,128,512]{2,1,0:T(8,128)(2,1)S(1)} %get-tuple-element.738) | copy-start | bytes 1179652 | tf_op jit(solution)/shard_map/while
  734.7 21.8 %copy-start.44 = (s32[128,512]{1,0:T(8,128)S(1)}, s32[128,512]{1,0:T(8,128)}, u32[]{:S(2)}) copy-start(s32[128,512]{1,0:T(8,128)} %copy-done.43) | copy-start | bytes 786436 | tf_op jit(solution)/shard_map/while
  756.4 21.8 %copy-start.38 = (bf16[1,128,192]{1,2,0:T(8,128)(2,1)S(1)}, bf16[1,128,192]{1,2,0:T(8,128)(2,1)}, u32[]{:S(2)}) copy-start(bf16[1,128,192]{1,2,0:T(8,128)(2,1)} %copy-done.37) | copy-start | bytes 147460 | tf_op jit(solution)/shard_map/while
  756.4 22.9 %copy-start.28 = (bf16[2,3,64,512]{3,2,1,0:T(8,128)(2,1)S(1)}, bf16[2,3,64,512]{3,2,1,0:T(8,128)(2,1)}, u32[]{:S(2)}) copy-start(bf16[2,3,64,512]{3,2,1,0:T(8,128)(2,1)} %convolution_convert_fusion.14) | copy-start | bytes 1179652 | tf_op jit(solution)/shard_map/while
  779.3 52.1 %reduce-scatter.59.cloned.1.call-start = ((), (), s32[]{:S(2)}) async-start(), calls=%async_computation.28 | async-start | bytes 983040 | tf_op jit(solution)/shard_map/while
  785.7 25.4 %copy-start.51 = (f32[2,1,768]{2,1,0:T(1,128)S(1)}, f32[2,1,768]{2,1,0:T(1,128)}, u32[]{:S(2)}) copy-start(f32[2,1,768]{2,1,0:T(1,128)} %reshape.314) | copy-start | bytes 18436 | tf_op jit(solution)/shard_map/while
  785.7 26.8 %copy-start.11 = (bf16[3,128,512]{2,1,0:T(8,128)(2,1)S(1)}, bf16[3,128,512]{2,1,0:T(8,128)(2,1)}, u32[]{:S(2)}) copy-start(bf16[3,128,512]{2,1,0:T(8,128)(2,1)} %copy-done.10) | copy-start | bytes 1179652 | tf_op jit(solution)/shard_map/while
  785.7 26.8 %copy-start.24 = (bf16[1,512,192]{1,2,0:T(8,128)(2,1)S(1)}, bf16[1,512,192]{1,2,0:T(8,128)(2,1)}, u32[]{:S(2)}) copy-start(bf16[1,512,192]{1,2,0:T(8,128)(2,1)} %copy-done.23) | copy-start | bytes 589828 | tf_op jit(solution)/shard_map/while
  785.7 27.6 %copy-start.9 = (bf16[2,1,512,192]{2,3,1,0:T(8,128)(2,1)S(1)}, bf16[2,1,512,192]{2,3,1,0:T(8,128)(2,1)}, u32[]{:S(2)}) copy-start(bf16[2,1,512,192]{2,3,1,0:T(8,128)(2,1)} %copy-done.8) | copy-start | bytes 1179652 | tf_op jit(solution)/shard_map/while
  808.3 67.7 %all-reduce.14.cloned.1.call-start = ((), (), s32[]{:S(2)}) async-start(), calls=%async_computation.30 | async-start | bytes 1179648 | tf_op jit(solution)/shard_map/while/body/eval_jaxpr/psum | solution.py:261
  814.4 19.9 %copy-start.3 = (bf16[2,3,768,192]{2,3,1,0:T(8,128)(2,1)S(1)}, bf16[2,3,768,192]{2,3,1,0:T(8,128)(2,1)}, u32[]{:S(2)}) copy-start(bf16[2,3,768,192]{2,3,1,0:T(8,128)(2,1)} %get-tuple-element.918) | copy-start | bytes 5308420 | tf_op jit(solution)/shard_map/while
  887.2 62.6 %reduce-scatter.41.cloned.1.call-start = ((), (), s32[]{:S(2)}) async-start(), calls=%async_computation.16 | async-start | bytes 3981312
  902.1 105.3 %reduce-scatter.55.cloned.1.call-start = ((), (), s32[]{:S(2)}) async-start(), calls=%async_computation.23 | async-start | bytes 5308416
  915.8 149.7 %reduce-scatter.39.cloned.1.call-start = ((), (), s32[]{:S(2)}) async-start(), calls=%async_computation.13 | async-start | bytes 5308416 | tf_op jit(solution)/shard_map/reduce_scatter | solution.py:316
  916.4 186.1 %reduce-scatter.57.cloned.1.call-start = ((), (), s32[]{:S(2)}) async-start(), calls=%async_computation.24 | async-start | bytes 442368
  917.5 221.9 %reduce-scatter.53.cloned.1.call-start = ((), (), s32[]{:S(2)}) async-start(), calls=%async_computation.22 | async-start | bytes 442368
  918.6 257.1 %reduce-scatter.45.cloned.1.call-start = ((), (), s32[]{:S(2)}) async-start(), calls=%async_computation.18 | async-start | bytes 73728
  920.0 292.8 %reduce-scatter.49.cloned.1.call-start = ((), (), s32[]{:S(2)}) async-start(), calls=%async_computation.20 | async-start | bytes 442368
  921.8 328.1 %reduce-scatter.51.cloned.1.call-start = ((), (), s32[]{:S(2)}) async-start(), calls=%async_computation.21 | async-start | bytes 442368
  923.6 367.0 %reduce-scatter.43.cloned.1.call-start = ((), (), s32[]{:S(2)}) async-start(), calls=%async_computation.17 | async-start | bytes 1327104
  926.8 403.8 %reduce-scatter.47.cloned.1.call-start = ((), (), s32[]{:S(2)}) async-start(), calls=%async_computation.19 | async-start | bytes 1327104
  931.8 430.2 %all-gather.10.cloned.1.call-start = ((), (), s32[]{:S(2)}) async-start(), calls=%async_computation.12 | async-start | bytes 2654208 | tf_op jit(solution)/shard_map/all_gather | solution.py:322
  952.4 440.4 %all-gather.14.cloned.1.call-start = ((), (), s32[]{:S(2)}) async-start(), calls=%async_computation.15 | async-start | bytes 2654208 | tf_op jit(solution)/shard_map/all_gather | solution.py:346
  1009.7 414.6 %all-gather.12.cloned.1.call-start = ((), (), s32[]{:S(2)}) async-start(), calls=%async_computation.14 | async-start | bytes 2654208 | tf_op jit(solution)/shard_map/all_gather | solution.py:340
  (102 other events, 505.8 us)
Sparse Core Ops, SparseCore 0:
  175.3 35.3 all-reduce.7
  221.4 36.7 all-reduce.9
  267.1 36.6 all-reduce.11
  355.6 19.6 reduce-scatter.60
  384.6 22.8 reduce-scatter.58
  412.9 39.2 all-reduce.13
  600.0 34.4 all-reduce.7
  645.2 36.7 all-reduce.9
  691.0 36.6 all-reduce.11
  779.4 19.6 reduce-scatter.60
  808.4 22.8 reduce-scatter.58
  836.7 39.2 all-reduce.13
Sparse Core Ops, SparseCore 1:
  902.2 47.5 reduce-scatter.40
  953.7 53.7 reduce-scatter.54
  1011.7 53.7 reduce-scatter.38
  1068.6 33.8 reduce-scatter.56
  1105.5 33.8 reduce-scatter.52
  1142.4 33.2 reduce-scatter.44
  1178.9 33.9 reduce-scatter.48
  1216.1 33.8 reduce-scatter.50
  1254.0 36.6 reduce-scatter.42
  1293.9 36.6 reduce-scatter.46
  1333.1 28.8 all-gather.9
  1364.0 28.8 all-gather.13
  1395.4 28.8 all-gather.11
where the time goes:
time: 1440 us
  waiting for transfers between devices  669 us (46%)
  matrix products  453 us (31%)
  local copies, waits for them, and re-layouts  124 us (9%)
  blocking collectives  109 us (8%)
  other arithmetic  54.2 us (4%)
  between operations  16.5 us (1%)
    unnamed x22, waiting for transfers between devices  269 us
    dot_general x6, matrix products, page_pass(): jnp.einsum('shij,ijr->shr', d_scores, chosen_rows(indices[kind_index]), p...  132 us
    dot_general x6, matrix products, page_pass(): jnp.einsum('ijr,shr->shij', picked, relation_grid_remainder[:, kind_index...  111 us
    dot_general x6, matrix products, page_pass(): jnp.einsum('ijr,shr->shij', picked, relation_grid_fine[:, kind_index], pr...  111 us
    unnamed x57, local copies, waits for them, and re-layouts  76.5 us
    psum x2, waiting for transfers between devices, page_pass(): lax.psum(jnp.einsum('her,hrk->hek', nonzero_neurons_coarse, shrink_projec...  71.2 us
    psum x2, waiting for transfers between devices, page_pass(): lax.psum(jnp.einsum('lxr,lrg->xg', attended_values, exit_matrix, preferre...  70 us
    psum x2, waiting for transfers between devices, page_pass(): lax.psum(input_terms.astype(jnp.bfloat16), 'head').astype(jnp.float32)  67 us
  transfers between devices with their start and end apart: 25, of which 23 were waited for; matrix products, arithmetic and copies ran while one was open for 13% of the time, Pallas kernels for 0%

commit v1 on v0

v1 whole, which is shorter than its diff:
```python
import functools

import jax
import jax.numpy as jnp
from jax import lax
from jax.experimental import pallas as pl
from jax.experimental.pallas import tpu as pltpu
from jax.sharding import Mesh, PartitionSpec as P

DH = 64
NBUCK = 128
HALF = 64
EPSILON = 1e-05
F32 = jnp.float32
BF16 = jnp.bfloat16
VMEM_BYTES = 56 * 1024 * 1024
NN = (((1,), (0,)), ((), ()))
NT = (((1,), (1,)), ((), ()))
TN = (((0,), (0,)), ((), ()))


def mm(left, right, dims=NN):
    return lax.dot_general(left, right, dims, preferred_element_type=F32)


def kernel_call(body, stream, operands, outs, flops, scratch=()):
    specs, arrays, moved = [], [], 0
    for array, per_stream in operands:
        if per_stream:
            rest = array.shape[1:]
            specs.append(
                pl.BlockSpec(
                    (None,) + rest, lambda g, s, n=len(rest): (s[0],) + (0,) * n
                )
            )
        else:
            rest = array.shape
            specs.append(pl.BlockSpec(rest, lambda g, s, n=len(rest): (0,) * n))
        arrays.append(array)
        size = array.dtype.itemsize
        for extent in rest:
            size *= extent
        moved += size
    out_specs = [
        pl.BlockSpec(shape, lambda g, s, n=len(shape): (0,) * n) for shape, _ in outs
    ]
    for shape, dtype in outs:
        size = jnp.dtype(dtype).itemsize
        for extent in shape:
            size *= extent
        moved += size
    return pl.pallas_call(
        body,
        out_shape=[jax.ShapeDtypeStruct(shape, dtype) for shape, dtype in outs],
        grid_spec=pltpu.PrefetchScalarGridSpec(
            num_scalar_prefetch=1,
            grid=(1,),
            in_specs=specs,
            out_specs=out_specs,
            scratch_shapes=list(scratch),
        ),
        compiler_params=pltpu.CompilerParams(
            dimension_semantics=("arbitrary",), vmem_limit_bytes=VMEM_BYTES
        ),
        cost_estimate=pl.CostEstimate(
            flops=flops, bytes_accessed=moved, transcendentals=0
        ),
    )(stream, *arrays)


def centred(rows):
    centre = rows - jnp.mean(rows, axis=-1, keepdims=True)
    spread = lax.rsqrt(jnp.mean(centre * centre, axis=-1, keepdims=True) + EPSILON)
    return centre * spread, spread


def norm_back(unit, spread, tilted):
    return spread * (
        tilted
        - jnp.mean(tilted, axis=-1, keepdims=True)
        - unit * jnp.mean(tilted * unit, axis=-1, keepdims=True)
    )


def pick(table_row, index):
    width = index.shape[1]
    table = jnp.broadcast_to(table_row, (index.shape[0], NBUCK))
    parts = [
        jnp.take_along_axis(
            table,
            index[:, at : at + NBUCK],
            axis=1,
            mode="promise_in_bounds",
        )
        for at in range(0, width, NBUCK)
    ]
    return jnp.concatenate(parts, axis=1)


def attention_kernel(
    s_ref,
    x_ref,
    sp_ref,
    w_ref,
    ws_ref,
    table_ref,
    rowidx_ref,
    colidx_ref,
    exit_ref,
    proj_ref,
    spat_ref,
    soft_ref,
    att_ref,
    mixed_ref,
    *,
    heads,
    block,
):
    x = x_ref[...]
    sp = sp_ref[...]
    for k in range(3):
        proj_ref[k] = mm(x, w_ref[k]).astype(BF16)
    for k in range(2):
        spat_ref[k] = mm(sp, ws_ref[k]).astype(BF16)
    length = x.shape[0]

    def step(at, carry):
        rows = pl.ds(pl.multiple_of(at * block, block), block)
        index = []
        for kind in range(3):
            own = colidx_ref[rows, kind : kind + 1]
            every = rowidx_ref[kind : kind + 1, :]
            index.append(jnp.clip(every - own, -HALF, HALF - 1) + HALF)
        for h in range(heads):
            cols = slice(h * DH, (h + 1) * DH)
            bias = pick(table_ref[0, h : h + 1, :], index[0])
            bias = bias + pick(table_ref[1, h : h + 1, :], index[1])
            bias = bias + pick(table_ref[2, h : h + 1, :], index[2])
            left = jnp.concatenate(
                [proj_ref[0, rows, cols], spat_ref[0, rows, cols]], axis=1
            )
            right = jnp.concatenate([proj_ref[1, :, cols], spat_ref[1, :, cols]], axis=1)
            scores = mm(left, right, NT) * (DH**-0.5) + bias
            top = jnp.max(scores, axis=-1, keepdims=True)
            raised = jnp.exp(scores - top)
            soft = raised / jnp.sum(raised, axis=-1, keepdims=True)
            soft_ref[h, rows, :] = soft
            att_ref[rows, cols] = mm(soft.astype(BF16), proj_ref[2, :, cols]).astype(BF16)
        return carry

    lax.fori_loop(0, length // block, step, 0)
    mixed_ref[...] = mm(att_ref[...], exit_ref[...]).astype(BF16)


def forward_kernel(
    s_ref,
    x_ref,
    mixed_ref,
    gain_ref,
    shift_ref,
    up_ref,
    hidden_ref,
    down_ref,
    low_ref,
    active_ref,
    slope_ref,
):
    unit, _ = centred(x_ref[...].astype(F32) + mixed_ref[...].astype(F32))
    normed = unit * gain_ref[0:1, :] + shift_ref[0:1, :]
    normed_low = normed.astype(BF16)
    total = None
    for part in range(up_ref.shape[0]):
        upper = mm(normed_low, up_ref[part]) + hidden_ref[part]
        phi = 0.5 * (1.0 + lax.erf(upper * (0.5**0.5)))
        slope_ref[part] = phi + upper * (
            jnp.exp(-0.5 * upper * upper) * (0.5 / jnp.pi) ** 0.5
        )
        active = (upper * phi).astype(BF16)
        active_ref[part] = active
        term = mm(active, down_ref[part])
        total = term if total is None else total + term
    low_ref[...] = total.astype(BF16)


def middle_kernel(
    s_ref,
    x_ref,
    mixed_ref,
    lowered_ref,
    cot_ref,
    gain_ref,
    shift_ref,
    bdown_ref,
    up_ref,
    down_ref,
    slope_ref,
    out_ref,
    hid_ref,
    second_ref,
    dlow_ref,
    dup_ref,
    sums_ref,
):
    unit, _ = centred(x_ref[...].astype(F32) + mixed_ref[...].astype(F32))
    normed = unit * gain_ref[0:1, :] + shift_ref[0:1, :]
    unit2, spread2 = centred(normed + lowered_ref[...].astype(F32) + bdown_ref[...])
    out_ref[...] = (unit2 * gain_ref[1:2, :] + shift_ref[1:2, :]).astype(BF16)
    cot = cot_ref[...].astype(F32)
    second = norm_back(unit2, spread2, cot * gain_ref[1:2, :])
    second_ref[...] = second
    sums_ref[...] = jnp.zeros_like(sums_ref)
    sums_ref[0:1, :] = jnp.sum(cot * unit2, axis=0, keepdims=True)
    sums_ref[1:2, :] = jnp.sum(cot, axis=0, keepdims=True)
    sums_ref[2:3, :] = jnp.sum(second, axis=0, keepdims=True)
    dlow = second.astype(BF16)
    dlow_ref[...] = dlow
    total = None
    for part in range(up_ref.shape[0]):
        dup = (mm(dlow, down_ref[part], NT) * slope_ref[part]).astype(BF16)
        dup_ref[part] = dup
        term = mm(dup, up_ref[part], NT)
        total = term if total is None else total + term
    hid_ref[...] = total.astype(BF16)


def ffn_grad_kernel(
    s_ref,
    x_ref,
    mixed_ref,
    gain_ref,
    shift_ref,
    active_ref,
    dlow_ref,
    dup_ref,
    grad_ref,
):
    unit, _ = centred(x_ref[...].astype(F32) + mixed_ref[...].astype(F32))
    normed_low = (unit * gain_ref[0:1, :] + shift_ref[0:1, :]).astype(BF16)
    width = x_ref.shape[1]
    grad_ref[0:width, :] = mm(normed_low, dup_ref[...], TN).astype(BF16)
    grad_ref[width : 2 * width, :] = mm(active_ref[...], dlow_ref[...], TN).astype(BF16)
    bias = jnp.sum(dup_ref[...].astype(F32), axis=0, keepdims=True)
    grad_ref[2 * width :, :] = jnp.broadcast_to(bias, (16, width)).astype(BF16)


def first_kernel(
    s_ref,
    x_ref,
    mixed_ref,
    second_ref,
    hid_ref,
    gain_ref,
    first_ref,
    dmix_ref,
    sums_ref,
):
    unit, spread = centred(x_ref[...].astype(F32) + mixed_ref[...].astype(F32))
    dnormed = second_ref[...] + hid_ref[...].astype(F32)
    first = norm_back(unit, spread, dnormed * gain_ref[0:1, :])
    first_ref[...] = first
    dmix_ref[...] = first.astype(BF16)
    sums_ref[...] = jnp.zeros_like(sums_ref)
    sums_ref[0:1, :] = jnp.sum(dnormed * unit, axis=0, keepdims=True)
    sums_ref[1:2, :] = jnp.sum(dnormed, axis=0, keepdims=True)


def backward_kernel(
    s_ref,
    dmix_ref,
    first_ref,
    exit_ref,
    soft_ref,
    proj_ref,
    spat_ref,
    w_ref,
    ws_ref,
    dscore_ref,
    dproj_ref,
    dspat_ref,
    dx_ref,
    dsp_ref,
    *,
    heads,
    block,
):
    length = dmix_ref.shape[0]
    scale = DH**-0.5
    datt = mm(dmix_ref[...], exit_ref[...], NT).astype(BF16)
    for h in range(heads):
        cols = slice(h * DH, (h + 1) * DH)
        value = proj_ref[2, :, cols]
        left = jnp.concatenate([proj_ref[0, :, cols], spat_ref[0, :, cols]], axis=1)
        right = jnp.concatenate([proj_ref[1, :, cols], spat_ref[1, :, cols]], axis=1)
        own = datt[:, cols]
        for at in range(0, length, block):
            soft = soft_ref[h, at : at + block, :]
            dsoft = mm(own[at : at + block], value, NT)
            inner = jnp.sum(soft * dsoft, axis=-1, keepdims=True)
            dscore_ref[h, at : at + block, :] = (soft * (dsoft - inner)).astype(BF16)
        dscore = dscore_ref[h]
        dleft = (mm(dscore, right) * scale).astype(BF16)
        dright = (mm(dscore, left, TN) * scale).astype(BF16)
        dproj_ref[0, :, cols] = dleft[:, :DH]
        dspat_ref[0, :, cols] = dleft[:, DH:]
        dproj_ref[1, :, cols] = dright[:, :DH]
        dspat_ref[1, :, cols] = dright[:, DH:]
        dproj_ref[2, :, cols] = mm(soft_ref[h].astype(BF16), own, TN).astype(BF16)
    total = first_ref[...]
    for k in range(3):
        total = total + mm(dproj_ref[k], w_ref[k], NT)
    dx_ref[...] = total.astype(BF16)
    dsp_ref[...] = (mm(dspat_ref[0], ws_ref[0], NT) + mm(dspat_ref[1], ws_ref[1], NT)).astype(BF16)


def attention_grad_kernel(
    s_ref,
    dmix_ref,
    x_ref,
    sp_ref,
    att_ref,
    dscore_ref,
    dproj_ref,
    dspat_ref,
    rowidx_ref,
    colidx_ref,
    wgrad_ref,
    wsgrad_ref,
    exitgrad_ref,
    tables_ref,
    *,
    heads,
):
    x = x_ref[...]
    sp = sp_ref[...]
    length = x.shape[0]
    for k in range(3):
        wgrad_ref[k] = mm(x, dproj_ref[k], TN).astype(BF16)
    for k in range(2):
        wsgrad_ref[k] = mm(sp, dspat_ref[k], TN).astype(BF16)
    exitgrad_ref[...] = mm(att_ref[...], dmix_ref[...], TN).astype(BF16)
    tables_ref[...] = jnp.zeros_like(tables_ref)
    lane = lax.broadcasted_iota(jnp.int32, (1, NBUCK), 1)
    for kind in range(3):
        extent = length if kind == 0 else NBUCK
        own = colidx_ref[:, kind : kind + 1]
        level = lax.broadcasted_iota(jnp.int32, (length, extent), 1)
        chosen = (own == level).astype(BF16)
        place = own - HALF + lax.broadcasted_iota(jnp.int32, (length, NBUCK), 1)
        turn = place & (NBUCK - 1)
        piece = place >> 7
        for h in range(heads):
            spread = mm(dscore_ref[h], chosen)
            window = jnp.zeros((length, NBUCK), F32)
            for q in range(extent // NBUCK):
                part = jnp.take_along_axis(
                    spread[:, q * NBUCK : (q + 1) * NBUCK],
                    turn,
                    axis=1,
                    mode="promise_in_bounds",
                )
                window = window + jnp.where(piece == q, part, 0.0)
            row = jnp.sum(window, axis=0, keepdims=True)
            row = jnp.where((lane > 0) & (lane < NBUCK - 1), row, 0.0)
            least = jnp.sum(jnp.where(level <= own - HALF, spread, 0.0), axis=0, keepdims=True)
            most = jnp.sum(jnp.where(level >= own + HALF - 1, spread, 0.0), axis=0, keepdims=True)
            row = row + jnp.where(lane == 0, jnp.sum(least, axis=1, keepdims=True), 0.0)
            row = row + jnp.where(
                lane == NBUCK - 1, jnp.sum(most, axis=1, keepdims=True), 0.0
            )
            tables_ref[kind * heads + h : kind * heads + h + 1, :] = row


def swap(value, axis):
    return lax.ppermute(value, axis, [(0, 1), (1, 0)])


def shards(
    tokens,
    spatial,
    positions,
    boxes,
    query_key_value_weight,
    w_spatial,
    rel_tables,
    exit_matrix,
    ln_gains,
    ln_shifts,
    up_weight,
    hidden_bias,
    shrink_projection_array,
    b_down,
    cotangent,
):
    heads = rel_tables.shape[2]
    rows = tokens.shape[2]
    width = tokens.shape[3]
    inner = query_key_value_weight.shape[3]
    hidden = up_weight.shape[2]
    length = 4 * rows
    page = lax.axis_index("y")
    core = lax.axis_index("core")
    head = lax.axis_index("head")
    stream = core.reshape(1)

    def to_page(array):
        mine = lax.dynamic_index_in_dim(array, page, 1, keepdims=False)
        other = lax.dynamic_index_in_dim(array, 1 - page, 1, keepdims=False)
        return jnp.stack([mine, swap(other, "y")], axis=1)

    def to_stream(array):
        mine = lax.dynamic_index_in_dim(array, core, 0, keepdims=False)
        other = lax.dynamic_index_in_dim(array, 1 - core, 0, keepdims=False)
        return jnp.concatenate([mine, swap(other, "core")], axis=0).reshape(length, -1)

    x = to_stream(to_page(tokens))
    sp_half = to_page(spatial[None])[0]
    sp = jnp.concatenate([sp_half, swap(sp_half, "core")], axis=0).reshape(length, width)
    places = jnp.concatenate([positions[None], boxes], axis=0)
    places = to_page(places)
    places = jnp.concatenate([places, swap(places, "core")], axis=1).reshape(3, length)
    rowidx = jnp.pad(places, ((0, 5), (0, 0)))
    colidx = rowidx.T
    cot = to_stream(to_page(cotangent))

    own = (True,)
    whole = (False,)
    attention_flops = 2 * length * (width * inner * 6 + heads * length * DH * 3)
    proj, spat, soft, att, mixed_part = kernel_call(
        functools.partial(attention_kernel, heads=heads, block=128),
        stream,
        [
            (x, False),
            (sp, False),
            (query_key_value_weight, True),
            (w_spatial, False),
            (rel_tables, True),
            (rowidx, False),
            (colidx, False),
            (exit_matrix, True),
        ],
        [
            ((3, length, inner), BF16),
            ((2, length, inner), BF16),
            ((heads, length, length), F32),
            ((length, inner), BF16),
            ((length, width), BF16),
        ],
        attention_flops,
    )
    half = length // 2
    mixed_half = mixed_part[:half].astype(F32) + swap(mixed_part[half:], "core").astype(F32)
    mixed_half = lax.psum(mixed_half.astype(BF16), "head")
    mixed = jnp.concatenate([mixed_half, swap(mixed_half, "core")], axis=0)

    up = up_weight[:, None]
    down = shrink_projection_array[:, None]
    hidden_rows = hidden_bias[:, None, None]
    matrix_flops = 2 * length * width * hidden
    low_part, active, slope = kernel_call(
        forward_kernel,
        stream,
        [
            (x, False),
            (mixed, False),
            (ln_gains, True),
            (ln_shifts, True),
            (up, True),
            (hidden_rows, True),
            (down, True),
        ],
        [
            ((length, width), BF16),
            ((1, length, hidden), BF16),
            ((1, length, hidden), F32),
        ],
        2 * matrix_flops,
    )
    lowered = lax.psum(low_part, "head")
    out, hid_part, second, dlow, dup, sums_two = kernel_call(
        middle_kernel,
        stream,
        [
            (x, False),
            (mixed, False),
            (lowered, False),
            (cot, False),
            (ln_gains, True),
            (ln_shifts, True),
            (b_down[:, None], True),
            (up, True),
            (down, True),
            (slope, False),
        ],
        [
            ((length, width), BF16),
            ((length, width), BF16),
            ((length, width), F32),
            ((length, width), BF16),
            ((1, length, hidden), BF16),
            ((8, width), F32),
        ],
        2 * matrix_flops,
    )
    hid = lax.psum(hid_part, "head")
    (ffn_grad,) = kernel_call(
        ffn_grad_kernel,
        stream,
        [
            (x, False),
            (mixed, False),
            (ln_gains, True),
            (ln_shifts, True),
            (active[0], False),
            (dlow, False),
            (dup[0], False),
        ],
        [((2 * width + 16, hidden), BF16)],
        2 * matrix_flops,
    )
    ffn_grad = lax.psum(ffn_grad, ("batch", "y"))
    first, dmix_part, sums_one = kernel_call(
        first_kernel,
        stream,
        [
            (x, False),
            (mixed, False),
            (second, False),
            (hid, False),
            (ln_gains, True),
        ],
        [((length, width), F32), ((length, width), BF16), ((8, width), F32)],
        0,
    )
    other_dmix = swap(dmix_part, "core")
    other_dmix = jnp.concatenate([other_dmix[half:], other_dmix[:half]], axis=0)
    dmix = (first + other_dmix.astype(F32)).astype(BF16)

    first_once = jnp.where(head == 0, first, 0.0)
    dscore, dproj, dspat, dx, dsp = kernel_call(
        functools.partial(backward_kernel, heads=heads, block=128),
        stream,
        [
            (dmix, False),
            (first_once, False),
            (exit_matrix, True),
            (soft, False),
            (proj, False),
            (spat, False),
            (query_key_value_weight, True),
            (w_spatial, False),
        ],
        [
            ((heads, length, length), BF16),
            ((3, length, inner), BF16),
            ((2, length, inner), BF16),
            ((length, width), BF16),
            ((length, width), BF16),
        ],
        2 * length * (width * inner * 6 + heads * length * DH * 6),
    )
    dx_mine, dx_other = dx[:half], swap(dx[half:], "core")
    dsp_mine = (dsp[:half].astype(F32) + swap(dsp[half:], "core").astype(F32)).astype(BF16)
    ends = jnp.stack([dx_mine, dx_other, dsp_mine]).reshape(3, 2, rows, width)
    out_ends = jnp.stack([out[:half], swap(out[half:], "core")]).reshape(2, 2, rows, width)

    def to_owner(array):
        other = swap(array[:, 1], "y")
        return jnp.stack([array[:, 0], other], axis=1)

    def in_place(array, index, axis):
        return jnp.where(index == 0, array, jnp.flip(array, axis))

    ends = lax.psum(to_owner(ends), "head")
    ends = in_place(ends, page, 1)
    grad_tokens = in_place(ends[:2], core, 0).astype(F32)
    grad_spatial = ends[2].astype(F32)
    output = in_place(in_place(to_owner(out_ends), page, 1), core, 0)

    wgrad, wsgrad, exitgrad, tables = kernel_call(
        functools.partial(attention_grad_kernel, heads=heads),
        stream,
        [
            (dmix, False),
            (x, False),
            (sp, False),
            (att, False),
            (dscore, False),
            (dproj, False),
            (dspat, False),
            (rowidx, False),
            (colidx, False),
        ],
        [
            ((3, width, inner), BF16),
            ((2, width, inner), BF16),
            ((inner, width), BF16),
            ((16, NBUCK), F32),
        ],
        2 * length * (width * inner * 6 + heads * length * width),
    )
    part = width // lax.axis_size("head")
    sums = jnp.stack([sums_one[0], sums_two[0], sums_one[1], sums_two[1], sums_two[2]])
    sums = lax.dynamic_slice_in_dim(sums, head * part, part, 1)
    tables = tables[: 3 * heads].reshape(3, heads, NBUCK)
    wsgrad = (wsgrad.astype(F32) + swap(wsgrad, "core").astype(F32)).astype(BF16)
    wgrad, wsgrad, exitgrad, tables, sums = lax.psum(
        (wgrad, wsgrad, exitgrad, tables, sums), ("batch", "y")
    )

    def both(array):
        return in_place(jnp.stack([array, swap(array, "core")]), core, 0)

    grad_qkv = both(wgrad).astype(F32)
    grad_exit = both(exitgrad).astype(F32)
    grad_tables = both(tables)
    sums = both(sums)
    ffn = both(ffn_grad).astype(F32)
    return (
        output,
        grad_tokens,
        grad_spatial,
        grad_qkv,
        wsgrad.astype(F32),
        grad_tables,
        grad_exit,
        sums[:, 0:2],
        sums[:, 2:4],
        ffn[:, :width],
        ffn[:, 2 * width],
        ffn[:, width : 2 * width],
        sums[:, 4],
    )


def solution(mesh):
    devices = mesh.devices
    batch, seq, head = devices.shape
    fine = Mesh(
        devices.reshape(batch, seq // 2, 2, head), ("batch", "y", "core", "head")
    )
    seq_axes = ("y", "core")
    return jax.shard_map(
        shards,
        mesh=fine,
        in_specs=(
            P(None, "batch", seq_axes, None),
            P("batch", seq_axes, None),
            P("batch", seq_axes),
            P(None, "batch", seq_axes),
            P(None, None, None, "head"),
            P(None, None, "head"),
            P(None, None, "head", None),
            P(None, "head", None),
            P(),
            P(),
            P(None, None, "head"),
            P(None, "head"),
            P(None, "head", None),
            P(),
            P(None, "batch", seq_axes, None),
        ),
        out_specs=(
            P(None, "batch", seq_axes, None),
            P(None, "batch", seq_axes, None),
            P("batch", seq_axes, None),
            P(None, None, None, "head"),
            P(None, None, "head"),
            P(None, None, "head", None),
            P(None, "head", None),
            P(None, None, "head"),
            P(None, None, "head"),
            P(None, None, "head"),
            P(None, "head"),
            P(None, "head", None),
            P(None, "head"),
        ),
        check_vma=False,
    )
```

time: 1440 us -> 464 us (0.32)
  matrix products: 453 us -> 0 us
  waiting for transfers between devices: 669 us -> 300 us
  blocking collectives: 109 us -> 16.3 us
  local copies, waits for them, and re-layouts: 124 us -> 35.4 us
  Pallas kernels: 0 us -> 59 us
  other arithmetic: 54.2 us -> 26.6 us
    dot_general x60 -> x0, matrix products: 428 us -> none  [the longest x6 132 us: page_pass(): jnp.einsum('shij,ijr->shr', d_scores, chosen_rows(indices[kind_index]), p...]
    unnamed x22 -> x5, waiting for transfers between devices: 269 us -> 0.08 us
    all_gather x13 -> x0, blocking collectives: 109 us -> none  [the longest x2 17.4 us: page_pass(): lax.all_gather(projected_rows[:, 1:], 'seq', axis=2, tiled=True)]
    all_gather x3 -> x0, waiting for transfers between devices: 65.5 us -> none  [the longest x1 23.9 us: shards(): lax.all_gather(totals[6].astype(jnp.bfloat16), ('batch', 'seq'), axis=1,...]
    ppermute x0 -> x22, waiting for transfers between devices: none -> 61.4 us  [swap(): return lax.ppermute(value, axis, [(0, 1), (1, 0)])]
    unnamed x57 -> x55, local copies, waits for them, and re-layouts: 76.5 us -> 16.6 us
    pallas_call x0 -> x7, Pallas kernels: none -> 59 us  [kernel_call(): pl.pallas_call(body, out_shape=[jax.ShapeDtypeStruct(shape, dtype) for sh...]
    reduce_scatter x1 -> x0, waiting for transfers between devices: 55.8 us -> none  [shards(): lax.psum_scatter(totals[6], ('batch', 'seq'), scatter_dimension=1, tiled=...]
  transfers between devices with their start and end apart: 25 -> 27, of which waited for: 23 -> 12; matrix products, arithmetic and copies ran while one was open for 13% -> 9% of each run, Pallas kernels for 0% -> 2%
where the time goes in v1:
time: 464 us; the launch traced here: 463 us
  waiting for transfers between devices  300 us (65%)
  Pallas kernels  59 us (13%)
  local copies, waits for them, and re-layouts  35.4 us (8%)
  other arithmetic  26.6 us (6%)
  blocking collectives  16.3 us (4%)
  between operations  14.2 us (3%)
  starting transfers between devices  12.4 us (3%)
    psum x1, waiting for transfers between devices, shards(): lax.psum((wgrad, wsgrad, exitgrad, tables, sums), ('batch', 'y'))  62.2 us
    ppermute x22, waiting for transfers between devices, swap(): return lax.ppermute(value, axis, [(0, 1), (1, 0)])  61.4 us
    pallas_call x7, Pallas kernels, kernel_call(): pl.pallas_call(body, out_shape=[jax.ShapeDtypeStruct(shape, dtype) for sh...  59 us
    psum x1, waiting for transfers between devices, shards(): ends = lax.psum(to_owner(ends), 'head')  57.1 us
    psum x1, waiting for transfers between devices, shards(): hid = lax.psum(hid_part, 'head')  42.9 us
    psum x1, waiting for transfers between devices, shards(): mixed_half = lax.psum(mixed_half.astype(BF16), 'head')  38.7 us
    psum x1, waiting for transfers between devices, shards(): lowered = lax.psum(low_part, 'head')  37.2 us
    unnamed x55, local copies, waits for them, and re-layouts  16.6 us
  transfers between devices with their start and end apart: 27, of which 12 were waited for; matrix products, arithmetic and copies ran while one was open for 9% of the time, Pallas kernels for 2%

profile of v1, /device:TPU:0, one launch (start us, length us, event | category | flops | bytes accessed | tf_op | source)
XLA Modules:
  0.0 463.4 jit_solution(4485744233710873933)
XLA Ops:
  7.3 2.0 dynamic-slice_bitcast_fusion.1
  9.2 3.0 collective-permute-start
  12.4 2.0 collective-permute-start.4
  14.4 11.3 %collective-permute-done.2 = bf16[1,128,768]{2,1,0:T(8,128)(2,1)S(1)} collective-permute-done((bf16[1,128,768]{2,1,0:T(8,128)(2,1)S(1)}, bf16[1,128,768]{2,1,0:T(8,128)(2,1)S(1)}, u32[]{:S(2)}, u32[]{:S(2)}) %collective-permute-start.2) | collective-permute-done | bytes 196640 | tf_op jit(solution)/shard_map/ppermute | solution.py:374
  28.4 2.4 copy.67.w_ref
  30.8 1.2 copy.68.ws_ref
  34.9 1.9 pad_maximum_fusion.5
  37.8 17.6 %shard_map.246 = (bf16[3,512,192]{2,1,0:T(8,128)(2,1)}, bf16[2,512,192]{2,1,0:T(8,128)(2,1)}, f32[3,512,512]{2,1,0:T(8,128)}, bf16[512,192]{1,0:T(8,128)(2,1)}, bf16[512,768]{1,0:T(8,128)(2,1)}) custom-call(s32[1]{0:T(128)} %bitcast.s_ref, bf16[512,768]{1,0:T(8,128)(2,1)} %bitcast.81, bf16[512,768]{1,0:T(8,128)(2,1)} %bitcast.93, ...), custom_call_target="tpu_custom_call" | custom-call | flops 1207959552 | bytes 8491520 | tf_op jit(solution)/shard_map/pallas_call | solution.py:52
  55.4 1.1 slice.84
  57.1 1.3 collective-permute-done.6
  58.4 1.8 add_convert_fusion.3
  60.3 38.7 %all-reduce.9.cloned.1.call-done = bf16[256,768]{1,0:T(8,128)(2,1)} async-done(((bf16[256,768]{1,0:T(8,128)(2,1)}), bf16[256,768]{1,0:T(8,128)(2,1)}) %all-reduce.9.cloned.1.call-update) | async-done | bytes 393232 | tf_op jit(solution)/shard_map/psum | solution.py:452
  99.1 1.3 collective-permute-start.8
  102.0 5.4 %shard_map.247 = (bf16[512,768]{1,0:T(8,128)(2,1)}, bf16[1,512,768]{2,1,0:T(8,128)(2,1)}, f32[1,512,768]{2,1,0:T(8,128)}) custom-call(s32[1]{0:T(128)} %bitcast.s_ref, bf16[512,768]{1,0:T(8,128)(2,1)} %bitcast.82, bf16[512,768]{1,0:T(8,128)(2,1)} %copy-done, f32[2,2,768]{2,1,0:T(2,128)} %gain_ref.7, f32[2,2,768]{2,1,0:T(2,128)} %shift_ref.5, ...), custom_call_target="tpu_custom_call" | custom-call | flops 1207959552 | bytes 7093248 | tf_op jit(solution)/shard_map/pallas_call | solution.py:52
  107.5 3.2 collective-permute-done.8
  111.4 1.1 collective-permute-done.9
  112.5 1.0 pad_maximum_fusion.6
  113.5 37.2 %all-reduce.11.cloned.1.call-done.lowered_ref = bf16[512,768]{1,0:T(8,128)(2,1)} async-done(((bf16[512,768]{1,0:T(8,128)(2,1)}), bf16[512,768]{1,0:T(8,128)(2,1)}) %all-reduce.11.cloned.1.call-update) | async-done | bytes 786448 | tf_op jit(solution)/shard_map/psum | solution.py:478
  150.7 7.9 %shard_map.248 = (bf16[512,768]{1,0:T(8,128)(2,1)}, bf16[512,768]{1,0:T(8,128)(2,1)}, f32[512,768]{1,0:T(8,128)}, bf16[512,768]{1,0:T(8,128)(2,1)}, bf16[1,512,768]{2,1,0:T(8,128)(2,1)}, /*index=5*/f32[8,768]{1,0:T(8,128)}) custom-call(s32[1]{0:T(128)} %bitcast.s_ref, bf16[512,768]{1,0:T(8,128)(2,1)} %bitcast.83, bf16[512,768]{1,0:T(8,128)(2,1)} %copy-done, ...), custom_call_target="tpu_custom_call" | custom-call | flops 1207959552 | bytes 11836416 | tf_op jit(solution)/shard_map/pallas_call | solution.py:52
  158.9 42.9 %all-reduce.13.cloned.1.call-done.hid_ref = bf16[512,768]{1,0:T(8,128)(2,1)} async-done(((bf16[512,768]{1,0:T(8,128)(2,1)}), bf16[512,768]{1,0:T(8,128)(2,1)}) %all-reduce.13.cloned.1.call-update) | async-done | bytes 786448 | tf_op jit(solution)/shard_map/psum | solution.py:504
  201.8 4.8 %shard_map.249 = (f32[512,768]{1,0:T(8,128)}, bf16[512,768]{1,0:T(8,128)(2,1)}, f32[8,768]{1,0:T(8,128)}) custom-call(s32[1]{0:T(128)} %bitcast.s_ref, bf16[512,768]{1,0:T(8,128)(2,1)} %bitcast.84, bf16[512,768]{1,0:T(8,128)(2,1)} %copy-done, f32[512,768]{1,0:T(8,128)} %get-tuple-element.43.second_ref, ...), custom_call_target="tpu_custom_call" | custom-call | bytes 6322176 | tf_op jit(solution)/shard_map/pallas_call | solution.py:52
  206.6 2.5 collective-permute-done.12
  209.1 1.7 broadcast_select_fusion
  210.8 8.7 %shard_map.250 = (bf16[3,512,512]{2,1,0:T(8,128)(2,1)}, bf16[3,512,192]{2,1,0:T(8,128)(2,1)}, bf16[2,512,192]{2,1,0:T(8,128)(2,1)}, bf16[512,768]{1,0:T(8,128)(2,1)}, bf16[512,768]{1,0:T(8,128)(2,1)}) custom-call(s32[1]{0:T(128)} %bitcast.s_ref, bf16[512,768]{1,0:T(8,128)(2,1)} %get-tuple-element.113.dmix_ref, f32[512,768]{1,0:T(8,128)} %get-tuple-element.112.first_ref, ...), custom_call_target="tpu_custom_call" | custom-call | flops 1509949440 | bytes 12386304 | tf_op jit(solution)/shard_map/pallas_call | solution.py:52
  219.5 8.9 %shard_map.251 = (bf16[3,768,192]{2,1,0:T(8,128)(2,1)}, bf16[2,768,192]{2,1,0:T(8,128)(2,1)}, bf16[192,768]{1,0:T(8,128)(2,1)}, f32[16,128]{1,0:T(8,128)}) custom-call(s32[1]{0:T(128)} %bitcast.s_ref, bf16[512,768]{1,0:T(8,128)(2,1)} %get-tuple-element.113.dmix_ref, bf16[512,768]{1,0:T(8,128)(2,1)} %bitcast.85, bf16[512,768]{1,0:T(8,128)(2,1)} %bitcast.94, ...), custom_call_target="tpu_custom_call" | custom-call | flops 2113929216 | bytes 6922240 | tf_op jit(solution)/shard_map/pallas_call | solution.py:52
  228.4 1.4 copy.83
  230.0 5.7 %shard_map.252 = bf16[1552,768]{1,0:T(8,128)(2,1)} custom-call(s32[1]{0:T(128)} %bitcast.s_ref, bf16[512,768]{1,0:T(8,128)(2,1)} %bitcast.86, bf16[512,768]{1,0:T(8,128)(2,1)} %copy-done, f32[2,2,768]{2,1,0:T(2,128)} %gain_ref.7, f32[2,2,768]{2,1,0:T(2,128)} %shift_ref.5, bf16[512,768]{1,0:T(8,128)(2,1)} %bitcast.102, ...), custom_call_target="tpu_custom_call" | custom-call | flops 1207959552 | bytes 6328320 | tf_op jit(solution)/shard_map/pallas_call | solution.py:52
  236.9 1.1 add_convert_fusion
  238.0 1.0 copy-done.6
  243.1 1.1 fusion.5
  244.2 1.6 collective-permute-start.11
  246.7 17.9 %collective-permute-done.11 = bf16[2,128,768]{2,1,0:T(8,128)(2,1)S(1)} collective-permute-done((bf16[2,128,768]{2,1,0:T(8,128)(2,1)S(1)}, bf16[2,128,768]{2,1,0:T(8,128)(2,1)S(1)}, u32[]{:S(2)}, u32[]{:S(2)}) %collective-permute-start.11) | collective-permute-done | bytes 393248 | tf_op jit(solution)/shard_map/ppermute | solution.py:374
  265.7 24.0 %collective-permute-done.15 = bf16[3,128,768]{2,1,0:T(8,128)(2,1)S(1)} collective-permute-done((bf16[3,128,768]{2,1,0:T(8,128)(2,1)S(1)}, bf16[3,128,768]{2,1,0:T(8,128)(2,1)S(1)}, u32[]{:S(2)}, u32[]{:S(2)}) %collective-permute-start.15) | collective-permute-done | bytes 589856 | tf_op jit(solution)/shard_map/ppermute | solution.py:374
  289.7 1.1 pad_maximum_fusion.3
  290.9 16.3 %all-reduce.1 = (f32[3,3,128]{2,1,0:T(4,128)S(1)}, f32[5,192]{1,0:T(8,128)S(1)}) all-reduce(f32[3,3,128]{2,1,0:T(4,128)S(1)} %reshape.66, f32[5,192]{1,0:T(8,128)S(1)} %fusion.18), channel_id=1, replica_groups=mesh['batch'=2,'y'=2,'core'=2,'head'=4] {'batch','y'}, use_global_device_ids=true, to_apply=%region_6.7 | all-reduce | flops 2112 | bytes 16896 | tf_op jit(solution)/shard_map/psum | solution.py:606
  307.2 1.0 reverse_select_fusion.4
  308.7 62.2 %all-reduce.17.cloned.1.call-done = (bf16[2,768,192]{2,1,0:T(8,128)(2,1)}, bf16[3,768,192]{2,1,0:T(8,128)(2,1)}, bf16[192,768]{1,0:T(8,128)(2,1)}, bf16[1552,768]{1,0:T(8,128)(2,1)}) async-done(((bf16[2,768,192]{2,1,0:T(8,128)(2,1)}, bf16[3,768,192]{2,1,0:T(8,128)(2,1)}, bf16[192,768]{1,0:T(8,128)(2,1)}, bf16[1552,768]{1,0:T(8,128)(2,1)}), (bf16[2,768,192]{2,1,0:T(8,128)(2,1)}, ...) | async-done | bytes 4153360 | tf_op jit(solution)/shard_map/psum | solution.py:606
  372.7 57.1 %all-reduce.15.cloned.1.call-done = bf16[3,2,128,768]{3,2,1,0:T(8,128)(2,1)} async-done(((bf16[3,2,128,768]{3,2,1,0:T(8,128)(2,1)}), bf16[3,2,128,768]{3,2,1,0:T(8,128)(2,1)}) %all-reduce.15.cloned.1.call-update) | async-done | bytes 1179664 | tf_op jit(solution)/shard_map/psum | solution.py:573
  429.8 1.9 reverse_select_fusion.2
  431.9 1.3 copy.81
  434.6 1.3 fusion.2
  436.0 1.3 copy.86
  437.2 1.0 pad_maximum_fusion.8
  438.3 1.1 fusion.3
  440.4 2.6 fusion.1
  443.1 5.8 %copy.85 = f32[2,3,768,192]{2,3,1,0:T(8,128)} copy(f32[2,3,768,192]{3,2,1,0:T(8,128)} %fusion.1) | data formatting | bytes 7077888
  448.8 2.1 pad_maximum_fusion
  451.7 4.6 fusion.22
  (135 shorter events, 23.8 us)
Async XLA Ops:
  7.2 5.0 %copy-start.12 = (bf16[2,128,768]{2,1,0:T(8,128)(2,1)S(1)}, bf16[2,128,768]{2,1,0:T(8,128)(2,1)}, u32[]{:S(2)}) copy-start(bf16[2,128,768]{2,1,0:T(8,128)(2,1)} %param.16) | copy-start | bytes 1179652
  7.2 5.1 %copy-start.20 = (s32[2,2,128]{2,1,0:T(2,128)S(1)}, s32[2,2,128]{2,1,0:T(2,128)}, u32[]{:S(2)}) copy-start(s32[2,2,128]{2,1,0:T(2,128)} %param.18) | copy-start | bytes 6148
  7.2 5.1 %copy-start.21 = (s32[2,128]{1,0:T(2,128)S(1)}, s32[2,128]{1,0:T(2,128)}, u32[]{:S(2)}) copy-start(s32[2,128]{1,0:T(2,128)} %param.17) | copy-start | bytes 3076
  7.2 91.8 %all-reduce.9.cloned.1.call-start = ((), (), s32[]{:S(2)}) async-start(), calls=%async_computation | async-start | bytes 786432 | tf_op jit(solution)/shard_map/psum | solution.py:452
  9.2 19.2 %copy-start.4 = (bf16[2,3,768,192]{2,3,1,0:T(8,128)(2,1)S(1)}, bf16[2,3,768,192]{2,3,1,0:T(8,128)(2,1)}, u32[]{:S(2)}) copy-start(bf16[2,3,768,192]{2,3,1,0:T(8,128)(2,1)} %param.19) | copy-start | bytes 5308420
  9.2 16.6 %collective-permute-start = (bf16[2,128,768]{2,1,0:T(8,128)(2,1)}, bf16[2,128,768]{2,1,0:T(8,128)(2,1)S(1)}, u32[]{:S(2)}, u32[]{:S(2)}) collective-permute-start(bf16[2,128,768]{2,1,0:T(8,128)(2,1)} %get-tuple-element.130), channel_id=1, source_target_pairs={{0,8},{8,0},{1,9},{9,1},{2,10},{10,2},{3,11},{11,3},{4,12},{12,4},... | collective-permute-start | bytes 1179656 | tf_op jit(solution)/shard_map/ppermute | solution.py:374
  12.2 13.5 %collective-permute-start.2 = (bf16[1,128,768]{2,1,0:T(8,128)(2,1)S(1)}, bf16[1,128,768]{2,1,0:T(8,128)(2,1)S(1)}, u32[]{:S(2)}, u32[]{:S(2)}) collective-permute-start(bf16[1,128,768]{2,1,0:T(8,128)(2,1)S(1)} %get-tuple-element.133), channel_id=1, source_target_pairs={{0,8},{8,0},{1,9},{9,1},{2,10},{10,2},{3,11},{11,3},{4,12},{12,4},... | collective-permute-start | bytes 589832 | tf_op jit(solution)/shard_map/ppermute | solution.py:374
  12.4 14.8 %collective-permute-start.4 = (s32[3,128]{1,0:T(4,128)S(1)}, s32[3,128]{1,0:T(4,128)S(1)}, u32[]{:S(2)}, u32[]{:S(2)}) collective-permute-start(s32[3,128]{1,0:T(4,128)S(1)} %get-tuple-element.139), channel_id=1, source_target_pairs={{0,8},{8,0},{1,9},{9,1},{2,10},{10,2},{3,11},{11,3},{4,12},{12,4},... | collective-permute-start | bytes 4616 | tf_op jit(solution)/shard_map/ppermute | solution.py:374
  25.8 9.1 %collective-permute-start.3 = (bf16[2,128,768]{2,1,0:T(8,128)(2,1)S(1)}, bf16[2,128,768]{2,1,0:T(8,128)(2,1)}, u32[]{:S(2)}, u32[]{:S(2)}) collective-permute-start(bf16[2,128,768]{2,1,0:T(8,128)(2,1)S(1)} %maximum_bitcast_fusion), channel_id=1, source_target_pairs={{0,4},{4,0},{1,5},{5,1},{2,6},{6,2},{3,7},{7,3},{8,12},{12,8},{9,1... | collective-permute-start | bytes 1179656 | tf_op jit(solution)/shard_map/ppermute | solution.py:374
  26.7 10.1 %collective-permute-start.1 = (bf16[2,128,768]{2,1,0:T(8,128)(2,1)}, bf16[2,128,768]{2,1,0:T(8,128)(2,1)S(1)}, u32[]{:S(2)}, u32[]{:S(2)}) collective-permute-start(bf16[2,128,768]{2,1,0:T(8,128)(2,1)} %get-tuple-element.129), channel_id=1, source_target_pairs={{0,4},{4,0},{1,5},{5,1},{2,6},{6,2},{3,7},{7,3},{8,12},{12,8},{9,1... | collective-permute-start | bytes 1179656 | tf_op jit(solution)/shard_map/ppermute | solution.py:374
  28.4 2.4 copy-start.11
  28.4 3.6 copy-start.15
  28.4 4.2 collective-permute-start.5
  55.4 43.6 %copy-start.9 = (bf16[2,2,128,768]{3,2,1,0:T(8,128)(2,1)S(1)}, bf16[2,2,128,768]{3,2,1,0:T(8,128)(2,1)}, u32[]{:S(2)}) copy-start(bf16[2,2,128,768]{3,2,1,0:T(8,128)(2,1)} %param.29) | copy-start | bytes 2359300
  56.5 43.9 %copy-start.18 = (f32[2,768]{1,0:T(2,128)S(1)}, f32[2,768]{1,0:T(2,128)}, u32[]{:S(2)}) copy-start(f32[2,768]{1,0:T(2,128)} %param.26) | copy-start | bytes 18436
  56.5 1.9 collective-permute-start.6
  60.3 90.5 %all-reduce.11.cloned.1.call-start = ((), (), s32[]{:S(2)}) async-start(), calls=%async_computation.1 | async-start | bytes 1572864 | tf_op jit(solution)/shard_map/psum | solution.py:478
  99.0 2.0 copy-start.13
  99.0 2.0 collective-permute-start.7
  99.1 11.6 %collective-permute-start.8 = (bf16[2,128,768]{2,1,0:T(8,128)(2,1)S(1)}, bf16[2,128,768]{2,1,0:T(8,128)(2,1)S(1)}, u32[]{:S(2)}, u32[]{:S(2)}) collective-permute-start(bf16[2,128,768]{2,1,0:T(8,128)(2,1)S(1)} %get-tuple-element.126), channel_id=1, source_target_pairs={{0,8},{8,0},{1,9},{9,1},{2,10},{10,2},{3,11},{11,3},{4,12},{12,4},... | collective-permute-start | bytes 1179656 | tf_op jit(solution)/shard_map/ppermute | solution.py:374
  101.1 0.9 copy-start
  107.4 3.4 copy-start.19
  107.4 94.3 %all-reduce.13.cloned.1.call-start = ((), (), s32[]{:S(2)}) async-start(), calls=%async_computation.2 | async-start | bytes 1572864 | tf_op jit(solution)/shard_map/psum | solution.py:504
  110.7 1.8 collective-permute-start.9
  158.6 212.3 %all-reduce.17.cloned.1.call-start = ((), (), s32[]{:S(2)}) async-start(), calls=%async_computation.4 | async-start | bytes 9289728 | tf_op jit(solution)/shard_map/psum | solution.py:606
  206.6 2.6 copy-start.5
  206.6 2.5 collective-permute-start.12
  229.8 5.9 %collective-permute-start.17 = (bf16[2,768,192]{1,2,0:T(8,128)(2,1)S(1)}, bf16[2,768,192]{1,2,0:T(8,128)(2,1)S(1)}, u32[]{:S(2)}, u32[]{:S(2)}) collective-permute-start(bf16[2,768,192]{1,2,0:T(8,128)(2,1)S(1)} %copy.83), channel_id=1, source_target_pairs={{0,4},{4,0},{1,5},{5,1},{2,6},{6,2},{3,7},{7,3},{8,12},{12,8},{9,1... | collective-permute-start | bytes 1769480 | tf_op jit(solution)/shard_map/ppermute | solution.py:374
  235.7 1.1 copy-start.2
  237.9 1.1 copy-start.6
  237.9 2.3 copy-start.8
  238.0 2.5 copy-start.7
  238.0 191.9 %all-reduce.15.cloned.1.call-start = ((), (), s32[]{:S(2)}) async-start(), calls=%async_computation.3 | async-start | bytes 2359296 | tf_op jit(solution)/shard_map/psum | solution.py:573
  239.9 3.3 collective-permute-start.10
  240.3 5.6 %collective-permute-start.14 = (bf16[256,768]{1,0:T(8,128)(2,1)S(1)}, bf16[256,768]{1,0:T(8,128)(2,1)S(1)}, u32[]{:S(2)}, u32[]{:S(2)}) collective-permute-start(bf16[256,768]{1,0:T(8,128)(2,1)S(1)} %slice.94), channel_id=1, source_target_pairs={{0,4},{4,0},{1,5},{5,1},{2,6},{6,2},{3,7},{7,3},{8,12},{12,8},{9,1... | collective-permute-start | bytes 1179656 | tf_op jit(solution)/shard_map/ppermute | solution.py:374
  241.3 4.7 %collective-permute-start.13 = (bf16[256,768]{1,0:T(8,128)(2,1)}, bf16[256,768]{1,0:T(8,128)(2,1)S(1)}, u32[]{:S(2)}, u32[]{:S(2)}) collective-permute-start(bf16[256,768]{1,0:T(8,128)(2,1)} %get-tuple-element.117), channel_id=1, source_target_pairs={{0,4},{4,0},{1,5},{5,1},{2,6},{6,2},{3,7},{7,3},{8,12},{12,8},{9,1... | collective-permute-start | bytes 1179656 | tf_op jit(solution)/shard_map/ppermute | solution.py:374
  244.2 20.4 %collective-permute-start.11 = (bf16[2,128,768]{2,1,0:T(8,128)(2,1)S(1)}, bf16[2,128,768]{2,1,0:T(8,128)(2,1)S(1)}, u32[]{:S(2)}, u32[]{:S(2)}) collective-permute-start(bf16[2,128,768]{2,1,0:T(8,128)(2,1)S(1)} %get-tuple-element.121), channel_id=1, source_target_pairs={{0,8},{8,0},{1,9},{9,1},{2,10},{10,2},{3,11},{11,3},{4,12},{12,4},... | collective-permute-start | bytes 1179656 | tf_op jit(solution)/shard_map/ppermute | solution.py:374
  246.2 43.5 %collective-permute-start.15 = (bf16[3,128,768]{2,1,0:T(8,128)(2,1)S(1)}, bf16[3,128,768]{2,1,0:T(8,128)(2,1)S(1)}, u32[]{:S(2)}, u32[]{:S(2)}) collective-permute-start(bf16[3,128,768]{2,1,0:T(8,128)(2,1)S(1)} %get-tuple-element.115), channel_id=1, source_target_pairs={{0,8},{8,0},{1,9},{9,1},{2,10},{10,2},{3,11},{11,3},{4,12},{12,4},... | collective-permute-start | bytes 1769480 | tf_op jit(solution)/shard_map/ppermute | solution.py:374
  289.7 1.2 copy-start.16
  307.2 1.5 collective-permute-start.20
  308.2 63.9 %collective-permute-start.18 = (f32[3,3,128]{2,1,0:T(4,128)S(1)}, f32[3,3,128]{2,1,0:T(4,128)S(1)}, u32[]{:S(2)}, u32[]{:S(2)}) collective-permute-start(f32[3,3,128]{2,1,0:T(4,128)S(1)} %get-tuple-element.104), channel_id=1, source_target_pairs={{0,4},{4,0},{1,5},{5,1},{2,6},{6,2},{3,7},{7,3},{8,12},{12,8},{9,1... | collective-permute-start | bytes 13832 | tf_op jit(solution)/shard_map/ppermute | solution.py:374
  370.9 60.8 %copy-start.14 = (bf16[192,768]{1,0:T(8,128)(2,1)S(1)}, bf16[192,768]{1,0:T(8,128)(2,1)}, u32[]{:S(2)}) copy-start(bf16[192,768]{1,0:T(8,128)(2,1)} %get-tuple-element.108) | copy-start | bytes 884740
  370.9 61.0 %copy-start.1 = (bf16[3,768,192]{2,1,0:T(8,128)(2,1)S(1)}, bf16[3,768,192]{2,1,0:T(8,128)(2,1)}, u32[]{:S(2)}) copy-start(bf16[3,768,192]{2,1,0:T(8,128)(2,1)} %get-tuple-element.107) | copy-start | bytes 2654212
  370.9 77.9 %collective-permute-start.21 = (bf16[1552,768]{1,0:T(8,128)(2,1)}, bf16[1552,768]{1,0:T(8,128)(2,1)}, u32[]{:S(2)}, u32[]{:S(2)}) collective-permute-start(bf16[1552,768]{1,0:T(8,128)(2,1)} %get-tuple-element.109), channel_id=1, source_target_pairs={{0,4},{4,0},{1,5},{5,1},{2,6},{6,2},{3,7},{7,3},{8,12},{12,8},{9,1... | collective-permute-start | bytes 7151624 | tf_op jit(solution)/shard_map/ppermute | solution.py:374
  431.7 5.5 %collective-permute-start.19 = (bf16[192,768]{1,0:T(8,128)(2,1)S(1)}, bf16[192,768]{1,0:T(8,128)(2,1)}, u32[]{:S(2)}, u32[]{:S(2)}) collective-permute-start(bf16[192,768]{1,0:T(8,128)(2,1)S(1)} %copy-done.14), channel_id=1, source_target_pairs={{0,4},{4,0},{1,5},{5,1},{2,6},{6,2},{3,7},{7,3},{8,12},{12,8},{9,1... | collective-permute-start | bytes 884744 | tf_op jit(solution)/shard_map/ppermute | solution.py:374
  433.2 6.2 %collective-permute-start.16 = (bf16[3,768,192]{1,2,0:T(8,128)(2,1)}, bf16[3,768,192]{1,2,0:T(8,128)(2,1)S(1)}, u32[]{:S(2)}, u32[]{:S(2)}) collective-permute-start(bf16[3,768,192]{1,2,0:T(8,128)(2,1)} %copy.81), channel_id=1, source_target_pairs={{0,4},{4,0},{1,5},{5,1},{2,6},{6,2},{3,7},{7,3},{8,12},{12,8},{9,1... | collective-permute-start | bytes 2654216 | tf_op jit(solution)/shard_map/ppermute | solution.py:374
  434.6 1.3 copy-start.10
  443.1 5.8 %copy-start.3 = (bf16[1552,768]{1,0:T(8,128)(2,1)S(1)}, bf16[1552,768]{1,0:T(8,128)(2,1)}, u32[]{:S(2)}) copy-start(bf16[1552,768]{1,0:T(8,128)(2,1)} %get-tuple-element.109) | copy-start | bytes 7151620
  (1 other events, 0.6 us)
Sparse Core Ops, SparseCore 0:
  60.4 38.5 all-reduce.8
  107.6 43.1 all-reduce.10
  158.7 42.9 all-reduce.12
  238.1 132.7 all-reduce.16
  373.8 55.9 all-reduce.14

commit v2 on v1

v2 whole, which is shorter than its diff:
```python
import functools

import jax
import jax.numpy as jnp
from jax import lax
from jax.experimental import pallas as pl
from jax.experimental.pallas import tpu as pltpu
from jax.sharding import Mesh, PartitionSpec as P

DH = 64
NBUCK = 128
HALF = 64
EPSILON = 1e-05
F32 = jnp.float32
BF16 = jnp.bfloat16
VMEM_BYTES = 56 * 1024 * 1024
NN = (((1,), (0,)), ((), ()))
NT = (((1,), (1,)), ((), ()))
TN = (((0,), (0,)), ((), ()))


def mm(left, right, dims=NN):
    return lax.dot_general(left, right, dims, preferred_element_type=F32)


def kernel_call(body, place, operands, outs, flops, scratch=()):
    specs, arrays, moved = [], [], 0
    for array, per_stream in operands:
        if per_stream:
            rest = array.shape[1:]
            specs.append(
                pl.BlockSpec(
                    (None,) + rest, lambda g, s, n=len(rest): (s[0],) + (0,) * n
                )
            )
        else:
            rest = array.shape
            specs.append(pl.BlockSpec(rest, lambda g, s, n=len(rest): (0,) * n))
        arrays.append(array)
        size = array.dtype.itemsize
        for extent in rest:
            size *= extent
        moved += size
    out_specs = [
        pl.BlockSpec(shape, lambda g, s, n=len(shape): (0,) * n) for shape, _ in outs
    ]
    for shape, dtype in outs:
        size = jnp.dtype(dtype).itemsize
        for extent in shape:
            size *= extent
        moved += size
    return pl.pallas_call(
        body,
        out_shape=[jax.ShapeDtypeStruct(shape, dtype) for shape, dtype in outs],
        grid_spec=pltpu.PrefetchScalarGridSpec(
            num_scalar_prefetch=1,
            grid=(1,),
            in_specs=specs,
            out_specs=out_specs,
            scratch_shapes=list(scratch),
        ),
        compiler_params=pltpu.CompilerParams(
            dimension_semantics=("arbitrary",), vmem_limit_bytes=VMEM_BYTES
        ),
        cost_estimate=pl.CostEstimate(
            flops=flops, bytes_accessed=moved, transcendentals=0
        ),
    )(place, *arrays)


def centred(rows):
    centre = rows - jnp.mean(rows, axis=-1, keepdims=True)
    spread = lax.rsqrt(jnp.mean(centre * centre, axis=-1, keepdims=True) + EPSILON)
    return centre * spread, spread


def norm_back(unit, spread, tilted):
    return spread * (
        tilted
        - jnp.mean(tilted, axis=-1, keepdims=True)
        - unit * jnp.mean(tilted * unit, axis=-1, keepdims=True)
    )


def pick(table_row, index):
    width = index.shape[1]
    table = jnp.broadcast_to(table_row, (index.shape[0], NBUCK))
    parts = [
        jnp.take_along_axis(
            table,
            index[:, at : at + NBUCK],
            axis=1,
            mode="promise_in_bounds",
        )
        for at in range(0, width, NBUCK)
    ]
    return jnp.concatenate(parts, axis=1)


def stack_rows(pieces):
    return jnp.concatenate(pieces, axis=0)


def turned(rows, size):
    pieces = [rows[at : at + size] for at in range(0, rows.shape[0], size)]
    return stack_rows([pieces[i ^ 1] for i in range(len(pieces))])


def residual(x_ref, half, mixed_refs):
    rest = mixed_refs[0].shape[0] // 2
    pieces = []
    for y in range(2):
        for c in range(2):
            own = x_ref[y, half, c * rest : (c + 1) * rest, :].astype(F32)
            pieces.append(own + mixed_refs[c][y * rest : (y + 1) * rest, :].astype(F32))
    return stack_rows(pieces)


def quarter(refs, place_ref, b, y, rows, straight):
    near_ref, far_ref = refs
    db = place_ref[1] ^ b
    dy = place_ref[2] ^ y
    near, far = (db, dy) if straight else (dy, db)
    return jnp.where(far == 0, near_ref[near, rows, :], far_ref[near, rows, :])


def attention_kernel(
    p_ref,
    x_ref,
    sp_ref,
    w_ref,
    ws_ref,
    table_ref,
    rowidx_ref,
    colidx_ref,
    proj_ref,
    spat_ref,
    soft_ref,
    own_ref,
    send_ref,
    att_ref,
    *,
    heads,
    block,
):
    width = x_ref.shape[-1]
    x = x_ref[...].reshape(-1, width)
    sp = sp_ref[...].reshape(-1, width)
    for k in range(3):
        proj_ref[k] = mm(x, w_ref[k], NT).astype(BF16)
    for k in range(2):
        spat_ref[k] = mm(sp, ws_ref[k], NT).astype(BF16)
    length = x.shape[0]
    level = lax.broadcasted_iota(jnp.int32, (length, NBUCK), 1)
    chosen = [(colidx_ref[:, kind : kind + 1] == level).astype(BF16) for kind in (1, 2)]
    chosen = jnp.concatenate(chosen, axis=1)

    def step(at, carry):
        rows = pl.ds(pl.multiple_of(at * block, block), block)
        lane = lax.broadcasted_iota(jnp.int32, (block, NBUCK), 1)
        index = jnp.clip(rowidx_ref[0:1, :] - colidx_ref[rows, 0:1], -HALF, HALF - 1) + HALF
        boxes = [
            jnp.clip(lane - colidx_ref[rows, kind : kind + 1], -HALF, HALF - 1) + HALF
            for kind in (1, 2)
        ]
        for h in range(heads):
            cols = slice(h * DH, (h + 1) * DH)
            bias = jnp.concatenate(
                [pick(table_ref[k, h : h + 1, :], boxes[k - 1]) for k in (1, 2)], axis=1
            )
            coarse = bias.astype(BF16)
            fine = (bias - coarse.astype(F32)).astype(BF16)
            left = jnp.concatenate(
                [proj_ref[0, rows, cols], spat_ref[0, rows, cols]], axis=1
            ) * jnp.asarray(DH**-0.5, BF16)
            right = jnp.concatenate([proj_ref[1, :, cols], spat_ref[1, :, cols]], axis=1)
            scores = mm(
                jnp.concatenate([left, coarse, fine], axis=1),
                jnp.concatenate([right, chosen, chosen], axis=1),
                NT,
            ) + pick(table_ref[0, h : h + 1, :], index)
            top = jnp.max(scores, axis=-1, keepdims=True)
            raised = jnp.exp(scores - top)
            soft = raised * (1.0 / jnp.sum(raised, axis=-1, keepdims=True))
            soft_ref[h, rows, :] = soft
            att_ref[rows, cols] = mm(soft.astype(BF16), proj_ref[2, :, cols]).astype(BF16)
        return carry

    lax.fori_loop(0, length // block, step, 0)
    part = length // 4
    own_ref[0:part, :] = att_ref[0:part, :]
    own_ref[part:, :] = att_ref[2 * part : 3 * part, :]
    send_ref[0:part, :] = att_ref[part : 2 * part, :]
    send_ref[part:, :] = att_ref[3 * part :, :]


def mixed_kernel(
    p_ref,
    own_ref,
    recv_ref,
    exit_ref,
    near_ref,
    far_ref,
    keep_ref,
    send_ref,
    partner_ref,
):
    share = exit_ref.shape[0] // 4
    for q in range(4):
        partner_ref[q * share : (q + 1) * share, :] = quarter(
            (near_ref, far_ref), p_ref, q // 2, q % 2, slice(0, share), True
        )
    total = mm(own_ref[...], exit_ref[...]) + mm(recv_ref[...], partner_ref[...])
    rest = total.shape[0] // 4
    for y in range(2):
        at = 2 * y * rest
        keep_ref[y * rest : (y + 1) * rest, :] = total[at : at + rest]
        send_ref[y * rest : (y + 1) * rest, :] = total[at + rest : at + 2 * rest].astype(BF16)


def gelu_parts(upper):
    phi = 0.5 * (1.0 + lax.erf(upper * (0.5**0.5)))
    slope = phi + upper * (jnp.exp(-0.5 * upper * upper) * (0.5 / jnp.pi) ** 0.5)
    return (upper * phi).astype(BF16), slope


def forward_kernel(
    p_ref,
    x_ref,
    mixed0_ref,
    mixed1_ref,
    gain_ref,
    shift_ref,
    up_ref,
    hidden_ref,
    down_ref,
    upn1_ref,
    upf1_ref,
    upn2_ref,
    upf2_ref,
    dnn1_ref,
    dnf1_ref,
    dnn2_ref,
    dnf2_ref,
    low_ref,
    active_ref,
    slope_ref,
    upp_ref,
    downp_ref,
):
    width = x_ref.shape[-1]
    first = upn1_ref.shape[1]
    skip = width // 16
    split = first - skip
    share = width // 4
    piece = dnn1_ref.shape[1]
    for q in range(4):
        b, y, at = q // 2, q % 2, q * share
        upp_ref[at : at + split, :] = quarter(
            (upn1_ref, upf1_ref), p_ref, b, y, slice(skip, first), True
        )
        upp_ref[at + split : at + share, :] = quarter(
            (upn2_ref, upf2_ref), p_ref, b, y, slice(0, share - split), False
        )
        downp_ref[at : at + piece, :] = quarter(
            (dnn1_ref, dnf1_ref), p_ref, b, y, slice(0, piece), True
        )
        downp_ref[at + piece : at + share, :] = quarter(
            (dnn2_ref, dnf2_ref), p_ref, b, y, slice(0, share - piece), False
        )
    extra = upn2_ref[0, share - split : share - split + 16, :].astype(F32)
    partner_bias = extra[0:1] + extra[1:2] + extra[2:3]
    unit, _ = centred(residual(x_ref, 0, (mixed0_ref, mixed1_ref)))
    normed_low = (unit * gain_ref[0:1, :] + shift_ref[0:1, :]).astype(BF16)
    active, slope = gelu_parts(mm(normed_low, up_ref[...]) + hidden_ref[...])
    active_ref[0] = active
    slope_ref[0] = slope
    total = mm(active, down_ref[...])
    active, slope = gelu_parts(mm(normed_low, upp_ref[...]) + partner_bias)
    active_ref[1] = active
    slope_ref[1] = slope
    low_ref[...] = (total + mm(active, downp_ref[...])).astype(BF16)


def other_kernel(
    p_ref,
    x_ref,
    mixed0_ref,
    mixed1_ref,
    gain_ref,
    shift_ref,
    up_ref,
    hidden_ref,
    normed_ref,
    active_ref,
    slope_ref,
):
    unit, _ = centred(residual(x_ref, 1, (mixed0_ref, mixed1_ref)))
    normed_low = (unit * gain_ref[0:1, :] + shift_ref[0:1, :]).astype(BF16)
    normed_ref[...] = normed_low
    active, slope = gelu_parts(mm(normed_low, up_ref[...]) + hidden_ref[...])
    active_ref[...] = active
    slope_ref[...] = slope


def middle_kernel(
    p_ref,
    x_ref,
    mixed0_ref,
    mixed1_ref,
    low_ref,
    lowr_ref,
    cot_ref,
    gain_ref,
    shift_ref,
    bdown_ref,
    up_ref,
    down_ref,
    upp_ref,
    downp_ref,
    slope_ref,
    outk_ref,
    outs_ref,
    hid_ref,
    second_ref,
    normed_ref,
    dlow_ref,
    dlows_ref,
    dup_ref,
    sums_ref,
):
    unit, _ = centred(residual(x_ref, 0, (mixed0_ref, mixed1_ref)))
    normed = unit * gain_ref[0:1, :] + shift_ref[0:1, :]
    normed_ref[...] = normed.astype(BF16)
    length = normed.shape[0]
    least = length // 8
    lowered = low_ref[...].astype(F32) + turned(lowr_ref[...], least).astype(F32)
    unit2, spread2 = centred(normed + lowered + bdown_ref[...])
    out = (unit2 * gain_ref[1:2, :] + shift_ref[1:2, :]).astype(BF16)
    for y in range(2):
        at = 4 * y * least
        outk_ref[y * least : (y + 1) * least, :] = out[at : at + least]
        outs_ref[y * least : (y + 1) * least, :] = out[at + 2 * least : at + 3 * least]
    cot = cot_ref[...].astype(F32)
    second = norm_back(unit2, spread2, cot * gain_ref[1:2, :])
    second_ref[...] = second
    sums_ref[...] = jnp.zeros_like(sums_ref)
    sums_ref[0:1, :] = jnp.sum(cot * unit2, axis=0, keepdims=True)
    sums_ref[1:2, :] = jnp.sum(cot, axis=0, keepdims=True)
    sums_ref[2:3, :] = jnp.sum(second, axis=0, keepdims=True)
    dlow = second.astype(BF16)
    dlow_ref[...] = dlow
    for i in range(4):
        dlows_ref[i * least : (i + 1) * least, :] = dlow[2 * i * least : (2 * i + 1) * least]
    dup = (mm(dlow, down_ref[...], NT) * slope_ref[0]).astype(BF16)
    dup_ref[...] = dup
    total = mm(dup, up_ref[...], NT)
    dup = (mm(dlow, downp_ref[...], NT) * slope_ref[1]).astype(BF16)
    hid_ref[...] = (total + mm(dup, upp_ref[...], NT)).astype(BF16)


def ffn_grad_kernel(
    p_ref,
    normed_ref,
    normedo_ref,
    active_ref,
    activeo_ref,
    dlow_ref,
    dlow0_ref,
    dlow1_ref,
    dup_ref,
    slopeo_ref,
    down_ref,
    upg_ref,
    downg_ref,
    bias_ref,
):
    least = dlow0_ref.shape[0] // 4
    pieces = []
    for i in range(4):
        pieces.append(dlow0_ref[i * least : (i + 1) * least, :])
        pieces.append(dlow1_ref[i * least : (i + 1) * least, :])
    dlowo = stack_rows(pieces)
    dupo = (mm(dlowo, down_ref[...], NT) * slopeo_ref[...]).astype(BF16)
    dup = dup_ref[...]
    upg_ref[...] = (mm(normed_ref[...], dup, TN) + mm(normedo_ref[...], dupo, TN)).astype(BF16)
    downg_ref[...] = (
        mm(active_ref[0], dlow_ref[...], TN) + mm(activeo_ref[...], dlowo, TN)
    ).astype(BF16)
    bias = jnp.sum(dup.astype(F32), axis=0, keepdims=True)
    bias = bias + jnp.sum(dupo.astype(F32), axis=0, keepdims=True)
    bias_ref[...] = jnp.broadcast_to(bias, bias_ref.shape)


def first_kernel(
    p_ref,
    x_ref,
    mixed0_ref,
    mixed1_ref,
    second_ref,
    hid_ref,
    hidr_ref,
    gain_ref,
    first_ref,
    dmix_ref,
    sums_ref,
):
    unit, spread = centred(residual(x_ref, 0, (mixed0_ref, mixed1_ref)))
    hid = hid_ref[...].astype(F32) + turned(hidr_ref[...], hid_ref.shape[0] // 8).astype(F32)
    dnormed = second_ref[...] + hid
    first = norm_back(unit, spread, dnormed * gain_ref[0:1, :])
    first_ref[...] = first
    dmix_ref[...] = first.astype(BF16)
    sums_ref[...] = jnp.zeros_like(sums_ref)
    sums_ref[0:1, :] = jnp.sum(dnormed * unit, axis=0, keepdims=True)
    sums_ref[1:2, :] = jnp.sum(dnormed, axis=0, keepdims=True)


def attended_kernel(
    p_ref,
    dmix_ref,
    dmixr_ref,
    exit_ref,
    exitp_ref,
    sums1_ref,
    sums2_ref,
    own_ref,
    send_ref,
    total_ref,
    pay_ref,
):
    length = dmix_ref.shape[0]
    rest = length // 4
    total = dmix_ref[...].astype(F32) + turned(dmixr_ref[...], rest).astype(F32)
    total = total.astype(BF16)
    total_ref[...] = total
    own_ref[...] = mm(total, exit_ref[...], NT).astype(BF16)
    send_ref[...] = mm(total, exitp_ref[...], NT).astype(BF16)
    pay_ref[0:rest, :] = total[0:rest]
    pay_ref[rest : 2 * rest, :] = total[2 * rest : 3 * rest]
    pay_ref[2 * rest :, :] = jnp.concatenate([sums1_ref[...], sums2_ref[...]], axis=0).astype(BF16)


def backward_kernel(
    p_ref,
    datt_ref,
    dattr_ref,
    first_ref,
    soft_ref,
    proj_ref,
    spat_ref,
    w_ref,
    ws_ref,
    dscore_ref,
    dproj_ref,
    dspat_ref,
    dxk0_ref,
    dxk1_ref,
    dxs0_ref,
    dxs1_ref,
    dsk0_ref,
    dsk1_ref,
    dss0_ref,
    dss1_ref,
    *,
    heads,
    block,
):
    length = 2 * datt_ref.shape[0]
    scale = DH**-0.5
    part = length // 4
    datt = stack_rows(
        [datt_ref[0:part, :], dattr_ref[0:part, :], datt_ref[part:, :], dattr_ref[part:, :]]
    )
    for h in range(heads):
        cols = slice(h * DH, (h + 1) * DH)
        value = proj_ref[2, :, cols]
        left = jnp.concatenate([proj_ref[0, :, cols], spat_ref[0, :, cols]], axis=1)
        right = jnp.concatenate([proj_ref[1, :, cols], spat_ref[1, :, cols]], axis=1)
        own = datt[:, cols]
        for at in range(0, length, block):
            soft = soft_ref[h, at : at + block, :]
            dsoft = mm(own[at : at + block], value, NT)
            inner = jnp.sum(soft * dsoft, axis=-1, keepdims=True)
            dscore_ref[h, at : at + block, :] = (soft * (dsoft - inner)).astype(BF16)
        dscore = dscore_ref[h]
        dleft = (mm(dscore, right) * scale).astype(BF16)
        dright = (mm(dscore, left, TN) * scale).astype(BF16)
        dproj_ref[0, :, cols] = dleft[:, :DH]
        dspat_ref[0, :, cols] = dleft[:, DH:]
        dproj_ref[1, :, cols] = dright[:, :DH]
        dspat_ref[1, :, cols] = dright[:, DH:]
        dproj_ref[2, :, cols] = mm(soft_ref[h].astype(BF16), own, TN).astype(BF16)
    once = (p_ref[3] == 0).astype(F32)
    total = mm(dproj_ref[0], w_ref[0])
    for k in range(1, 3):
        total = total + mm(dproj_ref[k], w_ref[k])
    least = part // 4

    def deal(rows, refs):
        for y in range(2):
            for zh in range(2):
                for c in range(2):
                    for zl in range(2):
                        at = (((y * 2 + zh) * 2 + c) * 2 + zl) * least
                        to = (zh * 2 + y) * least
                        value = rows[at : at + least]
                        if zh == 0 and first_ref is not None and refs[0][0] is dxk0_ref:
                            of = ((y * 2 + c) * 2 + zl) * least
                            value = value + once * first_ref[of : of + least, :]
                        refs[c][zl][to : to + least, :] = value.astype(BF16)

    deal(total, ((dxk0_ref, dxk1_ref), (dxs0_ref, dxs1_ref)))
    total = mm(dspat_ref[0], ws_ref[0]) + mm(dspat_ref[1], ws_ref[1])
    deal(total, ((dsk0_ref, dsk1_ref), (dss0_ref, dss1_ref)))


def attention_grad_kernel(
    p_ref,
    dmix_ref,
    pay_ref,
    payr_ref,
    payc_ref,
    atto_ref,
    atts_ref,
    x_ref,
    sp_ref,
    dscore_ref,
    dproj_ref,
    dspat_ref,
    colidx_ref,
    bup_ref,
    first_ref,
    second_ref,
    *,
    heads,
):
    width = x_ref.shape[-1]
    x = x_ref[...].reshape(-1, width)
    sp = sp_ref[...].reshape(-1, width)
    length = x.shape[0]
    inner = dproj_ref.shape[-1]
    for k in range(3):
        first_ref[k * inner : (k + 1) * inner, :] = mm(dproj_ref[k], x, TN).astype(BF16)
    rest = length // 8
    dmixo = stack_rows(
        [payr_ref[0:rest, :], payc_ref[0:rest, :], payr_ref[rest : 2 * rest, :], payc_ref[rest : 2 * rest, :]]
    )
    second_ref[0:inner, :] = (
        mm(atto_ref[...], dmix_ref[...], TN) + mm(atts_ref[...], dmixo, TN)
    ).astype(BF16)
    for k in range(2):
        second_ref[(k + 1) * inner : (k + 2) * inner, :] = mm(dspat_ref[k], sp, TN).astype(BF16)
    small = pay_ref[2 * rest :, :].astype(F32) + payr_ref[2 * rest :, :].astype(F32)
    lane = lax.broadcasted_iota(jnp.int32, (1, NBUCK), 1)
    found = []
    for kind in range(3):
        extent = length if kind == 0 else NBUCK
        own = colidx_ref[:, kind : kind + 1]
        level = lax.broadcasted_iota(jnp.int32, (length, extent), 1)
        chosen = (own == level).astype(BF16)
        place = own - HALF + lax.broadcasted_iota(jnp.int32, (length, NBUCK), 1)
        turn = place & (NBUCK - 1)
        piece = place >> 7
        for h in range(heads):
            spread = mm(dscore_ref[h], chosen)
            window = jnp.zeros((length, NBUCK), F32)
            for q in range(extent // NBUCK):
                part = jnp.take_along_axis(
                    spread[:, q * NBUCK : (q + 1) * NBUCK],
                    turn,
                    axis=1,
                    mode="promise_in_bounds",
                )
                window = window + jnp.where(piece == q, part, 0.0)
            row = jnp.sum(window, axis=0, keepdims=True)
            row = jnp.where((lane > 0) & (lane < NBUCK - 1), row, 0.0)
            least = jnp.sum(jnp.where(level <= own - HALF, spread, 0.0), axis=0, keepdims=True)
            most = jnp.sum(jnp.where(level >= own + HALF - 1, spread, 0.0), axis=0, keepdims=True)
            row = row + jnp.where(lane == 0, jnp.sum(least, axis=1, keepdims=True), 0.0)
            row = row + jnp.where(
                lane == NBUCK - 1, jnp.sum(most, axis=1, keepdims=True), 0.0
            )
            found.append(row)
    base = 3 * inner
    first_ref[base : base + 16, :] = small.astype(BF16)
    per = width // NBUCK
    found = found + [jnp.zeros((1, NBUCK), F32)] * (-len(found) % per)
    lines = [
        jnp.concatenate(found[at : at + per], axis=1) for at in range(0, len(found), per)
    ]
    lines.append(bup_ref[0:1, :])
    lines = jnp.concatenate(lines + [jnp.zeros((16 - len(lines), width), F32)], axis=0)
    first_ref[base + 16 : base + 32, :] = lines.astype(BF16)


def swap(value, axis, step=1):
    size = lax.axis_size(axis)
    return lax.ppermute(value, axis, [(i, i ^ step) for i in range(size)])


def added(left, right):
    return (left.astype(F32) + right.astype(F32)).astype(BF16)


def summed(straight, crossed):
    steps = [1 << bit for bit in range(lax.axis_size("batch").bit_length() - 1)]
    for step in steps:
        straight = added(straight, swap(straight, "batch", step))
    crossed = added(crossed, swap(crossed, "y"))
    straight = added(straight, swap(straight, "y"))
    for step in steps:
        crossed = added(crossed, swap(crossed, "batch", step))
    return straight, crossed


def in_place(array, index, axis):
    return jnp.where(index == 0, array, jnp.flip(array, axis))


def shards(
    tokens,
    spatial,
    positions,
    boxes,
    query_key_value_weight,
    w_spatial,
    rel_tables,
    exit_matrix,
    ln_gains,
    ln_shifts,
    up_weight,
    hidden_bias,
    shrink_projection_array,
    b_down,
    cotangent,
):
    heads = rel_tables.shape[2]
    rows = tokens.shape[2]
    width = tokens.shape[3]
    inner = query_key_value_weight.shape[3]
    hidden = up_weight.shape[2]
    least = rows // 4
    rest = rows // 2
    length = 4 * rows
    page = lax.axis_index("y")
    core = lax.axis_index("core")
    zh = lax.axis_index("zh")
    zl = lax.axis_index("zl")
    pair = lax.axis_index("batch") & 1
    place = jnp.stack([core, pair, page, zl]).astype(jnp.int32)
    call = functools.partial(kernel_call, place=place)

    def run(body, operands, outs, flops, scratch=()):
        marked = [a if isinstance(a, tuple) else (a, False) for a in operands]
        return kernel_call(body, place, marked, outs, flops, scratch)

    def take(array, index, axis):
        return lax.dynamic_index_in_dim(array, index, axis, keepdims=False)

    def near_first(array, axis):
        shape = array.shape
        array = array.reshape(shape[:axis] + (2, 2, least) + shape[axis + 1 :])
        return in_place(in_place(array, zh, axis), zl, axis + 1)

    def to_stream(array):
        mine, other = take(array, page, 1), take(array, 1 - page, 1)
        return mine, other

    token_blocks = near_first(tokens, 2)
    mine, other = take(token_blocks, page, 1), take(token_blocks, 1 - page, 1)
    far = swap(other, "y")
    both = jnp.stack([mine, far])
    kept, passed = take(both, core, 1), take(both, 1 - core, 1)
    x = jnp.stack([kept, swap(passed, "core")], axis=2).reshape(2, 2, rows, width)

    spatial_blocks = near_first(spatial, 1)
    mine, other = take(spatial_blocks, page, 0), take(spatial_blocks, 1 - page, 0)
    both = jnp.stack([mine, swap(other, "y")])
    sp = jnp.stack([both, swap(both, "core")], axis=2).reshape(2, 2, rows, width)

    places = jnp.concatenate([positions[None], boxes], axis=0)
    places = near_first(places, 2)
    mine, other = take(places, page, 1), take(places, 1 - page, 1)
    both = jnp.stack([mine, swap(other, "y")], axis=1)
    places = jnp.stack([both, swap(both, "core")], axis=3).reshape(3, length)
    rowidx = jnp.pad(places, ((0, 5), (0, 0)))
    colidx = rowidx.T

    mine = pair * 2 + page
    exit_own = take(exit_matrix, core, 0)
    up_own = take(up_weight, core, 0)
    down_own = take(shrink_projection_array, core, 0)
    bias_own = take(hidden_bias, core, 0)
    bias_rows = []
    left_over = bias_own
    for _ in range(3):
        bias_rows.append(left_over.astype(BF16))
        left_over = left_over - bias_rows[-1].astype(F32)
    bias_rows = jnp.pad(jnp.stack(bias_rows), ((0, 13), (0, 0)))
    share = hidden // 4
    exit_share = lax.dynamic_slice_in_dim(exit_own, mine * (inner // 4), inner // 4, 0)
    up_share = lax.dynamic_slice_in_dim(up_own, mine * share, share, 0)
    down_share = lax.dynamic_slice_in_dim(down_own, mine * share, share, 0)
    split = (share + 16 - inner // 4) // 2
    one = swap(jnp.concatenate([exit_share, up_share[:split]]), "zh")
    two = swap(jnp.concatenate([up_share[split:], bias_rows]), "zh")
    three = swap(down_share[: share // 2], "zh")
    four = swap(down_share[share // 2 :], "zh")

    def spread(array, axes):
        near = jnp.stack([array, swap(array, axes[0])])
        return near, swap(near, axes[1])

    up_parts = spread(one, ("batch", "y")) + spread(two, ("y", "batch"))
    down_parts = spread(three, ("batch", "y")) + spread(four, ("y", "batch"))

    cot = cotangent.reshape(2, 2, 2, 2, least, width)
    cot = in_place(take(cot, zh, 2), zl, 2)
    mine, other = take(cot, page, 1), take(cot, 1 - page, 1)
    both = jnp.stack([mine, swap(other, "y")])
    kept, passed = take(both, core, 1), take(both, 1 - core, 1)
    cot = jnp.stack([kept, swap(passed, "core")], axis=1).reshape(2 * rows, width)

    weights = jnp.swapaxes(query_key_value_weight, 2, 3)
    spatial_weights = jnp.swapaxes(w_spatial, 1, 2)
    half = length // 2
    proj, spat, soft, att_own, att_send = run(
        functools.partial(attention_kernel, heads=heads, block=128),
        [
            x,
            sp,
            (weights, True),
            spatial_weights,
            (rel_tables, True),
            rowidx,
            colidx,
        ],
        [
            ((3, length, inner), BF16),
            ((2, length, inner), BF16),
            ((heads, length, length), F32),
            ((half, inner), BF16),
            ((half, inner), BF16),
        ],
        2 * length * (width * inner * 5 + heads * length * DH * 12),
        [pltpu.VMEM((length, inner), BF16)],
    )
    att_recv = swap(att_send, "zh")
    keep, send, exit_partner = run(
        mixed_kernel,
        [att_own, att_recv, (exit_matrix, True), up_parts[0], up_parts[1]],
        [((rows, width), F32), ((rows, width), BF16), ((inner, width), BF16)],
        2 * length * inner * width,
    )
    mixed0 = added(keep, swap(send, "core"))
    far = swap(mixed0, "zl").reshape(2, 2, least, width)
    mixed0 = added(mixed0, jnp.flip(far, 1).reshape(rows, width))
    mixed1 = swap(mixed0, "core")
    mixed_far0 = swap(mixed0, "zh")
    mixed_far1 = swap(mixed_far0, "core")

    gains = (ln_gains, True)
    shifts = (ln_shifts, True)
    up = (up_weight, True)
    down = (shrink_projection_array, True)
    hidden_rows = (hidden_bias[:, None], True)
    matrix_flops = 2 * half * width * hidden
    low, active, slope, up_partner, down_partner = run(
        forward_kernel,
        [x, mixed0, mixed1, gains, shifts, up, hidden_rows, down, *up_parts, *down_parts],
        [
            ((half, width), BF16),
            ((2, half, hidden), BF16),
            ((2, half, hidden), F32),
            ((width, hidden), BF16),
            ((hidden, width), BF16),
        ],
        4 * matrix_flops,
    )
    low_recv = swap(low, "zl")
    normed_far, active_far, slope_far = run(
        other_kernel,
        [x, mixed_far0, mixed_far1, gains, shifts, up, hidden_rows],
        [((half, width), BF16), ((half, hidden), BF16), ((half, hidden), F32)],
        matrix_flops,
    )
    out_keep, out_send, hid, second, normed, dlow, dlow_send, dup, sums_two = run(
        middle_kernel,
        [
            x,
            mixed0,
            mixed1,
            low,
            low_recv,
            cot,
            gains,
            shifts,
            (b_down[:, None], True),
            up,
            down,
            up_partner,
            down_partner,
            slope,
        ],
        [
            ((rest, width), BF16),
            ((rest, width), BF16),
            ((half, width), BF16),
            ((half, width), F32),
            ((half, width), BF16),
            ((half, width), BF16),
            ((rows, width), BF16),
            ((half, hidden), BF16),
            ((8, width), F32),
        ],
        4 * matrix_flops,
    )
    hid_recv = swap(hid, "zl")
    dlow_far0 = swap(dlow_send, "zh")
    dlow_far1 = swap(dlow_far0, "zl")
    first, dmix, sums_one = run(
        first_kernel,
        [x, mixed0, mixed1, second, hid, hid_recv, gains],
        [((half, width), F32), ((half, width), BF16), ((8, width), F32)],
        0,
    )
    datt, datt_send, dmix, pay = run(
        attended_kernel,
        [dmix, swap(dmix, "core"), (exit_matrix, True), exit_partner, sums_one, sums_two],
        [
            ((half, inner), BF16),
            ((half, inner), BF16),
            ((half, width), BF16),
            ((rows + 16, width), BF16),
        ],
        2 * length * inner * width,
    )
    datt_recv = swap(datt_send, "zh")
    pay_recv = swap(pay, "zh")
    pay_core = swap(pay_recv, "core")
    piece = ((rows, width), BF16)
    dscore, dproj, dspat, dxk0, dxk1, dxs0, dxs1, dsk0, dsk1, dss0, dss1 = run(
        functools.partial(backward_kernel, heads=heads, block=128),
        [datt, datt_recv, first, soft, proj, spat, (weights, True), spatial_weights],
        [
            ((heads, length, length), BF16),
            ((3, length, inner), BF16),
            ((2, length, inner), BF16),
        ]
        + [piece] * 8,
        2 * length * (width * inner * 5 + heads * length * DH * 6),
    )

    dso1 = added(dsk1, swap(dss1, "core"))
    dso0 = added(dsk0, swap(dss0, "core"))
    units = (
        (dxk0, dxk1),
        (swap(dxs0, "core"), swap(dxs1, "core")),
        (dso0, dso1),
    )
    ends = []
    for near, far in units:
        total = added(near, swap(far, "zl"))
        ends.append(added(total[:rest], swap(total[rest:], "zh")))
    ends = jnp.stack(ends).reshape(3, 2, least, width)

    def to_owner(array):
        array = jnp.stack([array[:, 0], swap(array[:, 1], "y")], axis=1)
        array = jnp.stack([array, swap(array, "zh")])
        return jnp.stack([array, swap(array, "zl")])

    def in_order(array):
        array = in_place(in_place(array, zl, 0), zh, 1)
        array = in_place(array, page, 3)
        array = array.transpose(2, 3, 1, 0, 4, 5)
        return array.reshape(array.shape[0], 2, rows, width)

    ends = in_order(to_owner(ends))
    grad_tokens = in_place(ends[:2], core, 0).astype(F32)
    grad_spatial = ends[2].astype(F32)
    outs = jnp.stack([out_keep, swap(out_send, "core")]).reshape(2, 2, least, width)
    output = in_place(in_order(to_owner(outs)), core, 0)

    up_grad, down_grad, bias_grad = run(
        ffn_grad_kernel,
        [
            normed,
            normed_far,
            active,
            active_far,
            dlow,
            dlow_far0,
            dlow_far1,
            dup,
            slope_far,
            down,
        ],
        [((width, hidden), BF16), ((hidden, width), BF16), ((8, hidden), F32)],
        5 * matrix_flops,
    )
    up_grad, down_grad = summed(up_grad, down_grad)
    grads_one, grads_two = run(
        functools.partial(attention_grad_kernel, heads=heads),
        [
            dmix,
            pay,
            pay_recv,
            pay_core,
            att_own,
            att_send,
            x,
            sp,
            dscore,
            dproj,
            dspat,
            colidx,
            bias_grad,
        ],
        [((3 * inner + 32, width), BF16), ((3 * inner, width), BF16)],
        2 * length * (width * inner * 6 + heads * length * width),
    )
    grads_one, grads_two = summed(grads_one, grads_two)

    def both_streams(array):
        return in_place(jnp.stack([array, swap(array, "core")]), core, 0).astype(F32)

    grads_one = both_streams(grads_one)
    grads_two = both_streams(grads_two)
    grad_qkv = grads_one[:, : 3 * inner].reshape(2, 3, inner, width).swapaxes(2, 3)
    grad_exit = grads_two[:, :inner]
    grad_spatial_w = grads_two[0, inner:] + grads_two[1, inner:]
    grad_spatial_w = grad_spatial_w.reshape(2, inner, width).swapaxes(1, 2)
    small = grads_one[:, 3 * inner :]
    part = width // (2 * lax.axis_size("zh"))
    sums = lax.dynamic_slice_in_dim(small[:, :16], (2 * zh + zl) * part, part, 2)
    tables = small[:, 16:18].reshape(2, -1, NBUCK)[:, : 3 * heads]
    tables = tables.reshape(2, 3, heads, NBUCK)
    gains_grad = jnp.stack([sums[:, 0], sums[:, 8]], axis=1)
    shifts_grad = jnp.stack([sums[:, 1], sums[:, 9]], axis=1)
    return (
        output,
        grad_tokens,
        grad_spatial,
        grad_qkv,
        grad_spatial_w,
        tables,
        grad_exit,
        gains_grad,
        shifts_grad,
        both_streams(up_grad),
        small[:, 18],
        both_streams(down_grad),
        sums[:, 10],
    )


def solution(mesh):
    batch, seq, head = mesh.devices.shape
    fine = Mesh(
        mesh.devices.reshape(batch, seq // 2, 2, head // 2, 2),
        ("batch", "y", "core", "zh", "zl"),
    )
    seq = ("y", "core")
    head = ("zh", "zl")
    return jax.shard_map(
        shards,
        mesh=fine,
        in_specs=(
            P(None, "batch", seq, None),
            P("batch", seq, None),
            P("batch", seq),
            P(None, "batch", seq),
            P(None, None, None, head),
            P(None, None, head),
            P(None, None, head, None),
            P(None, head, None),
            P(),
            P(),
            P(None, None, head),
            P(None, head),
            P(None, head, None),
            P(),
            P(None, "batch", seq, None),
        ),
        out_specs=(
            P(None, "batch", seq, None),
            P(None, "batch", seq, None),
            P("batch", seq, None),
            P(None, None, None, head),
            P(None, None, head),
            P(None, None, head, None),
            P(None, head, None),
            P(None, None, head),
            P(None, None, head),
            P(None, None, head),
            P(None, head),
            P(None, head, None),
            P(None, head),
        ),
        check_vma=False,
    )
```

time: 464 us -> 342 us (0.74)
  waiting for transfers between devices: 300 us -> 160 us
  starting transfers between devices: 12.4 us -> 58.6 us
  blocking collectives: 16.3 us -> 0 us
  between operations: 14.2 us -> 1.63 us
  local copies, waits for them, and re-layouts: 35.4 us -> 25.5 us
  Pallas kernels: 59 us -> 68.8 us
    psum x5 -> x0, waiting for transfers between devices: 238 us -> none  [the longest x1 62.2 us: shards(): lax.psum((wgrad, wsgrad, exitgrad, tables, sums), ('batch', 'y'))]
    ppermute x22 -> x63, waiting for transfers between devices: 61.4 us -> 160 us  [swap(): return lax.ppermute(value, axis, [(i, i ^ step) for i in range(size)])]
    ppermute x22 -> x63, starting transfers between devices: 12 us -> 58.6 us  [swap(): return lax.ppermute(value, axis, [(i, i ^ step) for i in range(size)])]
    psum x1 -> x0, blocking collectives: 16.3 us -> none  [shards(): lax.psum((wgrad, wsgrad, exitgrad, tables, sums), ('batch', 'y'))]
    pallas_call x7 -> x10, Pallas kernels: 59 us -> 68.8 us  [kernel_call(): pl.pallas_call(body, out_shape=[jax.ShapeDtypeStruct(shape, dtype) for sh...]
    unnamed x55 -> x89, local copies, waits for them, and re-layouts: 16.6 us -> 10.4 us
    another operation x10 -> x27, other arithmetic: 5.6 us -> 9.8 us  [the longest x4 2.9 us: spread(): near = jnp.stack([array, swap(array, axes[0])])]
    convert_element_type x6 -> x22, other arithmetic: 7.46 us -> 10 us  [the longest x4 5.63 us: both_streams(): in_place(jnp.stack([array, swap(array, 'core')]), core, 0).astype(F32)]
  transfers between devices with their start and end apart: 27 -> 63, of which waited for: 12 -> 30; matrix products, arithmetic and copies ran while one was open for 9% -> 10% of each run, Pallas kernels for 2% -> 18%
where the time goes in v2:
time: 342 us; the launch traced here: 341 us
  waiting for transfers between devices  160 us (47%)
  Pallas kernels  68.8 us (20%)
  starting transfers between devices  58.6 us (17%)
  other arithmetic  25.9 us (8%)
  local copies, waits for them, and re-layouts  25.5 us (7%)
    ppermute x63, waiting for transfers between devices, swap(): return lax.ppermute(value, axis, [(i, i ^ step) for i in range(size)])  160 us
    pallas_call x10, Pallas kernels, kernel_call(): pl.pallas_call(body, out_shape=[jax.ShapeDtypeStruct(shape, dtype) for sh...  68.8 us
    ppermute x63, starting transfers between devices, swap(): return lax.ppermute(value, axis, [(i, i ^ step) for i in range(size)])  58.6 us
    unnamed x89, local copies, waits for them, and re-layouts  10.4 us
  transfers between devices with their start and end apart: 63, of which 30 were waited for; matrix products, arithmetic and copies ran while one was open for 10% of the time, Pallas kernels for 18%

profile of v2, /device:TPU:0, one launch (start us, length us, event | category | flops | bytes accessed | tf_op | source)
XLA Modules:
  0.0 340.8 jit_solution(17511640719008161702)
XLA Ops:
  2.4 3.0 collective-permute-start.4
  7.9 2.7 collective-permute-start.13
  15.8 1.8 dynamic-slice_bitcast_fusion.7
  18.9 2.6 collective-permute-start.16
  21.6 10.7 %collective-permute-done.7 = bf16[128,768]{1,0:T(8,128)(2,1)} collective-permute-done((bf16[128,768]{1,0:T(8,128)(2,1)S(1)}, bf16[128,768]{1,0:T(8,128)(2,1)}, u32[]{:S(2)}, u32[]{:S(2)}) %collective-permute-start.7) | collective-permute-done | bytes 196640 | tf_op jit(solution)/shard_map/ppermute | solution.py:599
  35.8 4.0 %collective-permute-done.8 = bf16[128,768]{1,0:T(8,128)(2,1)S(1)} collective-permute-done((bf16[128,768]{1,0:T(8,128)(2,1)}, bf16[128,768]{1,0:T(8,128)(2,1)S(1)}, u32[]{:S(2)}, u32[]{:S(2)}) %collective-permute-start.8) | collective-permute-done | bytes 196640 | tf_op jit(solution)/shard_map/ppermute | solution.py:599
  42.2 1.9 pad_maximum_fusion.5
  44.2 14.4 %shard_map.246 = (bf16[3,512,192]{2,1,0:T(8,128)(2,1)}, bf16[2,512,192]{2,1,0:T(8,128)(2,1)}, f32[3,512,512]{2,1,0:T(8,128)}, bf16[256,192]{1,0:T(8,128)(2,1)}, bf16[256,192]{1,0:T(8,128)(2,1)}) custom-call(s32[4]{0:T(128)} %pad_add_fusion.2.p_ref, bf16[2,2,128,768]{3,2,1,0:T(8,128)(2,1)} %bitcast.134, bf16[2,2,128,768]{3,2,1,0:T(8,128)(2,1)} %bitcast.158, ...), custom_call_target="tpu_custom_call" | custom-call | flops 1962934272 | bytes 7410176 | tf_op jit(solution)/shard_map/pallas_call | solution.py:52
  58.6 2.9 collective-permute-start.19
  63.1 7.4 %collective-permute-done.6.recv_ref = bf16[256,192]{1,0:T(8,128)(2,1)S(1)} collective-permute-done((bf16[256,192]{1,0:T(8,128)(2,1)}, bf16[256,192]{1,0:T(8,128)(2,1)S(1)}, u32[]{:S(2)}, u32[]{:S(2)}) %collective-permute-start.6) | collective-permute-done | bytes 98336 | tf_op jit(solution)/shard_map/ppermute | solution.py:599
  71.1 3.2 shard_map.247
  82.7 2.6 collective-permute-done.14
  91.2 6.6 %collective-permute-done.15.upf2_ref = bf16[2,128,768]{2,1,0:T(8,128)(2,1)S(1)} collective-permute-done((bf16[2,128,768]{2,1,0:T(8,128)(2,1)S(1)}, bf16[2,128,768]{2,1,0:T(8,128)(2,1)S(1)}, u32[]{:S(2)}, u32[]{:S(2)}) %collective-permute-start.15) | collective-permute-done | bytes 393248 | tf_op jit(solution)/shard_map/ppermute | solution.py:599
  99.2 7.2 %shard_map.248 = (bf16[256,768]{1,0:T(8,128)(2,1)}, bf16[2,256,768]{2,1,0:T(8,128)(2,1)}, f32[2,256,768]{2,1,0:T(8,128)}, bf16[768,768]{1,0:T(8,128)(2,1)}, bf16[768,768]{1,0:T(8,128)(2,1)}) custom-call(s32[4]{0:T(128)} %pad_add_fusion.2.p_ref, bf16[2,2,128,768]{3,2,1,0:T(8,128)(2,1)} %bitcast.135, bf16[128,768]{1,0:T(8,128)(2,1)} %copy-done.3, ...), custom_call_target="tpu_custom_call" | custom-call | flops 1207959552 | bytes 11418624 | tf_op jit(solution)/shard_map/pallas_call | solution.py:52
  110.0 6.7 %collective-permute-done.22.lowr_ref = bf16[256,768]{1,0:T(8,128)(2,1)S(1)} collective-permute-done((bf16[256,768]{1,0:T(8,128)(2,1)}, bf16[256,768]{1,0:T(8,128)(2,1)S(1)}, u32[]{:S(2)}, u32[]{:S(2)}) %collective-permute-start.22) | collective-permute-done | bytes 393248 | tf_op jit(solution)/shard_map/ppermute | solution.py:599
  117.4 7.8 %shard_map.249 = (bf16[64,768]{1,0:T(8,128)(2,1)}, bf16[64,768]{1,0:T(8,128)(2,1)}, bf16[256,768]{1,0:T(8,128)(2,1)}, f32[256,768]{1,0:T(8,128)}, bf16[256,768]{...) custom-call(s32[4]{0:T(128)} %pad_add_fusion.2.p_ref, ...), custom_call_target="tpu_custom_call" | custom-call | flops 1207959552 | bytes 11443200 | tf_op jit(solution)/shard_map/pallas_call | solution.py:52
  129.5 3.0 collective-permute-done.26
  133.2 2.4 collective-permute-start.47
  136.1 8.8 %collective-permute-done.29.hidr_ref = bf16[256,768]{1,0:T(8,128)(2,1)S(1)} collective-permute-done((bf16[256,768]{1,0:T(8,128)(2,1)}, bf16[256,768]{1,0:T(8,128)(2,1)S(1)}, u32[]{:S(2)}, u32[]{:S(2)}) %collective-permute-start.29) | collective-permute-done | bytes 393248 | tf_op jit(solution)/shard_map/ppermute | solution.py:599
  145.6 4.1 %shard_map.250 = (f32[256,768]{1,0:T(8,128)}, bf16[256,768]{1,0:T(8,128)(2,1)}, f32[8,768]{1,0:T(8,128)}) custom-call(s32[4]{0:T(128)} %pad_add_fusion.2.p_ref, bf16[2,2,128,768]{3,2,1,0:T(8,128)(2,1)} %bitcast.137, bf16[128,768]{1,0:T(8,128)(2,1)} %copy-done.3, bf16[128,768]{1,0:T(8,128)(2,1)} %copy-done.5, f32[256,768]{1,0:T(8,128)} %get-tuple-element.71.second_ref, ...), custom_call_target="tpu_custom_call" | custom-call | bytes 3962880 | tf_op jit(solution)/shard_map/pallas_call | solution.py:52
  149.8 4.4 %collective-permute-done.27 = bf16[2,2,32,768]{3,2,1,0:T(8,128)(2,1)S(1)} collective-permute-done((bf16[2,2,32,768]{3,2,1,0:T(8,128)(2,1)S(1)}, bf16[2,2,32,768]{3,2,1,0:T(8,128)(2,1)S(1)}, u32[]{:S(2)}, u32[]{:S(2)}) %collective-permute-start.27) | collective-permute-done | bytes 196640 | tf_op jit(solution)/shard_map/ppermute | solution.py:599
  154.3 4.1 %collective-permute-done.47.mixed0_ref = bf16[128,768]{1,0:T(8,128)(2,1)S(1)} collective-permute-done((bf16[128,768]{1,0:T(8,128)(2,1)S(1)}, bf16[128,768]{1,0:T(8,128)(2,1)S(1)}, u32[]{:S(2)}, u32[]{:S(2)}) %collective-permute-start.47) | collective-permute-done | bytes 196640 | tf_op jit(solution)/shard_map/ppermute | solution.py:599
  158.3 2.6 collective-permute-done.49.dlow0_ref
  161.6 4.1 %shard_map.253 = (bf16[256,768]{1,0:T(8,128)(2,1)}, bf16[256,768]{1,0:T(8,128)(2,1)}, f32[256,768]{1,0:T(8,128)}) custom-call(s32[4]{0:T(128)} %pad_add_fusion.2.p_ref, bf16[2,2,128,768]{3,2,1,0:T(8,128)(2,1)} %bitcast.138, bf16[128,768]{1,0:T(8,128)(2,1)} %copy-done.27, bf16[128,768]{1,0:T(8,128)(2,1)} %copy-done.28, f32[2,2,768]{2,1,0:T(2,128)} %gain_ref.7, ...), custom_call_target="tpu_custom_call" | custom-call | flops 301989888 | bytes 3947520 | tf_op jit(solution)/shard_map/pallas_call | solution.py:52
  165.8 7.7 %collective-permute-done.50.dlow1_ref = bf16[128,768]{1,0:T(8,128)(2,1)S(1)} collective-permute-done((bf16[128,768]{1,0:T(8,128)(2,1)S(1)}, bf16[128,768]{1,0:T(8,128)(2,1)S(1)}, u32[]{:S(2)}, u32[]{:S(2)}) %collective-permute-start.50) | collective-permute-done | bytes 196640 | tf_op jit(solution)/shard_map/ppermute | solution.py:599
  174.1 6.0 %shard_map.254 = (bf16[768,768]{1,0:T(8,128)(2,1)}, bf16[768,768]{1,0:T(8,128)(2,1)}, f32[8,768]{1,0:T(8,128)}) custom-call(s32[4]{0:T(128)} %pad_add_fusion.2.p_ref, bf16[256,768]{1,0:T(8,128)(2,1)} %get-tuple-element.96.normed_ref, bf16[256,768]{1,0:T(8,128)(2,1)} %get-tuple-element.97.normedo_ref, bf16[2,256,768]{2,1,0:T(8,128)(2,1)} %get-tuple-element.98.active_ref, ...), custom_call_target="tpu_custom_call" | custom-call | flops 1509949440 | bytes 7495680 | tf_op jit(solution)/shard_map/pallas_call | solution.py:52
  183.1 3.2 shard_map.251
  186.3 2.9 collective-permute-start.45
  189.7 9.4 %collective-permute-done.31.dattr_ref = bf16[256,192]{1,0:T(8,128)(2,1)S(1)} collective-permute-done((bf16[256,192]{1,0:T(8,128)(2,1)}, bf16[256,192]{1,0:T(8,128)(2,1)S(1)}, u32[]{:S(2)}, u32[]{:S(2)}) %collective-permute-start.31) | collective-permute-done | bytes 98336 | tf_op jit(solution)/shard_map/ppermute | solution.py:599
  199.8 9.1 %shard_map.252 = (bf16[3,512,512]{2,1,0:T(8,128)(2,1)}, bf16[3,512,192]{2,1,0:T(8,128)(2,1)}, bf16[2,512,192]{2,1,0:T(8,128)(2,1)}, bf16[128,768]{1,0:T(8,128)(2...) custom-call(s32[4]{0:T(128)} %pad_add_fusion.2.p_ref, ...), custom_call_target="tpu_custom_call" | custom-call | flops 1358954496 | bytes 10715136 | tf_op jit(solution)/shard_map/pallas_call | solution.py:52
  209.8 5.0 %collective-permute-done.32 = bf16[128,768]{1,0:T(8,128)(2,1)S(1)} collective-permute-done((bf16[128,768]{1,0:T(8,128)(2,1)}, bf16[128,768]{1,0:T(8,128)(2,1)S(1)}, u32[]{:S(2)}, u32[]{:S(2)}) %collective-permute-start.32) | collective-permute-done | bytes 196640 | tf_op jit(solution)/shard_map/ppermute | solution.py:599
  217.6 6.2 %collective-permute-done.33 = bf16[64,768]{1,0:T(8,128)(2,1)S(1)} collective-permute-done((bf16[64,768]{1,0:T(8,128)(2,1)S(1)}, bf16[64,768]{1,0:T(8,128)(2,1)S(1)}, u32[]{:S(2)}, u32[]{:S(2)}) %collective-permute-start.33) | collective-permute-done | bytes 98336 | tf_op jit(solution)/shard_map/ppermute | solution.py:599
  226.0 9.6 %shard_map.255 = (bf16[608,768]{1,0:T(8,128)(2,1)}, bf16[576,768]{1,0:T(8,128)(2,1)}) custom-call(s32[4]{0:T(128)} %pad_add_fusion.2.p_ref, bf16[256,768]{1,0:T(8,128)(2,1)} %get-tuple-element.91.dmix_ref, bf16[144,768]{1,0:T(8,128)(2,1)} %get-tuple-element.92.pay_ref, bf16[144,768]{1,0:T(8,128)(2,1)} %copy-done.35, bf16[144,768]{1,0:T(8,128)(2,1)} %copy-done.36, ...), custom_call_target="tpu_custom_call" | custom-call | flops 2113929216 | bytes 7241728 | tf_op jit(solution)/shard_map/pallas_call | solution.py:52
  237.0 2.1 collective-permute-start.54
  240.7 3.0 collective-permute-done.40
  243.8 2.0 collective-permute-start.41
  245.8 1.9 collective-permute-done.37
  247.8 2.9 collective-permute-done.41
  250.8 3.0 collective-permute-start.42
  255.3 6.6 %collective-permute-done.42 = bf16[3,32,768]{2,1,0:T(8,128)(2,1)S(1)} collective-permute-done((bf16[3,32,768]{2,1,0:T(8,128)(2,1)S(1)}, bf16[3,32,768]{2,1,0:T(8,128)(2,1)S(1)}, u32[]{:S(2)}, u32[]{:S(2)}) %collective-permute-start.42) | collective-permute-done | bytes 147488 | tf_op jit(solution)/shard_map/ppermute | solution.py:599
  261.9 1.8 collective-permute-start.43
  264.1 1.8 collective-permute-start.58
  265.9 11.2 %collective-permute-done.43 = bf16[3,2,32,768]{3,2,0,1:T(8,128)(2,1)S(1)} collective-permute-done((bf16[3,2,32,768]{3,2,0,1:T(8,128)(2,1)S(1)}, bf16[3,2,32,768]{3,2,0,1:T(8,128)(2,1)S(1)}, u32[]{:S(2)}, u32[]{:S(2)}) %collective-permute-start.43) | collective-permute-done | bytes 294944 | tf_op jit(solution)/shard_map/ppermute | solution.py:599
  281.8 9.9 %collective-permute-done.44 = bf16[2,3,2,32,768]{4,3,1,2,0:T(8,128)(2,1)S(1)} collective-permute-done((bf16[2,3,2,32,768]{4,3,1,2,0:T(8,128)(2,1)S(1)}, bf16[2,3,2,32,768]{4,3,1,2,0:T(8,128)(2,1)S(1)}, u32[]{:S(2)}, u32[]{:S(2)}) %collective-permute-start.44) | collective-permute-done | bytes 589856 | tf_op jit(solution)/shard_map/ppermute | solution.py:599
  295.2 28.5 %collective-permute-done.55 = bf16[576,768]{1,0:T(8,128)(2,1)S(1)} collective-permute-done((bf16[576,768]{1,0:T(8,128)(2,1)S(1)}, bf16[576,768]{1,0:T(8,128)(2,1)S(1)}, u32[]{:S(2)}, u32[]{:S(2)}) %collective-permute-start.55) | collective-permute-done | bytes 884768 | tf_op jit(solution)/shard_map/ppermute | solution.py:599
  330.1 2.6 fusion.1
  332.6 2.6 fusion
  335.7 2.0 slice.153
  (280 shorter events, 79.3 us)
Async XLA Ops:
  2.4 16.5 %collective-permute-start.4 = (s32[3,2,2,32]{3,2,1,0:T(2,128)S(1)}, s32[3,2,2,32]{3,2,1,0:T(2,128)S(1)}, u32[]{:S(2)}, u32[]{:S(2)}) collective-permute-start(s32[3,2,2,32]{3,2,1,0:T(2,128)S(1)} %get-tuple-element.156), channel_id=1, source_target_pairs={{0,8},{8,0},{1,9},{9,1},{2,10},{10,2},{3,11},{11,3},{4,12},{12,4},... | collective-permute-start | bytes 4616 | tf_op jit(solution)/shard_map/ppermute | solution.py:599
  7.9 68.1 %collective-permute-start.13 = (bf16[128,768]{1,0:T(8,128)(2,1)S(1)}, bf16[128,768]{1,0:T(8,128)(2,1)}, u32[]{:S(2)}, u32[]{:S(2)}) collective-permute-start(bf16[128,768]{1,0:T(8,128)(2,1)S(1)} %pad_maximum_fusion.19), channel_id=1, source_target_pairs={{0,2},{2,0},{1,3},{3,1},{4,6},{6,4},{5,7},{7,5},{8,10},{10,8},{9,1... | collective-permute-start | bytes 589832 | tf_op jit(solution)/shard_map/ppermute | solution.py:599
  12.4 19.8 %collective-permute-start.7 = (bf16[128,768]{1,0:T(8,128)(2,1)S(1)}, bf16[128,768]{1,0:T(8,128)(2,1)}, u32[]{:S(2)}, u32[]{:S(2)}) collective-permute-start(bf16[128,768]{1,0:T(8,128)(2,1)S(1)} %pad_maximum_fusion.18), channel_id=1, source_target_pairs={{0,2},{2,0},{1,3},{3,1},{4,6},{6,4},{5,7},{7,5},{8,10},{10,8},{9,1... | collective-permute-start | bytes 589832 | tf_op jit(solution)/shard_map/ppermute | solution.py:599
  13.2 8.3 %collective-permute-start.2 = (bf16[2,2,32,768]{3,2,1,0:T(8,128)(2,1)S(1)}, bf16[2,2,32,768]{3,2,1,0:T(8,128)(2,1)S(1)}, u32[]{:S(2)}, u32[]{:S(2)}) collective-permute-start(bf16[2,2,32,768]{3,2,1,0:T(8,128)(2,1)S(1)} %get-tuple-element.139), channel_id=1, source_target_pairs={{0,8},{8,0},{1,9},{9,1},{2,10},{10,2},{3,11},{11,3},{4,12},{12,4},... | collective-permute-start | bytes 589832 | tf_op jit(solution)/shard_map/ppermute | solution.py:599
  14.5 17.7 %collective-permute-start = (bf16[2,2,2,32,768]{4,3,2,1,0:T(8,128)(2,1)S(1)}, bf16[2,2,2,32,768]{4,3,2,1,0:T(8,128)(2,1)S(1)}, u32[]{:S(2)}, u32[]{:S(2)}) collective-permute-start(bf16[2,2,2,32,768]{4,3,2,1,0:T(8,128)(2,1)S(1)} %get-tuple-element.126), channel_id=1, source_target_pairs={{0,8},{8,0},{1,9},{9,1},{2,10},{10,2},{3,11},{11,3},{4,12},{12,4},... | collective-permute-start | bytes 1179656 | tf_op jit(solution)/shard_map/ppermute | solution.py:599
  18.9 42.7 %collective-permute-start.16 = (bf16[96,768]{1,0:T(8,128)(2,1)}, bf16[96,768]{1,0:T(8,128)(2,1)}, u32[]{:S(2)}, u32[]{:S(2)}) collective-permute-start(bf16[96,768]{1,0:T(8,128)(2,1)} %get-tuple-element.123), channel_id=1, source_target_pairs={{0,2},{2,0},{1,3},{3,1},{4,6},{6,4},{5,7},{7,5},{8,10},{10,8},{9,1... | collective-permute-start | bytes 442376 | tf_op jit(solution)/shard_map/ppermute | solution.py:599
  21.5 12.4 %collective-permute-start.5 = (s32[3,2,2,2,32]{4,3,2,1,0:T(2,128)S(1)}, s32[3,2,2,2,32]{4,3,2,1,0:T(2,128)S(1)}, u32[]{:S(2)}, u32[]{:S(2)}) collective-permute-start(s32[3,2,2,2,32]{4,3,2,1,0:T(2,128)S(1)} %get-tuple-element.154), channel_id=1, source_target_pairs={{0,4},{4,0},{1,5},{5,1},{2,6},{6,2},{3,7},{7,3},{8,12},{12,8},{9,1... | collective-permute-start | bytes 9224 | tf_op jit(solution)/shard_map/ppermute | solution.py:599
  32.3 9.0 %collective-permute-start.3 = (bf16[2,2,2,32,768]{4,3,2,1,0:T(8,128)(2,1)S(1)}, bf16[2,2,2,32,768]{4,3,2,1,0:T(8,128)(2,1)S(1)}, u32[]{:S(2)}, u32[]{:S(2)}) collective-permute-start(bf16[2,2,2,32,768]{4,3,2,1,0:T(8,128)(2,1)S(1)} %get-tuple-element.137), channel_id=1, source_target_pairs={{0,4},{4,0},{1,5},{5,1},{2,6},{6,2},{3,7},{7,3},{8,12},{12,8},{9,1... | collective-permute-start | bytes 1179656 | tf_op jit(solution)/shard_map/ppermute | solution.py:599
  33.9 8.4 %collective-permute-start.1 = (bf16[2,2,2,32,768]{4,3,2,1,0:T(8,128)(2,1)S(1)}, bf16[2,2,2,32,768]{4,3,2,1,0:T(8,128)(2,1)}, u32[]{:S(2)}, u32[]{:S(2)}) collective-permute-start(bf16[2,2,2,32,768]{4,3,2,1,0:T(8,128)(2,1)S(1)} %get-tuple-element.125), channel_id=1, source_target_pairs={{0,4},{4,0},{1,5},{5,1},{2,6},{6,2},{3,7},{7,3},{8,12},{12,8},{9,1... | collective-permute-start | bytes 1179656 | tf_op jit(solution)/shard_map/ppermute | solution.py:599
  40.8 22.3 %collective-permute-start.9 = (bf16[2,128,768]{2,1,0:T(8,128)(2,1)S(1)}, bf16[2,128,768]{2,1,0:T(8,128)(2,1)S(1)}, u32[]{:S(2)}, u32[]{:S(2)}) collective-permute-start(bf16[2,128,768]{2,1,0:T(8,128)(2,1)S(1)} %pad_maximum_fusion.10.near_ref.upn1_ref), channel_id=1, source_target_pairs={{0,8},{8,0},{1,9},{9,1},{2,10},{10,2},{3,11},{11,3},{4,12},{12,4},... | collective-permute-start | bytes 1179656 | tf_op jit(solution)/shard_map/ppermute | solution.py:599
  58.6 11.9 %collective-permute-start.6 = (bf16[256,192]{1,0:T(8,128)(2,1)}, bf16[256,192]{1,0:T(8,128)(2,1)S(1)}, u32[]{:S(2)}, u32[]{:S(2)}) collective-permute-start(bf16[256,192]{1,0:T(8,128)(2,1)} %get-tuple-element.62.atts_ref), channel_id=1, source_target_pairs={{0,2},{2,0},{1,3},{3,1},{4,6},{6,4},{5,7},{7,5},{8,10},{10,8},{9,1... | collective-permute-start | bytes 294920 | tf_op jit(solution)/shard_map/ppermute | solution.py:599
  58.6 15.7 %collective-permute-start.19 = (bf16[96,768]{1,0:T(8,128)(2,1)S(1)}, bf16[96,768]{1,0:T(8,128)(2,1)S(1)}, u32[]{:S(2)}, u32[]{:S(2)}) collective-permute-start(bf16[96,768]{1,0:T(8,128)(2,1)S(1)} %copy-done.29), channel_id=1, source_target_pairs={{0,2},{2,0},{1,3},{3,1},{4,6},{6,4},{5,7},{7,5},{8,10},{10,8},{9,1... | collective-permute-start | bytes 442376 | tf_op jit(solution)/shard_map/ppermute | solution.py:599
  61.5 14.9 %collective-permute-start.17 = (bf16[96,768]{1,0:T(8,128)(2,1)}, bf16[96,768]{1,0:T(8,128)(2,1)S(1)}, u32[]{:S(2)}, u32[]{:S(2)}) collective-permute-start(bf16[96,768]{1,0:T(8,128)(2,1)} %collective-permute-done.16), channel_id=1, source_target_pairs={{0,16},{16,0},{1,17},{17,1},{2,18},{18,2},{3,19},{19,3},{4,20},{20... | collective-permute-start | bytes 442376 | tf_op jit(solution)/shard_map/ppermute | solution.py:599
  76.0 9.3 %collective-permute-start.14 = (bf16[128,768]{1,0:T(8,128)(2,1)}, bf16[128,768]{1,0:T(8,128)(2,1)S(1)}, u32[]{:S(2)}, u32[]{:S(2)}) collective-permute-start(bf16[128,768]{1,0:T(8,128)(2,1)} %collective-permute-done.13), channel_id=1, source_target_pairs={{0,8},{8,0},{1,9},{9,1},{2,10},{10,2},{3,11},{11,3},{4,12},{12,4},... | collective-permute-start | bytes 589832 | tf_op jit(solution)/shard_map/ppermute | solution.py:599
  77.4 13.7 %collective-permute-start.18 = (bf16[2,96,768]{2,1,0:T(8,128)(2,1)S(1)}, bf16[2,96,768]{2,1,0:T(8,128)(2,1)S(1)}, u32[]{:S(2)}, u32[]{:S(2)}) collective-permute-start(bf16[2,96,768]{2,1,0:T(8,128)(2,1)S(1)} %pad_maximum_fusion.14.dnn1_ref), channel_id=1, source_target_pairs={{0,8},{8,0},{1,9},{9,1},{2,10},{10,2},{3,11},{11,3},{4,12},{12,4},... | collective-permute-start | bytes 884744 | tf_op jit(solution)/shard_map/ppermute | solution.py:599
  80.1 7.8 %collective-permute-start.11 = (bf16[128,768]{1,0:T(8,128)(2,1)S(1)}, bf16[128,768]{1,0:T(8,128)(2,1)S(1)}, u32[]{:S(2)}, u32[]{:S(2)}) collective-permute-start(bf16[128,768]{1,0:T(8,128)(2,1)S(1)} %add_convert_fusion.13), channel_id=1, source_target_pairs={{0,1},{1,0},{2,3},{3,2},{4,5},{5,4},{6,7},{7,6},{8,9},{9,8},{10,11... | collective-permute-start | bytes 589832 | tf_op jit(solution)/shard_map/ppermute | solution.py:599
  81.1 10.0 %collective-permute-start.21 = (bf16[2,96,768]{2,1,0:T(8,128)(2,1)S(1)}, bf16[2,96,768]{2,1,0:T(8,128)(2,1)S(1)}, u32[]{:S(2)}, u32[]{:S(2)}) collective-permute-start(bf16[2,96,768]{2,1,0:T(8,128)(2,1)S(1)} %pad_maximum_fusion.15.dnn2_ref), channel_id=1, source_target_pairs={{0,16},{16,0},{1,17},{17,1},{2,18},{18,2},{3,19},{19,3},{4,20},{20... | collective-permute-start | bytes 884744 | tf_op jit(solution)/shard_map/ppermute | solution.py:599
  86.3 11.4 %collective-permute-start.15 = (bf16[2,128,768]{2,1,0:T(8,128)(2,1)S(1)}, bf16[2,128,768]{2,1,0:T(8,128)(2,1)S(1)}, u32[]{:S(2)}, u32[]{:S(2)}) collective-permute-start(bf16[2,128,768]{2,1,0:T(8,128)(2,1)S(1)} %pad_maximum_fusion.11.upn2_ref), channel_id=1, source_target_pairs={{0,16},{16,0},{1,17},{17,1},{2,18},{18,2},{3,19},{19,3},{4,20},{20... | collective-permute-start | bytes 1179656 | tf_op jit(solution)/shard_map/ppermute | solution.py:599
  87.9 9.8 %collective-permute-start.12 = (bf16[128,768]{1,0:T(8,128)(2,1)S(1)}, bf16[128,768]{1,0:T(8,128)(2,1)S(1)}, u32[]{:S(2)}, u32[]{:S(2)}) collective-permute-start(bf16[128,768]{1,0:T(8,128)(2,1)S(1)} %fusion.11.mixed0_ref), channel_id=1, source_target_pairs={{0,4},{4,0},{1,5},{5,1},{2,6},{6,2},{3,7},{7,3},{8,12},{12,8},{9,1... | collective-permute-start | bytes 589832 | tf_op jit(solution)/shard_map/ppermute | solution.py:599
  88.1 19.6 %collective-permute-start.23 = (bf16[2,2,32,768]{3,2,1,0:T(8,128)(2,1)S(1)}, bf16[2,2,32,768]{3,2,1,0:T(8,128)(2,1)S(1)}, u32[]{:S(2)}, u32[]{:S(2)}) collective-permute-start(bf16[2,2,32,768]{3,2,1,0:T(8,128)(2,1)S(1)} %get-tuple-element.134), channel_id=1, source_target_pairs={{0,8},{8,0},{1,9},{9,1},{2,10},{10,2},{3,11},{11,3},{4,12},{12,4},... | collective-permute-start | bytes 589832 | tf_op jit(solution)/shard_map/ppermute | solution.py:599
  106.4 10.3 %collective-permute-start.22 = (bf16[256,768]{1,0:T(8,128)(2,1)}, bf16[256,768]{1,0:T(8,128)(2,1)S(1)}, u32[]{:S(2)}, u32[]{:S(2)}) collective-permute-start(bf16[256,768]{1,0:T(8,128)(2,1)} %get-tuple-element.65.low_ref), channel_id=1, source_target_pairs={{0,1},{1,0},{2,3},{3,2},{4,5},{5,4},{6,7},{7,6},{8,9},{9,8},{10,11... | collective-permute-start | bytes 1179656 | tf_op jit(solution)/shard_map/ppermute | solution.py:599
  129.2 15.7 %collective-permute-start.29 = (bf16[256,768]{1,0:T(8,128)(2,1)}, bf16[256,768]{1,0:T(8,128)(2,1)S(1)}, u32[]{:S(2)}, u32[]{:S(2)}) collective-permute-start(bf16[256,768]{1,0:T(8,128)(2,1)} %get-tuple-element.72.hid_ref), channel_id=1, source_target_pairs={{0,1},{1,0},{2,3},{3,2},{4,5},{5,4},{6,7},{7,6},{8,9},{9,8},{10,11... | collective-permute-start | bytes 1179656 | tf_op jit(solution)/shard_map/ppermute | solution.py:599
  132.6 21.5 %collective-permute-start.27 = (bf16[2,2,32,768]{3,2,1,0:T(8,128)(2,1)S(1)}, bf16[2,2,32,768]{3,2,1,0:T(8,128)(2,1)S(1)}, u32[]{:S(2)}, u32[]{:S(2)}) collective-permute-start(bf16[2,2,32,768]{3,2,1,0:T(8,128)(2,1)S(1)} %get-tuple-element.145), channel_id=1, source_target_pairs={{0,2},{2,0},{1,3},{3,1},{4,6},{6,4},{5,7},{7,5},{8,10},{10,8},{9,1... | collective-permute-start | bytes 589832 | tf_op jit(solution)/shard_map/ppermute | solution.py:599
  133.2 25.1 %collective-permute-start.47 = (bf16[128,768]{1,0:T(8,128)(2,1)S(1)}, bf16[128,768]{1,0:T(8,128)(2,1)S(1)}, u32[]{:S(2)}, u32[]{:S(2)}) collective-permute-start(bf16[128,768]{1,0:T(8,128)(2,1)S(1)} %copy-done.4), channel_id=1, source_target_pairs={{0,2},{2,0},{1,3},{3,1},{4,6},{6,4},{5,7},{7,5},{8,10},{10,8},{9,1... | collective-permute-start | bytes 589832 | tf_op jit(solution)/shard_map/ppermute | solution.py:599
  135.6 25.3 %collective-permute-start.49 = (bf16[128,768]{1,0:T(8,128)(2,1)}, bf16[128,768]{1,0:T(8,128)(2,1)S(1)}, u32[]{:S(2)}, u32[]{:S(2)}) collective-permute-start(bf16[128,768]{1,0:T(8,128)(2,1)} %get-tuple-element.101), channel_id=1, source_target_pairs={{0,2},{2,0},{1,3},{3,1},{4,6},{6,4},{5,7},{7,5},{8,10},{10,8},{9,1... | collective-permute-start | bytes 589832 | tf_op jit(solution)/shard_map/ppermute | solution.py:599
  149.8 32.6 %collective-permute-start.30 = (bf16[256,768]{1,0:T(8,128)(2,1)}, bf16[256,768]{1,0:T(8,128)(2,1)S(1)}, u32[]{:S(2)}, u32[]{:S(2)}) collective-permute-start(bf16[256,768]{1,0:T(8,128)(2,1)} %get-tuple-element.73.dmix_ref), channel_id=1, source_target_pairs={{0,4},{4,0},{1,5},{5,1},{2,6},{6,2},{3,7},{7,3},{8,12},{12,8},{9,1... | collective-permute-start | bytes 1179656 | tf_op jit(solution)/shard_map/ppermute | solution.py:599
  154.2 35.1 %collective-permute-start.28 = (bf16[2,2,2,32,768]{4,3,2,1,0:T(8,128)(2,1)S(1)}, bf16[2,2,2,32,768]{4,3,2,1,0:T(8,128)(2,1)S(1)}, u32[]{:S(2)}, u32[]{:S(2)}) collective-permute-start(bf16[2,2,2,32,768]{4,3,2,1,0:T(8,128)(2,1)S(1)} %get-tuple-element.131), channel_id=1, source_target_pairs={{0,1},{1,0},{2,3},{3,2},{4,5},{5,4},{6,7},{7,6},{8,9},{9,8},{10,11... | collective-permute-start | bytes 1179656 | tf_op jit(solution)/shard_map/ppermute | solution.py:599
  160.9 12.5 %collective-permute-start.50 = (bf16[128,768]{1,0:T(8,128)(2,1)S(1)}, bf16[128,768]{1,0:T(8,128)(2,1)S(1)}, u32[]{:S(2)}, u32[]{:S(2)}) collective-permute-start(bf16[128,768]{1,0:T(8,128)(2,1)S(1)} %collective-permute-done.49.dlow0_ref), channel_id=1, source_target_pairs={{0,1},{1,0},{2,3},{3,2},{4,5},{5,4},{6,7},{7,6},{8,9},{9,8},{10,11... | collective-permute-start | bytes 589832 | tf_op jit(solution)/shard_map/ppermute | solution.py:599
  180.1 83.6 %collective-permute-start.57 = (bf16[768,768]{1,0:T(8,128)(2,1)}, bf16[768,768]{1,0:T(8,128)(2,1)S(1)}, u32[]{:S(2)}, u32[]{:S(2)}) collective-permute-start(bf16[768,768]{1,0:T(8,128)(2,1)} %get-tuple-element.107), channel_id=1, source_target_pairs={{0,16},{16,0},{1,17},{17,1},{2,18},{18,2},{3,19},{19,3},{4,20},{20... | collective-permute-start | bytes 3538952 | tf_op jit(solution)/shard_map/ppermute | solution.py:599
  181.6 95.7 %collective-permute-start.60 = (bf16[768,768]{1,0:T(8,128)(2,1)}, bf16[768,768]{1,0:T(8,128)(2,1)S(1)}, u32[]{:S(2)}, u32[]{:S(2)}) collective-permute-start(bf16[768,768]{1,0:T(8,128)(2,1)} %get-tuple-element.108), channel_id=1, source_target_pairs={{0,8},{8,0},{1,9},{9,1},{2,10},{10,2},{3,11},{11,3},{4,12},{12,4},... | collective-permute-start | bytes 3538952 | tf_op jit(solution)/shard_map/ppermute | solution.py:599
  186.3 12.8 %collective-permute-start.31 = (bf16[256,192]{1,0:T(8,128)(2,1)}, bf16[256,192]{1,0:T(8,128)(2,1)S(1)}, u32[]{:S(2)}, u32[]{:S(2)}) collective-permute-start(bf16[256,192]{1,0:T(8,128)(2,1)} %get-tuple-element.78), channel_id=1, source_target_pairs={{0,2},{2,0},{1,3},{3,1},{4,6},{6,4},{5,7},{7,5},{8,10},{10,8},{9,1... | collective-permute-start | bytes 294920 | tf_op jit(solution)/shard_map/ppermute | solution.py:599
  186.3 31.2 %collective-permute-start.45 = (bf16[144,768]{1,0:T(8,128)(2,1)}, bf16[144,768]{1,0:T(8,128)(2,1)S(1)}, u32[]{:S(2)}, u32[]{:S(2)}) collective-permute-start(bf16[144,768]{1,0:T(8,128)(2,1)} %get-tuple-element.92.pay_ref), channel_id=1, source_target_pairs={{0,2},{2,0},{1,3},{3,1},{4,6},{6,4},{5,7},{7,5},{8,10},{10,8},{9,1... | collective-permute-start | bytes 663560 | tf_op jit(solution)/shard_map/ppermute | solution.py:599
  209.8 25.8 %collective-permute-start.34 = (bf16[128,768]{1,0:T(8,128)(2,1)S(1)}, bf16[128,768]{1,0:T(8,128)(2,1)S(1)}, u32[]{:S(2)}, u32[]{:S(2)}) collective-permute-start(bf16[128,768]{1,0:T(8,128)(2,1)S(1)} %copy-done.38), channel_id=1, source_target_pairs={{0,4},{4,0},{1,5},{5,1},{2,6},{6,2},{3,7},{7,3},{8,12},{12,8},{9,1... | collective-permute-start | bytes 589832 | tf_op jit(solution)/shard_map/ppermute | solution.py:599
  216.3 7.6 %collective-permute-start.33 = (bf16[64,768]{1,0:T(8,128)(2,1)S(1)}, bf16[64,768]{1,0:T(8,128)(2,1)S(1)}, u32[]{:S(2)}, u32[]{:S(2)}) collective-permute-start(bf16[64,768]{1,0:T(8,128)(2,1)S(1)} %slice.144), channel_id=1, source_target_pairs={{0,2},{2,0},{1,3},{3,1},{4,6},{6,4},{5,7},{7,5},{8,10},{10,8},{9,1... | collective-permute-start | bytes 294920 | tf_op jit(solution)/shard_map/ppermute | solution.py:599
  223.9 15.3 %collective-permute-start.38 = (bf16[128,768]{1,0:T(8,128)(2,1)S(1)}, bf16[128,768]{1,0:T(8,128)(2,1)S(1)}, u32[]{:S(2)}, u32[]{:S(2)}) collective-permute-start(bf16[128,768]{1,0:T(8,128)(2,1)S(1)} %copy-done.37), channel_id=1, source_target_pairs={{0,4},{4,0},{1,5},{5,1},{2,6},{6,2},{3,7},{7,3},{8,12},{12,8},{9,1... | collective-permute-start | bytes 589832 | tf_op jit(solution)/shard_map/ppermute | solution.py:599
  225.3 11.7 %collective-permute-start.36 = (bf16[128,768]{1,0:T(8,128)(2,1)S(1)}, bf16[128,768]{1,0:T(8,128)(2,1)S(1)}, u32[]{:S(2)}, u32[]{:S(2)}) collective-permute-start(bf16[128,768]{1,0:T(8,128)(2,1)S(1)} %collective-permute-done.35), channel_id=1, source_target_pairs={{0,1},{1,0},{2,3},{3,2},{4,5},{5,4},{6,7},{7,6},{8,9},{9,8},{10,11... | collective-permute-start | bytes 589832 | tf_op jit(solution)/shard_map/ppermute | solution.py:599
  235.6 8.1 %collective-permute-start.40 = (bf16[128,768]{1,0:T(8,128)(2,1)S(1)}, bf16[128,768]{1,0:T(8,128)(2,1)S(1)}, u32[]{:S(2)}, u32[]{:S(2)}) collective-permute-start(bf16[128,768]{1,0:T(8,128)(2,1)S(1)} %add_convert_fusion.9), channel_id=1, source_target_pairs={{0,1},{1,0},{2,3},{3,2},{4,5},{5,4},{6,7},{7,6},{8,9},{9,8},{10,11... | collective-permute-start | bytes 589832 | tf_op jit(solution)/shard_map/ppermute | solution.py:599
  237.0 41.2 %collective-permute-start.54 = (bf16[576,768]{1,0:T(8,128)(2,1)}, bf16[576,768]{1,0:T(8,128)(2,1)S(1)}, u32[]{:S(2)}, u32[]{:S(2)}) collective-permute-start(bf16[576,768]{1,0:T(8,128)(2,1)} %get-tuple-element.106), channel_id=1, source_target_pairs={{0,8},{8,0},{1,9},{9,1},{2,10},{10,2},{3,11},{11,3},{4,12},{12,4},... | collective-permute-start | bytes 2654216 | tf_op jit(solution)/shard_map/ppermute | solution.py:599
  239.2 8.5 %collective-permute-start.37 = (bf16[64,768]{1,0:T(8,128)(2,1)S(1)}, bf16[64,768]{1,0:T(8,128)(2,1)S(1)}, u32[]{:S(2)}, u32[]{:S(2)}) collective-permute-start(bf16[64,768]{1,0:T(8,128)(2,1)S(1)} %slice.146), channel_id=1, source_target_pairs={{0,2},{2,0},{1,3},{3,1},{4,6},{6,4},{5,7},{7,5},{8,10},{10,8},{9,1... | collective-permute-start | bytes 294920 | tf_op jit(solution)/shard_map/ppermute | solution.py:599
  250.8 11.1 %collective-permute-start.42 = (bf16[3,32,768]{2,1,0:T(8,128)(2,1)S(1)}, bf16[3,32,768]{2,1,0:T(8,128)(2,1)S(1)}, u32[]{:S(2)}, u32[]{:S(2)}) collective-permute-start(bf16[3,32,768]{2,1,0:T(8,128)(2,1)S(1)} %get-tuple-element.143), channel_id=1, source_target_pairs={{0,8},{8,0},{1,9},{9,1},{2,10},{10,2},{3,11},{11,3},{4,12},{12,4},... | collective-permute-start | bytes 442376 | tf_op jit(solution)/shard_map/ppermute | solution.py:599
  254.8 25.3 %collective-permute-start.51 = (bf16[608,768]{1,0:T(8,128)(2,1)S(1)}, bf16[608,768]{1,0:T(8,128)(2,1)S(1)}, u32[]{:S(2)}, u32[]{:S(2)}) collective-permute-start(bf16[608,768]{1,0:T(8,128)(2,1)S(1)} %copy-done.12), channel_id=1, source_target_pairs={{0,16},{16,0},{1,17},{17,1},{2,18},{18,2},{3,19},{19,3},{4,20},{20... | collective-permute-start | bytes 2801672 | tf_op jit(solution)/shard_map/ppermute | solution.py:599
  261.9 15.2 %collective-permute-start.43 = (bf16[3,2,32,768]{3,2,0,1:T(8,128)(2,1)S(1)}, bf16[3,2,32,768]{3,2,0,1:T(8,128)(2,1)S(1)}, u32[]{:S(2)}, u32[]{:S(2)}) collective-permute-start(bf16[3,2,32,768]{3,2,0,1:T(8,128)(2,1)S(1)} %get-tuple-element.141), channel_id=1, source_target_pairs={{0,2},{2,0},{1,3},{3,1},{4,6},{6,4},{5,7},{7,5},{8,10},{10,8},{9,1... | collective-permute-start | bytes 884744 | tf_op jit(solution)/shard_map/ppermute | solution.py:599
  264.1 60.0 %collective-permute-start.58 = (bf16[768,768]{1,0:T(8,128)(2,1)S(1)}, bf16[768,768]{1,0:T(8,128)(2,1)S(1)}, u32[]{:S(2)}, u32[]{:S(2)}) collective-permute-start(bf16[768,768]{1,0:T(8,128)(2,1)S(1)} %add_convert_fusion.3), channel_id=1, source_target_pairs={{0,8},{8,0},{1,9},{9,1},{2,10},{10,2},{3,11},{11,3},{4,12},{12,4},... | collective-permute-start | bytes 3538952 | tf_op jit(solution)/shard_map/ppermute | solution.py:599
  277.2 14.5 %collective-permute-start.44 = (bf16[2,3,2,32,768]{4,3,1,2,0:T(8,128)(2,1)S(1)}, bf16[2,3,2,32,768]{4,3,1,2,0:T(8,128)(2,1)S(1)}, u32[]{:S(2)}, u32[]{:S(2)}) collective-permute-start(bf16[2,3,2,32,768]{4,3,1,2,0:T(8,128)(2,1)S(1)} %get-tuple-element.129), channel_id=1, source_target_pairs={{0,1},{1,0},{2,3},{3,2},{4,5},{5,4},{6,7},{7,6},{8,9},{9,8},{10,11... | collective-permute-start | bytes 1769480 | tf_op jit(solution)/shard_map/ppermute | solution.py:599
  277.6 47.3 %collective-permute-start.61 = (bf16[768,768]{1,0:T(8,128)(2,1)S(1)}, bf16[768,768]{1,0:T(8,128)(2,1)S(1)}, u32[]{:S(2)}, u32[]{:S(2)}) collective-permute-start(bf16[768,768]{1,0:T(8,128)(2,1)S(1)} %add_convert_fusion.1), channel_id=1, source_target_pairs={{0,16},{16,0},{1,17},{17,1},{2,18},{18,2},{3,19},{19,3},{4,20},{20... | collective-permute-start | bytes 3538952 | tf_op jit(solution)/shard_map/ppermute | solution.py:599
  278.6 45.1 %collective-permute-start.55 = (bf16[576,768]{1,0:T(8,128)(2,1)S(1)}, bf16[576,768]{1,0:T(8,128)(2,1)S(1)}, u32[]{:S(2)}, u32[]{:S(2)}) collective-permute-start(bf16[576,768]{1,0:T(8,128)(2,1)S(1)} %add_convert_fusion.7), channel_id=1, source_target_pairs={{0,16},{16,0},{1,17},{17,1},{2,18},{18,2},{3,19},{19,3},{4,20},{20... | collective-permute-start | bytes 2654216 | tf_op jit(solution)/shard_map/ppermute | solution.py:599
  280.3 45.0 %collective-permute-start.52 = (bf16[608,768]{1,0:T(8,128)(2,1)S(1)}, bf16[608,768]{1,0:T(8,128)(2,1)S(1)}, u32[]{:S(2)}, u32[]{:S(2)}) collective-permute-start(bf16[608,768]{1,0:T(8,128)(2,1)S(1)} %add_convert_fusion.5), channel_id=1, source_target_pairs={{0,8},{8,0},{1,9},{9,1},{2,10},{10,2},{3,11},{11,3},{4,12},{12,4},... | collective-permute-start | bytes 2801672 | tf_op jit(solution)/shard_map/ppermute | solution.py:599
  325.6 9.6 %collective-permute-start.53 = (bf16[608,768]{1,0:T(8,128)(2,1)S(1)}, bf16[608,768]{1,0:T(8,128)(2,1)S(1)}, u32[]{:S(2)}, u32[]{:S(2)}) collective-permute-start(bf16[608,768]{1,0:T(8,128)(2,1)S(1)} %add_convert_fusion.4), channel_id=1, source_target_pairs={{0,4},{4,0},{1,5},{5,1},{2,6},{6,2},{3,7},{7,3},{8,12},{12,8},{9,1... | collective-permute-start | bytes 2801672 | tf_op jit(solution)/shard_map/ppermute | solution.py:599
  (56 other events, 365.5 us)

commit v3 on v2

v3 whole, which is shorter than its diff:
```python
import functools

import jax
import jax.numpy as jnp
from jax import lax
from jax.experimental import pallas as pl
from jax.experimental.pallas import tpu as pltpu
from jax.sharding import Mesh, PartitionSpec as P

DH = 64
NBUCK = 128
HALF = 64
EPSILON = 1e-05
F32 = jnp.float32
BF16 = jnp.bfloat16
VMEM_BYTES = 20 * 1024 * 1024
TICK = 0.1
PACK_VMEM = 60 * 1024 * 1024
NN = (((1,), (0,)), ((), ()))
NT = (((1,), (1,)), ((), ()))
TN = (((0,), (0,)), ((), ()))


def mm(left, right, dims=NN):
    return lax.dot_general(left, right, dims, preferred_element_type=F32)


def kernel_call(body, place, operands, outs, us, scratch=(), after=(), vmem=VMEM_BYTES):
    specs, arrays, hows = [], [], []
    for operand in operands:
        array, how = operand if isinstance(operand, tuple) else (operand, None)
        specs.append(pl.BlockSpec(memory_space=pltpu.HBM if how == "any" else pltpu.VMEM))
        arrays.append(array)
        hows.append(how)
    count = len(arrays)
    specs += [pl.BlockSpec(memory_space=pl.ANY)] * len(after)

    def view(s_ref, ref, how):
        if how == "stream":
            return ref.at[s_ref[0]]
        if how is None or how == "any":
            return ref
        return ref.at[tuple(slice(None) if at is None else at for at in how)]

    def kernel(s_ref, *refs):
        given = [view(s_ref, ref, how) for ref, how in zip(refs, hows)]
        body(s_ref, *given, *refs[count + len(after) :])

    return pl.pallas_call(
        kernel,
        out_shape=[jax.ShapeDtypeStruct(out[0], out[1]) for out in outs],
        in_specs=[pl.BlockSpec(memory_space=pltpu.SMEM)] + specs,
        out_specs=[
            pl.BlockSpec(memory_space=pltpu.HBM if len(out) > 2 else pltpu.VMEM) for out in outs
        ],
        scratch_shapes=list(scratch),
        compiler_params=pltpu.CompilerParams(vmem_limit_bytes=vmem),
        cost_estimate=pl.CostEstimate(
            flops=int(us * 1.1e9), bytes_accessed=int(us * 3.5e6), transcendentals=0
        ),
    )(place, *arrays, *after)


def centred(rows):
    centre = rows - jnp.mean(rows, axis=-1, keepdims=True)
    spread = lax.rsqrt(jnp.mean(centre * centre, axis=-1, keepdims=True) + EPSILON)
    return centre * spread, spread


def norm_back(unit, spread, tilted):
    return spread * (
        tilted
        - jnp.mean(tilted, axis=-1, keepdims=True)
        - unit * jnp.mean(tilted * unit, axis=-1, keepdims=True)
    )


def pick(table_row, index):
    width = index.shape[1]
    table = jnp.broadcast_to(table_row, (index.shape[0], NBUCK))
    parts = [
        jnp.take_along_axis(
            table,
            index[:, at : at + NBUCK],
            axis=1,
            mode="promise_in_bounds",
        )
        for at in range(0, width, NBUCK)
    ]
    return jnp.concatenate(parts, axis=1)


def stack_rows(pieces):
    return jnp.concatenate(pieces, axis=0)


def turned(rows, size):
    pieces = [rows[at : at + size] for at in range(0, rows.shape[0], size)]
    return stack_rows([pieces[i ^ 1] for i in range(len(pieces))])


def residual(x_ref, mixed_refs):
    rest = mixed_refs[0].shape[0] // 2
    pieces = []
    for y in range(2):
        for c in range(2):
            own = x_ref[y, c * rest : (c + 1) * rest, :].astype(F32)
            pieces.append(own + mixed_refs[c][y * rest : (y + 1) * rest, :].astype(F32))
    return stack_rows(pieces)


def dealt(rows_ref, side, keep_ref, send_ref):
    half = keep_ref.shape[0]
    keep_ref[...] = rows_ref[pl.ds(pl.multiple_of(side * half, 16), half), :]
    send_ref[...] = rows_ref[pl.ds(pl.multiple_of((1 - side) * half, 16), half), :]


def gathered(place_ref, refs, rows, to_ref):
    size = rows.stop - rows.start
    for turn, ref in enumerate(refs):
        q = (place_ref[1] ^ (turn // 2)) * 2 + (place_ref[2] ^ (turn % 2))
        to_ref[pl.ds(pl.multiple_of(q * size, 16), size), :] = ref[rows, :]


def pack_kernel(
    p_ref,
    tok_ref,
    sp_ref,
    pos_ref,
    box_ref,
    exit_ref,
    up_ref,
    down_ref,
    bias_ref,
    cot_ref,
    far_ref,
    near_ref,
    own_ref,
    ups_ref,
    downs_ref,
    cotfar_ref,
    cotnear_ref,
    cotown_ref,
    posv_ref,
    boxv_ref,
    biasv_ref,
    sems,
):
    c, y, zl, zh = p_ref[0], p_ref[2], p_ref[3], p_ref[4]
    block = zh * 2 + zl
    q = p_ref[1] * 2 + y
    least = tok_ref.shape[3]
    rows = 4 * least
    many = down_ref.shape[1] // 4
    few = exit_ref.shape[1] // 4
    pairs = [(pos_ref, posv_ref), (box_ref, boxv_ref), (bias_ref, biasv_ref)]
    for k in range(4):
        at = block ^ k
        to = k * least
        pairs += [
            (tok_ref.at[1 - c, 1 - y, at], far_ref.at[pl.ds(to, least)]),
            (sp_ref.at[1 - y, at], far_ref.at[pl.ds(rows + to, least)]),
            (tok_ref.at[c, 1 - y, at], far_ref.at[pl.ds(2 * rows + 16 + to, least)]),
            (tok_ref.at[1 - c, y, at], near_ref.at[pl.ds(to, least)]),
            (sp_ref.at[y, at], near_ref.at[pl.ds(rows + to, least)]),
            (tok_ref.at[c, y, at], own_ref.at[pl.ds(to, least)]),
        ]
    pairs += [
        (exit_ref.at[c, pl.ds(pl.multiple_of(q * few, 16), few)], ups_ref.at[pl.ds(many + 16, few)]),
        (up_ref.at[c, pl.ds(pl.multiple_of(q * many, 16), many)], ups_ref.at[pl.ds(0, many)]),
        (down_ref.at[c, pl.ds(pl.multiple_of(q * many, 16), many)], downs_ref),
    ]
    for k in range(2):
        at = zh * 2 + (zl ^ k)
        to = pl.ds(k * least, least)
        pairs += [
            (cot_ref.at[c, 1 - y, at], cotfar_ref.at[0, to]),
            (cot_ref.at[1 - c, 1 - y, at], cotfar_ref.at[1, to]),
            (cot_ref.at[1 - c, y, at], cotnear_ref.at[to]),
            (cot_ref.at[c, y, at], cotown_ref.at[to]),
        ]
    started = [
        pltpu.make_async_copy(source, target, sems.at[n])
        for n, (source, target) in enumerate(pairs)
    ]
    for copy in started:
        copy.start()
    for copy in started[:3]:
        copy.wait()
    lane = lax.broadcasted_iota(jnp.int32, (8, NBUCK), 1)
    width = far_ref.shape[1]
    for page, ref in ((1 - y, far_ref), (y, near_ref)):
        place = posv_ref[pl.ds(page, 1), :]
        lines = [place & 255, place >> 8, boxv_ref[0, pl.ds(page, 1), :], boxv_ref[1, pl.ds(page, 1), :]]
        value = jnp.concatenate(lines + [jnp.zeros((4, NBUCK), jnp.int32)], axis=0)
        crossed = jnp.where(
            (lane & 63) < 32, pltpu.roll(value, NBUCK - 32, 1), pltpu.roll(value, 32, 1)
        )
        value = jnp.where(zl == 0, value, crossed)
        value = jnp.where(zh == 0, value, pltpu.roll(value, 64, 1))
        value = jnp.concatenate([value.astype(F32), jnp.zeros((8, NBUCK), F32)], axis=0)
        ref[2 * rows : 2 * rows + 16, 0:NBUCK] = value.astype(BF16)
        ref[2 * rows : 2 * rows + 16, NBUCK:] = jnp.zeros((16, width - NBUCK), BF16)
    left = biasv_ref[pl.ds(c, 1), :]
    lines = []
    for _ in range(3):
        lines.append(left.astype(BF16).astype(F32))
        left = left - lines[-1]
    lines.append(jnp.zeros((13, left.shape[1]), F32))
    ups_ref[many : many + 16, :] = jnp.concatenate(lines, axis=0).astype(BF16)
    for copy in started[3:]:
        copy.wait()


def indices(ref, least):
    lines = ref[2 * least : 2 * least + 16, 0:NBUCK].astype(F32).astype(jnp.int32)
    place = lines[0:1] + lines[1:2] * 256
    return jnp.concatenate([place, lines[2:4], jnp.zeros((5, NBUCK), jnp.int32)], axis=0)


def two_cores(index0, index1, half):
    lane = lax.broadcasted_iota(jnp.int32, (8, NBUCK), 1)
    if half == 0:
        return jnp.where(lane < 64, index0, pltpu.roll(index1, 64, 1))
    return jnp.where(lane < 64, pltpu.roll(index0, 64, 1), index1)


def arrange(x0_ref, n0_ref, n1_ref, x_ref, sp_ref):
    least = x_ref.shape[1]
    rest = least // 2
    found = []
    index0, index1 = indices(n0_ref, least), indices(n1_ref, least)
    for half in range(2):
        at = half * rest
        x_ref[half, 0:rest, :] = x0_ref[at : at + rest, :]
        x_ref[half, rest:, :] = n1_ref[at : at + rest, :]
        sp_ref[half, 0:rest, :] = n0_ref[least + at : least + at + rest, :]
        sp_ref[half, rest:, :] = n1_ref[least + at : least + at + rest, :]
        found.append(two_cores(index0, index1, half))
    return found


def project(x_ref, sp_ref, w_ref, ws_ref, proj_ref, spat_ref, at):
    width = x_ref.shape[-1]
    x = x_ref[...].reshape(-1, width)
    sp = sp_ref[...].reshape(-1, width)
    rows = slice(at, at + x.shape[0])
    for k in range(3):
        proj_ref[k, rows, :] = mm(x, w_ref[k], NT).astype(BF16)
    for k in range(2):
        spat_ref[k, rows, :] = mm(sp, ws_ref[k], NT).astype(BF16)


def near_kernel(
    p_ref,
    x00_ref,
    n01_ref,
    n00_ref,
    w_ref,
    ws_ref,
    up_hbm,
    down_hbm,
    exit_hbm,
    x_ref,
    sp_ref,
    index_ref,
    proj_ref,
    spat_ref,
    up_ref,
    down_ref,
    exit_ref,
    sems,
):
    fetched = [
        pltpu.make_async_copy(source.at[p_ref[0]], target, sems.at[n])
        for n, (source, target) in enumerate(
            ((exit_hbm, exit_ref), (up_hbm, up_ref), (down_hbm, down_ref))
        )
    ]
    for copy in fetched:
        copy.start()
    found = arrange(x00_ref, n00_ref, n01_ref, x_ref, sp_ref)
    index_ref[...] = jnp.concatenate(found, axis=1)
    project(x_ref, sp_ref, w_ref, ws_ref, proj_ref, spat_ref, 0)
    for copy in fetched:
        copy.wait()


def attention_kernel(
    p_ref,
    n11_ref,
    n10_ref,
    x0_ref,
    sp0_ref,
    index_ref,
    proj0_ref,
    spat0_ref,
    w_ref,
    ws_ref,
    table_ref,
    x_ref,
    sp_ref,
    colidx_ref,
    proj_hbm,
    spat_hbm,
    soft_hbm,
    own_ref,
    send_ref,
    att_ref,
    proj_ref,
    spat_ref,
    soft_ref,
    sems,
    *,
    heads,
    block,
):
    least = x_ref.shape[2]
    near = 2 * least
    x_ref[0] = x0_ref[...]
    sp_ref[0] = sp0_ref[...]
    proj_ref[:, 0:near, :] = proj0_ref[...]
    spat_ref[:, 0:near, :] = spat0_ref[...]
    found = arrange(
        n10_ref.at[2 * least + 16 :], n10_ref, n11_ref, x_ref.at[1], sp_ref.at[1]
    )
    places = jnp.concatenate([index_ref[...]] + found, axis=1)
    colidx_ref[...] = jnp.transpose(places.astype(F32)).astype(jnp.int32)
    project(x_ref.at[1], sp_ref.at[1], w_ref, ws_ref, proj_ref, spat_ref, near)
    length = 2 * near
    stored = [
        pltpu.make_async_copy(proj_ref, proj_hbm, sems.at[0]),
        pltpu.make_async_copy(spat_ref, spat_hbm, sems.at[1]),
    ]
    for copy in stored:
        copy.start()
    level = lax.broadcasted_iota(jnp.int32, (length, NBUCK), 1)
    chosen = [(colidx_ref[:, kind : kind + 1] == level).astype(BF16) for kind in (1, 2)]
    chosen = jnp.concatenate(chosen, axis=1)

    def step(at, carry):
        rows = pl.ds(pl.multiple_of(at * block, block), block)
        lane = lax.broadcasted_iota(jnp.int32, (block, NBUCK), 1)
        index = jnp.clip(places[0:1, :] - colidx_ref[rows, 0:1], -HALF, HALF - 1) + HALF
        boxes = [
            jnp.clip(lane - colidx_ref[rows, kind : kind + 1], -HALF, HALF - 1) + HALF
            for kind in (1, 2)
        ]
        for h in range(heads):
            cols = slice(h * DH, (h + 1) * DH)
            bias = jnp.concatenate(
                [pick(table_ref[k, h : h + 1, :], boxes[k - 1]) for k in (1, 2)], axis=1
            )
            coarse = bias.astype(BF16)
            fine = (bias - coarse.astype(F32)).astype(BF16)
            left = jnp.concatenate(
                [proj_ref[0, rows, cols], spat_ref[0, rows, cols]], axis=1
            ) * jnp.asarray(DH**-0.5, BF16)
            right = jnp.concatenate([proj_ref[1, :, cols], spat_ref[1, :, cols]], axis=1)
            scores = mm(
                jnp.concatenate([left, coarse, fine], axis=1),
                jnp.concatenate([right, chosen, chosen], axis=1),
                NT,
            ) + pick(table_ref[0, h : h + 1, :], index)
            top = jnp.max(scores, axis=-1, keepdims=True)
            raised = jnp.exp(scores - top)
            soft = raised * (1.0 / jnp.sum(raised, axis=-1, keepdims=True))
            soft_ref[h, rows, :] = soft
            att_ref[rows, cols] = mm(soft.astype(BF16), proj_ref[2, :, cols]).astype(BF16)
        saved(at).start()
        return carry

    def saved(at):
        rows = pl.ds(pl.multiple_of(at * block, block), block)
        return pltpu.make_async_copy(
            soft_ref.at[:, rows, :], soft_hbm.at[:, rows, :], sems.at[2 + at]
        )

    lax.fori_loop(0, length // block, step, 0)
    for copy in stored + [saved(at) for at in range(length // block)]:
        copy.wait()
    part = length // 4
    own_ref[0:part, :] = att_ref[0:part, :]
    own_ref[part:, :] = att_ref[2 * part : 3 * part, :]
    send_ref[0:part, :] = att_ref[part : 2 * part, :]
    send_ref[part:, :] = att_ref[3 * part :, :]


def mixed_kernel(
    p_ref,
    own_ref,
    recv_ref,
    exit_ref,
    one0_ref,
    one1_ref,
    one2_ref,
    one3_ref,
    keep_ref,
    send_ref,
    partner_ref,
):
    rows = slice(one0_ref.shape[0] - exit_ref.shape[0] // 4, one0_ref.shape[0])
    gathered(p_ref, (one0_ref, one1_ref, one2_ref, one3_ref), rows, partner_ref)
    total = mm(own_ref[...], exit_ref[...]) + mm(recv_ref[...], partner_ref[...])
    rest = total.shape[0] // 4
    for y in range(2):
        at = 2 * y * rest
        keep_ref[y * rest : (y + 1) * rest, :] = total[at : at + rest]
        send_ref[y * rest : (y + 1) * rest, :] = total[at + rest : at + 2 * rest].astype(BF16)


def gelu_parts(upper):
    phi = 0.5 * (1.0 + lax.erf(upper * (0.5**0.5)))
    slope = phi + upper * (jnp.exp(-0.5 * upper * upper) * (0.5 / jnp.pi) ** 0.5)
    return (upper * phi).astype(BF16), slope


def forward_kernel(
    p_ref,
    x_ref,
    mixed0_ref,
    mixed1_ref,
    gain_ref,
    shift_ref,
    up_ref,
    hidden_ref,
    down_ref,
    one0_ref,
    one1_ref,
    one2_ref,
    one3_ref,
    two0_ref,
    two1_ref,
    two2_ref,
    two3_ref,
    low_ref,
    active_ref,
    slope_ref,
    upp_ref,
    downp_ref,
):
    many = two0_ref.shape[0]
    gathered(p_ref, (one0_ref, one1_ref, one2_ref, one3_ref), slice(0, many), upp_ref)
    gathered(p_ref, (two0_ref, two1_ref, two2_ref, two3_ref), slice(0, many), downp_ref)
    extra = one0_ref[many : many + 16, :].astype(F32)
    partner_bias = extra[0:1] + extra[1:2] + extra[2:3]
    unit, _ = centred(residual(x_ref, (mixed0_ref, mixed1_ref)))
    normed_low = (unit * gain_ref[0:1, :] + shift_ref[0:1, :]).astype(BF16)
    active, slope = gelu_parts(mm(normed_low, up_ref[...]) + hidden_ref[pl.ds(p_ref[0], 1), :])
    active_ref[0] = active
    slope_ref[0] = slope.astype(BF16)
    total = mm(active, down_ref[...])
    active, slope = gelu_parts(mm(normed_low, upp_ref[...]) + partner_bias)
    active_ref[1] = active
    slope_ref[1] = slope.astype(BF16)
    low_ref[...] = (total + mm(active, downp_ref[...])).astype(BF16)


def other_kernel(
    p_ref,
    x_ref,
    mixed0_ref,
    mixed1_ref,
    gain_ref,
    shift_ref,
    up_ref,
    hidden_ref,
    normed_ref,
    active_ref,
    slope_ref,
):
    unit, _ = centred(residual(x_ref, (mixed0_ref, mixed1_ref)))
    normed_low = (unit * gain_ref[0:1, :] + shift_ref[0:1, :]).astype(BF16)
    normed_ref[...] = normed_low
    active, slope = gelu_parts(mm(normed_low, up_ref[...]) + hidden_ref[pl.ds(p_ref[0], 1), :])
    active_ref[...] = active
    slope_ref[...] = slope.astype(BF16)


def middle_kernel(
    p_ref,
    x_ref,
    mixed0_ref,
    mixed1_ref,
    low_ref,
    lowr_ref,
    cot00_ref,
    cot10_ref,
    cot01_ref,
    cot11_ref,
    gain_ref,
    shift_ref,
    bdown_ref,
    up_ref,
    down_ref,
    upp_ref,
    downp_ref,
    slope_ref,
    outk_ref,
    outs_ref,
    hid_ref,
    second_ref,
    normed_ref,
    dlow_ref,
    dlows_ref,
    dup_ref,
    sums_ref,
):
    unit, _ = centred(residual(x_ref, (mixed0_ref, mixed1_ref)))
    normed = unit * gain_ref[0:1, :] + shift_ref[0:1, :]
    normed_ref[...] = normed.astype(BF16)
    length = normed.shape[0]
    least = length // 8
    lowered = low_ref[...].astype(F32) + turned(lowr_ref[...], least).astype(F32)
    unit2, spread2 = centred(normed + lowered + bdown_ref[pl.ds(p_ref[0], 1), :])
    out = (unit2 * gain_ref[1:2, :] + shift_ref[1:2, :]).astype(BF16)
    for y in range(2):
        at = 4 * y * least
        outk_ref[y * least : (y + 1) * least, :] = out[at : at + least]
        outs_ref[y * least : (y + 1) * least, :] = out[at + 2 * least : at + 3 * least]
    cot = stack_rows([cot00_ref[...], cot01_ref[...], cot10_ref[0], cot11_ref[1]]).astype(F32)
    second = norm_back(unit2, spread2, cot * gain_ref[1:2, :])
    second_ref[...] = second
    sums_ref[...] = jnp.zeros_like(sums_ref)
    sums_ref[0:1, :] = jnp.sum(cot * unit2, axis=0, keepdims=True)
    sums_ref[1:2, :] = jnp.sum(cot, axis=0, keepdims=True)
    sums_ref[2:3, :] = jnp.sum(second, axis=0, keepdims=True)
    dlow = second.astype(BF16)
    dlow_ref[...] = dlow
    for i in range(4):
        dlows_ref[i * least : (i + 1) * least, :] = dlow[2 * i * least : (2 * i + 1) * least]
    dup = (mm(dlow, down_ref[...], NT) * slope_ref[0].astype(F32)).astype(BF16)
    dup_ref[...] = dup
    total = mm(dup, up_ref[...], NT)
    dup = (mm(dlow, downp_ref[...], NT) * slope_ref[1].astype(F32)).astype(BF16)
    hid_ref[...] = (total + mm(dup, upp_ref[...], NT)).astype(BF16)


def ffn_grad_kernel(
    p_ref,
    normed_ref,
    normedo_ref,
    active_ref,
    activeo_ref,
    dlow_ref,
    dlow0_ref,
    dlow1_ref,
    dup_ref,
    slopeo_ref,
    down_ref,
    upk_ref,
    ups_ref,
    downk_ref,
    downs_ref,
    bias_ref,
    all_ref,
):
    least = dlow0_ref.shape[0] // 4
    pieces = []
    for i in range(4):
        pieces.append(dlow0_ref[i * least : (i + 1) * least, :])
        pieces.append(dlow1_ref[i * least : (i + 1) * least, :])
    dlowo = stack_rows(pieces)
    dupo = (mm(dlowo, down_ref[...], NT) * slopeo_ref[...].astype(F32)).astype(BF16)
    dup = dup_ref[...]
    all_ref[...] = (mm(normed_ref[...], dup, TN) + mm(normedo_ref[...], dupo, TN)).astype(BF16)
    dealt(all_ref, p_ref[1], upk_ref, ups_ref)
    all_ref[...] = (
        mm(active_ref[...], dlow_ref[...], TN) + mm(activeo_ref[...], dlowo, TN)
    ).astype(BF16)
    dealt(all_ref, p_ref[2], downk_ref, downs_ref)
    bias = jnp.sum(dup.astype(F32), axis=0, keepdims=True)
    bias = bias + jnp.sum(dupo.astype(F32), axis=0, keepdims=True)
    bias_ref[...] = jnp.broadcast_to(bias, bias_ref.shape)


def first_kernel(
    p_ref,
    x_ref,
    mixed0_ref,
    mixed1_ref,
    second_ref,
    hid_ref,
    hidr_ref,
    gain_ref,
    first_ref,
    dmix_ref,
    sums_ref,
):
    unit, spread = centred(residual(x_ref, (mixed0_ref, mixed1_ref)))
    hid = hid_ref[...].astype(F32) + turned(hidr_ref[...], hid_ref.shape[0] // 8).astype(F32)
    dnormed = second_ref[...] + hid
    first = norm_back(unit, spread, dnormed * gain_ref[0:1, :])
    first_ref[...] = first
    dmix_ref[...] = first.astype(BF16)
    sums_ref[...] = jnp.zeros_like(sums_ref)
    sums_ref[0:1, :] = jnp.sum(dnormed * unit, axis=0, keepdims=True)
    sums_ref[1:2, :] = jnp.sum(dnormed, axis=0, keepdims=True)


def attended_kernel(
    p_ref,
    dmix_ref,
    dmixr_ref,
    exit_ref,
    exitp_ref,
    sums1_ref,
    sums2_ref,
    own_ref,
    send_ref,
    total_ref,
    pay_ref,
):
    length = dmix_ref.shape[0]
    rest = length // 4
    total = dmix_ref[...].astype(F32) + turned(dmixr_ref[...], rest).astype(F32)
    total = total.astype(BF16)
    total_ref[...] = total
    own_ref[...] = mm(total, exit_ref[...], NT).astype(BF16)
    send_ref[...] = mm(total, exitp_ref[...], NT).astype(BF16)
    pay_ref[0:rest, :] = total[0:rest]
    pay_ref[rest : 2 * rest, :] = total[2 * rest : 3 * rest]
    pay_ref[2 * rest :, :] = jnp.concatenate([sums1_ref[...], sums2_ref[...]], axis=0).astype(BF16)


def backward_kernel(
    p_ref,
    datt_ref,
    dattr_ref,
    first_ref,
    soft_hbm,
    proj_ref,
    spat_ref,
    w_ref,
    ws_ref,
    dscore_ref,
    dproj_ref,
    dspat_ref,
    dxk0_ref,
    dxk1_ref,
    dxs_ref,
    dsk0_ref,
    dsk1_ref,
    dss_ref,
    soft_ref,
    sems,
    *,
    heads,
    block,
):
    fetched = [
        pltpu.make_async_copy(soft_hbm.at[h], soft_ref.at[h], sems.at[h]) for h in range(heads)
    ]
    for copy in fetched:
        copy.start()
    length = 2 * datt_ref.shape[0]
    scale = DH**-0.5
    part = length // 4
    datt = stack_rows(
        [datt_ref[0:part, :], dattr_ref[0:part, :], datt_ref[part:, :], dattr_ref[part:, :]]
    )
    for h in range(heads):
        cols = slice(h * DH, (h + 1) * DH)
        value = proj_ref[2, :, cols]
        left = jnp.concatenate([proj_ref[0, :, cols], spat_ref[0, :, cols]], axis=1)
        right = jnp.concatenate([proj_ref[1, :, cols], spat_ref[1, :, cols]], axis=1)
        own = datt[:, cols]
        fetched[h].wait()
        for at in range(0, length, block):
            soft = soft_ref[h, at : at + block, :]
            dsoft = mm(own[at : at + block], value, NT)
            inner = jnp.sum(soft * dsoft, axis=-1, keepdims=True)
            dscore_ref[h, at : at + block, :] = (soft * (dsoft - inner)).astype(BF16)
        dscore = dscore_ref[h]
        dleft = (mm(dscore, right) * scale).astype(BF16)
        dright = (mm(dscore, left, TN) * scale).astype(BF16)
        dproj_ref[0, :, cols] = dleft[:, :DH]
        dspat_ref[0, :, cols] = dleft[:, DH:]
        dproj_ref[1, :, cols] = dright[:, :DH]
        dspat_ref[1, :, cols] = dright[:, DH:]
        dproj_ref[2, :, cols] = mm(soft_ref[h].astype(BF16), own, TN).astype(BF16)
    once = (p_ref[3] == 0).astype(F32)
    total = mm(dproj_ref[0], w_ref[0])
    for k in range(1, 3):
        total = total + mm(dproj_ref[k], w_ref[k])
    least = part // 4

    def deal(rows, refs):
        for y in range(2):
            for zh in range(2):
                for c in range(2):
                    for zl in range(2):
                        at = (((y * 2 + zh) * 2 + c) * 2 + zl) * least
                        to = (zh * 2 + y) * least
                        value = rows[at : at + least]
                        if zh == 0 and refs[0][0] is dxk0_ref:
                            of = ((y * 2 + c) * 2 + zl) * least
                            value = value + once * first_ref[of : of + least, :]
                        refs[c][zl][to : to + least, :] = value.astype(BF16)

    deal(total, ((dxk0_ref, dxk1_ref), (dxs_ref.at[0], dxs_ref.at[1])))
    total = mm(dspat_ref[0], ws_ref[0]) + mm(dspat_ref[1], ws_ref[1])
    deal(total, ((dsk0_ref, dsk1_ref), (dss_ref.at[0], dss_ref.at[1])))


def second_grad_kernel(
    p_ref,
    dmix_ref,
    pay_ref,
    payr_ref,
    payc_ref,
    atto_ref,
    atts_ref,
    sp_ref,
    dspat_ref,
    lines_ref,
    keep_ref,
    send_ref,
    second_ref,
):
    width = sp_ref.shape[-1]
    sp = sp_ref[...].reshape(-1, width)
    inner = dspat_ref.shape[-1]
    rest = sp.shape[0] // 8
    dmixo = stack_rows(
        [payr_ref[0:rest, :], payc_ref[0:rest, :], payr_ref[rest : 2 * rest, :], payc_ref[rest : 2 * rest, :]]
    )
    second_ref[0:inner, :] = (
        mm(atto_ref[...], dmix_ref[...], TN) + mm(atts_ref[...], dmixo, TN)
    ).astype(BF16)
    for k in range(2):
        second_ref[(k + 1) * inner : (k + 2) * inner, :] = mm(dspat_ref[k], sp, TN).astype(BF16)
    base = 3 * inner
    small = pay_ref[2 * rest :, :].astype(F32) + payr_ref[2 * rest :, :].astype(F32)
    second_ref[base : base + 16, :] = small.astype(BF16)
    second_ref[base + 16 : base + 32, :] = lines_ref[...].astype(BF16)
    dealt(second_ref, p_ref[2], keep_ref, send_ref)


def first_grad_kernel(
    p_ref,
    x_ref,
    dscore_ref,
    dproj_ref,
    colidx_ref,
    bup_ref,
    keep_ref,
    send_ref,
    lines_ref,
    first_ref,
    *,
    heads,
):
    width = x_ref.shape[-1]
    x = x_ref[...].reshape(-1, width)
    length = x.shape[0]
    inner = dproj_ref.shape[-1]
    for k in range(3):
        first_ref[k * inner : (k + 1) * inner, :] = mm(dproj_ref[k], x, TN).astype(BF16)
    dealt(first_ref, p_ref[1], keep_ref, send_ref)
    lane = lax.broadcasted_iota(jnp.int32, (1, NBUCK), 1)
    found = []
    for kind in range(3):
        extent = length if kind == 0 else NBUCK
        own = colidx_ref[:, kind : kind + 1]
        level = lax.broadcasted_iota(jnp.int32, (length, extent), 1)
        chosen = (own == level).astype(BF16)
        place = own - HALF + lax.broadcasted_iota(jnp.int32, (length, NBUCK), 1)
        turn = place & (NBUCK - 1)
        piece = place >> 7
        for h in range(heads):
            spread = mm(dscore_ref[h], chosen)
            window = jnp.zeros((length, NBUCK), F32)
            for q in range(extent // NBUCK):
                part = jnp.take_along_axis(
                    spread[:, q * NBUCK : (q + 1) * NBUCK],
                    turn,
                    axis=1,
                    mode="promise_in_bounds",
                )
                window = window + jnp.where(piece == q, part, 0.0)
            row = jnp.sum(window, axis=0, keepdims=True)
            row = jnp.where((lane > 0) & (lane < NBUCK - 1), row, 0.0)
            least = jnp.sum(jnp.where(level <= own - HALF, spread, 0.0), axis=0, keepdims=True)
            most = jnp.sum(jnp.where(level >= own + HALF - 1, spread, 0.0), axis=0, keepdims=True)
            row = row + jnp.where(lane == 0, jnp.sum(least, axis=1, keepdims=True), 0.0)
            row = row + jnp.where(
                lane == NBUCK - 1, jnp.sum(most, axis=1, keepdims=True), 0.0
            )
            found.append(row)
    per = width // NBUCK
    found = found + [jnp.zeros((1, NBUCK), F32)] * (-len(found) % per)
    lines = [
        jnp.concatenate(found[at : at + per], axis=1) for at in range(0, len(found), per)
    ]
    lines.append(bup_ref[0:1, :])
    lines_ref[...] = jnp.concatenate(
        lines + [jnp.zeros((16 - len(lines), width), F32)], axis=0
    )


def ends_kernel(
    p_ref,
    w_ref,
    y_ref,
    zhw_ref,
    zlw_ref,
    zzw_ref,
    tok_ref,
    sp_ref,
    event_ref,
):
    c, y, block = p_ref[0], p_ref[2], p_ref[4] * 2 + p_ref[3]
    for turn, ref in enumerate((None, zlw_ref, zhw_ref, zzw_ref)):
        at = block ^ turn
        for far in range(2):
            for unit in range(3):
                if ref is None:
                    value = (y_ref if far else w_ref)[unit]
                else:
                    value = ref[far, unit]
                value = value.astype(F32)
                if unit < 2:
                    tok_ref[c ^ unit, y ^ far, at] = value
                else:
                    sp_ref[y ^ far, at] = value
    event_ref[...] = jnp.zeros_like(event_ref)


def out_kernel(p_ref, w_ref, y_ref, zh_ref, zl_ref, zz_ref, out_ref):
    c, y, block = p_ref[0], p_ref[2], p_ref[4] * 2 + p_ref[3]
    for turn, ref in enumerate((None, zl_ref, zh_ref, zz_ref)):
        at = block ^ turn
        for far in range(2):
            for unit in range(2):
                if ref is None:
                    value = (y_ref if far else w_ref)[unit]
                else:
                    value = ref[far, unit]
                out_ref[c ^ unit, y ^ far, at] = value


def turn_kernel(p_ref, own_ref, far_ref, sum_ref, *, size):
    far = turned(far_ref[...], size).astype(F32)
    sum_ref[...] = (own_ref[...].astype(F32) + far).astype(BF16)


def units_kernel(p_ref, near_ref, far_ref, other_ref, spat_ref, nears_ref, fars_ref):
    nears_ref[0] = other_ref[0]
    fars_ref[0] = other_ref[1]
    nears_ref[1] = (near_ref[...].astype(F32) + spat_ref[0].astype(F32)).astype(BF16)
    fars_ref[1] = (far_ref[...].astype(F32) + spat_ref[1].astype(F32)).astype(BF16)


def fold_kernel(p_ref, own_ref, far_ref, keep_ref, send_ref):
    total = (own_ref[...].astype(F32) + far_ref[...].astype(F32)).astype(BF16)
    half = total.shape[-2] // 2
    keep_ref[...] = total[..., :half, :]
    send_ref[...] = total[..., half:, :]


def ends_first_kernel(p_ref, ownk_ref, ownf_ref, bothk_ref, bothf_ref, mine_ref, other_ref):
    least = mine_ref.shape[1]
    for unit in range(3):
        if unit == 0:
            total = ownk_ref[...].astype(F32) + ownf_ref[...].astype(F32)
        else:
            total = bothk_ref[unit - 1].astype(F32) + bothf_ref[unit - 1].astype(F32)
        total = total.astype(BF16)
        mine_ref[unit] = total[:least]
        other_ref[unit] = total[least:]


def spread_kernel(p_ref, *refs):
    c = p_ref[0]
    event_ref = refs[10]
    for n, out_ref in enumerate(refs[8:10]):
        side = p_ref[1 + n]
        for other in range(2):
            for far in range(2):
                out_ref[c ^ other, side ^ far] = refs[n * 4 + other * 2 + far][...].astype(F32)
    event_ref[...] = jnp.zeros_like(event_ref)


def last_kernel(
    p_ref,
    one0_ref,
    one1_ref,
    one2_ref,
    one3_ref,
    two0_ref,
    two1_ref,
    two2_ref,
    two3_ref,
    qkv_ref,
    spat_ref,
    exit_ref,
    tables_ref,
    gains_ref,
    shifts_ref,
    bup_ref,
    bdown_ref,
    first_ref,
    second_ref,
    *,
    heads,
):
    c, head = p_ref[0], p_ref[4] * 2 + p_ref[3]
    inner = exit_ref.shape[1]
    width = exit_ref.shape[2]
    part = gains_ref.shape[2]
    per = width // NBUCK
    base = 3 * inner
    firsts = ((one0_ref, one1_ref), (one2_ref, one3_ref))
    seconds = ((two0_ref, two1_ref), (two2_ref, two3_ref))

    def whole(halves, side, to_ref):
        size = halves[0].shape[0]
        for far in range(2):
            at = pl.multiple_of((side ^ far) * size, 16)
            to_ref[pl.ds(at, size), :] = halves[far][...].astype(F32)

    for other in range(2):
        s = c ^ other
        whole(firsts[other], p_ref[1], first_ref)
        qkv_ref[s] = first_ref[...]
        whole(seconds[other], p_ref[2], second_ref)
        exit_ref[s] = second_ref[0:inner, :]
        if other:
            spat_ref[...] += second_ref[inner:base, :]
        else:
            spat_ref[...] = second_ref[inner:base, :]
        sums = second_ref[base : base + 16, :]
        cut = sums[:, 0:part]
        for at in range(1, width // part):
            cut = jnp.where(head == at, sums[:, at * part : (at + 1) * part], cut)
        gains_ref[s] = jnp.concatenate([cut[0:1], cut[8:9]], axis=0)
        shifts_ref[s] = jnp.concatenate([cut[1:2], cut[9:10]], axis=0)
        bdown_ref[pl.ds(s, 1), :] = cut[10:11]
        lines = second_ref[base + 16 : base + 32, :]
        for n in range(3 * heads):
            at = (n % per) * NBUCK
            tables_ref[s, n // heads, n % heads : n % heads + 1, :] = lines[
                n // per : n // per + 1, at : at + NBUCK
            ]
        bup_ref[pl.ds(s, 1), :] = lines[2:3]


def swap(value, axis, step=1):
    size = lax.axis_size(axis)
    return lax.ppermute(value, axis, [(i, i ^ step) for i in range(size)])


def swap_both(value):
    size = lax.axis_size("batch") * 2
    return lax.ppermute(value, ("batch", "y"), [(i, i ^ 3) for i in range(size)])


def added(left, right):
    return (left.astype(F32) + right.astype(F32)).astype(BF16)


def batch_steps():
    return [1 << bit for bit in range(lax.axis_size("batch").bit_length() - 1)]


def join(*values):
    return lax.optimization_barrier(values)


def shards(
    tokens,
    spatial,
    positions,
    boxes,
    query_key_value_weight,
    w_spatial,
    rel_tables,
    exit_matrix,
    ln_gains,
    ln_shifts,
    up_weight,
    hidden_bias,
    shrink_projection_array,
    b_down,
    cotangent,
):
    heads = rel_tables.shape[2]
    rows = tokens.shape[2]
    width = tokens.shape[3]
    inner = query_key_value_weight.shape[3]
    hidden = up_weight.shape[2]
    least = rows // 4
    rest = rows // 2
    length = 4 * rows
    half = length // 2
    page = lax.axis_index("y")
    core = lax.axis_index("core")
    zh = lax.axis_index("zh")
    zl = lax.axis_index("zl")
    pair = lax.axis_index("batch") & 1
    place = jnp.stack([core, pair, page, zl, zh]).astype(jnp.int32)

    def run(body, operands, outs, us=TICK, scratch=(), after=(), vmem=VMEM_BYTES):
        return kernel_call(body, place, operands, outs, us, scratch, after, vmem)

    def rows_of(count, dtype=BF16):
        return ((count, width), dtype)

    share = hidden // 4
    anywhere = [
        tokens.reshape(2, 2, 4, least, width),
        spatial.reshape(2, 4, least, width),
        positions,
        boxes,
        exit_matrix,
        up_weight,
        shrink_projection_array,
        hidden_bias,
        cotangent.reshape(2, 2, 4, least, width),
    ]
    far, near, x00, up_part, down_part, cot_far, cot_near, cot00 = run(
        pack_kernel,
        [(array, "any") for array in anywhere],
        [
            rows_of(3 * rows + 16),
            rows_of(2 * rows + 16),
            rows_of(rows),
            rows_of(share + 16 + inner // 4),
            rows_of(share),
            ((2, 2 * least, width), BF16),
            rows_of(2 * least),
            rows_of(2 * least),
        ],
        scratch=[
            pltpu.VMEM(positions.shape, jnp.int32),
            pltpu.VMEM(boxes.shape, jnp.int32),
            pltpu.VMEM(hidden_bias.shape, F32),
            pltpu.SemaphoreType.DMA((38,)),
        ],
        vmem=PACK_VMEM,
    )
    n10 = swap(far, "y")
    n01 = swap(near, "core")
    up_part = swap(up_part, "zh")
    weights = (jnp.swapaxes(query_key_value_weight, 2, 3), "stream")
    spatial_weights = jnp.swapaxes(w_spatial, 1, 2)
    x0, sp0, index0, proj0, spat0, up, down, exit_own = run(
        near_kernel,
        [
            x00,
            n01,
            near,
            weights,
            spatial_weights,
            (up_weight, "any"),
            (shrink_projection_array, "any"),
            (exit_matrix, "any"),
        ],
        [
            ((2, rows, width), BF16),
            ((2, rows, width), BF16),
            ((8, 2 * rows), jnp.int32),
            ((3, 2 * rows, inner), BF16),
            ((2, 2 * rows, inner), BF16),
            ((width, hidden), BF16),
            ((hidden, width), BF16),
            rows_of(inner),
        ],
        scratch=[pltpu.SemaphoreType.DMA((3,))],
    )
    n10, x0, up_part, down_part = join(n10, x0, up_part, down_part)
    n11 = swap(n10, "core")
    ups = [up_part, swap(up_part, "y"), swap(up_part, "batch"), swap_both(up_part)]
    down_part = swap(down_part, "zh")

    x, sp, colidx, proj, spat, soft, att_own, att_send = run(
        functools.partial(attention_kernel, heads=heads, block=128),
        [
            n11,
            n10,
            x0,
            sp0,
            index0,
            proj0,
            spat0,
            weights,
            spatial_weights,
            (rel_tables, "stream"),
        ],
        [
            ((2, 2, rows, width), BF16),
            ((2, 2, rows, width), BF16),
            ((length, 8), jnp.int32),
            ((3, length, inner), BF16, "any"),
            ((2, length, inner), BF16, "any"),
            ((heads, length, length), F32, "any"),
            ((half, inner), BF16),
            ((half, inner), BF16),
        ],
        us=30,
        scratch=[
            pltpu.VMEM((length, inner), BF16),
            pltpu.VMEM((3, length, inner), BF16),
            pltpu.VMEM((2, length, inner), BF16),
            pltpu.VMEM((heads, length, length), F32),
            pltpu.SemaphoreType.DMA((2 + length // 128,)),
        ],
    )
    att_send, att_own, *ups, down_part = join(att_send, att_own, *ups, down_part)
    att_recv = swap(att_send, "zh")
    downs = [down_part, swap(down_part, "y"), swap(down_part, "batch"), swap_both(down_part)]

    keep, send, exit_partner = run(
        mixed_kernel,
        [att_own, att_recv, exit_own, *ups],
        [rows_of(rows, F32), rows_of(rows), rows_of(inner)],
    )
    mixed0 = added(keep, swap(send, "core"))
    mixed_zl = swap(mixed0, "zl")
    (mixed0,) = run(
        functools.partial(turn_kernel, size=least), [mixed0, mixed_zl], [rows_of(rows)]
    )
    mixed0, cot_far, cot_near, *downs = join(mixed0, cot_far, cot_near, *downs)
    mixed1 = swap(mixed0, "core")
    cot10 = swap(cot_far, "y")
    cot01 = swap(cot_near, "core")
    mixed_far0 = swap(mixed0, "zh")

    gains = (ln_gains, "stream")
    shifts = (ln_shifts, "stream")
    x_own = (x, (None, 0, None, None))
    x_far = (x, (None, 1, None, None))
    low, active, slope, up_partner, down_partner = run(
        forward_kernel,
        [x_own, mixed0, mixed1, gains, shifts, up, hidden_bias, down, *ups, *downs],
        [
            rows_of(half),
            ((2, half, hidden), BF16),
            ((2, half, hidden), BF16),
            ((width, hidden), BF16),
            ((hidden, width), BF16),
        ],
    )
    low_recv = swap(low, "zl")
    cot11 = swap(cot10, "core")
    mixed_far1 = swap(mixed_far0, "core")
    normed_far, active_far, slope_far = run(
        other_kernel,
        [x_far, mixed_far0, mixed_far1, gains, shifts, up, hidden_bias],
        [rows_of(half), ((half, hidden), BF16), ((half, hidden), BF16)],
        after=[low],
    )
    out_keep, out_send, hid, second, normed, dlow, dlow_send, dup, sums_two = run(
        middle_kernel,
        [
            x_own,
            mixed0,
            mixed1,
            low,
            low_recv,
            cot00,
            cot10,
            cot01,
            cot11,
            gains,
            shifts,
            b_down,
            up,
            down,
            up_partner,
            down_partner,
            slope,
        ],
        [
            rows_of(rest),
            rows_of(rest),
            rows_of(half),
            rows_of(half, F32),
            rows_of(half),
            rows_of(half),
            rows_of(rows),
            ((half, hidden), BF16),
            rows_of(8, F32),
        ],
        after=[slope_far],
    )
    hid_recv = swap(hid, "zl")
    dlow_far0 = swap(dlow_send, "zh")
    out_core = swap(out_send, "core")
    hid_recv, dlow_far0, out_core = join(hid_recv, dlow_far0, out_core)
    dlow_far1 = swap(dlow_far0, "zl")
    first, dmix, sums_one = run(
        first_kernel,
        [x_own, mixed0, mixed1, second, hid, hid_recv, gains],
        [rows_of(half, F32), rows_of(half), rows_of(8, F32)],
    )
    datt, datt_send, dmix, pay = run(
        attended_kernel,
        [dmix, swap(dmix, "core"), exit_own, exit_partner, sums_one, sums_two],
        [
            ((half, inner), BF16),
            ((half, inner), BF16),
            rows_of(half),
            rows_of(rows + 16),
        ],
    )
    datt_recv = swap(datt_send, "zh")
    up_keep, up_send, down_keep, down_send, bias_grad = run(
        ffn_grad_kernel,
        [
            normed,
            normed_far,
            (active, (0, None, None)),
            active_far,
            dlow,
            dlow_far0,
            dlow_far1,
            dup,
            slope_far,
            down,
        ],
        [
            ((width // 2, hidden), BF16),
            ((width // 2, hidden), BF16),
            rows_of(hidden // 2),
            rows_of(hidden // 2),
            ((8, hidden), F32),
        ],
        us=30,
        scratch=[pltpu.VMEM((width, hidden), BF16)],
        after=[datt],
    )
    datt_recv, up_send, down_send, pay = join(datt_recv, up_send, down_send, pay)
    pay_recv = swap(pay, "zh")
    up_recv = swap(up_send, "batch")
    down_recv = swap(down_send, "y")
    piece = rows_of(rows)
    dscore, dproj, dspat, dxk0, dxk1, dxs, dsk0, dsk1, dss = run(
        functools.partial(backward_kernel, heads=heads, block=128),
        [datt, datt_recv, first, (soft, "any"), proj, spat, weights, spatial_weights],
        [
            ((heads, length, length), BF16),
            ((3, length, inner), BF16),
            ((2, length, inner), BF16),
            piece,
            piece,
            ((2, rows, width), BF16),
            piece,
            piece,
            ((2, rows, width), BF16),
        ],
        us=30,
        scratch=[pltpu.VMEM((heads, length, length), F32), pltpu.SemaphoreType.DMA((heads,))],
        after=[bias_grad],
    )

    dxk1, dxs, dss = join(dxk1, dxs, dss)
    own_far = swap(dxk1, "zl")
    dxs, dss = swap(dxs, "core"), swap(dss, "core")
    near, far = run(
        units_kernel,
        [dsk0, dsk1, dxs, dss],
        [((2, rows, width), BF16), ((2, rows, width), BF16)],
    )
    far, own_far, up_recv, down_recv, pay_recv = join(
        far, own_far, up_recv, down_recv, pay_recv
    )
    both_far = swap(far, "zl")
    up_half = added(up_keep, up_recv)
    down_half = added(down_keep, down_recv)
    up_other = swap(up_half, "y")
    down_other = swap(down_half, "batch")
    own_keep, own_send = run(fold_kernel, [dxk0, own_far], [rows_of(rest), rows_of(rest)])
    own_zh = swap(own_send, "zh")
    one_keep, one_send, lines = run(
        functools.partial(first_grad_kernel, heads=heads),
        [x, dscore, dproj, colidx, bias_grad],
        [rows_of(3 * inner // 2), rows_of(3 * inner // 2), rows_of(16, F32)],
        scratch=[pltpu.VMEM((3 * inner, width), BF16)],
        after=[own_send],
    )
    both_far, own_zh, lines = join(both_far, own_zh, lines)
    both_keep, both_send = run(
        fold_kernel, [near, both_far], [((2, rest, width), BF16), ((2, rest, width), BF16)]
    )
    both_zh = swap(both_send, "zh")
    pay_core = swap(pay_recv, "core")
    base = 3 * inner + 32
    two_keep, two_send = run(
        second_grad_kernel,
        [dmix, pay, pay_recv, pay_core, att_own, att_send, sp, dspat, lines],
        [rows_of(base // 2), rows_of(base // 2)],
        scratch=[pltpu.VMEM((base, width), BF16)],
        after=[both_send],
    )
    steps = batch_steps()[1:]

    def total(left, right):
        left = added(left, right)
        for step in steps:
            left = added(left, swap(left, "batch", step))
        return left

    up_other, down_other, two_keep = join(up_other, down_other, two_keep)
    up_half = total(up_half, up_other)
    down_half = total(down_half, down_other)
    up_far = swap(up_half, "batch")
    down_far = swap(down_half, "y")
    both_zh, one_send, two_send, up_half, down_half = join(
        both_zh, one_send, two_send, up_half, down_half
    )
    mine, other = run(
        ends_first_kernel,
        [own_keep, own_zh, both_keep, both_zh],
        [((3, least, width), BF16), ((3, least, width), BF16)],
    )
    got = swap(other, "y")
    got, up_far, down_far, one_send, two_send, out_core = join(
        got, up_far, down_far, one_send, two_send, out_core
    )
    pages = jnp.stack([mine, got])
    pages_zh = swap(pages, "zh")
    pages_zl = swap(pages, "zl")
    one_recv = swap(one_send, "batch")
    two_recv = swap(two_send, "y")
    halves = [up_half, up_far, down_half, down_far]
    others = [swap(value, "core") for value in halves]
    grad_up, grad_down, spread_event = run(
        spread_kernel,
        halves[:2] + others[:2] + halves[2:] + others[2:],
        [
            ((2, 2, width // 2, hidden), F32),
            ((2, 2, hidden // 2, width), F32),
            ((8, NBUCK), F32),
        ],
    )
    one_recv, two_recv, pages_zl, spread_event = join(one_recv, two_recv, pages_zl, spread_event)
    one_half = added(one_keep, one_recv)
    two_half = added(two_keep, two_recv)
    one_other = swap(one_half, "y")
    two_other = swap(two_half, "batch")
    pages_zh, out_core = join(pages_zh, out_core)
    pages_zz = swap(pages_zh, "zl")
    outs = jnp.stack([out_keep, out_core]).reshape(2, 2, least, width)
    out_y = swap(outs[:, 1], "y")
    one_other, two_other, out_y, pages_zz = join(one_other, two_other, out_y, pages_zz)
    one_half = total(one_half, one_other)
    two_half = total(two_half, two_other)
    one_far = swap(one_half, "batch")
    two_far = swap(two_half, "y")
    out_pages = jnp.stack([outs[:, 0], out_y])
    out_zh = swap(out_pages, "zh")
    out_zl = swap(out_pages, "zl")
    grad_tokens, grad_spatial, ends_event = run(
        ends_kernel,
        [mine, got, pages_zh, pages_zl, pages_zz],
        [((2, 2, 4, least, width), F32), ((2, 4, least, width), F32), ((8, NBUCK), F32)],
        after=[one_half, two_half],
    )
    out_zh, out_zl, one_far, two_far, ends_event = join(
        out_zh, out_zl, one_far, two_far, ends_event
    )
    out_zz = swap(out_zh, "zl")
    halves = [one_half, one_far, two_half, two_far]
    others = [swap(value, "core") for value in halves]
    part = width // (2 * lax.axis_size("zh"))
    grad_qkv, grad_spatial_w, grad_exit, tables, gains_grad, shifts_grad, grad_b_up, grad_b_down = run(
        functools.partial(last_kernel, heads=heads),
        halves[:2] + others[:2] + halves[2:] + others[2:],
        [
            ((2, 3 * inner, width), F32),
            rows_of(2 * inner, F32),
            ((2, inner, width), F32),
            ((2, 3, heads, NBUCK), F32),
            ((2, 2, part), F32),
            ((2, 2, part), F32),
            ((2, hidden), F32),
            ((2, part), F32),
        ],
        scratch=[pltpu.VMEM((3 * inner, width), F32), pltpu.VMEM((base, width), F32)],
        after=[spread_event, ends_event],
    )
    (output,) = run(
        out_kernel,
        [outs[:, 0], out_y, out_zh, out_zl, out_zz],
        [((2, 2, 4, least, width), BF16)],
    )
    return (
        output.reshape(tokens.shape),
        grad_tokens.reshape(tokens.shape),
        grad_spatial.reshape(spatial.shape),
        grad_qkv.reshape(2, 3, inner, width).swapaxes(2, 3),
        grad_spatial_w.reshape(2, inner, width).swapaxes(1, 2),
        tables,
        grad_exit,
        gains_grad,
        shifts_grad,
        grad_up.reshape(2, width, hidden),
        grad_b_up,
        grad_down.reshape(2, hidden, width),
        grad_b_down,
    )


def solution(mesh):
    batch, seq, head = mesh.devices.shape
    fine = Mesh(
        mesh.devices.reshape(batch, seq // 2, 2, head // 2, 2),
        ("batch", "y", "core", "zh", "zl"),
    )
    seq = ("y", "core")
    head = ("zh", "zl")
    return jax.shard_map(
        shards,
        mesh=fine,
        in_specs=(
            P(None, "batch", seq, None),
            P("batch", seq, None),
            P("batch", seq),
            P(None, "batch", seq),
            P(None, None, None, head),
            P(None, None, head),
            P(None, None, head, None),
            P(None, head, None),
            P(),
            P(),
            P(None, None, head),
            P(None, head),
            P(None, head, None),
            P(),
            P(None, "batch", seq, None),
        ),
        out_specs=(
            P(None, "batch", seq, None),
            P(None, "batch", seq, None),
            P("batch", seq, None),
            P(None, None, None, head),
            P(None, None, head),
            P(None, None, head, None),
            P(None, head, None),
            P(None, None, head),
            P(None, None, head),
            P(None, None, head),
            P(None, head),
            P(None, head, None),
            P(None, head),
        ),
        check_vma=False,
    )
```

time: 342 us -> 241 us (0.70)
  waiting for transfers between devices: 160 us -> 124 us
  other arithmetic: 25.9 us -> 1.13 us
  local copies, waits for them, and re-layouts: 25.5 us -> 6.36 us
  Pallas kernels: 68.8 us -> 58.5 us
  starting transfers between devices: 58.6 us -> 49.1 us
    ppermute x63 -> x61, waiting for transfers between devices: 160 us -> 116 us  [swap(): return lax.ppermute(value, axis, [(i, i ^ step) for i in range(size)])]
    ppermute x63 -> x61, starting transfers between devices: 58.6 us -> 46.1 us  [swap(): return lax.ppermute(value, axis, [(i, i ^ step) for i in range(size)])]
    pallas_call x10 -> x22, Pallas kernels: 68.8 us -> 58.5 us  [kernel_call(): pl.pallas_call(kernel, out_shape=[jax.ShapeDtypeStruct(out[0], out[1]) fo...]
    another operation x27 -> x3, other arithmetic: 9.8 us -> 0.07 us  [the longest x2 0.04 us: shards(): out_pages = jnp.stack([outs[:, 0], out_y])]
    ppermute x0 -> x2, waiting for transfers between devices: none -> 8.07 us  [swap_both(): lax.ppermute(value, ('batch', 'y'), [(i, i ^ 3) for i in range(size)])]
    slice x15 -> x0, local copies, waits for them, and re-layouts: 7.92 us -> none  [the longest x1 2.02 us: shards(): grads_one[:, :3 * inner].reshape(2, 3, inner, width).swapaxes(2, 3)]
    convert_element_type x7 -> x0, other arithmetic: 7.67 us -> none  [the longest x4 5.63 us: both_streams(): in_place(jnp.stack([array, swap(array, 'core')]), core, 0).astype(F32)]
    unnamed x89 -> x38, local copies, waits for them, and re-layouts: 10.4 us -> 5.74 us
  transfers between devices with their start and end apart: 63 -> 63, of which waited for: 30 -> 30; matrix products, arithmetic and copies ran while one was open for 10% -> 0% of each run, Pallas kernels for 18% -> 16%
where the time goes in v3:
time: 241 us
  waiting for transfers between devices  124 us (51%)
  Pallas kernels  58.5 us (24%)
  starting transfers between devices  49.1 us (20%)
  local copies, waits for them, and re-layouts  6.36 us (3%)
    ppermute x61, waiting for transfers between devices, swap(): return lax.ppermute(value, axis, [(i, i ^ step) for i in range(size)])  116 us
    pallas_call x22, Pallas kernels, kernel_call(): pl.pallas_call(kernel, out_shape=[jax.ShapeDtypeStruct(out[0], out[1]) fo...  58.5 us
    ppermute x61, starting transfers between devices, swap(): return lax.ppermute(value, axis, [(i, i ^ step) for i in range(size)])  46.1 us
    ppermute x2, waiting for transfers between devices, swap_both(): lax.ppermute(value, ('batch', 'y'), [(i, i ^ 3) for i in range(size)])  8.07 us
    unnamed x38, local copies, waits for them, and re-layouts  5.74 us
  transfers between devices with their start and end apart: 63, of which 30 were waited for; matrix products, arithmetic and copies ran while one was open for 0% of the time, Pallas kernels for 16%

profile of v3, /device:TPU:0, one launch (start us, length us, event | category | flops | bytes accessed | tf_op | source)
XLA Modules:
  0.0 240.6 jit_solution(17456264246016729339)
XLA Ops:
  1.3 4.4 %shard_map.246 = (bf16[400,768]{1,0:T(8,128)(2,1)}, bf16[272,768]{1,0:T(8,128)(2,1)}, bf16[128,768]{1,0:T(8,128)(2,1)}, bf16[256,768]{1,0:T(8,128)(2,1)}, bf16[1...) custom-call(s32[5]{0:T(128)} %stack.47.s_ref, ...), custom_call_target="tpu_custom_call" | custom-call | flops 110000000 | bytes 350000 | tf_op jit(solution)/shard_map/pallas_call | solution.py:49
  5.6 3.0 %collective-permute-start = (bf16[400,768]{1,0:T(8,128)(2,1)}, bf16[400,768]{1,0:T(8,128)(2,1)S(1)}, u32[]{:S(2)}, u32[]{:S(2)}) collective-permute-start(bf16[400,768]{1,0:T(8,128)(2,1)} %get-tuple-element.170), channel_id=1, source_target_pairs={{0,8},{8,0},{1,9},{9,1},{2,10},{10,2},{3,11},{11,3},{4,12},{12,4},... | collective-permute-start | bytes 1843208 | tf_op jit(solution)/shard_map/ppermute | solution.py:951
  8.7 2.6 %collective-permute-start.2 = (bf16[256,768]{1,0:T(8,128)(2,1)}, bf16[256,768]{1,0:T(8,128)(2,1)S(1)}, u32[]{:S(2)}, u32[]{:S(2)}) collective-permute-start(bf16[256,768]{1,0:T(8,128)(2,1)} %get-tuple-element.174), channel_id=1, source_target_pairs={{0,2},{2,0},{1,3},{3,1},{4,6},{6,4},{5,7},{7,5},{8,10},{10,8},{9,1... | collective-permute-start | bytes 1179656 | tf_op jit(solution)/shard_map/ppermute | solution.py:951
  11.3 1.7 copy-done.1
  16.4 1.8 shard_map.247
  18.2 11.5 %collective-permute-done.2.refs_3_.refs_8_ = bf16[256,768]{1,0:T(8,128)(2,1)S(1)} collective-permute-done((bf16[256,768]{1,0:T(8,128)(2,1)}, bf16[256,768]{1,0:T(8,128)(2,1)S(1)}, u32[]{:S(2)}, u32[]{:S(2)}) %collective-permute-start.2) | collective-permute-done | bytes 393248 | tf_op jit(solution)/shard_map/ppermute | solution.py:951
  30.3 1.5 collective-permute-start.5
  31.8 1.5 collective-permute-start.6
  33.3 11.3 %shard_map.248 = (bf16[2,2,128,768]{3,2,1,0:T(8,128)(2,1)S(1)}, bf16[2,2,128,768]{3,2,1,0:T(8,128)(2,1)S(1)}, s32[512,8]{1,0:T(8,128)S(1)}, bf16[3,512,192]{2,1,...) custom-call(s32[5]{0:T(128)S(1)} %copy-done.9, ...), custom_call_target="tpu_custom_call" | custom-call | flops 32999999488 | bytes 105000000 | tf_op jit(solution)/shard_map/pallas_call | solution.py:49
  44.7 4.4 %collective-permute-done.7.refs_12_ = bf16[192,768]{1,0:T(8,128)(2,1)S(1)} collective-permute-done((bf16[192,768]{1,0:T(8,128)(2,1)S(1)}, bf16[192,768]{1,0:T(8,128)(2,1)S(1)}, u32[]{:S(2)}, u32[]{:S(2)}) %collective-permute-start.7) | collective-permute-done | bytes 294944 | tf_op jit(solution)/shard_map/ppermute | solution.py:951
  49.1 1.8 collective-permute-done.6.refs_6_.refs_11_
  50.9 8.4 %collective-permute-done.8.refs_1_ = bf16[256,192]{1,0:T(8,128)(2,1)S(1)} collective-permute-done((bf16[256,192]{1,0:T(8,128)(2,1)S(1)}, bf16[256,192]{1,0:T(8,128)(2,1)S(1)}, u32[]{:S(2)}, u32[]{:S(2)}) %collective-permute-start.8) | collective-permute-done | bytes 98336 | tf_op jit(solution)/shard_map/ppermute | solution.py:951
  60.9 1.5 collective-permute-start.12
  64.1 6.4 %collective-permute-done.10.refs_1_ = bf16[128,768]{1,0:T(8,128)(2,1)S(1)} collective-permute-done((bf16[128,768]{1,0:T(8,128)(2,1)S(1)}, bf16[128,768]{1,0:T(8,128)(2,1)S(1)}, u32[]{:S(2)}, u32[]{:S(2)}) %collective-permute-start.10) | collective-permute-done | bytes 196640 | tf_op jit(solution)/shard_map/ppermute | solution.py:951
  71.1 6.2 %collective-permute-done.13.refs_15_ = bf16[192,768]{1,0:T(8,128)(2,1)S(1)} collective-permute-done((bf16[192,768]{1,0:T(8,128)(2,1)S(1)}, bf16[192,768]{1,0:T(8,128)(2,1)S(1)}, u32[]{:S(2)}, u32[]{:S(2)}) %collective-permute-start.13) | collective-permute-done | bytes 294944 | tf_op jit(solution)/shard_map/ppermute | solution.py:956
  78.8 2.7 %shard_map.251 = (bf16[256,768]{1,0:T(8,128)(2,1)S(1)}, bf16[2,256,768]{2,1,0:T(8,128)(2,1)S(1)}, bf16[2,256,768]{2,1,0:T(8,128)(2,1)S(1)}, bf16[768,768]{1,0:T(8,128)(2,1)S(1)}, bf16[768,768]{1,0:T(8,128)(2,1)S(1)}) custom-call(s32[5]{0:T(128)S(1)} %copy-done.9, bf16[2,2,128,768]{3,2,1,0:T(8,128)(2,1)S(1)} %get-tuple-element.182.refs_0_, ...), custom_call_target="tpu_custom_call" | custom-call | flops 110000000 | bytes 350000 | tf_op jit(solution)/shard_map/pallas_call | solution.py:49
  82.4 6.0 %collective-permute-done.19.refs_1_ = bf16[128,768]{1,0:T(8,128)(2,1)S(1)} collective-permute-done((bf16[128,768]{1,0:T(8,128)(2,1)S(1)}, bf16[128,768]{1,0:T(8,128)(2,1)S(1)}, u32[]{:S(2)}, u32[]{:S(2)}) %collective-permute-start.19) | collective-permute-done | bytes 196640 | tf_op jit(solution)/shard_map/ppermute | solution.py:951
  91.3 5.5 %collective-permute-done.15.refs_4_ = bf16[256,768]{1,0:T(8,128)(2,1)S(1)} collective-permute-done((bf16[256,768]{1,0:T(8,128)(2,1)S(1)}, bf16[256,768]{1,0:T(8,128)(2,1)S(1)}, u32[]{:S(2)}, u32[]{:S(2)}) %collective-permute-start.15) | collective-permute-done | bytes 393248 | tf_op jit(solution)/shard_map/ppermute | solution.py:951
  96.7 3.2 %shard_map.253 = (bf16[64,768]{1,0:T(8,128)(2,1)S(1)}, bf16[64,768]{1,0:T(8,128)(2,1)S(1)}, bf16[256,768]{1,0:T(8,128)(2,1)S(1)}, f32[256,768]{1,0:T(8,128)S(1)}...) custom-call(s32[5]{0:T(128)S(1)} %copy-done.9, ...), custom_call_target="tpu_custom_call" | custom-call | flops 110000000 | bytes 350000 | tf_op jit(solution)/shard_map/pallas_call | solution.py:49
  100.0 2.2 collective-permute-start.22
  103.5 9.6 %collective-permute-done.22.refs_5_ = bf16[128,768]{1,0:T(8,128)(2,1)S(1)} collective-permute-done((bf16[128,768]{1,0:T(8,128)(2,1)S(1)}, bf16[128,768]{1,0:T(8,128)(2,1)S(1)}, u32[]{:S(2)}, u32[]{:S(2)}) %collective-permute-start.22) | collective-permute-done | bytes 196640 | tf_op jit(solution)/shard_map/ppermute | solution.py:951
  113.1 2.2 collective-permute-done.21.refs_5_
  116.7 1.6 collective-permute-done.24.refs_1_
  120.5 5.1 %collective-permute-done.26.refs_6_ = bf16[128,768]{1,0:T(8,128)(2,1)S(1)} collective-permute-done((bf16[128,768]{1,0:T(8,128)(2,1)S(1)}, bf16[128,768]{1,0:T(8,128)(2,1)S(1)}, u32[]{:S(2)}, u32[]{:S(2)}) %collective-permute-start.26) | collective-permute-done | bytes 196640 | tf_op jit(solution)/shard_map/ppermute | solution.py:951
  125.6 2.6 %shard_map.256 = (bf16[384,768]{1,0:T(8,128)(2,1)S(1)}, bf16[384,768]{1,0:T(8,128)(2,1)S(1)}, bf16[384,768]{1,0:T(8,128)(2,1)S(1)}, bf16[384,768]{1,0:T(8,128)(2,1)S(1)}, f32[8,768]{1,0:T(8,128)S(1)}) custom-call(s32[5]{0:T(128)S(1)} %copy-done.9, bf16[256,768]{1,0:T(8,128)(2,1)S(1)} %get-tuple-element.226.refs_0_, ...), custom_call_target="tpu_custom_call" | custom-call | flops 32999999488 | bytes 105000000 | tf_op jit(solution)/shard_map/pallas_call | solution.py:49
  128.6 5.3 %shard_map.257 = (bf16[3,512,512]{2,1,0:T(8,128)(2,1)S(1)}, bf16[3,512,192]{2,1,0:T(8,128)(2,1)S(1)}, bf16[2,512,192]{2,1,0:T(8,128)(2,1)S(1)}, bf16[128,768]{1,...) custom-call(s32[5]{0:T(128)S(1)} %copy-done.9, ...), custom_call_target="tpu_custom_call" | custom-call | flops 32999999488 | bytes 105000000 | tf_op jit(solution)/shard_map/pallas_call | solution.py:49
  134.0 1.6 collective-permute-start.30
  136.7 2.6 %collective-permute-start.29 = (bf16[128,768]{1,0:T(8,128)(2,1)S(1)}, bf16[128,768]{1,0:T(8,128)(2,1)S(1)}, u32[]{:S(2)}, u32[]{:S(2)}) collective-permute-start(bf16[128,768]{1,0:T(8,128)(2,1)S(1)} %get-tuple-element.251), channel_id=1, source_target_pairs={{0,1},{1,0},{2,3},{3,2},{4,5},{5,4},{6,7},{7,6},{8,9},{9,8},{10,11... | collective-permute-start | bytes 589832 | tf_op jit(solution)/shard_map/ppermute | solution.py:951
  140.0 6.3 %collective-permute-done.29.refs_1_ = bf16[128,768]{1,0:T(8,128)(2,1)S(1)} collective-permute-done((bf16[128,768]{1,0:T(8,128)(2,1)S(1)}, bf16[128,768]{1,0:T(8,128)(2,1)S(1)}, u32[]{:S(2)}, u32[]{:S(2)}) %collective-permute-start.29) | collective-permute-done | bytes 196640 | tf_op jit(solution)/shard_map/ppermute | solution.py:951
  146.3 3.3 %collective-permute-done.32.refs_2_ = bf16[144,768]{1,0:T(8,128)(2,1)S(1)} collective-permute-done((bf16[144,768]{1,0:T(8,128)(2,1)S(1)}, bf16[144,768]{1,0:T(8,128)(2,1)S(1)}, u32[]{:S(2)}, u32[]{:S(2)}) %collective-permute-start.32) | collective-permute-done | bytes 221216 | tf_op jit(solution)/shard_map/ppermute | solution.py:951
  153.0 3.3 %collective-permute-start.34 = (bf16[64,768]{1,0:T(8,128)(2,1)S(1)}, bf16[64,768]{1,0:T(8,128)(2,1)S(1)}, u32[]{:S(2)}, u32[]{:S(2)}) collective-permute-start(bf16[64,768]{1,0:T(8,128)(2,1)S(1)} %get-tuple-element.258.refs_5_), channel_id=1, source_target_pairs={{0,2},{2,0},{1,3},{3,1},{4,6},{6,4},{5,7},{7,5},{8,10},{10,8},{9,1... | collective-permute-start | bytes 294920 | tf_op jit(solution)/shard_map/ppermute | solution.py:951
  156.3 5.8 %shard_map.260 = (bf16[288,768]{1,0:T(8,128)(2,1)S(1)}, bf16[288,768]{1,0:T(8,128)(2,1)S(1)}, f32[16,768]{1,0:T(8,128)S(1)}) custom-call(s32[5]{0:T(128)S(1)} %copy-done.9, bf16[2,2,128,768]{3,2,1,0:T(8,128)(2,1)S(1)} %get-tuple-element.182.refs_0_, bf16[3,512,512]{2,1,0:T(8,128)(2,1)S(1)} %get-tuple-element.259.refs_1_, ...), custom_call_target="tpu_custom_call" | custom-call | flops 110000000 | bytes 350000 | tf_op jit(solution)/shard_map/pallas_call | solution.py:49
  162.3 2.2 collective-permute-done.33.refs_1_
  167.8 1.6 collective-permute-start.41
  171.0 4.1 %collective-permute-done.35.refs_3_ = bf16[2,64,768]{2,1,0:T(8,128)(2,1)S(1)} collective-permute-done((bf16[2,64,768]{2,1,0:T(8,128)(2,1)S(1)}, bf16[2,64,768]{2,1,0:T(8,128)(2,1)S(1)}, u32[]{:S(2)}, u32[]{:S(2)}) %collective-permute-start.35) | collective-permute-done | bytes 196640 | tf_op jit(solution)/shard_map/ppermute | solution.py:951
  176.2 1.5 collective-permute-start.39
  177.7 6.2 %collective-permute-done.39.refs_1_ = bf16[3,32,768]{2,1,0:T(8,128)(2,1)S(1)} collective-permute-done((bf16[3,32,768]{2,1,0:T(8,128)(2,1)S(1)}, bf16[3,32,768]{2,1,0:T(8,128)(2,1)S(1)}, u32[]{:S(2)}, u32[]{:S(2)}) %collective-permute-start.39) | collective-permute-done | bytes 147488 | tf_op jit(solution)/shard_map/ppermute | solution.py:951
  187.3 1.5 collective-permute-start.45
  190.0 5.1 %shard_map.264 = (f32[2,2,384,768]{3,2,1,0:T(8,128)}, f32[2,2,384,768]{3,2,1,0:T(8,128)}, f32[8,128]{1,0:T(8,128)S(1)}) custom-call(s32[5]{0:T(128)S(1)} %copy-done.9, bf16[384,768]{1,0:T(8,128)(2,1)S(1)} %add_convert_fusion.1.refs_0_, bf16[384,768]{1,0:T(8,128)(2,1)S(1)} %collective-permute-done.40.refs_1_, ...), custom_call_target="tpu_custom_call" | custom-call | flops 110000000 | bytes 350000 | tf_op jit(solution)/shard_map/pallas_call | solution.py:49
  195.1 6.2 %collective-permute-done.45.refs_3_ = bf16[2,3,32,768]{3,2,1,0:T(8,128)(2,1)S(1)} collective-permute-done((bf16[2,3,32,768]{3,2,1,0:T(8,128)(2,1)S(1)}, bf16[2,3,32,768]{3,2,1,0:T(8,128)(2,1)S(1)}, u32[]{:S(2)}, u32[]{:S(2)}) %collective-permute-start.45) | collective-permute-done | bytes 294944 | tf_op jit(solution)/shard_map/ppermute | solution.py:951
  202.6 1.7 collective-permute-done.42.refs_2_
  205.5 9.6 %collective-permute-done.52.refs_1_ = bf16[2,32,768]{2,1,0:T(8,128)(2,1)S(1)} collective-permute-done((bf16[2,32,768]{2,1,0:T(8,128)(2,1)S(1)}, bf16[2,32,768]{2,1,0:T(8,128)(2,1)S(1)}, u32[]{:S(2)}, u32[]{:S(2)}) %collective-permute-start.52) | collective-permute-done | bytes 98336 | tf_op jit(solution)/shard_map/ppermute | solution.py:951
  215.7 1.6 collective-permute-start.56
  218.6 2.5 %collective-permute-start.55 = (bf16[2,2,32,768]{3,2,1,0:T(8,128)(2,1)S(1)}, bf16[2,2,32,768]{3,2,1,0:T(8,128)(2,1)S(1)}, u32[]{:S(2)}, u32[]{:S(2)}) collective-permute-start(bf16[2,2,32,768]{3,2,1,0:T(8,128)(2,1)S(1)} %pad_maximum_fusion.1), channel_id=1, source_target_pairs={{0,1},{1,0},{2,3},{3,2},{4,5},{5,4},{6,7},{7,6},{8,9},{9,8},{10,11... | collective-permute-start | bytes 589832 | tf_op jit(solution)/shard_map/ppermute | solution.py:951
  221.1 2.1 shard_map.265
  223.2 3.4 %collective-permute-done.54.refs_2_ = bf16[2,2,32,768]{3,2,1,0:T(8,128)(2,1)S(1)} collective-permute-done((bf16[2,2,32,768]{3,2,1,0:T(8,128)(2,1)S(1)}, bf16[2,2,32,768]{3,2,1,0:T(8,128)(2,1)S(1)}, u32[]{:S(2)}, u32[]{:S(2)}) %collective-permute-start.54) | collective-permute-done | bytes 196640 | tf_op jit(solution)/shard_map/ppermute | solution.py:951
  227.3 7.2 %collective-permute-done.58.refs_4_ = bf16[2,2,32,768]{3,2,1,0:T(8,128)(2,1)S(1)} collective-permute-done((bf16[2,2,32,768]{3,2,1,0:T(8,128)(2,1)S(1)}, bf16[2,2,32,768]{3,2,1,0:T(8,128)(2,1)S(1)}, u32[]{:S(2)}, u32[]{:S(2)}) %collective-permute-start.58) | collective-permute-done | bytes 196640 | tf_op jit(solution)/shard_map/ppermute | solution.py:951
  236.1 3.9 %shard_map.267 = (f32[2,576,768]{2,1,0:T(8,128)}, f32[384,768]{1,0:T(8,128)}, f32[2,192,768]{2,1,0:T(8,128)}, f32[2,3,3,128]{3,2,1,0:T(4,128)S(1)}, f32[2,2,192]...) custom-call(s32[5]{0:T(128)S(1)} %copy-done.9, ...), custom_call_target="tpu_custom_call" | custom-call | flops 110000000 | bytes 350000 | tf_op jit(solution)/shard_map/pallas_call | solution.py:49
  (151 shorter events, 42.0 us)
Async XLA Ops:
  5.6 24.1 %collective-permute-start = (bf16[400,768]{1,0:T(8,128)(2,1)}, bf16[400,768]{1,0:T(8,128)(2,1)S(1)}, u32[]{:S(2)}, u32[]{:S(2)}) collective-permute-start(bf16[400,768]{1,0:T(8,128)(2,1)} %get-tuple-element.170), channel_id=1, source_target_pairs={{0,8},{8,0},{1,9},{9,1},{2,10},{10,2},{3,11},{11,3},{4,12},{12,4},... | collective-permute-start | bytes 1843208 | tf_op jit(solution)/shard_map/ppermute | solution.py:951
  8.7 21.1 %collective-permute-start.2 = (bf16[256,768]{1,0:T(8,128)(2,1)}, bf16[256,768]{1,0:T(8,128)(2,1)S(1)}, u32[]{:S(2)}, u32[]{:S(2)}) collective-permute-start(bf16[256,768]{1,0:T(8,128)(2,1)} %get-tuple-element.174), channel_id=1, source_target_pairs={{0,2},{2,0},{1,3},{3,1},{4,6},{6,4},{5,7},{7,5},{8,10},{10,8},{9,1... | collective-permute-start | bytes 1179656 | tf_op jit(solution)/shard_map/ppermute | solution.py:951
  29.8 19.3 %collective-permute-start.4 = (bf16[256,768]{1,0:T(8,128)(2,1)S(1)}, bf16[256,768]{1,0:T(8,128)(2,1)S(1)}, u32[]{:S(2)}, u32[]{:S(2)}) collective-permute-start(bf16[256,768]{1,0:T(8,128)(2,1)S(1)} %collective-permute-done.2.refs_3_.refs_8_), channel_id=1, source_target_pairs={{0,8},{8,0},{1,9},{9,1},{2,10},{10,2},{3,11},{11,3},{4,12},{12,4},... | collective-permute-start | bytes 1179656 | tf_op jit(solution)/shard_map/ppermute | solution.py:951
  30.3 18.8 %collective-permute-start.5 = (bf16[256,768]{1,0:T(8,128)(2,1)S(1)}, bf16[256,768]{1,0:T(8,128)(2,1)S(1)}, u32[]{:S(2)}, u32[]{:S(2)}) collective-permute-start(bf16[256,768]{1,0:T(8,128)(2,1)S(1)} %collective-permute-done.2.refs_3_.refs_8_), channel_id=1, source_target_pairs={{0,16},{16,0},{1,17},{17,1},{2,18},{18,2},{3,19},{19,3},{4,20},{20... | collective-permute-start | bytes 1179656 | tf_op jit(solution)/shard_map/ppermute | solution.py:951
  31.8 19.1 %collective-permute-start.6 = (bf16[256,768]{1,0:T(8,128)(2,1)S(1)}, bf16[256,768]{1,0:T(8,128)(2,1)S(1)}, u32[]{:S(2)}, u32[]{:S(2)}) collective-permute-start(bf16[256,768]{1,0:T(8,128)(2,1)S(1)} %collective-permute-done.2.refs_3_.refs_8_), channel_id=1, source_target_pairs={{0,24},{8,16},{16,8},{24,0},{1,25},{9,17},{17,9},{25,1},{2,26},{10... | collective-permute-start | bytes 1179656 | tf_op jit(solution)/shard_map/ppermute | solution.py:956
  33.3 15.7 %collective-permute-start.7 = (bf16[192,768]{1,0:T(8,128)(2,1)S(1)}, bf16[192,768]{1,0:T(8,128)(2,1)S(1)}, u32[]{:S(2)}, u32[]{:S(2)}) collective-permute-start(bf16[192,768]{1,0:T(8,128)(2,1)S(1)} %copy-done.15), channel_id=1, source_target_pairs={{0,2},{2,0},{1,3},{3,1},{4,6},{6,4},{5,7},{7,5},{8,10},{10,8},{9,1... | collective-permute-start | bytes 884744 | tf_op jit(solution)/shard_map/ppermute | solution.py:951
  50.9 8.4 %collective-permute-start.8 = (bf16[256,192]{1,0:T(8,128)(2,1)S(1)}, bf16[256,192]{1,0:T(8,128)(2,1)S(1)}, u32[]{:S(2)}, u32[]{:S(2)}) collective-permute-start(bf16[256,192]{1,0:T(8,128)(2,1)S(1)} %get-tuple-element.188.refs_5_), channel_id=1, source_target_pairs={{0,2},{2,0},{1,3},{3,1},{4,6},{6,4},{5,7},{7,5},{8,10},{10,8},{9,1... | collective-permute-start | bytes 294920 | tf_op jit(solution)/shard_map/ppermute | solution.py:951
  60.4 10.7 %collective-permute-start.11 = (bf16[192,768]{1,0:T(8,128)(2,1)S(1)}, bf16[192,768]{1,0:T(8,128)(2,1)S(1)}, u32[]{:S(2)}, u32[]{:S(2)}) collective-permute-start(bf16[192,768]{1,0:T(8,128)(2,1)S(1)} %collective-permute-done.7.refs_12_), channel_id=1, source_target_pairs={{0,8},{8,0},{1,9},{9,1},{2,10},{10,2},{3,11},{11,3},{4,12},{12,4},... | collective-permute-start | bytes 884744 | tf_op jit(solution)/shard_map/ppermute | solution.py:951
  60.9 10.2 %collective-permute-start.12 = (bf16[192,768]{1,0:T(8,128)(2,1)S(1)}, bf16[192,768]{1,0:T(8,128)(2,1)S(1)}, u32[]{:S(2)}, u32[]{:S(2)}) collective-permute-start(bf16[192,768]{1,0:T(8,128)(2,1)S(1)} %collective-permute-done.7.refs_12_), channel_id=1, source_target_pairs={{0,16},{16,0},{1,17},{17,1},{2,18},{18,2},{3,19},{19,3},{4,20},{20... | collective-permute-start | bytes 884744 | tf_op jit(solution)/shard_map/ppermute | solution.py:951
  62.5 14.9 %collective-permute-start.13 = (bf16[192,768]{1,0:T(8,128)(2,1)S(1)}, bf16[192,768]{1,0:T(8,128)(2,1)S(1)}, u32[]{:S(2)}, u32[]{:S(2)}) collective-permute-start(bf16[192,768]{1,0:T(8,128)(2,1)S(1)} %collective-permute-done.7.refs_12_), channel_id=1, source_target_pairs={{0,24},{8,16},{16,8},{24,0},{1,25},{9,17},{17,9},{25,1},{2,26},{10... | collective-permute-start | bytes 884744 | tf_op jit(solution)/shard_map/ppermute | solution.py:956
  77.3 11.1 %collective-permute-start.19 = (bf16[128,768]{1,0:T(8,128)(2,1)S(1)}, bf16[128,768]{1,0:T(8,128)(2,1)S(1)}, u32[]{:S(2)}, u32[]{:S(2)}) collective-permute-start(bf16[128,768]{1,0:T(8,128)(2,1)S(1)} %shard_map.250.refs_1_), channel_id=1, source_target_pairs={{0,2},{2,0},{1,3},{3,1},{4,6},{6,4},{5,7},{7,5},{8,10},{10,8},{9,1... | collective-permute-start | bytes 589832 | tf_op jit(solution)/shard_map/ppermute | solution.py:951
  77.3 11.1 %collective-permute-start.16 = (bf16[2,64,768]{2,1,0:T(8,128)(2,1)S(1)}, bf16[2,64,768]{2,1,0:T(8,128)(2,1)S(1)}, u32[]{:S(2)}, u32[]{:S(2)}) collective-permute-start(bf16[2,64,768]{2,1,0:T(8,128)(2,1)S(1)} %copy-done.16), channel_id=1, source_target_pairs={{0,8},{8,0},{1,9},{9,1},{2,10},{10,2},{3,11},{11,3},{4,12},{12,4},... | collective-permute-start | bytes 589832 | tf_op jit(solution)/shard_map/ppermute | solution.py:951
  81.5 15.2 %collective-permute-start.15 = (bf16[256,768]{1,0:T(8,128)(2,1)S(1)}, bf16[256,768]{1,0:T(8,128)(2,1)S(1)}, u32[]{:S(2)}, u32[]{:S(2)}) collective-permute-start(bf16[256,768]{1,0:T(8,128)(2,1)S(1)} %get-tuple-element.206.refs_7_.refs_3_), channel_id=1, source_target_pairs={{0,1},{1,0},{2,3},{3,2},{4,5},{5,4},{6,7},{7,6},{8,9},{9,8},{10,11... | collective-permute-start | bytes 1179656 | tf_op jit(solution)/shard_map/ppermute | solution.py:951
  100.0 15.3 %collective-permute-start.21 = (bf16[256,768]{1,0:T(8,128)(2,1)S(1)}, bf16[256,768]{1,0:T(8,128)(2,1)S(1)}, u32[]{:S(2)}, u32[]{:S(2)}) collective-permute-start(bf16[256,768]{1,0:T(8,128)(2,1)S(1)} %get-tuple-element.216.refs_4_), channel_id=1, source_target_pairs={{0,1},{1,0},{2,3},{3,2},{4,5},{5,4},{6,7},{7,6},{8,9},{9,8},{10,11... | collective-permute-start | bytes 1179656 | tf_op jit(solution)/shard_map/ppermute | solution.py:951
  100.0 13.1 %collective-permute-start.22 = (bf16[128,768]{1,0:T(8,128)(2,1)S(1)}, bf16[128,768]{1,0:T(8,128)(2,1)S(1)}, u32[]{:S(2)}, u32[]{:S(2)}) collective-permute-start(bf16[128,768]{1,0:T(8,128)(2,1)S(1)} %get-tuple-element.217), channel_id=1, source_target_pairs={{0,2},{2,0},{1,3},{3,1},{4,6},{6,4},{5,7},{7,5},{8,10},{10,8},{9,1... | collective-permute-start | bytes 589832 | tf_op jit(solution)/shard_map/ppermute | solution.py:951
  116.6 9.0 %collective-permute-start.26 = (bf16[128,768]{1,0:T(8,128)(2,1)S(1)}, bf16[128,768]{1,0:T(8,128)(2,1)S(1)}, u32[]{:S(2)}, u32[]{:S(2)}) collective-permute-start(bf16[128,768]{1,0:T(8,128)(2,1)S(1)} %collective-permute-done.22.refs_5_), channel_id=1, source_target_pairs={{0,1},{1,0},{2,3},{3,2},{4,5},{5,4},{6,7},{7,6},{8,9},{9,8},{10,11... | collective-permute-start | bytes 589832 | tf_op jit(solution)/shard_map/ppermute | solution.py:951
  119.3 9.3 %collective-permute-start.25 = (bf16[256,192]{1,0:T(8,128)(2,1)S(1)}, bf16[256,192]{1,0:T(8,128)(2,1)S(1)}, u32[]{:S(2)}, u32[]{:S(2)}) collective-permute-start(bf16[256,192]{1,0:T(8,128)(2,1)S(1)} %get-tuple-element.225), channel_id=1, source_target_pairs={{0,2},{2,0},{1,3},{3,1},{4,6},{6,4},{5,7},{7,5},{8,10},{10,8},{9,1... | collective-permute-start | bytes 294920 | tf_op jit(solution)/shard_map/ppermute | solution.py:951
  134.0 15.7 %collective-permute-start.30 = (bf16[384,768]{1,0:T(8,128)(2,1)S(1)}, bf16[384,768]{1,0:T(8,128)(2,1)S(1)}, u32[]{:S(2)}, u32[]{:S(2)}) collective-permute-start(bf16[384,768]{1,0:T(8,128)(2,1)S(1)} %get-tuple-element.252), channel_id=1, source_target_pairs={{0,16},{16,0},{1,17},{17,1},{2,18},{18,2},{3,19},{19,3},{4,20},{20... | collective-permute-start | bytes 1769480 | tf_op jit(solution)/shard_map/ppermute | solution.py:951
  135.6 15.4 %collective-permute-start.31 = (bf16[384,768]{1,0:T(8,128)(2,1)S(1)}, bf16[384,768]{1,0:T(8,128)(2,1)S(1)}, u32[]{:S(2)}, u32[]{:S(2)}) collective-permute-start(bf16[384,768]{1,0:T(8,128)(2,1)S(1)} %get-tuple-element.253), channel_id=1, source_target_pairs={{0,8},{8,0},{1,9},{9,1},{2,10},{10,2},{3,11},{11,3},{4,12},{12,4},... | collective-permute-start | bytes 1769480 | tf_op jit(solution)/shard_map/ppermute | solution.py:951
  136.1 13.5 %collective-permute-start.32 = (bf16[144,768]{1,0:T(8,128)(2,1)S(1)}, bf16[144,768]{1,0:T(8,128)(2,1)S(1)}, u32[]{:S(2)}, u32[]{:S(2)}) collective-permute-start(bf16[144,768]{1,0:T(8,128)(2,1)S(1)} %get-tuple-element.254.refs_1_), channel_id=1, source_target_pairs={{0,2},{2,0},{1,3},{3,1},{4,6},{6,4},{5,7},{7,5},{8,10},{10,8},{9,1... | collective-permute-start | bytes 663560 | tf_op jit(solution)/shard_map/ppermute | solution.py:951
  136.7 9.6 %collective-permute-start.29 = (bf16[128,768]{1,0:T(8,128)(2,1)S(1)}, bf16[128,768]{1,0:T(8,128)(2,1)S(1)}, u32[]{:S(2)}, u32[]{:S(2)}) collective-permute-start(bf16[128,768]{1,0:T(8,128)(2,1)S(1)} %get-tuple-element.251), channel_id=1, source_target_pairs={{0,1},{1,0},{2,3},{3,2},{4,5},{5,4},{6,7},{7,6},{8,9},{9,8},{10,11... | collective-permute-start | bytes 589832 | tf_op jit(solution)/shard_map/ppermute | solution.py:951
  151.2 16.5 %collective-permute-start.38 = (bf16[384,768]{1,0:T(8,128)(2,1)S(1)}, bf16[384,768]{1,0:T(8,128)(2,1)S(1)}, u32[]{:S(2)}, u32[]{:S(2)}) collective-permute-start(bf16[384,768]{1,0:T(8,128)(2,1)S(1)} %add_convert_fusion.2), channel_id=1, source_target_pairs={{0,16},{16,0},{1,17},{17,1},{2,18},{18,2},{3,19},{19,3},{4,20},{20... | collective-permute-start | bytes 1769480 | tf_op jit(solution)/shard_map/ppermute | solution.py:951
  151.9 15.7 %collective-permute-start.37 = (bf16[384,768]{1,0:T(8,128)(2,1)S(1)}, bf16[384,768]{1,0:T(8,128)(2,1)S(1)}, u32[]{:S(2)}, u32[]{:S(2)}) collective-permute-start(bf16[384,768]{1,0:T(8,128)(2,1)S(1)} %add_convert_fusion.3), channel_id=1, source_target_pairs={{0,8},{8,0},{1,9},{9,1},{2,10},{10,2},{3,11},{11,3},{4,12},{12,4},... | collective-permute-start | bytes 1769480 | tf_op jit(solution)/shard_map/ppermute | solution.py:951
  152.4 12.0 %collective-permute-start.33 = (bf16[2,128,768]{2,1,0:T(8,128)(2,1)S(1)}, bf16[2,128,768]{2,1,0:T(8,128)(2,1)S(1)}, u32[]{:S(2)}, u32[]{:S(2)}) collective-permute-start(bf16[2,128,768]{2,1,0:T(8,128)(2,1)S(1)} %get-tuple-element.257), channel_id=1, source_target_pairs={{0,1},{1,0},{2,3},{3,2},{4,5},{5,4},{6,7},{7,6},{8,9},{9,8},{10,11... | collective-permute-start | bytes 1179656 | tf_op jit(solution)/shard_map/ppermute | solution.py:951
  152.4 13.9 %collective-permute-start.36 = (bf16[144,768]{1,0:T(8,128)(2,1)S(1)}, bf16[144,768]{1,0:T(8,128)(2,1)S(1)}, u32[]{:S(2)}, u32[]{:S(2)}) collective-permute-start(bf16[144,768]{1,0:T(8,128)(2,1)S(1)} %collective-permute-done.32.refs_2_), channel_id=1, source_target_pairs={{0,4},{4,0},{1,5},{5,1},{2,6},{6,2},{3,7},{7,3},{8,12},{12,8},{9,1... | collective-permute-start | bytes 663560 | tf_op jit(solution)/shard_map/ppermute | solution.py:951
  153.0 9.2 %collective-permute-start.34 = (bf16[64,768]{1,0:T(8,128)(2,1)S(1)}, bf16[64,768]{1,0:T(8,128)(2,1)S(1)}, u32[]{:S(2)}, u32[]{:S(2)}) collective-permute-start(bf16[64,768]{1,0:T(8,128)(2,1)S(1)} %get-tuple-element.258.refs_5_), channel_id=1, source_target_pairs={{0,2},{2,0},{1,3},{3,1},{4,6},{6,4},{5,7},{7,5},{8,10},{10,8},{9,1... | collective-permute-start | bytes 294920 | tf_op jit(solution)/shard_map/ppermute | solution.py:951
  165.1 10.0 %collective-permute-start.35 = (bf16[2,64,768]{2,1,0:T(8,128)(2,1)S(1)}, bf16[2,64,768]{2,1,0:T(8,128)(2,1)S(1)}, u32[]{:S(2)}, u32[]{:S(2)}) collective-permute-start(bf16[2,64,768]{2,1,0:T(8,128)(2,1)S(1)} %get-tuple-element.267.refs_9_), channel_id=1, source_target_pairs={{0,2},{2,0},{1,3},{3,1},{4,6},{6,4},{5,7},{7,5},{8,10},{10,8},{9,1... | collective-permute-start | bytes 589832 | tf_op jit(solution)/shard_map/ppermute | solution.py:951
  167.8 16.1 %collective-permute-start.41 = (bf16[384,768]{1,0:T(8,128)(2,1)S(1)}, bf16[384,768]{1,0:T(8,128)(2,1)S(1)}, u32[]{:S(2)}, u32[]{:S(2)}) collective-permute-start(bf16[384,768]{1,0:T(8,128)(2,1)S(1)} %add_convert_fusion.refs_4_), channel_id=1, source_target_pairs={{0,8},{8,0},{1,9},{9,1},{2,10},{10,2},{3,11},{11,3},{4,12},{12,4},... | collective-permute-start | bytes 1769480 | tf_op jit(solution)/shard_map/ppermute | solution.py:951
  169.5 14.4 %collective-permute-start.40 = (bf16[384,768]{1,0:T(8,128)(2,1)S(1)}, bf16[384,768]{1,0:T(8,128)(2,1)S(1)}, u32[]{:S(2)}, u32[]{:S(2)}) collective-permute-start(bf16[384,768]{1,0:T(8,128)(2,1)S(1)} %add_convert_fusion.1.refs_0_), channel_id=1, source_target_pairs={{0,16},{16,0},{1,17},{17,1},{2,18},{18,2},{3,19},{19,3},{4,20},{20... | collective-permute-start | bytes 1769480 | tf_op jit(solution)/shard_map/ppermute | solution.py:951
  175.1 10.9 %collective-permute-start.46 = (bf16[384,768]{1,0:T(8,128)(2,1)S(1)}, bf16[384,768]{1,0:T(8,128)(2,1)S(1)}, u32[]{:S(2)}, u32[]{:S(2)}) collective-permute-start(bf16[384,768]{1,0:T(8,128)(2,1)S(1)} %add_convert_fusion.1.refs_0_), channel_id=1, source_target_pairs={{0,4},{4,0},{1,5},{5,1},{2,6},{6,2},{3,7},{7,3},{8,12},{12,8},{9,1... | collective-permute-start | bytes 1769480 | tf_op jit(solution)/shard_map/ppermute | solution.py:951
  175.1 12.2 %collective-permute-start.48 = (bf16[384,768]{1,0:T(8,128)(2,1)S(1)}, bf16[384,768]{1,0:T(8,128)(2,1)S(1)}, u32[]{:S(2)}, u32[]{:S(2)}) collective-permute-start(bf16[384,768]{1,0:T(8,128)(2,1)S(1)} %add_convert_fusion.refs_4_), channel_id=1, source_target_pairs={{0,4},{4,0},{1,5},{5,1},{2,6},{6,2},{3,7},{7,3},{8,12},{12,8},{9,1... | collective-permute-start | bytes 1769480 | tf_op jit(solution)/shard_map/ppermute | solution.py:951
  176.2 7.7 %collective-permute-start.39 = (bf16[3,32,768]{2,1,0:T(8,128)(2,1)S(1)}, bf16[3,32,768]{2,1,0:T(8,128)(2,1)S(1)}, u32[]{:S(2)}, u32[]{:S(2)}) collective-permute-start(bf16[3,32,768]{2,1,0:T(8,128)(2,1)S(1)} %get-tuple-element.284), channel_id=1, source_target_pairs={{0,8},{8,0},{1,9},{9,1},{2,10},{10,2},{3,11},{11,3},{4,12},{12,4},... | collective-permute-start | bytes 442376 | tf_op jit(solution)/shard_map/ppermute | solution.py:951
  184.5 16.8 %collective-permute-start.44 = (bf16[304,768]{1,0:T(8,128)(2,1)S(1)}, bf16[304,768]{1,0:T(8,128)(2,1)S(1)}, u32[]{:S(2)}, u32[]{:S(2)}) collective-permute-start(bf16[304,768]{1,0:T(8,128)(2,1)S(1)} %get-tuple-element.293), channel_id=1, source_target_pairs={{0,8},{8,0},{1,9},{9,1},{2,10},{10,2},{3,11},{11,3},{4,12},{12,4},... | collective-permute-start | bytes 1400840 | tf_op jit(solution)/shard_map/ppermute | solution.py:951
  185.9 15.4 %collective-permute-start.43 = (bf16[288,768]{1,0:T(8,128)(2,1)S(1)}, bf16[288,768]{1,0:T(8,128)(2,1)S(1)}, u32[]{:S(2)}, u32[]{:S(2)}) collective-permute-start(bf16[288,768]{1,0:T(8,128)(2,1)S(1)} %get-tuple-element.292), channel_id=1, source_target_pairs={{0,16},{16,0},{1,17},{17,1},{2,18},{18,2},{3,19},{19,3},{4,20},{20... | collective-permute-start | bytes 1327112 | tf_op jit(solution)/shard_map/ppermute | solution.py:951
  187.3 14.0 %collective-permute-start.45 = (bf16[2,3,32,768]{3,2,1,0:T(8,128)(2,1)S(1)}, bf16[2,3,32,768]{3,2,1,0:T(8,128)(2,1)S(1)}, u32[]{:S(2)}, u32[]{:S(2)}) collective-permute-start(bf16[2,3,32,768]{3,2,1,0:T(8,128)(2,1)S(1)} %pad_maximum_fusion), channel_id=1, source_target_pairs={{0,1},{1,0},{2,3},{3,2},{4,5},{5,4},{6,7},{7,6},{8,9},{9,8},{10,11... | collective-permute-start | bytes 884744 | tf_op jit(solution)/shard_map/ppermute | solution.py:951
  188.8 15.5 %collective-permute-start.42 = (bf16[2,3,32,768]{3,2,1,0:T(8,128)(2,1)S(1)}, bf16[2,3,32,768]{3,2,1,0:T(8,128)(2,1)S(1)}, u32[]{:S(2)}, u32[]{:S(2)}) collective-permute-start(bf16[2,3,32,768]{3,2,1,0:T(8,128)(2,1)S(1)} %pad_maximum_fusion), channel_id=1, source_target_pairs={{0,2},{2,0},{1,3},{3,1},{4,6},{6,4},{5,7},{7,5},{8,10},{10,8},{9,1... | collective-permute-start | bytes 884744 | tf_op jit(solution)/shard_map/ppermute | solution.py:951
  201.4 13.7 %collective-permute-start.51 = (bf16[304,768]{1,0:T(8,128)(2,1)S(1)}, bf16[304,768]{1,0:T(8,128)(2,1)S(1)}, u32[]{:S(2)}, u32[]{:S(2)}) collective-permute-start(bf16[304,768]{1,0:T(8,128)(2,1)S(1)} %add_convert_fusion.5), channel_id=1, source_target_pairs={{0,16},{16,0},{1,17},{17,1},{2,18},{18,2},{3,19},{19,3},{4,20},{20... | collective-permute-start | bytes 1400840 | tf_op jit(solution)/shard_map/ppermute | solution.py:951
  202.5 12.6 %collective-permute-start.50 = (bf16[288,768]{1,0:T(8,128)(2,1)S(1)}, bf16[288,768]{1,0:T(8,128)(2,1)S(1)}, u32[]{:S(2)}, u32[]{:S(2)}) collective-permute-start(bf16[288,768]{1,0:T(8,128)(2,1)S(1)} %add_convert_fusion.7), channel_id=1, source_target_pairs={{0,8},{8,0},{1,9},{9,1},{2,10},{10,2},{3,11},{11,3},{4,12},{12,4},... | collective-permute-start | bytes 1327112 | tf_op jit(solution)/shard_map/ppermute | solution.py:951
  204.3 10.7 %collective-permute-start.53 = (bf16[2,3,32,768]{3,2,1,0:T(8,128)(2,1)S(1)}, bf16[2,3,32,768]{3,2,1,0:T(8,128)(2,1)S(1)}, u32[]{:S(2)}, u32[]{:S(2)}) collective-permute-start(bf16[2,3,32,768]{3,2,1,0:T(8,128)(2,1)S(1)} %collective-permute-done.42.refs_2_), channel_id=1, source_target_pairs={{0,1},{1,0},{2,3},{3,2},{4,5},{5,4},{6,7},{7,6},{8,9},{9,8},{10,11... | collective-permute-start | bytes 884744 | tf_op jit(solution)/shard_map/ppermute | solution.py:951
  204.3 10.7 %collective-permute-start.52 = (bf16[2,32,768]{2,1,0:T(8,128)(2,1)S(1)}, bf16[2,32,768]{2,1,0:T(8,128)(2,1)S(1)}, u32[]{:S(2)}, u32[]{:S(2)}) collective-permute-start(bf16[2,32,768]{2,1,0:T(8,128)(2,1)S(1)} %get-tuple-element.341), channel_id=1, source_target_pairs={{0,8},{8,0},{1,9},{9,1},{2,10},{10,2},{3,11},{11,3},{4,12},{12,4},... | collective-permute-start | bytes 294920 | tf_op jit(solution)/shard_map/ppermute | solution.py:951
  215.2 11.6 %collective-permute-start.57 = (bf16[304,768]{1,0:T(8,128)(2,1)S(1)}, bf16[304,768]{1,0:T(8,128)(2,1)S(1)}, u32[]{:S(2)}, u32[]{:S(2)}) collective-permute-start(bf16[304,768]{1,0:T(8,128)(2,1)S(1)} %add_convert_fusion.4.refs_6_.refs_4_), channel_id=1, source_target_pairs={{0,8},{8,0},{1,9},{9,1},{2,10},{10,2},{3,11},{11,3},{4,12},{12,4},... | collective-permute-start | bytes 1400840 | tf_op jit(solution)/shard_map/ppermute | solution.py:951
  215.7 11.0 %collective-permute-start.56 = (bf16[288,768]{1,0:T(8,128)(2,1)S(1)}, bf16[288,768]{1,0:T(8,128)(2,1)S(1)}, u32[]{:S(2)}, u32[]{:S(2)}) collective-permute-start(bf16[288,768]{1,0:T(8,128)(2,1)S(1)} %add_convert_fusion.6.refs_5_.refs_0_), channel_id=1, source_target_pairs={{0,16},{16,0},{1,17},{17,1},{2,18},{18,2},{3,19},{19,3},{4,20},{20... | collective-permute-start | bytes 1327112 | tf_op jit(solution)/shard_map/ppermute | solution.py:951
  217.3 9.3 %collective-permute-start.54 = (bf16[2,2,32,768]{3,2,1,0:T(8,128)(2,1)S(1)}, bf16[2,2,32,768]{3,2,1,0:T(8,128)(2,1)S(1)}, u32[]{:S(2)}, u32[]{:S(2)}) collective-permute-start(bf16[2,2,32,768]{3,2,1,0:T(8,128)(2,1)S(1)} %pad_maximum_fusion.1), channel_id=1, source_target_pairs={{0,2},{2,0},{1,3},{3,1},{4,6},{6,4},{5,7},{7,5},{8,10},{10,8},{9,1... | collective-permute-start | bytes 589832 | tf_op jit(solution)/shard_map/ppermute | solution.py:951
  218.6 8.2 %collective-permute-start.55 = (bf16[2,2,32,768]{3,2,1,0:T(8,128)(2,1)S(1)}, bf16[2,2,32,768]{3,2,1,0:T(8,128)(2,1)S(1)}, u32[]{:S(2)}, u32[]{:S(2)}) collective-permute-start(bf16[2,2,32,768]{3,2,1,0:T(8,128)(2,1)S(1)} %pad_maximum_fusion.1), channel_id=1, source_target_pairs={{0,1},{1,0},{2,3},{3,2},{4,5},{5,4},{6,7},{7,6},{8,9},{9,8},{10,11... | collective-permute-start | bytes 589832 | tf_op jit(solution)/shard_map/ppermute | solution.py:951
  221.1 15.0 %collective-permute-start.61 = (bf16[304,768]{1,0:T(8,128)(2,1)S(1)}, bf16[304,768]{1,0:T(8,128)(2,1)S(1)}, u32[]{:S(2)}, u32[]{:S(2)}) collective-permute-start(bf16[304,768]{1,0:T(8,128)(2,1)S(1)} %add_convert_fusion.4.refs_6_.refs_4_), channel_id=1, source_target_pairs={{0,4},{4,0},{1,5},{5,1},{2,6},{6,2},{3,7},{7,3},{8,12},{12,8},{9,1... | collective-permute-start | bytes 1400840 | tf_op jit(solution)/shard_map/ppermute | solution.py:951
  226.8 9.3 %collective-permute-start.62 = (bf16[304,768]{1,0:T(8,128)(2,1)S(1)}, bf16[304,768]{1,0:T(8,128)(2,1)S(1)}, u32[]{:S(2)}, u32[]{:S(2)}) collective-permute-start(bf16[304,768]{1,0:T(8,128)(2,1)S(1)} %collective-permute-done.57.refs_5_), channel_id=1, source_target_pairs={{0,4},{4,0},{1,5},{5,1},{2,6},{6,2},{3,7},{7,3},{8,12},{12,8},{9,1... | collective-permute-start | bytes 1400840 | tf_op jit(solution)/shard_map/ppermute | solution.py:951
  226.8 9.3 %collective-permute-start.59 = (bf16[288,768]{1,0:T(8,128)(2,1)S(1)}, bf16[288,768]{1,0:T(8,128)(2,1)S(1)}, u32[]{:S(2)}, u32[]{:S(2)}) collective-permute-start(bf16[288,768]{1,0:T(8,128)(2,1)S(1)} %add_convert_fusion.6.refs_5_.refs_0_), channel_id=1, source_target_pairs={{0,4},{4,0},{1,5},{5,1},{2,6},{6,2},{3,7},{7,3},{8,12},{12,8},{9,1... | collective-permute-start | bytes 1327112 | tf_op jit(solution)/shard_map/ppermute | solution.py:951
  227.3 8.8 %collective-permute-start.60 = (bf16[288,768]{1,0:T(8,128)(2,1)S(1)}, bf16[288,768]{1,0:T(8,128)(2,1)S(1)}, u32[]{:S(2)}, u32[]{:S(2)}) collective-permute-start(bf16[288,768]{1,0:T(8,128)(2,1)S(1)} %collective-permute-done.56.refs_1_), channel_id=1, source_target_pairs={{0,4},{4,0},{1,5},{5,1},{2,6},{6,2},{3,7},{7,3},{8,12},{12,8},{9,1... | collective-permute-start | bytes 1327112 | tf_op jit(solution)/shard_map/ppermute | solution.py:951
  (33 other events, 257.1 us)

commit v4 on v3

--- a/solution.py
+++ b/solution.py
@@ -170,8 +170,8 @@
         (up_ref.at[c, pl.ds(pl.multiple_of(q * many, 16), many)], ups_ref.at[pl.ds(0, many)]),
         (down_ref.at[c, pl.ds(pl.multiple_of(q * many, 16), many)], downs_ref),
     ]
-    for k in range(2):
-        at = zh * 2 + (zl ^ k)
+    for k in range(4):
+        at = block ^ k
         to = pl.ds(k * least, least)
         pairs += [
             (cot_ref.at[c, 1 - y, at], cotfar_ref.at[0, to]),
@@ -434,6 +434,7 @@
     two2_ref,
     two3_ref,
     low_ref,
+    normed_ref,
     active_ref,
     slope_ref,
     upp_ref,
@@ -446,6 +447,7 @@
     partner_bias = extra[0:1] + extra[1:2] + extra[2:3]
     unit, _ = centred(residual(x_ref, (mixed0_ref, mixed1_ref)))
     normed_low = (unit * gain_ref[0:1, :] + shift_ref[0:1, :]).astype(BF16)
+    normed_ref[...] = normed_low
     active, slope = gelu_parts(mm(normed_low, up_ref[...]) + hidden_ref[pl.ds(p_ref[0], 1), :])
     active_ref[0] = active
     slope_ref[0] = slope.astype(BF16)
@@ -458,32 +460,40 @@
 
 def other_kernel(
     p_ref,
+    normed_ref,
+    up_ref,
+    hidden_ref,
+    active_ref,
+    slope_ref,
+):
+    active, slope = gelu_parts(
+        mm(normed_ref[...], up_ref[...]) + hidden_ref[pl.ds(p_ref[0], 1), :]
+    )
+    active_ref[...] = active
+    slope_ref[...] = slope.astype(BF16)
+
+
+def first_norm_kernel(p_ref, x_ref, mixed0_ref, mixed1_ref, gain_ref, shift_ref, normed_ref):
+    unit, _ = centred(residual(x_ref, (mixed0_ref, mixed1_ref)))
+    normed_ref[...] = (unit * gain_ref[0:1, :] + shift_ref[0:1, :]).astype(BF16)
+
+
+def lowered_kernel(p_ref, own_ref, far_ref, low0_ref, low1_ref):
+    least = own_ref.shape[0] // 8
+    total = own_ref[...].astype(F32) + turned(far_ref[...], least).astype(F32)
+    total = total.astype(BF16)
+    for i in range(4):
+        low0_ref[i * least : (i + 1) * least, :] = total[2 * i * least : (2 * i + 1) * least]
+        low1_ref[i * least : (i + 1) * least, :] = total[(2 * i + 1) * least : (2 * i + 2) * least]
+
+
+def final_kernel(
+    p_ref,
     x_ref,
     mixed0_ref,
     mixed1_ref,
-    gain_ref,
-    shift_ref,
-    up_ref,
-    hidden_ref,
-    normed_ref,
-    active_ref,
-    slope_ref,
-):
-    unit, _ = centred(residual(x_ref, (mixed0_ref, mixed1_ref)))
-    normed_low = (unit * gain_ref[0:1, :] + shift_ref[0:1, :]).astype(BF16)
-    normed_ref[...] = normed_low
-    active, slope = gelu_parts(mm(normed_low, up_ref[...]) + hidden_ref[pl.ds(p_ref[0], 1), :])
-    active_ref[...] = active
-    slope_ref[...] = slope.astype(BF16)
-
-
-def middle_kernel(
-    p_ref,
-    x_ref,
-    mixed0_ref,
-    mixed1_ref,
-    low_ref,
-    lowr_ref,
+    low0_ref,
+    low1_ref,
     cot00_ref,
     cot10_ref,
     cot01_ref,
@@ -491,44 +501,48 @@
     gain_ref,
     shift_ref,
     bdown_ref,
+    outk_ref,
+    outs_ref,
+    second_ref,
+    dlow_ref,
+    sums_ref,
+):
+    unit, _ = centred(residual(x_ref, (mixed0_ref, mixed1_ref)))
+    normed = unit * gain_ref[0:1, :] + shift_ref[0:1, :]
+    least = low0_ref.shape[0] // 4
+    pieces = []
+    for i in range(4):
+        pieces.append(low0_ref[i * least : (i + 1) * least, :])
+        pieces.append(low1_ref[i * least : (i + 1) * least, :])
+    lowered = stack_rows(pieces).astype(F32)
+    unit2, spread2 = centred(normed + lowered + bdown_ref[pl.ds(p_ref[0], 1), :])
+    out = (unit2 * gain_ref[1:2, :] + shift_ref[1:2, :]).astype(BF16)
+    for y in range(2):
+        at = 4 * y * least
+        outk_ref[y] = out[at : at + 2 * least]
+        outs_ref[y] = out[at + 2 * least : at + 4 * least]
+    cot = stack_rows([cot00_ref[...], cot01_ref[...], cot10_ref[...], cot11_ref[...]]).astype(F32)
+    second = norm_back(unit2, spread2, cot * gain_ref[1:2, :])
+    second_ref[...] = second
+    dlow_ref[...] = second.astype(BF16)
+    sums_ref[...] = jnp.zeros_like(sums_ref)
+    sums_ref[0:1, :] = jnp.sum(cot * unit2, axis=0, keepdims=True)
+    sums_ref[1:2, :] = jnp.sum(cot, axis=0, keepdims=True)
+    sums_ref[2:3, :] = jnp.sum(second, axis=0, keepdims=True)
+
+
+def middle_kernel(
+    p_ref,
+    dlow_ref,
     up_ref,
     down_ref,
     upp_ref,
     downp_ref,
     slope_ref,
-    outk_ref,
-    outs_ref,
     hid_ref,
-    second_ref,
-    normed_ref,
-    dlow_ref,
-    dlows_ref,
     dup_ref,
-    sums_ref,
-):
-    unit, _ = centred(residual(x_ref, (mixed0_ref, mixed1_ref)))
-    normed = unit * gain_ref[0:1, :] + shift_ref[0:1, :]
-    normed_ref[...] = normed.astype(BF16)
-    length = normed.shape[0]
-    least = length // 8
-    lowered = low_ref[...].astype(F32) + turned(lowr_ref[...], least).astype(F32)
-    unit2, spread2 = centred(normed + lowered + bdown_ref[pl.ds(p_ref[0], 1), :])
-    out = (unit2 * gain_ref[1:2, :] + shift_ref[1:2, :]).astype(BF16)
-    for y in range(2):
-        at = 4 * y * least
-        outk_ref[y * least : (y + 1) * least, :] = out[at : at + least]
-        outs_ref[y * least : (y + 1) * least, :] = out[at + 2 * least : at + 3 * least]
-    cot = stack_rows([cot00_ref[...], cot01_ref[...], cot10_ref[0], cot11_ref[1]]).astype(F32)
-    second = norm_back(unit2, spread2, cot * gain_ref[1:2, :])
-    second_ref[...] = second
-    sums_ref[...] = jnp.zeros_like(sums_ref)
-    sums_ref[0:1, :] = jnp.sum(cot * unit2, axis=0, keepdims=True)
-    sums_ref[1:2, :] = jnp.sum(cot, axis=0, keepdims=True)
-    sums_ref[2:3, :] = jnp.sum(second, axis=0, keepdims=True)
-    dlow = second.astype(BF16)
-    dlow_ref[...] = dlow
-    for i in range(4):
-        dlows_ref[i * least : (i + 1) * least, :] = dlow[2 * i * least : (2 * i + 1) * least]
+):
+    dlow = dlow_ref[...]
     dup = (mm(dlow, down_ref[...], NT) * slope_ref[0].astype(F32)).astype(BF16)
     dup_ref[...] = dup
     total = mm(dup, up_ref[...], NT)
@@ -543,8 +557,7 @@
     active_ref,
     activeo_ref,
     dlow_ref,
-    dlow0_ref,
-    dlow1_ref,
+    dlowo_ref,
     dup_ref,
     slopeo_ref,
     down_ref,
@@ -555,12 +568,7 @@
     bias_ref,
     all_ref,
 ):
-    least = dlow0_ref.shape[0] // 4
-    pieces = []
-    for i in range(4):
-        pieces.append(dlow0_ref[i * least : (i + 1) * least, :])
-        pieces.append(dlow1_ref[i * least : (i + 1) * least, :])
-    dlowo = stack_rows(pieces)
+    dlowo = dlowo_ref[...]
     dupo = (mm(dlowo, down_ref[...], NT) * slopeo_ref[...].astype(F32)).astype(BF16)
     dup = dup_ref[...]
     all_ref[...] = (mm(normed_ref[...], dup, TN) + mm(normedo_ref[...], dupo, TN)).astype(BF16)
@@ -618,9 +626,10 @@
     total_ref[...] = total
     own_ref[...] = mm(total, exit_ref[...], NT).astype(BF16)
     send_ref[...] = mm(total, exitp_ref[...], NT).astype(BF16)
-    pay_ref[0:rest, :] = total[0:rest]
-    pay_ref[rest : 2 * rest, :] = total[2 * rest : 3 * rest]
-    pay_ref[2 * rest :, :] = jnp.concatenate([sums1_ref[...], sums2_ref[...]], axis=0).astype(BF16)
+    least = rest // 2
+    pay_ref[0:least, :] = total[0:least]
+    pay_ref[least:rest, :] = total[2 * rest : 2 * rest + least]
+    pay_ref[rest:, :] = jnp.concatenate([sums1_ref[...], sums2_ref[...]], axis=0).astype(BF16)
 
 
 def backward_kernel(
@@ -708,7 +717,9 @@
     dmix_ref,
     pay_ref,
     payr_ref,
+    payl_ref,
     payc_ref,
+    paylc_ref,
     atto_ref,
     atts_ref,
     sp_ref,
@@ -721,9 +732,14 @@
     width = sp_ref.shape[-1]
     sp = sp_ref[...].reshape(-1, width)
     inner = dspat_ref.shape[-1]
-    rest = sp.shape[0] // 8
+    least = sp.shape[0] // 16
+    rest = 2 * least
     dmixo = stack_rows(
-        [payr_ref[0:rest, :], payc_ref[0:rest, :], payr_ref[rest : 2 * rest, :], payc_ref[rest : 2 * rest, :]]
+        [
+            ref[y * least : (y + 1) * least, :]
+            for y in range(2)
+            for ref in (payr_ref, payl_ref, payc_ref, paylc_ref)
+        ]
     )
     second_ref[0:inner, :] = (
         mm(atto_ref[...], dmix_ref[...], TN) + mm(atts_ref[...], dmixo, TN)
@@ -731,7 +747,7 @@
     for k in range(2):
         second_ref[(k + 1) * inner : (k + 2) * inner, :] = mm(dspat_ref[k], sp, TN).astype(BF16)
     base = 3 * inner
-    small = pay_ref[2 * rest :, :].astype(F32) + payr_ref[2 * rest :, :].astype(F32)
+    small = pay_ref[rest:, :].astype(F32) + payr_ref[rest:, :].astype(F32)
     second_ref[base : base + 16, :] = small.astype(BF16)
     second_ref[base + 16 : base + 32, :] = lines_ref[...].astype(BF16)
     dealt(second_ref, p_ref[2], keep_ref, send_ref)
@@ -827,17 +843,18 @@
     event_ref[...] = jnp.zeros_like(event_ref)
 
 
-def out_kernel(p_ref, w_ref, y_ref, zh_ref, zl_ref, zz_ref, out_ref):
+def out_kernel(p_ref, *refs):
     c, y, block = p_ref[0], p_ref[2], p_ref[4] * 2 + p_ref[3]
-    for turn, ref in enumerate((None, zl_ref, zh_ref, zz_ref)):
-        at = block ^ turn
+    out_ref, event_ref = refs[8:]
+    least = out_ref.shape[3]
+    for half in range(2):
         for far in range(2):
             for unit in range(2):
-                if ref is None:
-                    value = (y_ref if far else w_ref)[unit]
-                else:
-                    value = ref[far, unit]
-                out_ref[c ^ unit, y ^ far, at] = value
+                ref = refs[half * 4 + far * 2 + unit]
+                for turn in range(2):
+                    at = block ^ (half * 2 + turn)
+                    out_ref[c ^ unit, y ^ far, at] = ref[turn * least : (turn + 1) * least, :]
+    event_ref[...] = jnp.zeros_like(event_ref)
 
 
 def turn_kernel(p_ref, own_ref, far_ref, sum_ref, *, size):
@@ -845,11 +862,22 @@
     sum_ref[...] = (own_ref[...].astype(F32) + far).astype(BF16)
 
 
-def units_kernel(p_ref, near_ref, far_ref, other_ref, spat_ref, nears_ref, fars_ref):
-    nears_ref[0] = other_ref[0]
-    fars_ref[0] = other_ref[1]
-    nears_ref[1] = (near_ref[...].astype(F32) + spat_ref[0].astype(F32)).astype(BF16)
-    fars_ref[1] = (far_ref[...].astype(F32) + spat_ref[1].astype(F32)).astype(BF16)
+def plus_kernel(p_ref, *refs):
+    count = len(refs) // 3
+    for n in range(count):
+        total = refs[2 * n][...].astype(F32) + refs[2 * n + 1][...].astype(F32)
+        refs[2 * count + n][...] = total.astype(BF16)
+
+
+def units_kernel(
+    p_ref, own0_ref, own1_ref, other_ref, near_ref, far_ref, spat_ref, nears_ref, fars_ref
+):
+    nears_ref[0] = own0_ref[...]
+    fars_ref[0] = own1_ref[...]
+    nears_ref[1] = other_ref[0]
+    fars_ref[1] = other_ref[1]
+    nears_ref[2] = (near_ref[...].astype(F32) + spat_ref[0].astype(F32)).astype(BF16)
+    fars_ref[2] = (far_ref[...].astype(F32) + spat_ref[1].astype(F32)).astype(BF16)
 
 
 def fold_kernel(p_ref, own_ref, far_ref, keep_ref, send_ref):
@@ -859,16 +887,11 @@
     send_ref[...] = total[..., half:, :]
 
 
-def ends_first_kernel(p_ref, ownk_ref, ownf_ref, bothk_ref, bothf_ref, mine_ref, other_ref):
+def ends_first_kernel(p_ref, keep_ref, far_ref, mine_ref, other_ref):
     least = mine_ref.shape[1]
-    for unit in range(3):
-        if unit == 0:
-            total = ownk_ref[...].astype(F32) + ownf_ref[...].astype(F32)
-        else:
-            total = bothk_ref[unit - 1].astype(F32) + bothf_ref[unit - 1].astype(F32)
-        total = total.astype(BF16)
-        mine_ref[unit] = total[:least]
-        other_ref[unit] = total[least:]
+    total = (keep_ref[...].astype(F32) + far_ref[...].astype(F32)).astype(BF16)
+    mine_ref[...] = total[:, :least]
+    other_ref[...] = total[:, least:]
 
 
 def spread_kernel(p_ref, *refs):
@@ -1028,15 +1051,15 @@
             rows_of(rows),
             rows_of(share + 16 + inner // 4),
             rows_of(share),
-            ((2, 2 * least, width), BF16),
-            rows_of(2 * least),
-            rows_of(2 * least),
+            ((2, rows, width), BF16),
+            rows_of(rows),
+            rows_of(rows),
         ],
         scratch=[
             pltpu.VMEM(positions.shape, jnp.int32),
             pltpu.VMEM(boxes.shape, jnp.int32),
             pltpu.VMEM(hidden_bias.shape, F32),
-            pltpu.SemaphoreType.DMA((38,)),
+            pltpu.SemaphoreType.DMA((46,)),
         ],
         vmem=PACK_VMEM,
     )
@@ -1107,8 +1130,8 @@
             pltpu.SemaphoreType.DMA((2 + length // 128,)),
         ],
     )
-    att_send, att_own, *ups, down_part = join(att_send, att_own, *ups, down_part)
     att_recv = swap(att_send, "zh")
+    att_own, down_part, *ups = join(att_own, down_part, *ups)
     downs = [down_part, swap(down_part, "y"), swap(down_part, "batch"), swap_both(down_part)]
 
     keep, send, exit_partner = run(
@@ -1116,25 +1139,28 @@
         [att_own, att_recv, exit_own, *ups],
         [rows_of(rows, F32), rows_of(rows), rows_of(inner)],
     )
-    mixed0 = added(keep, swap(send, "core"))
+    (mixed0,) = run(
+        plus_kernel, [keep, swap(send, "core")], [rows_of(rows)], after=downs[1:3]
+    )
     mixed_zl = swap(mixed0, "zl")
     (mixed0,) = run(
         functools.partial(turn_kernel, size=least), [mixed0, mixed_zl], [rows_of(rows)]
     )
-    mixed0, cot_far, cot_near, *downs = join(mixed0, cot_far, cot_near, *downs)
     mixed1 = swap(mixed0, "core")
+    mixed_far0 = swap(mixed0, "zh")
+    mixed1, cot_far, cot_near, *downs = join(mixed1, cot_far, cot_near, *downs)
     cot10 = swap(cot_far, "y")
     cot01 = swap(cot_near, "core")
-    mixed_far0 = swap(mixed0, "zh")
 
     gains = (ln_gains, "stream")
     shifts = (ln_shifts, "stream")
     x_own = (x, (None, 0, None, None))
     x_far = (x, (None, 1, None, None))
-    low, active, slope, up_partner, down_partner = run(
+    low, normed, active, slope, up_partner, down_partner = run(
         forward_kernel,
         [x_own, mixed0, mixed1, gains, shifts, up, hidden_bias, down, *ups, *downs],
         [
+            rows_of(half),
             rows_of(half),
             ((2, half, hidden), BF16),
             ((2, half, hidden), BF16),
@@ -1143,69 +1169,77 @@
         ],
     )
     low_recv = swap(low, "zl")
+    mixed_far0, cot10, low = join(mixed_far0, cot10, low)
+    mixed_far1 = swap(mixed_far0, "core")
     cot11 = swap(cot10, "core")
-    mixed_far1 = swap(mixed_far0, "core")
-    normed_far, active_far, slope_far = run(
+    (normed_far,) = run(
+        first_norm_kernel,
+        [x_far, mixed_far0, mixed_far1, gains, shifts],
+        [rows_of(half)],
+        after=[low],
+    )
+    active_far, slope_far = run(
         other_kernel,
-        [x_far, mixed_far0, mixed_far1, gains, shifts, up, hidden_bias],
-        [rows_of(half), ((half, hidden), BF16), ((half, hidden), BF16)],
-        after=[low],
-    )
-    out_keep, out_send, hid, second, normed, dlow, dlow_send, dup, sums_two = run(
+        [normed_far, up, hidden_bias],
+        [((half, hidden), BF16), ((half, hidden), BF16)],
+    )
+    low0, low1 = run(
+        lowered_kernel, [low, low_recv], [rows_of(rows), rows_of(rows)], after=[slope_far, cot11]
+    )
+    far_low0 = swap(low0, "zh")
+
+    def finish(x_half, pieces, part, after=()):
+        rows_part = slice(part * rest, (part + 1) * rest)
+        cots = [
+            cot00[rows_part],
+            cot10[0, rows_part],
+            cot01[rows_part],
+            cot11[1, rows_part],
+        ]
+        return run(
+            final_kernel,
+            [x_half, *pieces, *cots, gains, shifts, b_down],
+            [
+                ((2, rest, width), BF16),
+                ((2, rest, width), BF16),
+                rows_of(half, F32),
+                rows_of(half),
+                rows_of(8, F32),
+            ],
+            after=after,
+        )
+
+    out_keep, out_send, second, dlow, sums_two = finish(x_own, [mixed0, mixed1, low0, low1], 0)
+    hid, dup = run(
         middle_kernel,
-        [
-            x_own,
-            mixed0,
-            mixed1,
-            low,
-            low_recv,
-            cot00,
-            cot10,
-            cot01,
-            cot11,
-            gains,
-            shifts,
-            b_down,
-            up,
-            down,
-            up_partner,
-            down_partner,
-            slope,
-        ],
-        [
-            rows_of(rest),
-            rows_of(rest),
-            rows_of(half),
-            rows_of(half, F32),
-            rows_of(half),
-            rows_of(half),
-            rows_of(rows),
-            ((half, hidden), BF16),
-            rows_of(8, F32),
-        ],
-        after=[slope_far],
+        [dlow, up, down, up_partner, down_partner, slope],
+        [rows_of(half), ((half, hidden), BF16)],
     )
     hid_recv = swap(hid, "zl")
-    dlow_far0 = swap(dlow_send, "zh")
     out_core = swap(out_send, "core")
-    hid_recv, dlow_far0, out_core = join(hid_recv, dlow_far0, out_core)
-    dlow_far1 = swap(dlow_far0, "zl")
+    out_y = swap(jnp.stack([out_keep[1], out_core[1]]), "y")
+    hid_recv, far_low0, out_y = join(hid_recv, far_low0, out_y)
+    far_low1 = swap(far_low0, "zl")
     first, dmix, sums_one = run(
         first_kernel,
         [x_own, mixed0, mixed1, second, hid, hid_recv, gains],
         [rows_of(half, F32), rows_of(half), rows_of(8, F32)],
     )
+    dmix_core = swap(dmix, "core")
     datt, datt_send, dmix, pay = run(
         attended_kernel,
-        [dmix, swap(dmix, "core"), exit_own, exit_partner, sums_one, sums_two],
+        [dmix, dmix_core, exit_own, exit_partner, sums_one, sums_two],
         [
             ((half, inner), BF16),
             ((half, inner), BF16),
             rows_of(half),
-            rows_of(rows + 16),
+            rows_of(rest + 16),
         ],
     )
     datt_recv = swap(datt_send, "zh")
+    far_keep, far_send, _, dlow_far, _ = finish(
+        x_far, [mixed_far0, mixed_far1, far_low0, far_low1], 1, [datt]
+    )
     up_keep, up_send, down_keep, down_send, bias_grad = run(
         ffn_grad_kernel,
         [
@@ -1214,8 +1248,7 @@
             (active, (0, None, None)),
             active_far,
             dlow,
-            dlow_far0,
-            dlow_far1,
+            dlow_far,
             dup,
             slope_far,
             down,
@@ -1231,10 +1264,10 @@
         scratch=[pltpu.VMEM((width, hidden), BF16)],
         after=[datt],
     )
-    datt_recv, up_send, down_send, pay = join(datt_recv, up_send, down_send, pay)
-    pay_recv = swap(pay, "zh")
     up_recv = swap(up_send, "batch")
     down_recv = swap(down_send, "y")
+    datt_recv, pay = join(datt_recv, pay)
+    pay_recv = swap(pay, "zh")
     piece = rows_of(rows)
     dscore, dproj, dspat, dxk0, dxk1, dxs, dsk0, dsk1, dss = run(
         functools.partial(backward_kernel, heads=heads, block=128),
@@ -1255,75 +1288,79 @@
         after=[bias_grad],
     )
 
-    dxk1, dxs, dss = join(dxk1, dxs, dss)
-    own_far = swap(dxk1, "zl")
+    steps = batch_steps()[1:]
+
+    def plus(pairs, after=(), over_batch=False):
+        sums = run(
+            plus_kernel,
+            [array for pair_of in pairs for array in pair_of],
+            [(left.shape, BF16) for left, _ in pairs],
+            after=after,
+        )
+        if over_batch:
+            for step in steps:
+                sums = [added(value, swap(value, "batch", step)) for value in sums]
+        return sums
+
+    dxk1, dxs, dss, pay_recv = join(dxk1, dxs, dss, pay_recv)
     dxs, dss = swap(dxs, "core"), swap(dss, "core")
     near, far = run(
         units_kernel,
-        [dsk0, dsk1, dxs, dss],
-        [((2, rows, width), BF16), ((2, rows, width), BF16)],
-    )
-    far, own_far, up_recv, down_recv, pay_recv = join(
-        far, own_far, up_recv, down_recv, pay_recv
-    )
-    both_far = swap(far, "zl")
-    up_half = added(up_keep, up_recv)
-    down_half = added(down_keep, down_recv)
+        [dxk0, dxk1, dxs, dsk0, dsk1, dss],
+        [((3, rows, width), BF16), ((3, rows, width), BF16)],
+    )
+    far_zl = swap(far, "zl")
+    up_half, down_half = plus([(up_keep, up_recv), (down_keep, down_recv)], after=[far])
     up_other = swap(up_half, "y")
     down_other = swap(down_half, "batch")
-    own_keep, own_send = run(fold_kernel, [dxk0, own_far], [rows_of(rest), rows_of(rest)])
-    own_zh = swap(own_send, "zh")
+    pay_zl = swap(join(pay_recv, far)[0], "zl")
     one_keep, one_send, lines = run(
         functools.partial(first_grad_kernel, heads=heads),
         [x, dscore, dproj, colidx, bias_grad],
         [rows_of(3 * inner // 2), rows_of(3 * inner // 2), rows_of(16, F32)],
         scratch=[pltpu.VMEM((3 * inner, width), BF16)],
-        after=[own_send],
-    )
-    both_far, own_zh, lines = join(both_far, own_zh, lines)
-    both_keep, both_send = run(
-        fold_kernel, [near, both_far], [((2, rest, width), BF16), ((2, rest, width), BF16)]
-    )
-    both_zh = swap(both_send, "zh")
-    pay_core = swap(pay_recv, "core")
+        after=[up_half],
+    )
+    keep, send = run(
+        fold_kernel,
+        [near, far_zl],
+        [((3, rest, width), BF16), ((3, rest, width), BF16)],
+        after=[lines],
+    )
+    send_zh = swap(send, "zh")
+    up_half, down_half = plus(
+        [(up_half, up_other), (down_half, down_other)], after=[send], over_batch=True
+    )
+    up_far = swap(up_half, "batch")
+    down_far = swap(down_half, "y")
+    mine, other = run(
+        ends_first_kernel,
+        [keep, send_zh],
+        [((3, least, width), BF16), ((3, least, width), BF16)],
+        after=[up_half],
+    )
+    got = swap(other, "y")
+    pay_recv, pay_zl, far_send, mine = join(pay_recv, pay_zl, far_send, mine)
+    pay_core, pay_zlcore = swap(pay_recv, "core"), swap(pay_zl, "core")
+    far_core = swap(far_send, "core")
     base = 3 * inner + 32
     two_keep, two_send = run(
         second_grad_kernel,
-        [dmix, pay, pay_recv, pay_core, att_own, att_send, sp, dspat, lines],
+        [dmix, pay, pay_recv, pay_zl, pay_core, pay_zlcore, att_own, att_send, sp, dspat, lines],
         [rows_of(base // 2), rows_of(base // 2)],
         scratch=[pltpu.VMEM((base, width), BF16)],
-        after=[both_send],
-    )
-    steps = batch_steps()[1:]
-
-    def total(left, right):
-        left = added(left, right)
-        for step in steps:
-            left = added(left, swap(left, "batch", step))
-        return left
-
-    up_other, down_other, two_keep = join(up_other, down_other, two_keep)
-    up_half = total(up_half, up_other)
-    down_half = total(down_half, down_other)
-    up_far = swap(up_half, "batch")
-    down_far = swap(down_half, "y")
-    both_zh, one_send, two_send, up_half, down_half = join(
-        both_zh, one_send, two_send, up_half, down_half
-    )
-    mine, other = run(
-        ends_first_kernel,
-        [own_keep, own_zh, both_keep, both_zh],
-        [((3, least, width), BF16), ((3, least, width), BF16)],
-    )
-    got = swap(other, "y")
-    got, up_far, down_far, one_send, two_send, out_core = join(
-        got, up_far, down_far, one_send, two_send, out_core
-    )
+        after=[mine, up_far, down_far],
+    )
+    one_send, two_send, got, two_keep = join(one_send, two_send, got, two_keep)
+    one_recv = swap(one_send, "batch")
+    two_recv = swap(two_send, "y")
     pages = jnp.stack([mine, got])
     pages_zh = swap(pages, "zh")
     pages_zl = swap(pages, "zl")
-    one_recv = swap(one_send, "batch")
-    two_recv = swap(two_send, "y")
+    one_half, two_half = plus([(one_keep, one_recv), (two_keep, two_recv)], after=[pages])
+    one_other = swap(one_half, "y")
+    two_other = swap(two_half, "batch")
+    far_y = swap(jnp.stack([far_keep[1], far_core[1]]), "y")
     halves = [up_half, up_far, down_half, down_far]
     others = [swap(value, "core") for value in halves]
     grad_up, grad_down, spread_event = run(
@@ -1334,34 +1371,37 @@
             ((2, 2, hidden // 2, width), F32),
             ((8, NBUCK), F32),
         ],
-    )
-    one_recv, two_recv, pages_zl, spread_event = join(one_recv, two_recv, pages_zl, spread_event)
-    one_half = added(one_keep, one_recv)
-    two_half = added(two_keep, two_recv)
-    one_other = swap(one_half, "y")
-    two_other = swap(two_half, "batch")
-    pages_zh, out_core = join(pages_zh, out_core)
-    pages_zz = swap(pages_zh, "zl")
-    outs = jnp.stack([out_keep, out_core]).reshape(2, 2, least, width)
-    out_y = swap(outs[:, 1], "y")
-    one_other, two_other, out_y, pages_zz = join(one_other, two_other, out_y, pages_zz)
-    one_half = total(one_half, one_other)
-    two_half = total(two_half, two_other)
+        after=[one_half],
+    )
+    one_half, two_half = plus(
+        [(one_half, one_other), (two_half, two_other)], after=[spread_event], over_batch=True
+    )
     one_far = swap(one_half, "batch")
     two_far = swap(two_half, "y")
-    out_pages = jnp.stack([outs[:, 0], out_y])
-    out_zh = swap(out_pages, "zh")
-    out_zl = swap(out_pages, "zl")
+    pages_zh, one_half = join(pages_zh, one_half)
+    pages_zz = swap(pages_zh, "zl")
     grad_tokens, grad_spatial, ends_event = run(
         ends_kernel,
         [mine, got, pages_zh, pages_zl, pages_zz],
         [((2, 2, 4, least, width), F32), ((2, 4, least, width), F32), ((8, NBUCK), F32)],
-        after=[one_half, two_half],
-    )
-    out_zh, out_zl, one_far, two_far, ends_event = join(
-        out_zh, out_zl, one_far, two_far, ends_event
-    )
-    out_zz = swap(out_zh, "zl")
+        after=[one_half],
+    )
+    output, out_event = run(
+        out_kernel,
+        [
+            out_keep[0],
+            out_core[0],
+            out_y[0],
+            out_y[1],
+            far_keep[0],
+            far_core[0],
+            far_y[0],
+            far_y[1],
+        ],
+        [((2, 2, 4, least, width), BF16), ((8, NBUCK), F32)],
+        after=[one_half],
+    )
+    one_far, two_far, out_event, ends_event = join(one_far, two_far, out_event, ends_event)
     halves = [one_half, one_far, two_half, two_far]
     others = [swap(value, "core") for value in halves]
     part = width // (2 * lax.axis_size("zh"))
@@ -1379,12 +1419,7 @@
             ((2, part), F32),
         ],
         scratch=[pltpu.VMEM((3 * inner, width), F32), pltpu.VMEM((base, width), F32)],
-        after=[spread_event, ends_event],
-    )
-    (output,) = run(
-        out_kernel,
-        [outs[:, 0], out_y, out_zh, out_zl, out_zz],
-        [((2, 2, 4, least, width), BF16)],
+        after=[spread_event, out_event, ends_event],
     )
     return (
         output.reshape(tokens.shape),

time: 241 us -> 231 us (0.959)
  waiting for transfers between devices: 124 us -> 106 us
  Pallas kernels: 58.5 us -> 66.4 us
    ppermute x61 -> x60, waiting for transfers between devices: 116 us -> 104 us  [swap(): return lax.ppermute(value, axis, [(i, i ^ step) for i in range(size)])]
    pallas_call x22 -> x30, Pallas kernels: 58.5 us -> 66.4 us  [kernel_call(): pl.pallas_call(kernel, out_shape=[jax.ShapeDtypeStruct(out[0], out[1]) fo...]
    ppermute x2, waiting for transfers between devices: 8.07 us -> 2.83 us  [swap_both(): lax.ppermute(value, ('batch', 'y'), [(i, i ^ 3) for i in range(size)])]
    ppermute x61 -> x60, starting transfers between devices: 46.1 us -> 47.9 us  [swap(): return lax.ppermute(value, axis, [(i, i ^ step) for i in range(size)])]
  transfers between devices with their start and end apart: 63 -> 62, of which waited for: 30 -> 35; matrix products, arithmetic and copies ran while one was open for 0% -> 0% of each run, Pallas kernels for 16% -> 24%
where the time goes in v4:
time: 231 us; the launch traced here: 230 us
  waiting for transfers between devices  106 us (46%)
  Pallas kernels  66.4 us (29%)
  starting transfers between devices  49.8 us (22%)
  local copies, waits for them, and re-layouts  6.45 us (3%)
    ppermute x60, waiting for transfers between devices, swap(): return lax.ppermute(value, axis, [(i, i ^ step) for i in range(size)])  104 us
    pallas_call x30, Pallas kernels, kernel_call(): pl.pallas_call(kernel, out_shape=[jax.ShapeDtypeStruct(out[0], out[1]) fo...  66.4 us
    ppermute x60, starting transfers between devices, swap(): return lax.ppermute(value, axis, [(i, i ^ step) for i in range(size)])  47.9 us
    unnamed x38, local copies, waits for them, and re-layouts  5.74 us
  transfers between devices with their start and end apart: 62, of which 35 were waited for; matrix products, arithmetic and copies ran while one was open for 0% of the time, Pallas kernels for 24%

profile of v4, /device:TPU:0, one launch (start us, length us, event | category | flops | bytes accessed | tf_op | source)
XLA Modules:
  0.0 230.4 jit_solution(5420922380765723837)
XLA Ops:
  1.2 4.7 %shard_map.246 = (bf16[400,768]{1,0:T(8,128)(2,1)}, bf16[272,768]{1,0:T(8,128)(2,1)}, bf16[128,768]{1,0:T(8,128)(2,1)}, bf16[256,768]{1,0:T(8,128)(2,1)}, bf16[1...) custom-call(s32[5]{0:T(128)} %stack.38.s_ref, ...), custom_call_target="tpu_custom_call" | custom-call | flops 110000000 | bytes 350000 | tf_op jit(solution)/shard_map/pallas_call | solution.py:49
  5.9 3.0 %collective-permute-start = (bf16[400,768]{1,0:T(8,128)(2,1)}, bf16[400,768]{1,0:T(8,128)(2,1)S(1)}, u32[]{:S(2)}, u32[]{:S(2)}) collective-permute-start(bf16[400,768]{1,0:T(8,128)(2,1)} %get-tuple-element.160), channel_id=1, source_target_pairs={{0,8},{8,0},{1,9},{9,1},{2,10},{10,2},{3,11},{11,3},{4,12},{12,4},... | collective-permute-start | bytes 1843208 | tf_op jit(solution)/shard_map/ppermute | solution.py:974
  9.0 2.6 %collective-permute-start.2 = (bf16[256,768]{1,0:T(8,128)(2,1)}, bf16[256,768]{1,0:T(8,128)(2,1)S(1)}, u32[]{:S(2)}, u32[]{:S(2)}) collective-permute-start(bf16[256,768]{1,0:T(8,128)(2,1)} %get-tuple-element.164), channel_id=1, source_target_pairs={{0,2},{2,0},{1,3},{3,1},{4,6},{6,4},{5,7},{7,5},{8,10},{10,8},{9,1... | collective-permute-start | bytes 1179656 | tf_op jit(solution)/shard_map/ppermute | solution.py:974
  11.6 1.7 copy-done.1
  16.7 1.8 shard_map.247
  18.5 11.5 %collective-permute-done.2.refs_3_.refs_8_ = bf16[256,768]{1,0:T(8,128)(2,1)S(1)} collective-permute-done((bf16[256,768]{1,0:T(8,128)(2,1)}, bf16[256,768]{1,0:T(8,128)(2,1)S(1)}, u32[]{:S(2)}, u32[]{:S(2)}) %collective-permute-start.2) | collective-permute-done | bytes 393248 | tf_op jit(solution)/shard_map/ppermute | solution.py:974
  32.0 1.6 collective-permute-start.5
  33.6 11.3 %shard_map.248 = (bf16[2,2,128,768]{3,2,1,0:T(8,128)(2,1)S(1)}, bf16[2,2,128,768]{3,2,1,0:T(8,128)(2,1)S(1)}, s32[512,8]{1,0:T(8,128)S(1)}, bf16[3,512,192]{2,1,...) custom-call(s32[5]{0:T(128)S(1)} %copy-done.7, ...), custom_call_target="tpu_custom_call" | custom-call | flops 32999999488 | bytes 105000000 | tf_op jit(solution)/shard_map/pallas_call | solution.py:49
  44.9 3.0 %collective-permute-start.8 = (bf16[256,192]{1,0:T(8,128)(2,1)S(1)}, bf16[256,192]{1,0:T(8,128)(2,1)S(1)}, u32[]{:S(2)}, u32[]{:S(2)}) collective-permute-start(bf16[256,192]{1,0:T(8,128)(2,1)S(1)} %get-tuple-element.177.refs_7_), channel_id=1, source_target_pairs={{0,2},{2,0},{1,3},{3,1},{4,6},{6,4},{5,7},{7,5},{8,10},{10,8},{9,1... | collective-permute-start | bytes 294920 | tf_op jit(solution)/shard_map/ppermute | solution.py:974
  47.9 2.4 %collective-permute-done.4.refs_12_ = bf16[192,768]{1,0:T(8,128)(2,1)S(1)} collective-permute-done((bf16[192,768]{1,0:T(8,128)(2,1)S(1)}, bf16[192,768]{1,0:T(8,128)(2,1)S(1)}, u32[]{:S(2)}, u32[]{:S(2)}) %collective-permute-start.4) | collective-permute-done | bytes 294944 | tf_op jit(solution)/shard_map/ppermute | solution.py:974
  53.0 2.0 collective-permute-done.8.refs_1_
  56.0 3.8 %collective-permute-done.11.refs_3_.refs_14_ = bf16[192,768]{1,0:T(8,128)(2,1)S(1)} collective-permute-done((bf16[192,768]{1,0:T(8,128)(2,1)S(1)}, bf16[192,768]{1,0:T(8,128)(2,1)S(1)}, u32[]{:S(2)}, u32[]{:S(2)}) %collective-permute-start.11) | collective-permute-done | bytes 294944 | tf_op jit(solution)/shard_map/ppermute | solution.py:974
  63.0 4.4 %collective-permute-done.12.refs_1_ = bf16[128,768]{1,0:T(8,128)(2,1)S(1)} collective-permute-done((bf16[128,768]{1,0:T(8,128)(2,1)S(1)}, bf16[128,768]{1,0:T(8,128)(2,1)S(1)}, u32[]{:S(2)}, u32[]{:S(2)}) %collective-permute-start.12) | collective-permute-done | bytes 196640 | tf_op jit(solution)/shard_map/ppermute | solution.py:974
  68.0 2.8 %collective-permute-done.14.refs_15_ = bf16[192,768]{1,0:T(8,128)(2,1)S(1)} collective-permute-done((bf16[192,768]{1,0:T(8,128)(2,1)S(1)}, bf16[192,768]{1,0:T(8,128)(2,1)S(1)}, u32[]{:S(2)}, u32[]{:S(2)}) %collective-permute-start.14) | collective-permute-done | bytes 294944 | tf_op jit(solution)/shard_map/ppermute | solution.py:979
  71.3 3.3 %collective-permute-start.15 = (bf16[128,768]{1,0:T(8,128)(2,1)S(1)}, bf16[128,768]{1,0:T(8,128)(2,1)S(1)}, u32[]{:S(2)}, u32[]{:S(2)}) collective-permute-start(bf16[128,768]{1,0:T(8,128)(2,1)S(1)} %shard_map.251.refs_1_), channel_id=1, source_target_pairs={{0,2},{2,0},{1,3},{3,1},{4,6},{6,4},{5,7},{7,5},{8,10},{10,8},{9,1... | collective-permute-start | bytes 589832 | tf_op jit(solution)/shard_map/ppermute | solution.py:974
  74.6 2.8 %shard_map.252 = (bf16[256,768]{1,0:T(8,128)(2,1)S(1)}, bf16[256,768]{1,0:T(8,128)(2,1)S(1)}, bf16[2,256,768]{2,1,0:T(8,128)(2,1)S(1)}, bf16[2,256,768]{2,1,0:T(...) custom-call(s32[5]{0:T(128)S(1)} %copy-done.7, ...), custom_call_target="tpu_custom_call" | custom-call | flops 110000000 | bytes 350000 | tf_op jit(solution)/shard_map/pallas_call | solution.py:49
  77.8 4.1 %collective-permute-done.15.refs_1_ = bf16[128,768]{1,0:T(8,128)(2,1)S(1)} collective-permute-done((bf16[128,768]{1,0:T(8,128)(2,1)S(1)}, bf16[128,768]{1,0:T(8,128)(2,1)S(1)}, u32[]{:S(2)}, u32[]{:S(2)}) %collective-permute-start.15) | collective-permute-done | bytes 196640 | tf_op jit(solution)/shard_map/ppermute | solution.py:974
  85.9 4.3 %collective-permute-done.17.refs_1_ = bf16[256,768]{1,0:T(8,128)(2,1)S(1)} collective-permute-done((bf16[256,768]{1,0:T(8,128)(2,1)S(1)}, bf16[256,768]{1,0:T(8,128)(2,1)S(1)}, u32[]{:S(2)}, u32[]{:S(2)}) %collective-permute-start.17) | collective-permute-done | bytes 393248 | tf_op jit(solution)/shard_map/ppermute | solution.py:974
  92.6 2.3 shard_map.257
  94.9 2.4 %collective-permute-start.22 = (bf16[256,768]{1,0:T(8,128)(2,1)S(1)}, bf16[256,768]{1,0:T(8,128)(2,1)S(1)}, u32[]{:S(2)}, u32[]{:S(2)}) collective-permute-start(bf16[256,768]{1,0:T(8,128)(2,1)S(1)} %get-tuple-element.211.refs_4_), channel_id=1, source_target_pairs={{0,1},{1,0},{2,3},{3,2},{4,5},{5,4},{6,7},{7,6},{8,9},{9,8},{10,11... | collective-permute-start | bytes 1179656 | tf_op jit(solution)/shard_map/ppermute | solution.py:974
  97.4 1.7 collective-permute-start.24
  99.1 2.9 %collective-permute-done.23.refs_3_ = bf16[128,768]{1,0:T(8,128)(2,1)S(1)} collective-permute-done((bf16[128,768]{1,0:T(8,128)(2,1)S(1)}, bf16[128,768]{1,0:T(8,128)(2,1)S(1)}, u32[]{:S(2)}, u32[]{:S(2)}) %collective-permute-start.23) | collective-permute-done | bytes 196640 | tf_op jit(solution)/shard_map/ppermute | solution.py:974
  102.0 8.3 %collective-permute-done.22.refs_5_ = bf16[256,768]{1,0:T(8,128)(2,1)S(1)} collective-permute-done((bf16[256,768]{1,0:T(8,128)(2,1)S(1)}, bf16[256,768]{1,0:T(8,128)(2,1)S(1)}, u32[]{:S(2)}, u32[]{:S(2)}) %collective-permute-start.22) | collective-permute-done | bytes 393248 | tf_op jit(solution)/shard_map/ppermute | solution.py:974
  111.7 1.6 collective-permute-done.26.refs_1_
  115.5 4.9 %collective-permute-done.25.refs_4_ = bf16[128,768]{1,0:T(8,128)(2,1)S(1)} collective-permute-done((bf16[128,768]{1,0:T(8,128)(2,1)S(1)}, bf16[128,768]{1,0:T(8,128)(2,1)S(1)}, u32[]{:S(2)}, u32[]{:S(2)}) %collective-permute-start.25) | collective-permute-done | bytes 196640 | tf_op jit(solution)/shard_map/ppermute | solution.py:974
  120.4 2.4 %shard_map.260 = (bf16[2,64,768]{2,1,0:T(8,128)(2,1)S(1)}, bf16[2,64,768]{2,1,0:T(8,128)(2,1)S(1)}, f32[256,768]{1,0:T(8,128)}, bf16[256,768]{1,0:T(8,128)(2,1)S(1)}, f32[8,768]{1,0:T(8,128)}) custom-call(s32[5]{0:T(128)S(1)} %copy-done.7, bf16[2,2,128,768]{3,2,1,0:T(8,128)(2,1)S(1)} %get-tuple-element.172.refs_0_, ...), custom_call_target="tpu_custom_call" | custom-call | flops 110000000 | bytes 350000 | tf_op jit(solution)/shard_map/pallas_call | solution.py:49
  122.8 2.6 %shard_map.261 = (bf16[384,768]{1,0:T(8,128)(2,1)S(1)}, bf16[384,768]{1,0:T(8,128)(2,1)S(1)}, bf16[384,768]{1,0:T(8,128)(2,1)S(1)}, bf16[384,768]{1,0:T(8,128)(2,1)S(1)}, f32[8,768]{1,0:T(8,128)S(1)}) custom-call(s32[5]{0:T(128)S(1)} %copy-done.7, bf16[256,768]{1,0:T(8,128)(2,1)S(1)} %get-tuple-element.229.refs_0_, ...), custom_call_target="tpu_custom_call" | custom-call | flops 32999999488 | bytes 105000000 | tf_op jit(solution)/shard_map/pallas_call | solution.py:49
  126.0 1.6 collective-permute-start.34
  127.6 5.3 %shard_map.262 = (bf16[3,512,512]{2,1,0:T(8,128)(2,1)S(1)}, bf16[3,512,192]{2,1,0:T(8,128)(2,1)S(1)}, bf16[2,512,192]{2,1,0:T(8,128)(2,1)S(1)}, bf16[128,768]{1,...) custom-call(s32[5]{0:T(128)S(1)} %copy-done.7, ...), custom_call_target="tpu_custom_call" | custom-call | flops 32999999488 | bytes 105000000 | tf_op jit(solution)/shard_map/pallas_call | solution.py:49
  138.3 2.1 collective-permute-done.33.refs_1_
  141.4 1.6 collective-permute-start.37
  144.5 5.8 %shard_map.265 = (bf16[288,768]{1,0:T(8,128)(2,1)S(1)}, bf16[288,768]{1,0:T(8,128)(2,1)S(1)}, f32[16,768]{1,0:T(8,128)S(1)}) custom-call(s32[5]{0:T(128)S(1)} %copy-done.7, bf16[2,2,128,768]{3,2,1,0:T(8,128)(2,1)S(1)} %get-tuple-element.172.refs_0_, bf16[3,512,512]{2,1,0:T(8,128)(2,1)S(1)} %get-tuple-element.250.refs_1_, ...), custom_call_target="tpu_custom_call" | custom-call | flops 110000000 | bytes 350000 | tf_op jit(solution)/shard_map/pallas_call | solution.py:49
  150.4 2.5 %collective-permute-done.32.refs_1_ = bf16[3,128,768]{2,1,0:T(8,128)(2,1)S(1)} collective-permute-done((bf16[3,128,768]{2,1,0:T(8,128)(2,1)S(1)}, bf16[3,128,768]{2,1,0:T(8,128)(2,1)S(1)}, u32[]{:S(2)}, u32[]{:S(2)}) %collective-permute-start.32) | collective-permute-done | bytes 589856 | tf_op jit(solution)/shard_map/ppermute | solution.py:974
  153.6 1.6 collective-permute-done.37.refs_3_
  157.2 1.6 collective-permute-start.43
  159.4 2.2 collective-permute-start.31
  161.6 10.4 %collective-permute-done.35.refs_1_ = bf16[3,64,768]{2,1,0:T(8,128)(2,1)S(1)} collective-permute-done((bf16[3,64,768]{2,1,0:T(8,128)(2,1)S(1)}, bf16[3,64,768]{2,1,0:T(8,128)(2,1)S(1)}, u32[]{:S(2)}, u32[]{:S(2)}) %collective-permute-start.35) | collective-permute-done | bytes 294944 | tf_op jit(solution)/shard_map/ppermute | solution.py:974
  176.3 1.6 collective-permute-done.44.refs_1_
  180.5 10.7 %collective-permute-done.46.refs_1_ = bf16[288,768]{1,0:T(8,128)(2,1)S(1)} collective-permute-done((bf16[288,768]{1,0:T(8,128)(2,1)S(1)}, bf16[288,768]{1,0:T(8,128)(2,1)S(1)}, u32[]{:S(2)}, u32[]{:S(2)}) %collective-permute-start.46) | collective-permute-done | bytes 442400 | tf_op jit(solution)/shard_map/ppermute | solution.py:974
  196.2 2.2 collective-permute-start.54
  198.4 5.1 %shard_map.271 = (f32[2,2,384,768]{3,2,1,0:T(8,128)}, f32[2,2,384,768]{3,2,1,0:T(8,128)}, f32[8,128]{1,0:T(8,128)S(1)}) custom-call(s32[5]{0:T(128)S(1)} %copy-done.7, bf16[384,768]{1,0:T(8,128)(2,1)S(1)} %get-tuple-element.262.refs_2_.refs_0_, bf16[384,768]{1,0:T(8,128)(2,1)S(1)} %collective-permute-done.42.refs_12_.refs_1_, ...), custom_call_target="tpu_custom_call" | custom-call | flops 110000000 | bytes 350000 | tf_op jit(solution)/shard_map/pallas_call | solution.py:49
  203.5 2.2 collective-permute-done.48.refs_1_
  208.3 1.9 collective-permute-done.45.refs_2_
  212.4 6.7 %collective-permute-done.55.refs_4_ = bf16[2,3,32,768]{3,2,1,0:T(8,128)(2,1)S(1)} collective-permute-done((bf16[2,3,32,768]{3,2,1,0:T(8,128)(2,1)S(1)}, bf16[2,3,32,768]{3,2,1,0:T(8,128)(2,1)S(1)}, u32[]{:S(2)}, u32[]{:S(2)}) %collective-permute-start.55) | collective-permute-done | bytes 294944 | tf_op jit(solution)/shard_map/ppermute | solution.py:974
  219.1 2.1 shard_map.274
  221.2 1.6 collective-permute-done.57.refs_5_
  223.3 1.9 collective-permute-done.58.refs_2_
  225.9 3.9 %shard_map.275 = (f32[2,576,768]{2,1,0:T(8,128)}, f32[384,768]{1,0:T(8,128)}, f32[2,192,768]{2,1,0:T(8,128)}, f32[2,3,3,128]{3,2,1,0:T(4,128)S(1)}, f32[2,2,192]...) custom-call(s32[5]{0:T(128)S(1)} %copy-done.7, ...), custom_call_target="tpu_custom_call" | custom-call | flops 110000000 | bytes 350000 | tf_op jit(solution)/shard_map/pallas_call | solution.py:49
  (158 shorter events, 54.3 us)
Async XLA Ops:
  5.9 24.1 %collective-permute-start = (bf16[400,768]{1,0:T(8,128)(2,1)}, bf16[400,768]{1,0:T(8,128)(2,1)S(1)}, u32[]{:S(2)}, u32[]{:S(2)}) collective-permute-start(bf16[400,768]{1,0:T(8,128)(2,1)} %get-tuple-element.160), channel_id=1, source_target_pairs={{0,8},{8,0},{1,9},{9,1},{2,10},{10,2},{3,11},{11,3},{4,12},{12,4},... | collective-permute-start | bytes 1843208 | tf_op jit(solution)/shard_map/ppermute | solution.py:974
  9.0 21.1 %collective-permute-start.2 = (bf16[256,768]{1,0:T(8,128)(2,1)}, bf16[256,768]{1,0:T(8,128)(2,1)S(1)}, u32[]{:S(2)}, u32[]{:S(2)}) collective-permute-start(bf16[256,768]{1,0:T(8,128)(2,1)} %get-tuple-element.164), channel_id=1, source_target_pairs={{0,2},{2,0},{1,3},{3,1},{4,6},{6,4},{5,7},{7,5},{8,10},{10,8},{9,1... | collective-permute-start | bytes 1179656 | tf_op jit(solution)/shard_map/ppermute | solution.py:974
  30.0 20.3 %collective-permute-start.7 = (bf16[256,768]{1,0:T(8,128)(2,1)S(1)}, bf16[256,768]{1,0:T(8,128)(2,1)S(1)}, u32[]{:S(2)}, u32[]{:S(2)}) collective-permute-start(bf16[256,768]{1,0:T(8,128)(2,1)S(1)} %collective-permute-done.2.refs_3_.refs_8_), channel_id=1, source_target_pairs={{0,24},{8,16},{16,8},{24,0},{1,25},{9,17},{17,9},{25,1},{2,26},{10... | collective-permute-start | bytes 1179656 | tf_op jit(solution)/shard_map/ppermute | solution.py:979
  31.5 18.8 %collective-permute-start.6 = (bf16[256,768]{1,0:T(8,128)(2,1)S(1)}, bf16[256,768]{1,0:T(8,128)(2,1)S(1)}, u32[]{:S(2)}, u32[]{:S(2)}) collective-permute-start(bf16[256,768]{1,0:T(8,128)(2,1)S(1)} %collective-permute-done.2.refs_3_.refs_8_), channel_id=1, source_target_pairs={{0,16},{16,0},{1,17},{17,1},{2,18},{18,2},{3,19},{19,3},{4,20},{20... | collective-permute-start | bytes 1179656 | tf_op jit(solution)/shard_map/ppermute | solution.py:974
  32.0 18.9 %collective-permute-start.5 = (bf16[256,768]{1,0:T(8,128)(2,1)S(1)}, bf16[256,768]{1,0:T(8,128)(2,1)S(1)}, u32[]{:S(2)}, u32[]{:S(2)}) collective-permute-start(bf16[256,768]{1,0:T(8,128)(2,1)S(1)} %collective-permute-done.2.refs_3_.refs_8_), channel_id=1, source_target_pairs={{0,8},{8,0},{1,9},{9,1},{2,10},{10,2},{3,11},{11,3},{4,12},{12,4},... | collective-permute-start | bytes 1179656 | tf_op jit(solution)/shard_map/ppermute | solution.py:974
  33.6 16.7 %collective-permute-start.4 = (bf16[192,768]{1,0:T(8,128)(2,1)S(1)}, bf16[192,768]{1,0:T(8,128)(2,1)S(1)}, u32[]{:S(2)}, u32[]{:S(2)}) collective-permute-start(bf16[192,768]{1,0:T(8,128)(2,1)S(1)} %copy-done.16), channel_id=1, source_target_pairs={{0,2},{2,0},{1,3},{3,1},{4,6},{6,4},{5,7},{7,5},{8,10},{10,8},{9,1... | collective-permute-start | bytes 884744 | tf_op jit(solution)/shard_map/ppermute | solution.py:974
  44.9 10.0 %collective-permute-start.8 = (bf16[256,192]{1,0:T(8,128)(2,1)S(1)}, bf16[256,192]{1,0:T(8,128)(2,1)S(1)}, u32[]{:S(2)}, u32[]{:S(2)}) collective-permute-start(bf16[256,192]{1,0:T(8,128)(2,1)S(1)} %get-tuple-element.177.refs_7_), channel_id=1, source_target_pairs={{0,2},{2,0},{1,3},{3,1},{4,6},{6,4},{5,7},{7,5},{8,10},{10,8},{9,1... | collective-permute-start | bytes 294920 | tf_op jit(solution)/shard_map/ppermute | solution.py:974
  50.9 8.9 %collective-permute-start.11 = (bf16[192,768]{1,0:T(8,128)(2,1)S(1)}, bf16[192,768]{1,0:T(8,128)(2,1)S(1)}, u32[]{:S(2)}, u32[]{:S(2)}) collective-permute-start(bf16[192,768]{1,0:T(8,128)(2,1)S(1)} %collective-permute-done.4.refs_12_), channel_id=1, source_target_pairs={{0,16},{16,0},{1,17},{17,1},{2,18},{18,2},{3,19},{19,3},{4,20},{20... | collective-permute-start | bytes 884744 | tf_op jit(solution)/shard_map/ppermute | solution.py:974
  52.4 8.7 %collective-permute-start.10 = (bf16[192,768]{1,0:T(8,128)(2,1)S(1)}, bf16[192,768]{1,0:T(8,128)(2,1)S(1)}, u32[]{:S(2)}, u32[]{:S(2)}) collective-permute-start(bf16[192,768]{1,0:T(8,128)(2,1)S(1)} %collective-permute-done.4.refs_12_), channel_id=1, source_target_pairs={{0,8},{8,0},{1,9},{9,1},{2,10},{10,2},{3,11},{11,3},{4,12},{12,4},... | collective-permute-start | bytes 884744 | tf_op jit(solution)/shard_map/ppermute | solution.py:974
  55.9 5.1 %collective-permute-start.9 = (bf16[128,768]{1,0:T(8,128)(2,1)S(1)}, bf16[128,768]{1,0:T(8,128)(2,1)S(1)}, u32[]{:S(2)}, u32[]{:S(2)}) collective-permute-start(bf16[128,768]{1,0:T(8,128)(2,1)S(1)} %get-tuple-element.184), channel_id=1, source_target_pairs={{0,4},{4,0},{1,5},{5,1},{2,6},{6,2},{3,7},{7,3},{8,12},{12,8},{9,1... | collective-permute-start | bytes 589832 | tf_op jit(solution)/shard_map/ppermute | solution.py:974
  61.6 5.7 %collective-permute-start.12 = (bf16[128,768]{1,0:T(8,128)(2,1)S(1)}, bf16[128,768]{1,0:T(8,128)(2,1)S(1)}, u32[]{:S(2)}, u32[]{:S(2)}) collective-permute-start(bf16[128,768]{1,0:T(8,128)(2,1)S(1)} %shard_map.250.refs_0_), channel_id=1, source_target_pairs={{0,1},{1,0},{2,3},{3,2},{4,5},{5,4},{6,7},{7,6},{8,9},{9,8},{10,11... | collective-permute-start | bytes 589832 | tf_op jit(solution)/shard_map/ppermute | solution.py:974
  62.5 8.4 %collective-permute-start.14 = (bf16[192,768]{1,0:T(8,128)(2,1)S(1)}, bf16[192,768]{1,0:T(8,128)(2,1)S(1)}, u32[]{:S(2)}, u32[]{:S(2)}) collective-permute-start(bf16[192,768]{1,0:T(8,128)(2,1)S(1)} %collective-permute-done.4.refs_12_), channel_id=1, source_target_pairs={{0,24},{8,16},{16,8},{24,0},{1,25},{9,17},{17,9},{25,1},{2,26},{10... | collective-permute-start | bytes 884744 | tf_op jit(solution)/shard_map/ppermute | solution.py:979
  70.9 11.0 %collective-permute-start.16 = (bf16[2,128,768]{2,1,0:T(8,128)(2,1)S(1)}, bf16[2,128,768]{2,1,0:T(8,128)(2,1)S(1)}, u32[]{:S(2)}, u32[]{:S(2)}) collective-permute-start(bf16[2,128,768]{2,1,0:T(8,128)(2,1)S(1)} %copy-done.15), channel_id=1, source_target_pairs={{0,8},{8,0},{1,9},{9,1},{2,10},{10,2},{3,11},{11,3},{4,12},{12,4},... | collective-permute-start | bytes 1179656 | tf_op jit(solution)/shard_map/ppermute | solution.py:974
  71.3 10.6 %collective-permute-start.15 = (bf16[128,768]{1,0:T(8,128)(2,1)S(1)}, bf16[128,768]{1,0:T(8,128)(2,1)S(1)}, u32[]{:S(2)}, u32[]{:S(2)}) collective-permute-start(bf16[128,768]{1,0:T(8,128)(2,1)S(1)} %shard_map.251.refs_1_), channel_id=1, source_target_pairs={{0,2},{2,0},{1,3},{3,1},{4,6},{6,4},{5,7},{7,5},{8,10},{10,8},{9,1... | collective-permute-start | bytes 589832 | tf_op jit(solution)/shard_map/ppermute | solution.py:974
  74.5 7.3 %collective-permute-start.20 = (bf16[128,768]{1,0:T(8,128)(2,1)S(1)}, bf16[128,768]{1,0:T(8,128)(2,1)S(1)}, u32[]{:S(2)}, u32[]{:S(2)}) collective-permute-start(bf16[128,768]{1,0:T(8,128)(2,1)S(1)} %copy-done.17), channel_id=1, source_target_pairs={{0,4},{4,0},{1,5},{5,1},{2,6},{6,2},{3,7},{7,3},{8,12},{12,8},{9,1... | collective-permute-start | bytes 589832 | tf_op jit(solution)/shard_map/ppermute | solution.py:974
  77.4 12.8 %collective-permute-start.17 = (bf16[256,768]{1,0:T(8,128)(2,1)S(1)}, bf16[256,768]{1,0:T(8,128)(2,1)S(1)}, u32[]{:S(2)}, u32[]{:S(2)}) collective-permute-start(bf16[256,768]{1,0:T(8,128)(2,1)S(1)} %get-tuple-element.197.refs_5_.refs_0_), channel_id=1, source_target_pairs={{0,1},{1,0},{2,3},{3,2},{4,5},{5,4},{6,7},{7,6},{8,9},{9,8},{10,11... | collective-permute-start | bytes 1179656 | tf_op jit(solution)/shard_map/ppermute | solution.py:974
  81.9 8.3 %collective-permute-start.19 = (bf16[2,128,768]{2,1,0:T(8,128)(2,1)S(1)}, bf16[2,128,768]{2,1,0:T(8,128)(2,1)S(1)}, u32[]{:S(2)}, u32[]{:S(2)}) collective-permute-start(bf16[2,128,768]{2,1,0:T(8,128)(2,1)S(1)} %collective-permute-done.16), channel_id=1, source_target_pairs={{0,4},{4,0},{1,5},{5,1},{2,6},{6,2},{3,7},{7,3},{8,12},{12,8},{9,1... | collective-permute-start | bytes 1179656 | tf_op jit(solution)/shard_map/ppermute | solution.py:974
  90.8 11.1 %collective-permute-start.23 = (bf16[128,768]{1,0:T(8,128)(2,1)S(1)}, bf16[128,768]{1,0:T(8,128)(2,1)S(1)}, u32[]{:S(2)}, u32[]{:S(2)}) collective-permute-start(bf16[128,768]{1,0:T(8,128)(2,1)S(1)} %get-tuple-element.201.refs_3_), channel_id=1, source_target_pairs={{0,2},{2,0},{1,3},{3,1},{4,6},{6,4},{5,7},{7,5},{8,10},{10,8},{9,1... | collective-permute-start | bytes 589832 | tf_op jit(solution)/shard_map/ppermute | solution.py:974
  94.9 15.4 %collective-permute-start.22 = (bf16[256,768]{1,0:T(8,128)(2,1)S(1)}, bf16[256,768]{1,0:T(8,128)(2,1)S(1)}, u32[]{:S(2)}, u32[]{:S(2)}) collective-permute-start(bf16[256,768]{1,0:T(8,128)(2,1)S(1)} %get-tuple-element.211.refs_4_), channel_id=1, source_target_pairs={{0,1},{1,0},{2,3},{3,2},{4,5},{5,4},{6,7},{7,6},{8,9},{9,8},{10,11... | collective-permute-start | bytes 1179656 | tf_op jit(solution)/shard_map/ppermute | solution.py:974
  97.4 12.9 %collective-permute-start.24 = (bf16[2,64,768]{2,1,0:T(8,128)(2,1)S(1)}, bf16[2,64,768]{2,1,0:T(8,128)(2,1)S(1)}, u32[]{:S(2)}, u32[]{:S(2)}) collective-permute-start(bf16[2,64,768]{2,1,0:T(8,128)(2,1)S(1)} %pad_maximum_fusion.1), channel_id=1, source_target_pairs={{0,8},{8,0},{1,9},{9,1},{2,10},{10,2},{3,11},{11,3},{4,12},{12,4},... | collective-permute-start | bytes 589832 | tf_op jit(solution)/shard_map/ppermute | solution.py:974
  111.7 8.7 %collective-permute-start.25 = (bf16[128,768]{1,0:T(8,128)(2,1)S(1)}, bf16[128,768]{1,0:T(8,128)(2,1)S(1)}, u32[]{:S(2)}, u32[]{:S(2)}) collective-permute-start(bf16[128,768]{1,0:T(8,128)(2,1)S(1)} %collective-permute-done.23.refs_3_), channel_id=1, source_target_pairs={{0,1},{1,0},{2,3},{3,2},{4,5},{5,4},{6,7},{7,6},{8,9},{9,8},{10,11... | collective-permute-start | bytes 589832 | tf_op jit(solution)/shard_map/ppermute | solution.py:974
  114.3 13.4 %collective-permute-start.27 = (bf16[256,192]{1,0:T(8,128)(2,1)S(1)}, bf16[256,192]{1,0:T(8,128)(2,1)S(1)}, u32[]{:S(2)}, u32[]{:S(2)}) collective-permute-start(bf16[256,192]{1,0:T(8,128)(2,1)S(1)} %get-tuple-element.222), channel_id=1, source_target_pairs={{0,2},{2,0},{1,3},{3,1},{4,6},{6,4},{5,7},{7,5},{8,10},{10,8},{9,1... | collective-permute-start | bytes 294920 | tf_op jit(solution)/shard_map/ppermute | solution.py:974
  125.4 14.9 %collective-permute-start.33 = (bf16[384,768]{1,0:T(8,128)(2,1)S(1)}, bf16[384,768]{1,0:T(8,128)(2,1)S(1)}, u32[]{:S(2)}, u32[]{:S(2)}) collective-permute-start(bf16[384,768]{1,0:T(8,128)(2,1)S(1)} %get-tuple-element.254), channel_id=1, source_target_pairs={{0,16},{16,0},{1,17},{17,1},{2,18},{18,2},{3,19},{19,3},{4,20},{20... | collective-permute-start | bytes 1769480 | tf_op jit(solution)/shard_map/ppermute | solution.py:974
  126.0 14.6 %collective-permute-start.34 = (bf16[384,768]{1,0:T(8,128)(2,1)S(1)}, bf16[384,768]{1,0:T(8,128)(2,1)S(1)}, u32[]{:S(2)}, u32[]{:S(2)}) collective-permute-start(bf16[384,768]{1,0:T(8,128)(2,1)S(1)} %get-tuple-element.256), channel_id=1, source_target_pairs={{0,8},{8,0},{1,9},{9,1},{2,10},{10,2},{3,11},{11,3},{4,12},{12,4},... | collective-permute-start | bytes 1769480 | tf_op jit(solution)/shard_map/ppermute | solution.py:974
  127.6 6.9 %collective-permute-start.28 = (bf16[80,768]{1,0:T(8,128)(2,1)S(1)}, bf16[80,768]{1,0:T(8,128)(2,1)S(1)}, u32[]{:S(2)}, u32[]{:S(2)}) collective-permute-start(bf16[80,768]{1,0:T(8,128)(2,1)S(1)} %get-tuple-element.238.refs_1_), channel_id=1, source_target_pairs={{0,2},{2,0},{1,3},{3,1},{4,6},{6,4},{5,7},{7,5},{8,10},{10,8},{9,1... | collective-permute-start | bytes 368648 | tf_op jit(solution)/shard_map/ppermute | solution.py:974
  137.5 15.4 %collective-permute-start.32 = (bf16[3,128,768]{2,1,0:T(8,128)(2,1)S(1)}, bf16[3,128,768]{2,1,0:T(8,128)(2,1)S(1)}, u32[]{:S(2)}, u32[]{:S(2)}) collective-permute-start(bf16[3,128,768]{2,1,0:T(8,128)(2,1)S(1)} %get-tuple-element.246.refs_4_), channel_id=1, source_target_pairs={{0,1},{1,0},{2,3},{3,2},{4,5},{5,4},{6,7},{7,6},{8,9},{9,8},{10,11... | collective-permute-start | bytes 1769480 | tf_op jit(solution)/shard_map/ppermute | solution.py:974
  141.4 13.8 %collective-permute-start.37 = (bf16[384,768]{1,0:T(8,128)(2,1)S(1)}, bf16[384,768]{1,0:T(8,128)(2,1)S(1)}, u32[]{:S(2)}, u32[]{:S(2)}) collective-permute-start(bf16[384,768]{1,0:T(8,128)(2,1)S(1)} %get-tuple-element.261.refs_2_), channel_id=1, source_target_pairs={{0,16},{16,0},{1,17},{17,1},{2,18},{18,2},{3,19},{19,3},{4,20},{20... | collective-permute-start | bytes 1769480 | tf_op jit(solution)/shard_map/ppermute | solution.py:974
  143.0 13.4 %collective-permute-start.36 = (bf16[384,768]{1,0:T(8,128)(2,1)S(1)}, bf16[384,768]{1,0:T(8,128)(2,1)S(1)}, u32[]{:S(2)}, u32[]{:S(2)}) collective-permute-start(bf16[384,768]{1,0:T(8,128)(2,1)S(1)} %get-tuple-element.257.refs_5_.refs_0_), channel_id=1, source_target_pairs={{0,8},{8,0},{1,9},{9,1},{2,10},{10,2},{3,11},{11,3},{4,12},{12,4},... | collective-permute-start | bytes 1769480 | tf_op jit(solution)/shard_map/ppermute | solution.py:974
  157.2 17.8 %collective-permute-start.43 = (bf16[384,768]{1,0:T(8,128)(2,1)S(1)}, bf16[384,768]{1,0:T(8,128)(2,1)S(1)}, u32[]{:S(2)}, u32[]{:S(2)}) collective-permute-start(bf16[384,768]{1,0:T(8,128)(2,1)S(1)} %get-tuple-element.272.refs_4_), channel_id=1, source_target_pairs={{0,8},{8,0},{1,9},{9,1},{2,10},{10,2},{3,11},{11,3},{4,12},{12,4},... | collective-permute-start | bytes 1769480 | tf_op jit(solution)/shard_map/ppermute | solution.py:974
  158.8 16.2 %collective-permute-start.42 = (bf16[384,768]{1,0:T(8,128)(2,1)S(1)}, bf16[384,768]{1,0:T(8,128)(2,1)S(1)}, u32[]{:S(2)}, u32[]{:S(2)}) collective-permute-start(bf16[384,768]{1,0:T(8,128)(2,1)S(1)} %get-tuple-element.262.refs_2_.refs_0_), channel_id=1, source_target_pairs={{0,16},{16,0},{1,17},{17,1},{2,18},{18,2},{3,19},{19,3},{4,20},{20... | collective-permute-start | bytes 1769480 | tf_op jit(solution)/shard_map/ppermute | solution.py:974
  159.4 12.7 %collective-permute-start.35 = (bf16[3,64,768]{2,1,0:T(8,128)(2,1)S(1)}, bf16[3,64,768]{2,1,0:T(8,128)(2,1)S(1)}, u32[]{:S(2)}, u32[]{:S(2)}) collective-permute-start(bf16[3,64,768]{2,1,0:T(8,128)(2,1)S(1)} %get-tuple-element.260.refs_4_), channel_id=1, source_target_pairs={{0,2},{2,0},{1,3},{3,1},{4,6},{6,4},{5,7},{7,5},{8,10},{10,8},{9,1... | collective-permute-start | bytes 884744 | tf_op jit(solution)/shard_map/ppermute | solution.py:974
  159.4 14.1 %collective-permute-start.31 = (bf16[80,768]{1,0:T(8,128)(2,1)S(1)}, bf16[80,768]{1,0:T(8,128)(2,1)S(1)}, u32[]{:S(2)}, u32[]{:S(2)}) collective-permute-start(bf16[80,768]{1,0:T(8,128)(2,1)S(1)} %collective-permute-done.28.refs_2_), channel_id=1, source_target_pairs={{0,1},{1,0},{2,3},{3,2},{4,5},{5,4},{6,7},{7,6},{8,9},{9,8},{10,11... | collective-permute-start | bytes 368648 | tf_op jit(solution)/shard_map/ppermute | solution.py:974
  172.7 5.2 %collective-permute-start.44 = (bf16[3,32,768]{2,1,0:T(8,128)(2,1)S(1)}, bf16[3,32,768]{2,1,0:T(8,128)(2,1)S(1)}, u32[]{:S(2)}, u32[]{:S(2)}) collective-permute-start(bf16[3,32,768]{2,1,0:T(8,128)(2,1)S(1)} %get-tuple-element.274), channel_id=1, source_target_pairs={{0,8},{8,0},{1,9},{9,1},{2,10},{10,2},{3,11},{11,3},{4,12},{12,4},... | collective-permute-start | bytes 442376 | tf_op jit(solution)/shard_map/ppermute | solution.py:974
  177.9 13.4 %collective-permute-start.47 = (bf16[304,768]{1,0:T(8,128)(2,1)S(1)}, bf16[304,768]{1,0:T(8,128)(2,1)S(1)}, u32[]{:S(2)}, u32[]{:S(2)}) collective-permute-start(bf16[304,768]{1,0:T(8,128)(2,1)S(1)} %get-tuple-element.280), channel_id=1, source_target_pairs={{0,8},{8,0},{1,9},{9,1},{2,10},{10,2},{3,11},{11,3},{4,12},{12,4},... | collective-permute-start | bytes 1400840 | tf_op jit(solution)/shard_map/ppermute | solution.py:974
  178.6 15.2 %collective-permute-start.52 = (bf16[384,768]{1,0:T(8,128)(2,1)S(1)}, bf16[384,768]{1,0:T(8,128)(2,1)S(1)}, u32[]{:S(2)}, u32[]{:S(2)}) collective-permute-start(bf16[384,768]{1,0:T(8,128)(2,1)S(1)} %get-tuple-element.272.refs_4_), channel_id=1, source_target_pairs={{0,4},{4,0},{1,5},{5,1},{2,6},{6,2},{3,7},{7,3},{8,12},{12,8},{9,1... | collective-permute-start | bytes 1769480 | tf_op jit(solution)/shard_map/ppermute | solution.py:974
  178.6 12.6 %collective-permute-start.46 = (bf16[288,768]{1,0:T(8,128)(2,1)S(1)}, bf16[288,768]{1,0:T(8,128)(2,1)S(1)}, u32[]{:S(2)}, u32[]{:S(2)}) collective-permute-start(bf16[288,768]{1,0:T(8,128)(2,1)S(1)} %get-tuple-element.278), channel_id=1, source_target_pairs={{0,16},{16,0},{1,17},{17,1},{2,18},{18,2},{3,19},{19,3},{4,20},{20... | collective-permute-start | bytes 1327112 | tf_op jit(solution)/shard_map/ppermute | solution.py:974
  180.0 15.2 %collective-permute-start.50 = (bf16[384,768]{1,0:T(8,128)(2,1)S(1)}, bf16[384,768]{1,0:T(8,128)(2,1)S(1)}, u32[]{:S(2)}, u32[]{:S(2)}) collective-permute-start(bf16[384,768]{1,0:T(8,128)(2,1)S(1)} %get-tuple-element.262.refs_2_.refs_0_), channel_id=1, source_target_pairs={{0,4},{4,0},{1,5},{5,1},{2,6},{6,2},{3,7},{7,3},{8,12},{12,8},{9,1... | collective-permute-start | bytes 1769480 | tf_op jit(solution)/shard_map/ppermute | solution.py:974
  180.2 12.3 %collective-permute-start.38 = (bf16[2,64,768]{2,1,0:T(8,128)(2,1)S(1)}, bf16[2,64,768]{2,1,0:T(8,128)(2,1)S(1)}, u32[]{:S(2)}, u32[]{:S(2)}) collective-permute-start(bf16[2,64,768]{2,1,0:T(8,128)(2,1)S(1)} %get-tuple-element.264), channel_id=1, source_target_pairs={{0,4},{4,0},{1,5},{5,1},{2,6},{6,2},{3,7},{7,3},{8,12},{12,8},{9,1... | collective-permute-start | bytes 589832 | tf_op jit(solution)/shard_map/ppermute | solution.py:974
  191.2 5.0 %collective-permute-start.51 = (bf16[384,768]{1,0:T(8,128)(2,1)S(1)}, bf16[384,768]{1,0:T(8,128)(2,1)S(1)}, u32[]{:S(2)}, u32[]{:S(2)}) collective-permute-start(bf16[384,768]{1,0:T(8,128)(2,1)S(1)} %collective-permute-done.42.refs_12_.refs_1_), channel_id=1, source_target_pairs={{0,4},{4,0},{1,5},{5,1},{2,6},{6,2},{3,7},{7,3},{8,12},{12,8},{9,1... | collective-permute-start | bytes 1769480 | tf_op jit(solution)/shard_map/ppermute | solution.py:974
  192.5 13.1 %collective-permute-start.48 = (bf16[288,768]{1,0:T(8,128)(2,1)S(1)}, bf16[288,768]{1,0:T(8,128)(2,1)S(1)}, u32[]{:S(2)}, u32[]{:S(2)}) collective-permute-start(bf16[288,768]{1,0:T(8,128)(2,1)S(1)} %get-tuple-element.281.refs_8_.refs_0_), channel_id=1, source_target_pairs={{0,8},{8,0},{1,9},{9,1},{2,10},{10,2},{3,11},{11,3},{4,12},{12,4},... | collective-permute-start | bytes 1327112 | tf_op jit(solution)/shard_map/ppermute | solution.py:974
  193.9 12.3 %collective-permute-start.49 = (bf16[304,768]{1,0:T(8,128)(2,1)S(1)}, bf16[304,768]{1,0:T(8,128)(2,1)S(1)}, u32[]{:S(2)}, u32[]{:S(2)}) collective-permute-start(bf16[304,768]{1,0:T(8,128)(2,1)S(1)} %get-tuple-element.282.refs_2_), channel_id=1, source_target_pairs={{0,16},{16,0},{1,17},{17,1},{2,18},{18,2},{3,19},{19,3},{4,20},{20... | collective-permute-start | bytes 1400840 | tf_op jit(solution)/shard_map/ppermute | solution.py:974
  195.2 15.0 %collective-permute-start.45 = (bf16[2,3,32,768]{3,2,1,0:T(8,128)(2,1)S(1)}, bf16[2,3,32,768]{3,2,1,0:T(8,128)(2,1)S(1)}, u32[]{:S(2)}, u32[]{:S(2)}) collective-permute-start(bf16[2,3,32,768]{3,2,1,0:T(8,128)(2,1)S(1)} %pad_maximum_fusion.refs_4_), channel_id=1, source_target_pairs={{0,2},{2,0},{1,3},{3,1},{4,6},{6,4},{5,7},{7,5},{8,10},{10,8},{9,1... | collective-permute-start | bytes 884744 | tf_op jit(solution)/shard_map/ppermute | solution.py:974
  195.3 15.4 %collective-permute-start.39 = (bf16[2,64,768]{2,1,0:T(8,128)(2,1)S(1)}, bf16[2,64,768]{2,1,0:T(8,128)(2,1)S(1)}, u32[]{:S(2)}, u32[]{:S(2)}) collective-permute-start(bf16[2,64,768]{2,1,0:T(8,128)(2,1)S(1)} %pad_maximum_fusion.2), channel_id=1, source_target_pairs={{0,8},{8,0},{1,9},{9,1},{2,10},{10,2},{3,11},{11,3},{4,12},{12,4},... | collective-permute-start | bytes 589832 | tf_op jit(solution)/shard_map/ppermute | solution.py:974
  196.2 16.2 %collective-permute-start.54 = (bf16[2,3,32,768]{3,2,1,0:T(8,128)(2,1)S(1)}, bf16[2,3,32,768]{3,2,1,0:T(8,128)(2,1)S(1)}, u32[]{:S(2)}, u32[]{:S(2)}) collective-permute-start(bf16[2,3,32,768]{3,2,1,0:T(8,128)(2,1)S(1)} %pad_maximum_fusion.refs_4_), channel_id=1, source_target_pairs={{0,1},{1,0},{2,3},{3,2},{4,5},{5,4},{6,7},{7,6},{8,9},{9,8},{10,11... | collective-permute-start | bytes 884744 | tf_op jit(solution)/shard_map/ppermute | solution.py:974
  206.9 14.3 %collective-permute-start.56 = (bf16[288,768]{1,0:T(8,128)(2,1)S(1)}, bf16[288,768]{1,0:T(8,128)(2,1)S(1)}, u32[]{:S(2)}, u32[]{:S(2)}) collective-permute-start(bf16[288,768]{1,0:T(8,128)(2,1)S(1)} %get-tuple-element.285.refs_8_.refs_5_.refs_0_), channel_id=1, source_target_pairs={{0,16},{16,0},{1,17},{17,1},{2,18},{18,2},{3,19},{19,3},{4,20},{20... | collective-permute-start | bytes 1327112 | tf_op jit(solution)/shard_map/ppermute | solution.py:974
  210.2 8.9 %collective-permute-start.55 = (bf16[2,3,32,768]{3,2,1,0:T(8,128)(2,1)S(1)}, bf16[2,3,32,768]{3,2,1,0:T(8,128)(2,1)S(1)}, u32[]{:S(2)}, u32[]{:S(2)}) collective-permute-start(bf16[2,3,32,768]{3,2,1,0:T(8,128)(2,1)S(1)} %collective-permute-done.45.refs_2_), channel_id=1, source_target_pairs={{0,1},{1,0},{2,3},{3,2},{4,5},{5,4},{6,7},{7,6},{8,9},{9,8},{10,11... | collective-permute-start | bytes 884744 | tf_op jit(solution)/shard_map/ppermute | solution.py:974
  210.3 12.6 %collective-permute-start.57 = (bf16[304,768]{1,0:T(8,128)(2,1)S(1)}, bf16[304,768]{1,0:T(8,128)(2,1)S(1)}, u32[]{:S(2)}, u32[]{:S(2)}) collective-permute-start(bf16[304,768]{1,0:T(8,128)(2,1)S(1)} %get-tuple-element.290.refs_4_), channel_id=1, source_target_pairs={{0,8},{8,0},{1,9},{9,1},{2,10},{10,2},{3,11},{11,3},{4,12},{12,4},... | collective-permute-start | bytes 1400840 | tf_op jit(solution)/shard_map/ppermute | solution.py:974
  210.8 14.5 %collective-permute-start.60 = (bf16[304,768]{1,0:T(8,128)(2,1)S(1)}, bf16[304,768]{1,0:T(8,128)(2,1)S(1)}, u32[]{:S(2)}, u32[]{:S(2)}) collective-permute-start(bf16[304,768]{1,0:T(8,128)(2,1)S(1)} %get-tuple-element.290.refs_4_), channel_id=1, source_target_pairs={{0,4},{4,0},{1,5},{5,1},{2,6},{6,2},{3,7},{7,3},{8,12},{12,8},{9,1... | collective-permute-start | bytes 1400840 | tf_op jit(solution)/shard_map/ppermute | solution.py:974
  (32 other events, 247.8 us)

commit v5 on v4

--- a/solution.py
+++ b/solution.py
@@ -122,76 +122,89 @@
         to_ref[pl.ds(pl.multiple_of(q * size, 16), size), :] = ref[rows, :]
 
 
+def copied(pairs, sems):
+    started = [
+        pltpu.make_async_copy(source, target, sems.at[n])
+        for n, (source, target) in enumerate(pairs)
+    ]
+    for copy in started:
+        copy.start()
+    return started
+
+
+def share_kernel(p_ref, exit_ref, up_ref, down_ref, bias_ref, ups_ref, downs_ref, biasv_ref, sems):
+    c = p_ref[0]
+    q = p_ref[1] * 2 + p_ref[2]
+    many = down_ref.shape[1] // 4
+    few = exit_ref.shape[1] // 4
+    started = copied(
+        [
+            (bias_ref, biasv_ref),
+            (up_ref.at[c, pl.ds(pl.multiple_of(q * many, 16), many)], ups_ref.at[pl.ds(0, many)]),
+            (
+                exit_ref.at[c, pl.ds(pl.multiple_of(q * few, 16), few)],
+                ups_ref.at[pl.ds(many + 16, few)],
+            ),
+            (down_ref.at[c, pl.ds(pl.multiple_of(q * many, 16), many)], downs_ref),
+        ],
+        sems,
+    )
+    started[0].wait()
+    left = biasv_ref[pl.ds(c, 1), :]
+    lines = []
+    for _ in range(3):
+        lines.append(left.astype(BF16).astype(F32))
+        left = left - lines[-1]
+    lines.append(jnp.zeros((13, left.shape[1]), F32))
+    ups_ref[many : many + 16, :] = jnp.concatenate(lines, axis=0).astype(BF16)
+    for copy in started[1:]:
+        copy.wait()
+
+
 def pack_kernel(
     p_ref,
     tok_ref,
     sp_ref,
     pos_ref,
     box_ref,
-    exit_ref,
-    up_ref,
-    down_ref,
-    bias_ref,
-    cot_ref,
-    far_ref,
+    far0_ref,
+    far1_ref,
+    far2_ref,
     near_ref,
     own_ref,
-    ups_ref,
-    downs_ref,
-    cotfar_ref,
-    cotnear_ref,
-    cotown_ref,
     posv_ref,
     boxv_ref,
-    biasv_ref,
     sems,
 ):
     c, y, zl, zh = p_ref[0], p_ref[2], p_ref[3], p_ref[4]
     block = zh * 2 + zl
-    q = p_ref[1] * 2 + y
     least = tok_ref.shape[3]
     rows = 4 * least
-    many = down_ref.shape[1] // 4
-    few = exit_ref.shape[1] // 4
-    pairs = [(pos_ref, posv_ref), (box_ref, boxv_ref), (bias_ref, biasv_ref)]
-    for k in range(4):
-        at = block ^ k
-        to = k * least
-        pairs += [
-            (tok_ref.at[1 - c, 1 - y, at], far_ref.at[pl.ds(to, least)]),
-            (sp_ref.at[1 - y, at], far_ref.at[pl.ds(rows + to, least)]),
-            (tok_ref.at[c, 1 - y, at], far_ref.at[pl.ds(2 * rows + 16 + to, least)]),
-            (tok_ref.at[1 - c, y, at], near_ref.at[pl.ds(to, least)]),
-            (sp_ref.at[y, at], near_ref.at[pl.ds(rows + to, least)]),
-            (tok_ref.at[c, y, at], own_ref.at[pl.ds(to, least)]),
-        ]
-    pairs += [
-        (exit_ref.at[c, pl.ds(pl.multiple_of(q * few, 16), few)], ups_ref.at[pl.ds(many + 16, few)]),
-        (up_ref.at[c, pl.ds(pl.multiple_of(q * many, 16), many)], ups_ref.at[pl.ds(0, many)]),
-        (down_ref.at[c, pl.ds(pl.multiple_of(q * many, 16), many)], downs_ref),
-    ]
+    pairs = [(pos_ref, posv_ref), (box_ref, boxv_ref)]
     for k in range(4):
         at = block ^ k
         to = pl.ds(k * least, least)
         pairs += [
-            (cot_ref.at[c, 1 - y, at], cotfar_ref.at[0, to]),
-            (cot_ref.at[1 - c, 1 - y, at], cotfar_ref.at[1, to]),
-            (cot_ref.at[1 - c, y, at], cotnear_ref.at[to]),
-            (cot_ref.at[c, y, at], cotown_ref.at[to]),
+            (tok_ref.at[1 - c, 1 - y, at], far0_ref.at[to]),
+            (sp_ref.at[1 - y, at], far1_ref.at[to]),
+            (tok_ref.at[c, 1 - y, at], far2_ref.at[to]),
+            (tok_ref.at[1 - c, y, at], near_ref.at[to]),
+            (sp_ref.at[y, at], near_ref.at[pl.ds(rows + k * least, least)]),
+            (tok_ref.at[c, y, at], own_ref.at[to]),
         ]
-    started = [
-        pltpu.make_async_copy(source, target, sems.at[n])
-        for n, (source, target) in enumerate(pairs)
-    ]
-    for copy in started:
-        copy.start()
-    for copy in started[:3]:
+    started = copied(pairs, sems)
+    for copy in started[:2]:
         copy.wait()
     lane = lax.broadcasted_iota(jnp.int32, (8, NBUCK), 1)
-    width = far_ref.shape[1]
-    for page, ref in ((1 - y, far_ref), (y, near_ref)):
+    width = far0_ref.shape[1]
+    for page, ref, at in ((1 - y, far0_ref, rows), (y, near_ref, 2 * rows)):
         place = posv_ref[pl.ds(page, 1), :]
-        lines = [place & 255, place >> 8, boxv_ref[0, pl.ds(page, 1), :], boxv_ref[1, pl.ds(page, 1), :]]
+        lines = [
+            place & 255,
+            place >> 8,
+            boxv_ref[0, pl.ds(page, 1), :],
+            boxv_ref[1, pl.ds(page, 1), :],
+        ]
         value = jnp.concatenate(lines + [jnp.zeros((4, NBUCK), jnp.int32)], axis=0)
         crossed = jnp.where(
             (lane & 63) < 32, pltpu.roll(value, NBUCK - 32, 1), pltpu.roll(value, 32, 1)
@@ -199,21 +212,31 @@
         value = jnp.where(zl == 0, value, crossed)
         value = jnp.where(zh == 0, value, pltpu.roll(value, 64, 1))
         value = jnp.concatenate([value.astype(F32), jnp.zeros((8, NBUCK), F32)], axis=0)
-        ref[2 * rows : 2 * rows + 16, 0:NBUCK] = value.astype(BF16)
-        ref[2 * rows : 2 * rows + 16, NBUCK:] = jnp.zeros((16, width - NBUCK), BF16)
-    left = biasv_ref[pl.ds(c, 1), :]
-    lines = []
-    for _ in range(3):
-        lines.append(left.astype(BF16).astype(F32))
-        left = left - lines[-1]
-    lines.append(jnp.zeros((13, left.shape[1]), F32))
-    ups_ref[many : many + 16, :] = jnp.concatenate(lines, axis=0).astype(BF16)
-    for copy in started[3:]:
+        ref[at : at + 16, 0:NBUCK] = value.astype(BF16)
+        ref[at : at + 16, NBUCK:] = jnp.zeros((16, width - NBUCK), BF16)
+    for copy in started[2:]:
         copy.wait()
 
 
-def indices(ref, least):
-    lines = ref[2 * least : 2 * least + 16, 0:NBUCK].astype(F32).astype(jnp.int32)
+def cotangent_kernel(p_ref, cot_ref, far_ref, near_ref, own_ref, sems):
+    c, y, block = p_ref[0], p_ref[2], p_ref[4] * 2 + p_ref[3]
+    least = cot_ref.shape[3]
+    pairs = []
+    for k in range(4):
+        at = block ^ k
+        to = pl.ds(k * least, least)
+        pairs += [
+            (cot_ref.at[c, 1 - y, at], far_ref.at[0, to]),
+            (cot_ref.at[1 - c, 1 - y, at], far_ref.at[1, to]),
+            (cot_ref.at[1 - c, y, at], near_ref.at[to]),
+            (cot_ref.at[c, y, at], own_ref.at[to]),
+        ]
+    for copy in copied(pairs, sems):
+        copy.wait()
+
+
+def indices(ref, at):
+    lines = ref[at : at + 16, 0:NBUCK].astype(F32).astype(jnp.int32)
     place = lines[0:1] + lines[1:2] * 256
     return jnp.concatenate([place, lines[2:4], jnp.zeros((5, NBUCK), jnp.int32)], axis=0)
 
@@ -225,17 +248,17 @@
     return jnp.where(lane < 64, pltpu.roll(index0, 64, 1), index1)
 
 
-def arrange(x0_ref, n0_ref, n1_ref, x_ref, sp_ref):
+def arrange(x0_ref, x1_ref, s0_ref, s1_ref, i0_ref, i1_ref, at, x_ref, sp_ref):
     least = x_ref.shape[1]
     rest = least // 2
     found = []
-    index0, index1 = indices(n0_ref, least), indices(n1_ref, least)
+    index0, index1 = indices(i0_ref, at), indices(i1_ref, at)
     for half in range(2):
         at = half * rest
         x_ref[half, 0:rest, :] = x0_ref[at : at + rest, :]
-        x_ref[half, rest:, :] = n1_ref[at : at + rest, :]
-        sp_ref[half, 0:rest, :] = n0_ref[least + at : least + at + rest, :]
-        sp_ref[half, rest:, :] = n1_ref[least + at : least + at + rest, :]
+        x_ref[half, rest:, :] = x1_ref[at : at + rest, :]
+        sp_ref[half, 0:rest, :] = s0_ref[at : at + rest, :]
+        sp_ref[half, rest:, :] = s1_ref[at : at + rest, :]
         found.append(two_cores(index0, index1, half))
     return found
 
@@ -279,7 +302,18 @@
     ]
     for copy in fetched:
         copy.start()
-    found = arrange(x00_ref, n00_ref, n01_ref, x_ref, sp_ref)
+    least = x_ref.shape[1]
+    found = arrange(
+        x00_ref,
+        n01_ref,
+        n00_ref.at[least:],
+        n01_ref.at[least:],
+        n00_ref,
+        n01_ref,
+        2 * least,
+        x_ref,
+        sp_ref,
+    )
     index_ref[...] = jnp.concatenate(found, axis=1)
     project(x_ref, sp_ref, w_ref, ws_ref, proj_ref, spat_ref, 0)
     for copy in fetched:
@@ -288,8 +322,11 @@
 
 def attention_kernel(
     p_ref,
-    n11_ref,
-    n10_ref,
+    x10_ref,
+    x11_ref,
+    s10_ref,
+    s11_ref,
+    i10_ref,
     x0_ref,
     sp0_ref,
     index_ref,
@@ -313,7 +350,6 @@
     sems,
     *,
     heads,
-    block,
 ):
     least = x_ref.shape[2]
     near = 2 * least
@@ -322,7 +358,7 @@
     proj_ref[:, 0:near, :] = proj0_ref[...]
     spat_ref[:, 0:near, :] = spat0_ref[...]
     found = arrange(
-        n10_ref.at[2 * least + 16 :], n10_ref, n11_ref, x_ref.at[1], sp_ref.at[1]
+        x10_ref, x11_ref, s10_ref, s11_ref, i10_ref, x11_ref, least, x_ref.at[1], sp_ref.at[1]
     )
     places = jnp.concatenate([index_ref[...]] + found, axis=1)
     colidx_ref[...] = jnp.transpose(places.astype(F32)).astype(jnp.int32)
@@ -338,46 +374,36 @@
     chosen = [(colidx_ref[:, kind : kind + 1] == level).astype(BF16) for kind in (1, 2)]
     chosen = jnp.concatenate(chosen, axis=1)
 
-    def step(at, carry):
-        rows = pl.ds(pl.multiple_of(at * block, block), block)
-        lane = lax.broadcasted_iota(jnp.int32, (block, NBUCK), 1)
-        index = jnp.clip(places[0:1, :] - colidx_ref[rows, 0:1], -HALF, HALF - 1) + HALF
-        boxes = [
-            jnp.clip(lane - colidx_ref[rows, kind : kind + 1], -HALF, HALF - 1) + HALF
-            for kind in (1, 2)
-        ]
-        for h in range(heads):
-            cols = slice(h * DH, (h + 1) * DH)
-            bias = jnp.concatenate(
-                [pick(table_ref[k, h : h + 1, :], boxes[k - 1]) for k in (1, 2)], axis=1
-            )
-            coarse = bias.astype(BF16)
-            fine = (bias - coarse.astype(F32)).astype(BF16)
-            left = jnp.concatenate(
-                [proj_ref[0, rows, cols], spat_ref[0, rows, cols]], axis=1
-            ) * jnp.asarray(DH**-0.5, BF16)
-            right = jnp.concatenate([proj_ref[1, :, cols], spat_ref[1, :, cols]], axis=1)
-            scores = mm(
-                jnp.concatenate([left, coarse, fine], axis=1),
-                jnp.concatenate([right, chosen, chosen], axis=1),
-                NT,
-            ) + pick(table_ref[0, h : h + 1, :], index)
-            top = jnp.max(scores, axis=-1, keepdims=True)
-            raised = jnp.exp(scores - top)
-            soft = raised * (1.0 / jnp.sum(raised, axis=-1, keepdims=True))
-            soft_ref[h, rows, :] = soft
-            att_ref[rows, cols] = mm(soft.astype(BF16), proj_ref[2, :, cols]).astype(BF16)
-        saved(at).start()
-        return carry
-
-    def saved(at):
-        rows = pl.ds(pl.multiple_of(at * block, block), block)
-        return pltpu.make_async_copy(
-            soft_ref.at[:, rows, :], soft_hbm.at[:, rows, :], sems.at[2 + at]
+    lane = lax.broadcasted_iota(jnp.int32, (length, NBUCK), 1)
+    boxes = [
+        jnp.clip(lane - colidx_ref[:, kind : kind + 1], -HALF, HALF - 1) + HALF
+        for kind in (1, 2)
+    ]
+    index = jnp.clip(places[0:1, :] - colidx_ref[:, 0:1], -HALF, HALF - 1) + HALF
+    for h in range(heads):
+        cols = slice(h * DH, (h + 1) * DH)
+        bias = jnp.concatenate(
+            [pick(table_ref[k, h : h + 1, :], boxes[k - 1]) for k in (1, 2)], axis=1
         )
-
-    lax.fori_loop(0, length // block, step, 0)
-    for copy in stored + [saved(at) for at in range(length // block)]:
+        coarse = bias.astype(BF16)
+        fine = (bias - coarse.astype(F32)).astype(BF16)
+        left = jnp.concatenate(
+            [proj_ref[0, :, cols], spat_ref[0, :, cols]], axis=1
+        ) * jnp.asarray(DH**-0.5, BF16)
+        right = jnp.concatenate([proj_ref[1, :, cols], spat_ref[1, :, cols]], axis=1)
+        scores = mm(
+            jnp.concatenate([left, coarse, fine], axis=1),
+            jnp.concatenate([right, chosen, chosen], axis=1),
+            NT,
+        ) + pick(table_ref[0, h : h + 1, :], index)
+        top = jnp.max(scores, axis=-1, keepdims=True)
+        raised = jnp.exp(scores - top)
+        soft = raised * (1.0 / jnp.sum(raised, axis=-1, keepdims=True))
+        soft_ref[h] = soft
+        stored.append(pltpu.make_async_copy(soft_ref.at[h], soft_hbm.at[h], sems.at[2 + h]))
+        stored[-1].start()
+        att_ref[:, cols] = mm(soft.astype(BF16), proj_ref[2, :, cols]).astype(BF16)
+    for copy in stored:
         copy.wait()
     part = length // 4
     own_ref[0:part, :] = att_ref[0:part, :]
@@ -712,6 +738,12 @@
     deal(total, ((dsk0_ref, dsk1_ref), (dss_ref.at[0], dss_ref.at[1])))
 
 
+def spatial_grad_kernel(p_ref, sp_ref, dspat_ref, keep_ref, send_ref):
+    sp = sp_ref[...].reshape(-1, sp_ref.shape[-1])
+    keep_ref[...] = mm(dspat_ref[p_ref[0]], sp, TN).astype(BF16)
+    send_ref[...] = mm(dspat_ref[1 - p_ref[0]], sp, TN).astype(BF16)
+
+
 def second_grad_kernel(
     p_ref,
     dmix_ref,
@@ -722,17 +754,17 @@
     paylc_ref,
     atto_ref,
     atts_ref,
-    sp_ref,
-    dspat_ref,
+    rest_ref,
+    spk_ref,
+    spr_ref,
     lines_ref,
     keep_ref,
     send_ref,
     second_ref,
 ):
-    width = sp_ref.shape[-1]
-    sp = sp_ref[...].reshape(-1, width)
-    inner = dspat_ref.shape[-1]
-    least = sp.shape[0] // 16
+    inner = spk_ref.shape[0]
+    length = dmix_ref.shape[0]
+    least = length // 8
     rest = 2 * least
     dmixo = stack_rows(
         [
@@ -741,12 +773,16 @@
             for ref in (payr_ref, payl_ref, payc_ref, paylc_ref)
         ]
     )
-    second_ref[0:inner, :] = (
+    base = rest_ref.shape[0]
+    second_ref[0:base, :] = rest_ref[...]
+    second_ref[base : base + inner, :] = (
         mm(atto_ref[...], dmix_ref[...], TN) + mm(atts_ref[...], dmixo, TN)
     ).astype(BF16)
-    for k in range(2):
-        second_ref[(k + 1) * inner : (k + 2) * inner, :] = mm(dspat_ref[k], sp, TN).astype(BF16)
-    base = 3 * inner
+    base += inner
+    second_ref[base : base + inner, :] = (
+        spk_ref[...].astype(F32) + spr_ref[...].astype(F32)
+    ).astype(BF16)
+    base += inner
     small = pay_ref[rest:, :].astype(F32) + payr_ref[rest:, :].astype(F32)
     second_ref[base : base + 16, :] = small.astype(BF16)
     second_ref[base + 16 : base + 32, :] = lines_ref[...].astype(BF16)
@@ -762,6 +798,7 @@
     bup_ref,
     keep_ref,
     send_ref,
+    rest_ref,
     lines_ref,
     first_ref,
     *,
@@ -774,6 +811,7 @@
     for k in range(3):
         first_ref[k * inner : (k + 1) * inner, :] = mm(dproj_ref[k], x, TN).astype(BF16)
     dealt(first_ref, p_ref[1], keep_ref, send_ref)
+    rest_ref[...] = first_ref[2 * keep_ref.shape[0] :, :]
     lane = lax.broadcasted_iota(jnp.int32, (1, NBUCK), 1)
     found = []
     for kind in range(3):
@@ -923,7 +961,6 @@
     shifts_ref,
     bup_ref,
     bdown_ref,
-    first_ref,
     second_ref,
     *,
     heads,
@@ -933,26 +970,23 @@
     width = exit_ref.shape[2]
     part = gains_ref.shape[2]
     per = width // NBUCK
-    base = 3 * inner
     firsts = ((one0_ref, one1_ref), (one2_ref, one3_ref))
     seconds = ((two0_ref, two1_ref), (two2_ref, two3_ref))
-
-    def whole(halves, side, to_ref):
-        size = halves[0].shape[0]
-        for far in range(2):
-            at = pl.multiple_of((side ^ far) * size, 16)
-            to_ref[pl.ds(at, size), :] = halves[far][...].astype(F32)
-
     for other in range(2):
         s = c ^ other
-        whole(firsts[other], p_ref[1], first_ref)
-        qkv_ref[s] = first_ref[...]
-        whole(seconds[other], p_ref[2], second_ref)
-        exit_ref[s] = second_ref[0:inner, :]
-        if other:
-            spat_ref[...] += second_ref[inner:base, :]
-        else:
-            spat_ref[...] = second_ref[inner:base, :]
+        for far in range(2):
+            size = one0_ref.shape[0]
+            at = pl.multiple_of((p_ref[1] ^ far) * size, 16)
+            qkv_ref[s, pl.ds(at, size), :] = firsts[other][far][...].astype(F32)
+            size = two0_ref.shape[0]
+            at = pl.multiple_of((p_ref[2] ^ far) * size, 16)
+            second_ref[pl.ds(at, size), :] = seconds[other][far][...].astype(F32)
+        base = 3 * inner - 2 * one0_ref.shape[0]
+        qkv_ref[s, 2 * one0_ref.shape[0] :, :] = second_ref[0:base, :]
+        exit_ref[s] = second_ref[base : base + inner, :]
+        base += inner
+        spat_ref[s] = second_ref[base : base + inner, :]
+        base += inner
         sums = second_ref[base : base + 16, :]
         cut = sums[:, 0:part]
         for at in range(1, width // part):
@@ -963,7 +997,7 @@
         lines = second_ref[base + 16 : base + 32, :]
         for n in range(3 * heads):
             at = (n % per) * NBUCK
-            tables_ref[s, n // heads, n % heads : n % heads + 1, :] = lines[
+            tables_ref[n // heads, n % heads, pl.ds(s, 1), :] = lines[
                 n // per : n // per + 1, at : at + NBUCK
             ]
         bup_ref[pl.ds(s, 1), :] = lines[2:3]
@@ -1031,41 +1065,53 @@
         return ((count, width), dtype)
 
     share = hidden // 4
-    anywhere = [
-        tokens.reshape(2, 2, 4, least, width),
-        spatial.reshape(2, 4, least, width),
-        positions,
-        boxes,
-        exit_matrix,
-        up_weight,
-        shrink_projection_array,
-        hidden_bias,
-        cotangent.reshape(2, 2, 4, least, width),
-    ]
-    far, near, x00, up_part, down_part, cot_far, cot_near, cot00 = run(
+    up_part, down_part = run(
+        share_kernel,
+        [
+            (exit_matrix, "any"),
+            (up_weight, "any"),
+            (shrink_projection_array, "any"),
+            (hidden_bias, "any"),
+        ],
+        [rows_of(share + 16 + inner // 4), rows_of(share)],
+        scratch=[pltpu.VMEM(hidden_bias.shape, F32), pltpu.SemaphoreType.DMA((4,))],
+        vmem=PACK_VMEM,
+    )
+    up_part = swap(up_part, "zh")
+    far0, far1, far2, near, x00 = run(
         pack_kernel,
-        [(array, "any") for array in anywhere],
-        [
-            rows_of(3 * rows + 16),
+        [
+            (tokens.reshape(2, 2, 4, least, width), "any"),
+            (spatial.reshape(2, 4, least, width), "any"),
+            (positions, "any"),
+            (boxes, "any"),
+        ],
+        [
+            rows_of(rows + 16),
+            rows_of(rows),
+            rows_of(rows),
             rows_of(2 * rows + 16),
             rows_of(rows),
-            rows_of(share + 16 + inner // 4),
-            rows_of(share),
-            ((2, rows, width), BF16),
-            rows_of(rows),
-            rows_of(rows),
-        ],
+        ],
+        us=30,
         scratch=[
             pltpu.VMEM(positions.shape, jnp.int32),
             pltpu.VMEM(boxes.shape, jnp.int32),
-            pltpu.VMEM(hidden_bias.shape, F32),
-            pltpu.SemaphoreType.DMA((46,)),
+            pltpu.SemaphoreType.DMA((26,)),
         ],
         vmem=PACK_VMEM,
-    )
-    n10 = swap(far, "y")
+        after=[down_part],
+    )
+    i10, s10, x10 = swap(far0, "y"), swap(far1, "y"), swap(far2, "y")
+    cot_far, cot_near, cot00 = run(
+        cotangent_kernel,
+        [(cotangent.reshape(2, 2, 4, least, width), "any")],
+        [((2, rows, width), BF16), rows_of(rows), rows_of(rows)],
+        scratch=[pltpu.SemaphoreType.DMA((16,))],
+        vmem=PACK_VMEM,
+        after=[x00],
+    )
     n01 = swap(near, "core")
-    up_part = swap(up_part, "zh")
     weights = (jnp.swapaxes(query_key_value_weight, 2, 3), "stream")
     spatial_weights = jnp.swapaxes(w_spatial, 1, 2)
     x0, sp0, index0, proj0, spat0, up, down, exit_own = run(
@@ -1091,17 +1137,21 @@
             rows_of(inner),
         ],
         scratch=[pltpu.SemaphoreType.DMA((3,))],
-    )
-    n10, x0, up_part, down_part = join(n10, x0, up_part, down_part)
-    n11 = swap(n10, "core")
+        after=[cot00],
+    )
+    i10, s10, x10, x0, up_part, down_part = join(i10, s10, x10, x0, up_part, down_part)
+    x11, s11 = swap(i10, "core"), swap(s10, "core")
     ups = [up_part, swap(up_part, "y"), swap(up_part, "batch"), swap_both(up_part)]
     down_part = swap(down_part, "zh")
 
     x, sp, colidx, proj, spat, soft, att_own, att_send = run(
-        functools.partial(attention_kernel, heads=heads, block=128),
-        [
-            n11,
-            n10,
+        functools.partial(attention_kernel, heads=heads),
+        [
+            x10,
+            x11,
+            s10,
+            s11,
+            i10,
             x0,
             sp0,
             index0,
@@ -1127,7 +1177,7 @@
             pltpu.VMEM((3, length, inner), BF16),
             pltpu.VMEM((2, length, inner), BF16),
             pltpu.VMEM((heads, length, length), F32),
-            pltpu.SemaphoreType.DMA((2 + length // 128,)),
+            pltpu.SemaphoreType.DMA((2 + heads,)),
         ],
     )
     att_recv = swap(att_send, "zh")
@@ -1148,9 +1198,7 @@
     )
     mixed1 = swap(mixed0, "core")
     mixed_far0 = swap(mixed0, "zh")
-    mixed1, cot_far, cot_near, *downs = join(mixed1, cot_far, cot_near, *downs)
-    cot10 = swap(cot_far, "y")
-    cot01 = swap(cot_near, "core")
+    mixed1, *downs = join(mixed1, *downs)
 
     gains = (ln_gains, "stream")
     shifts = (ln_shifts, "stream")
@@ -1169,7 +1217,9 @@
         ],
     )
     low_recv = swap(low, "zl")
-    mixed_far0, cot10, low = join(mixed_far0, cot10, low)
+    cot_far, cot_near, low = join(cot_far, cot_near, low)
+    cot10 = swap(cot_far, "y")
+    cot01 = swap(cot_near, "core")
     mixed_far1 = swap(mixed_far0, "core")
     cot11 = swap(cot10, "core")
     (normed_far,) = run(
@@ -1184,7 +1234,7 @@
         [((half, hidden), BF16), ((half, hidden), BF16)],
     )
     low0, low1 = run(
-        lowered_kernel, [low, low_recv], [rows_of(rows), rows_of(rows)], after=[slope_far, cot11]
+        lowered_kernel, [low, low_recv], [rows_of(rows), rows_of(rows)], after=[slope_far]
     )
     far_low0 = swap(low0, "zh")
 
@@ -1314,12 +1364,18 @@
     up_other = swap(up_half, "y")
     down_other = swap(down_half, "batch")
     pay_zl = swap(join(pay_recv, far)[0], "zl")
-    one_keep, one_send, lines = run(
+    few = inner // 2
+    main = 3 * inner - few
+    sp_keep, sp_send = run(
+        spatial_grad_kernel, [sp, dspat], [rows_of(inner), rows_of(inner)], after=[up_half]
+    )
+    sp_recv = swap(sp_send, "core")
+    one_keep, one_send, value_rest, lines = run(
         functools.partial(first_grad_kernel, heads=heads),
         [x, dscore, dproj, colidx, bias_grad],
-        [rows_of(3 * inner // 2), rows_of(3 * inner // 2), rows_of(16, F32)],
+        [rows_of(main // 2), rows_of(main // 2), rows_of(few), rows_of(16, F32)],
         scratch=[pltpu.VMEM((3 * inner, width), BF16)],
-        after=[up_half],
+        after=[sp_keep],
     )
     keep, send = run(
         fold_kernel,
@@ -1343,10 +1399,23 @@
     pay_recv, pay_zl, far_send, mine = join(pay_recv, pay_zl, far_send, mine)
     pay_core, pay_zlcore = swap(pay_recv, "core"), swap(pay_zl, "core")
     far_core = swap(far_send, "core")
-    base = 3 * inner + 32
+    base = few + 2 * inner + 32
     two_keep, two_send = run(
         second_grad_kernel,
-        [dmix, pay, pay_recv, pay_zl, pay_core, pay_zlcore, att_own, att_send, sp, dspat, lines],
+        [
+            dmix,
+            pay,
+            pay_recv,
+            pay_zl,
+            pay_core,
+            pay_zlcore,
+            att_own,
+            att_send,
+            value_rest,
+            sp_keep,
+            sp_recv,
+            lines,
+        ],
         [rows_of(base // 2), rows_of(base // 2)],
         scratch=[pltpu.VMEM((base, width), BF16)],
         after=[mine, up_far, down_far],
@@ -1373,13 +1442,14 @@
         ],
         after=[one_half],
     )
+    pages_zz = swap(pages_zh, "zl")
     one_half, two_half = plus(
-        [(one_half, one_other), (two_half, two_other)], after=[spread_event], over_batch=True
+        [(one_half, one_other), (two_half, two_other)],
+        after=[spread_event, pages_zz],
+        over_batch=True,
     )
     one_far = swap(one_half, "batch")
     two_far = swap(two_half, "y")
-    pages_zh, one_half = join(pages_zh, one_half)
-    pages_zz = swap(pages_zh, "zl")
     grad_tokens, grad_spatial, ends_event = run(
         ends_kernel,
         [mine, got, pages_zh, pages_zl, pages_zz],
@@ -1410,15 +1480,15 @@
         halves[:2] + others[:2] + halves[2:] + others[2:],
         [
             ((2, 3 * inner, width), F32),
-            rows_of(2 * inner, F32),
             ((2, inner, width), F32),
-            ((2, 3, heads, NBUCK), F32),
+            ((2, inner, width), F32),
+            ((3, heads, 2, NBUCK), F32),
             ((2, 2, part), F32),
             ((2, 2, part), F32),
             ((2, hidden), F32),
             ((2, part), F32),
         ],
-        scratch=[pltpu.VMEM((3 * inner, width), F32), pltpu.VMEM((base, width), F32)],
+        scratch=[pltpu.VMEM((base, width), F32)],
         after=[spread_event, out_event, ends_event],
     )
     return (
@@ -1427,7 +1497,7 @@
         grad_spatial.reshape(spatial.shape),
         grad_qkv.reshape(2, 3, inner, width).swapaxes(2, 3),
         grad_spatial_w.reshape(2, inner, width).swapaxes(1, 2),
-        tables,
+        tables.transpose(2, 0, 1, 3),
         grad_exit,
         gains_grad,
         shifts_grad,

time: 231 us -> 225 us (0.974)
  waiting for transfers between devices: 106 us -> 98.7 us
    ppermute x60 -> x64, waiting for transfers between devices: 104 us -> 98.3 us  [swap(): return lax.ppermute(value, axis, [(i, i ^ step) for i in range(size)])]
    ppermute x60 -> x64, starting transfers between devices: 47.9 us -> 45 us  [swap(): return lax.ppermute(value, axis, [(i, i ^ step) for i in range(size)])]
    ppermute x2, waiting for transfers between devices: 2.83 us -> 0.46 us  [swap_both(): lax.ppermute(value, ('batch', 'y'), [(i, i ^ 3) for i in range(size)])]
    pallas_call x30 -> x33, Pallas kernels: 66.4 us -> 68.3 us  [kernel_call(): pl.pallas_call(kernel, out_shape=[jax.ShapeDtypeStruct(out[0], out[1]) fo...]
    unnamed x38 -> x39, local copies, waits for them, and re-layouts: 5.74 us -> 6.06 us
  transfers between devices with their start and end apart: 62 -> 66, of which waited for: 35 -> 36; matrix products, arithmetic and copies ran while one was open for 0% -> 0% of each run, Pallas kernels for 24% -> 25%
where the time goes in v5:
time: 225 us; the launch traced here: 224 us
  waiting for transfers between devices  98.7 us (44%)
  Pallas kernels  68.3 us (30%)
  starting transfers between devices  49 us (22%)
  local copies, waits for them, and re-layouts  7.14 us (3%)
    ppermute x64, waiting for transfers between devices, swap(): return lax.ppermute(value, axis, [(i, i ^ step) for i in range(size)])  98.3 us
    pallas_call x33, Pallas kernels, kernel_call(): pl.pallas_call(kernel, out_shape=[jax.ShapeDtypeStruct(out[0], out[1]) fo...  68.3 us
    ppermute x64, starting transfers between devices, swap(): return lax.ppermute(value, axis, [(i, i ^ step) for i in range(size)])  45 us
    unnamed x39, local copies, waits for them, and re-layouts  6.06 us
  transfers between devices with their start and end apart: 66, of which 36 were waited for; matrix products, arithmetic and copies ran while one was open for 0% of the time, Pallas kernels for 25%

profile of v5, /device:TPU:0, one launch (start us, length us, event | category | flops | bytes accessed | tf_op | source)
XLA Modules:
  0.0 224.5 jit_solution(6220832909976731916)
XLA Ops:
  1.3 2.6 %shard_map.246 = (bf16[256,768]{1,0:T(8,128)(2,1)}, bf16[192,768]{1,0:T(8,128)(2,1)}) custom-call(s32[5]{0:T(128)} %stack.38.s_ref, bf16[2,192,768]{2,1,0:T(8,128)(2,1)} %refs_7_.1, bf16[2,768,768]{2,1,0:T(8,128)(2,1)} %refs_5_.1, bf16[2,768,768]{2,1,0:T(8,128)(2,1)} %refs_6_.3, f32[2,768]{1,0:T(2,128)} %refs_2_.5), custom_call_target="tpu_custom_call" | custom-call | flops 110000000 | bytes 350000 | tf_op jit(solution)/shard_map/pallas_call | solution.py:49
  4.0 3.5 %shard_map.247 = (bf16[144,768]{1,0:T(8,128)(2,1)}, bf16[128,768]{1,0:T(8,128)(2,1)}, bf16[128,768]{1,0:T(8,128)(2,1)}, bf16[272,768]{1,0:T(8,128)(2,1)}, bf16[128,768]{1,0:T(8,128)(2,1)}) custom-call(s32[5]{0:T(128)} %stack.38.s_ref, bf16[2,2,4,32,768]{4,3,2,1,0:T(8,128)(2,1)} %bitcast.60, bf16[2,4,32,768]{3,2,1,0:T(8,128)(2,1)} %bitcast.63, ...), custom_call_target="tpu_custom_call" | custom-call | flops 32999999488 | bytes 105000000 | tf_op jit(solution)/shard_map/pallas_call | solution.py:49
  8.1 3.7 %collective-permute-start.4 = (bf16[256,768]{1,0:T(8,128)(2,1)}, bf16[256,768]{1,0:T(8,128)(2,1)S(1)}, u32[]{:S(2)}, u32[]{:S(2)}) collective-permute-start(bf16[256,768]{1,0:T(8,128)(2,1)} %get-tuple-element.171), channel_id=1, source_target_pairs={{0,2},{2,0},{1,3},{3,1},{4,6},{6,4},{5,7},{7,5},{8,10},{10,8},{9,1... | collective-permute-start | bytes 1179656 | tf_op jit(solution)/shard_map/ppermute | solution.py:1008
  11.7 1.5 collective-permute-start
  13.8 1.5 collective-permute-start.2
  15.3 2.8 %shard_map.248 = (bf16[2,128,768]{2,1,0:T(8,128)(2,1)}, bf16[128,768]{1,0:T(8,128)(2,1)}, bf16[128,768]{1,0:T(8,128)(2,1)}) custom-call(s32[5]{0:T(128)} %stack.38.s_ref, bf16[2,2,4,32,768]{4,3,2,1,0:T(8,128)(2,1)} %bitcast.54, bf16[128,768]{1,0:T(8,128)(2,1)} %get-tuple-element.167.refs_1_.refs_0_), custom_call_target="tpu_custom_call" | custom-call | flops 110000000 | bytes 350000 | tf_op jit(solution)/shard_map/pallas_call | solution.py:49
  18.2 1.7 copy-done.1
  24.2 2.5 %shard_map.249 = (bf16[2,128,768]{2,1,0:T(8,128)(2,1)S(1)}, bf16[2,128,768]{2,1,0:T(8,128)(2,1)S(1)}, s32[8,256]{1,0:T(8,128)S(1)}, bf16[3,256,192]{2,1,0:T(8,12...) custom-call(s32[5]{0:T(128)S(1)} %copy-done.9, ...), custom_call_target="tpu_custom_call" | custom-call | flops 110000000 | bytes 350000 | tf_op jit(solution)/shard_map/pallas_call | solution.py:49
  28.0 2.1 collective-permute-done.4.refs_3_.refs_8_
  30.6 2.5 %collective-permute-start.10 = (bf16[256,768]{1,0:T(8,128)(2,1)S(1)}, bf16[256,768]{1,0:T(8,128)(2,1)S(1)}, u32[]{:S(2)}, u32[]{:S(2)}) collective-permute-start(bf16[256,768]{1,0:T(8,128)(2,1)S(1)} %collective-permute-done.4.refs_3_.refs_8_), channel_id=1, source_target_pairs={{0,24},{8,16},{16,8},{24,0},{1,25},{9,17},{17,9},{25,1},{2,26},{10... | collective-permute-start | bytes 1179656 | tf_op jit(solution)/shard_map/ppermute | solution.py:1013
  34.1 7.9 %shard_map.250 = (bf16[2,2,128,768]{3,2,1,0:T(8,128)(2,1)S(1)}, bf16[2,2,128,768]{3,2,1,0:T(8,128)(2,1)S(1)}, s32[512,8]{1,0:T(8,128)S(1)}, bf16[3,512,192]{2,1,...) custom-call(s32[5]{0:T(128)S(1)} %copy-done.9, ...), custom_call_target="tpu_custom_call" | custom-call | flops 32999999488 | bytes 105000000 | tf_op jit(solution)/shard_map/pallas_call | solution.py:49
  42.1 3.0 %collective-permute-start.11 = (bf16[256,192]{1,0:T(8,128)(2,1)S(1)}, bf16[256,192]{1,0:T(8,128)(2,1)S(1)}, u32[]{:S(2)}, u32[]{:S(2)}) collective-permute-start(bf16[256,192]{1,0:T(8,128)(2,1)S(1)} %get-tuple-element.185.refs_7_), channel_id=1, source_target_pairs={{0,2},{2,0},{1,3},{3,1},{4,6},{6,4},{5,7},{7,5},{8,10},{10,8},{9,1... | collective-permute-start | bytes 294920 | tf_op jit(solution)/shard_map/ppermute | solution.py:1008
  45.0 8.4 %collective-permute-done.7.refs_12_ = bf16[192,768]{1,0:T(8,128)(2,1)S(1)} collective-permute-done((bf16[192,768]{1,0:T(8,128)(2,1)S(1)}, bf16[192,768]{1,0:T(8,128)(2,1)S(1)}, u32[]{:S(2)}, u32[]{:S(2)}) %collective-permute-start.7) | collective-permute-done | bytes 294944 | tf_op jit(solution)/shard_map/ppermute | solution.py:1008
  53.4 1.6 collective-permute-start.14
  55.0 1.5 collective-permute-start.13
  64.2 3.8 %collective-permute-done.15.refs_1_ = bf16[128,768]{1,0:T(8,128)(2,1)S(1)} collective-permute-done((bf16[128,768]{1,0:T(8,128)(2,1)S(1)}, bf16[128,768]{1,0:T(8,128)(2,1)S(1)}, u32[]{:S(2)}, u32[]{:S(2)}) %collective-permute-start.15) | collective-permute-done | bytes 196640 | tf_op jit(solution)/shard_map/ppermute | solution.py:1008
  68.7 1.8 collective-permute-start.19
  71.0 2.8 %shard_map.254 = (bf16[256,768]{1,0:T(8,128)(2,1)S(1)}, bf16[256,768]{1,0:T(8,128)(2,1)S(1)}, bf16[2,256,768]{2,1,0:T(8,128)(2,1)S(1)}, bf16[2,256,768]{2,1,0:T(...) custom-call(s32[5]{0:T(128)S(1)} %copy-done.9, ...), custom_call_target="tpu_custom_call" | custom-call | flops 110000000 | bytes 350000 | tf_op jit(solution)/shard_map/pallas_call | solution.py:49
  73.8 1.7 collective-permute-start.21
  76.8 4.4 %collective-permute-done.19.refs_1_ = bf16[128,768]{1,0:T(8,128)(2,1)S(1)} collective-permute-done((bf16[128,768]{1,0:T(8,128)(2,1)S(1)}, bf16[128,768]{1,0:T(8,128)(2,1)S(1)}, u32[]{:S(2)}, u32[]{:S(2)}) %collective-permute-start.19) | collective-permute-done | bytes 196640 | tf_op jit(solution)/shard_map/ppermute | solution.py:1008
  84.9 4.6 %collective-permute-done.18.refs_1_ = bf16[256,768]{1,0:T(8,128)(2,1)S(1)} collective-permute-done((bf16[256,768]{1,0:T(8,128)(2,1)S(1)}, bf16[256,768]{1,0:T(8,128)(2,1)S(1)}, u32[]{:S(2)}, u32[]{:S(2)}) %collective-permute-start.18) | collective-permute-done | bytes 393248 | tf_op jit(solution)/shard_map/ppermute | solution.py:1008
  91.1 1.6 shard_map.258
  92.7 2.3 %shard_map.259 = (bf16[256,768]{1,0:T(8,128)(2,1)S(1)}, bf16[256,768]{1,0:T(8,128)(2,1)S(1)}) custom-call(s32[5]{0:T(128)S(1)} %copy-done.9, bf16[256,768]{1,0:T(8,128)(2,1)S(1)} %get-tuple-element.212.refs_0_.refs_4_, bf16[768,768]{1,0:T(8,128)(2,1)S(1)} %get-tuple-element.197.refs_5_.refs_1_, ...), custom_call_target="tpu_custom_call" | custom-call | flops 110000000 | bytes 350000 | tf_op jit(solution)/shard_map/pallas_call | solution.py:49
  95.0 2.5 %collective-permute-start.25 = (bf16[256,768]{1,0:T(8,128)(2,1)S(1)}, bf16[256,768]{1,0:T(8,128)(2,1)S(1)}, u32[]{:S(2)}, u32[]{:S(2)}) collective-permute-start(bf16[256,768]{1,0:T(8,128)(2,1)S(1)} %get-tuple-element.216.refs_4_), channel_id=1, source_target_pairs={{0,1},{1,0},{2,3},{3,2},{4,5},{5,4},{6,7},{7,6},{8,9},{9,8},{10,11... | collective-permute-start | bytes 1179656 | tf_op jit(solution)/shard_map/ppermute | solution.py:1008
  98.6 3.7 %collective-permute-done.26.refs_3_ = bf16[128,768]{1,0:T(8,128)(2,1)S(1)} collective-permute-done((bf16[128,768]{1,0:T(8,128)(2,1)S(1)}, bf16[128,768]{1,0:T(8,128)(2,1)S(1)}, u32[]{:S(2)}, u32[]{:S(2)}) %collective-permute-start.26) | collective-permute-done | bytes 196640 | tf_op jit(solution)/shard_map/ppermute | solution.py:1008
  102.3 8.3 %collective-permute-done.25.refs_5_ = bf16[256,768]{1,0:T(8,128)(2,1)S(1)} collective-permute-done((bf16[256,768]{1,0:T(8,128)(2,1)S(1)}, bf16[256,768]{1,0:T(8,128)(2,1)S(1)}, u32[]{:S(2)}, u32[]{:S(2)}) %collective-permute-start.25) | collective-permute-done | bytes 393248 | tf_op jit(solution)/shard_map/ppermute | solution.py:1008
  112.0 1.6 collective-permute-done.29.refs_1_
  115.2 5.0 %collective-permute-done.28.refs_4_ = bf16[128,768]{1,0:T(8,128)(2,1)S(1)} collective-permute-done((bf16[128,768]{1,0:T(8,128)(2,1)S(1)}, bf16[128,768]{1,0:T(8,128)(2,1)S(1)}, u32[]{:S(2)}, u32[]{:S(2)}) %collective-permute-start.28) | collective-permute-done | bytes 196640 | tf_op jit(solution)/shard_map/ppermute | solution.py:1008
  120.2 2.4 %shard_map.262 = (bf16[2,64,768]{2,1,0:T(8,128)(2,1)S(1)}, bf16[2,64,768]{2,1,0:T(8,128)(2,1)S(1)}, f32[256,768]{1,0:T(8,128)}, bf16[256,768]{1,0:T(8,128)(2,1)S(1)}, f32[8,768]{1,0:T(8,128)}) custom-call(s32[5]{0:T(128)S(1)} %copy-done.9, bf16[2,2,128,768]{3,2,1,0:T(8,128)(2,1)S(1)} %get-tuple-element.180.refs_0_, ...), custom_call_target="tpu_custom_call" | custom-call | flops 110000000 | bytes 350000 | tf_op jit(solution)/shard_map/pallas_call | solution.py:49
  122.6 2.6 %shard_map.263 = (bf16[384,768]{1,0:T(8,128)(2,1)S(1)}, bf16[384,768]{1,0:T(8,128)(2,1)S(1)}, bf16[384,768]{1,0:T(8,128)(2,1)S(1)}, bf16[384,768]{1,0:T(8,128)(2,1)S(1)}, f32[8,768]{1,0:T(8,128)S(1)}) custom-call(s32[5]{0:T(128)S(1)} %copy-done.9, bf16[256,768]{1,0:T(8,128)(2,1)S(1)} %get-tuple-element.234.refs_0_, ...), custom_call_target="tpu_custom_call" | custom-call | flops 32999999488 | bytes 105000000 | tf_op jit(solution)/shard_map/pallas_call | solution.py:49
  126.0 5.3 %shard_map.264 = (bf16[3,512,512]{2,1,0:T(8,128)(2,1)S(1)}, bf16[3,512,192]{2,1,0:T(8,128)(2,1)S(1)}, bf16[2,512,192]{2,1,0:T(8,128)(2,1)S(1)}, bf16[128,768]{1,...) custom-call(s32[5]{0:T(128)S(1)} %copy-done.9, ...), custom_call_target="tpu_custom_call" | custom-call | flops 32999999488 | bytes 105000000 | tf_op jit(solution)/shard_map/pallas_call | solution.py:49
  131.4 2.1 collective-permute-done.31.refs_2_
  137.0 3.2 %collective-permute-done.36.refs_1_ = bf16[384,768]{1,0:T(8,128)(2,1)S(1)} collective-permute-done((bf16[384,768]{1,0:T(8,128)(2,1)S(1)}, bf16[384,768]{1,0:T(8,128)(2,1)S(1)}, u32[]{:S(2)}, u32[]{:S(2)}) %collective-permute-start.36) | collective-permute-done | bytes 589856 | tf_op jit(solution)/shard_map/ppermute | solution.py:1008
  144.1 5.8 %shard_map.268 = (bf16[240,768]{1,0:T(8,128)(2,1)S(1)}, bf16[240,768]{1,0:T(8,128)(2,1)S(1)}, bf16[96,768]{1,0:T(8,128)(2,1)S(1)}, f32[16,768]{1,0:T(8,128)S(1)}) custom-call(s32[5]{0:T(128)S(1)} %copy-done.9, bf16[2,2,128,768]{3,2,1,0:T(8,128)(2,1)S(1)} %get-tuple-element.180.refs_0_, bf16[3,512,512]{2,1,0:T(8,128)(2,1)S(1)} %get-tuple-element.255.refs_1_, ...), custom_call_target="tpu_custom_call" | custom-call | flops 110000000 | bytes 350000 | tf_op jit(solution)/shard_map/pallas_call | solution.py:49
  150.0 1.9 collective-permute-done.35.refs_1_
  153.4 1.6 collective-permute-done.40.refs_3_
  159.0 9.1 %collective-permute-done.38.refs_1_ = bf16[3,64,768]{2,1,0:T(8,128)(2,1)S(1)} collective-permute-done((bf16[3,64,768]{2,1,0:T(8,128)(2,1)S(1)}, bf16[3,64,768]{2,1,0:T(8,128)(2,1)S(1)}, u32[]{:S(2)}, u32[]{:S(2)}) %collective-permute-start.38) | collective-permute-done | bytes 294944 | tf_op jit(solution)/shard_map/ppermute | solution.py:1008
  174.0 3.8 %collective-permute-done.48.refs_1_ = bf16[3,32,768]{2,1,0:T(8,128)(2,1)S(1)} collective-permute-done((bf16[3,32,768]{2,1,0:T(8,128)(2,1)S(1)}, bf16[3,32,768]{2,1,0:T(8,128)(2,1)S(1)}, u32[]{:S(2)}, u32[]{:S(2)}) %collective-permute-start.48) | collective-permute-done | bytes 147488 | tf_op jit(solution)/shard_map/ppermute | solution.py:1008
  182.2 6.6 %collective-permute-done.49.refs_1_ = bf16[240,768]{1,0:T(8,128)(2,1)S(1)} collective-permute-done((bf16[240,768]{1,0:T(8,128)(2,1)S(1)}, bf16[240,768]{1,0:T(8,128)(2,1)S(1)}, u32[]{:S(2)}, u32[]{:S(2)}) %collective-permute-start.49) | collective-permute-done | bytes 368672 | tf_op jit(solution)/shard_map/ppermute | solution.py:1008
  192.6 5.1 %collective-permute-done.57.refs_2_ = bf16[2,3,32,768]{3,2,1,0:T(8,128)(2,1)S(1)} collective-permute-done((bf16[2,3,32,768]{3,2,1,0:T(8,128)(2,1)S(1)}, bf16[2,3,32,768]{3,2,1,0:T(8,128)(2,1)S(1)}, u32[]{:S(2)}, u32[]{:S(2)}) %collective-permute-start.57) | collective-permute-done | bytes 294944 | tf_op jit(solution)/shard_map/ppermute | solution.py:1008
  198.6 2.0 collective-permute-start.59
  200.7 4.8 %shard_map.274 = (f32[2,2,384,768]{3,2,1,0:T(8,128)}, f32[2,2,384,768]{3,2,1,0:T(8,128)}, f32[8,128]{1,0:T(8,128)S(1)}) custom-call(s32[5]{0:T(128)S(1)} %copy-done.9, bf16[384,768]{1,0:T(8,128)(2,1)S(1)} %get-tuple-element.270.refs_2_.refs_0_, bf16[384,768]{1,0:T(8,128)(2,1)S(1)} %collective-permute-done.46.refs_13_.refs_1_, ...), custom_call_target="tpu_custom_call" | custom-call | flops 110000000 | bytes 350000 | tf_op jit(solution)/shard_map/pallas_call | solution.py:49
  205.5 2.1 collective-permute-done.58.refs_5_.refs_4_
  211.3 1.6 collective-permute-done.59.refs_3_
  213.0 2.1 shard_map.277
  215.1 2.1 collective-permute-done.60.refs_1_
  218.5 1.7 collective-permute-done.62.refs_2_
  220.7 3.7 %shard_map.278 = (f32[2,576,768]{2,1,0:T(8,128)}, f32[2,192,768]{2,1,0:T(8,128)}, f32[2,192,768]{2,1,0:T(8,128)}, f32[3,3,2,128]{3,2,1,0:T(2,128)}, f32[2,2,192]...) custom-call(s32[5]{0:T(128)S(1)} %copy-done.9, ...), custom_call_target="tpu_custom_call" | custom-call | flops 110000000 | bytes 350000 | tf_op jit(solution)/shard_map/pallas_call | solution.py:49
  (170 shorter events, 62.5 us)
Async XLA Ops:
  7.6 10.6 %collective-permute-start.3 = (bf16[272,768]{1,0:T(8,128)(2,1)}, bf16[272,768]{1,0:T(8,128)(2,1)}, u32[]{:S(2)}, u32[]{:S(2)}) collective-permute-start(bf16[272,768]{1,0:T(8,128)(2,1)} %get-tuple-element.168.refs_2_), channel_id=1, source_target_pairs={{0,4},{4,0},{1,5},{5,1},{2,6},{6,2},{3,7},{7,3},{8,12},{12,8},{9,1... | collective-permute-start | bytes 1253384 | tf_op jit(solution)/shard_map/ppermute | solution.py:1008
  8.1 22.0 %collective-permute-start.4 = (bf16[256,768]{1,0:T(8,128)(2,1)}, bf16[256,768]{1,0:T(8,128)(2,1)S(1)}, u32[]{:S(2)}, u32[]{:S(2)}) collective-permute-start(bf16[256,768]{1,0:T(8,128)(2,1)} %get-tuple-element.171), channel_id=1, source_target_pairs={{0,2},{2,0},{1,3},{3,1},{4,6},{6,4},{5,7},{7,5},{8,10},{10,8},{9,1... | collective-permute-start | bytes 1179656 | tf_op jit(solution)/shard_map/ppermute | solution.py:1008
  11.7 16.2 %collective-permute-start = (bf16[144,768]{1,0:T(8,128)(2,1)}, bf16[144,768]{1,0:T(8,128)(2,1)}, u32[]{:S(2)}, u32[]{:S(2)}) collective-permute-start(bf16[144,768]{1,0:T(8,128)(2,1)} %get-tuple-element.164), channel_id=1, source_target_pairs={{0,8},{8,0},{1,9},{9,1},{2,10},{10,2},{3,11},{11,3},{4,12},{12,4},... | collective-permute-start | bytes 663560 | tf_op jit(solution)/shard_map/ppermute | solution.py:1008
  13.3 13.4 %collective-permute-start.1 = (bf16[128,768]{1,0:T(8,128)(2,1)}, bf16[128,768]{1,0:T(8,128)(2,1)}, u32[]{:S(2)}, u32[]{:S(2)}) collective-permute-start(bf16[128,768]{1,0:T(8,128)(2,1)} %get-tuple-element.165), channel_id=1, source_target_pairs={{0,8},{8,0},{1,9},{9,1},{2,10},{10,2},{3,11},{11,3},{4,12},{12,4},... | collective-permute-start | bytes 589832 | tf_op jit(solution)/shard_map/ppermute | solution.py:1008
  13.8 14.2 %collective-permute-start.2 = (bf16[128,768]{1,0:T(8,128)(2,1)}, bf16[128,768]{1,0:T(8,128)(2,1)}, u32[]{:S(2)}, u32[]{:S(2)}) collective-permute-start(bf16[128,768]{1,0:T(8,128)(2,1)} %get-tuple-element.166), channel_id=1, source_target_pairs={{0,8},{8,0},{1,9},{9,1},{2,10},{10,2},{3,11},{11,3},{4,12},{12,4},... | collective-permute-start | bytes 589832 | tf_op jit(solution)/shard_map/ppermute | solution.py:1008
  30.6 22.8 %collective-permute-start.10 = (bf16[256,768]{1,0:T(8,128)(2,1)S(1)}, bf16[256,768]{1,0:T(8,128)(2,1)S(1)}, u32[]{:S(2)}, u32[]{:S(2)}) collective-permute-start(bf16[256,768]{1,0:T(8,128)(2,1)S(1)} %collective-permute-done.4.refs_3_.refs_8_), channel_id=1, source_target_pairs={{0,24},{8,16},{16,8},{24,0},{1,25},{9,17},{17,9},{25,1},{2,26},{10... | collective-permute-start | bytes 1179656 | tf_op jit(solution)/shard_map/ppermute | solution.py:1013
  33.1 20.3 %collective-permute-start.9 = (bf16[256,768]{1,0:T(8,128)(2,1)S(1)}, bf16[256,768]{1,0:T(8,128)(2,1)S(1)}, u32[]{:S(2)}, u32[]{:S(2)}) collective-permute-start(bf16[256,768]{1,0:T(8,128)(2,1)S(1)} %collective-permute-done.4.refs_3_.refs_8_), channel_id=1, source_target_pairs={{0,16},{16,0},{1,17},{17,1},{2,18},{18,2},{3,19},{19,3},{4,20},{20... | collective-permute-start | bytes 1179656 | tf_op jit(solution)/shard_map/ppermute | solution.py:1008
  33.7 19.7 %collective-permute-start.8 = (bf16[256,768]{1,0:T(8,128)(2,1)S(1)}, bf16[256,768]{1,0:T(8,128)(2,1)S(1)}, u32[]{:S(2)}, u32[]{:S(2)}) collective-permute-start(bf16[256,768]{1,0:T(8,128)(2,1)S(1)} %collective-permute-done.4.refs_3_.refs_8_), channel_id=1, source_target_pairs={{0,8},{8,0},{1,9},{9,1},{2,10},{10,2},{3,11},{11,3},{4,12},{12,4},... | collective-permute-start | bytes 1179656 | tf_op jit(solution)/shard_map/ppermute | solution.py:1008
  34.1 19.3 %collective-permute-start.7 = (bf16[192,768]{1,0:T(8,128)(2,1)S(1)}, bf16[192,768]{1,0:T(8,128)(2,1)S(1)}, u32[]{:S(2)}, u32[]{:S(2)}) collective-permute-start(bf16[192,768]{1,0:T(8,128)(2,1)S(1)} %copy-done.17), channel_id=1, source_target_pairs={{0,2},{2,0},{1,3},{3,1},{4,6},{6,4},{5,7},{7,5},{8,10},{10,8},{9,1... | collective-permute-start | bytes 884744 | tf_op jit(solution)/shard_map/ppermute | solution.py:1008
  42.1 14.4 %collective-permute-start.11 = (bf16[256,192]{1,0:T(8,128)(2,1)S(1)}, bf16[256,192]{1,0:T(8,128)(2,1)S(1)}, u32[]{:S(2)}, u32[]{:S(2)}) collective-permute-start(bf16[256,192]{1,0:T(8,128)(2,1)S(1)} %get-tuple-element.185.refs_7_), channel_id=1, source_target_pairs={{0,2},{2,0},{1,3},{3,1},{4,6},{6,4},{5,7},{7,5},{8,10},{10,8},{9,1... | collective-permute-start | bytes 294920 | tf_op jit(solution)/shard_map/ppermute | solution.py:1008
  53.4 6.8 %collective-permute-start.14 = (bf16[192,768]{1,0:T(8,128)(2,1)S(1)}, bf16[192,768]{1,0:T(8,128)(2,1)S(1)}, u32[]{:S(2)}, u32[]{:S(2)}) collective-permute-start(bf16[192,768]{1,0:T(8,128)(2,1)S(1)} %collective-permute-done.7.refs_12_), channel_id=1, source_target_pairs={{0,16},{16,0},{1,17},{17,1},{2,18},{18,2},{3,19},{19,3},{4,20},{20... | collective-permute-start | bytes 884744 | tf_op jit(solution)/shard_map/ppermute | solution.py:1008
  55.0 6.7 %collective-permute-start.13 = (bf16[192,768]{1,0:T(8,128)(2,1)S(1)}, bf16[192,768]{1,0:T(8,128)(2,1)S(1)}, u32[]{:S(2)}, u32[]{:S(2)}) collective-permute-start(bf16[192,768]{1,0:T(8,128)(2,1)S(1)} %collective-permute-done.7.refs_12_), channel_id=1, source_target_pairs={{0,8},{8,0},{1,9},{9,1},{2,10},{10,2},{3,11},{11,3},{4,12},{12,4},... | collective-permute-start | bytes 884744 | tf_op jit(solution)/shard_map/ppermute | solution.py:1008
  62.7 8.3 %collective-permute-start.17 = (bf16[192,768]{1,0:T(8,128)(2,1)S(1)}, bf16[192,768]{1,0:T(8,128)(2,1)S(1)}, u32[]{:S(2)}, u32[]{:S(2)}) collective-permute-start(bf16[192,768]{1,0:T(8,128)(2,1)S(1)} %collective-permute-done.7.refs_12_), channel_id=1, source_target_pairs={{0,24},{8,16},{16,8},{24,0},{1,25},{9,17},{17,9},{25,1},{2,26},{10... | collective-permute-start | bytes 884744 | tf_op jit(solution)/shard_map/ppermute | solution.py:1013
  68.7 12.5 %collective-permute-start.19 = (bf16[128,768]{1,0:T(8,128)(2,1)S(1)}, bf16[128,768]{1,0:T(8,128)(2,1)S(1)}, u32[]{:S(2)}, u32[]{:S(2)}) collective-permute-start(bf16[128,768]{1,0:T(8,128)(2,1)S(1)} %shard_map.253.refs_1_), channel_id=1, source_target_pairs={{0,2},{2,0},{1,3},{3,1},{4,6},{6,4},{5,7},{7,5},{8,10},{10,8},{9,1... | collective-permute-start | bytes 589832 | tf_op jit(solution)/shard_map/ppermute | solution.py:1008
  73.8 10.9 %collective-permute-start.21 = (bf16[2,128,768]{2,1,0:T(8,128)(2,1)S(1)}, bf16[2,128,768]{2,1,0:T(8,128)(2,1)S(1)}, u32[]{:S(2)}, u32[]{:S(2)}) collective-permute-start(bf16[2,128,768]{2,1,0:T(8,128)(2,1)S(1)} %copy-done.16), channel_id=1, source_target_pairs={{0,8},{8,0},{1,9},{9,1},{2,10},{10,2},{3,11},{11,3},{4,12},{12,4},... | collective-permute-start | bytes 1179656 | tf_op jit(solution)/shard_map/ppermute | solution.py:1008
  75.5 14.0 %collective-permute-start.18 = (bf16[256,768]{1,0:T(8,128)(2,1)S(1)}, bf16[256,768]{1,0:T(8,128)(2,1)S(1)}, u32[]{:S(2)}, u32[]{:S(2)}) collective-permute-start(bf16[256,768]{1,0:T(8,128)(2,1)S(1)} %get-tuple-element.204.refs_5_.refs_0_), channel_id=1, source_target_pairs={{0,1},{1,0},{2,3},{3,2},{4,5},{5,4},{6,7},{7,6},{8,9},{9,8},{10,11... | collective-permute-start | bytes 1179656 | tf_op jit(solution)/shard_map/ppermute | solution.py:1008
  76.8 8.1 %collective-permute-start.22 = (bf16[128,768]{1,0:T(8,128)(2,1)S(1)}, bf16[128,768]{1,0:T(8,128)(2,1)S(1)}, u32[]{:S(2)}, u32[]{:S(2)}) collective-permute-start(bf16[128,768]{1,0:T(8,128)(2,1)S(1)} %copy-done.18), channel_id=1, source_target_pairs={{0,4},{4,0},{1,5},{5,1},{2,6},{6,2},{3,7},{7,3},{8,12},{12,8},{9,1... | collective-permute-start | bytes 589832 | tf_op jit(solution)/shard_map/ppermute | solution.py:1008
  90.2 12.1 %collective-permute-start.26 = (bf16[128,768]{1,0:T(8,128)(2,1)S(1)}, bf16[128,768]{1,0:T(8,128)(2,1)S(1)}, u32[]{:S(2)}, u32[]{:S(2)}) collective-permute-start(bf16[128,768]{1,0:T(8,128)(2,1)S(1)} %get-tuple-element.206.refs_3_), channel_id=1, source_target_pairs={{0,2},{2,0},{1,3},{3,1},{4,6},{6,4},{5,7},{7,5},{8,10},{10,8},{9,1... | collective-permute-start | bytes 589832 | tf_op jit(solution)/shard_map/ppermute | solution.py:1008
  95.0 15.6 %collective-permute-start.25 = (bf16[256,768]{1,0:T(8,128)(2,1)S(1)}, bf16[256,768]{1,0:T(8,128)(2,1)S(1)}, u32[]{:S(2)}, u32[]{:S(2)}) collective-permute-start(bf16[256,768]{1,0:T(8,128)(2,1)S(1)} %get-tuple-element.216.refs_4_), channel_id=1, source_target_pairs={{0,1},{1,0},{2,3},{3,2},{4,5},{5,4},{6,7},{7,6},{8,9},{9,8},{10,11... | collective-permute-start | bytes 1179656 | tf_op jit(solution)/shard_map/ppermute | solution.py:1008
  97.6 13.0 %collective-permute-start.27 = (bf16[2,64,768]{2,1,0:T(8,128)(2,1)S(1)}, bf16[2,64,768]{2,1,0:T(8,128)(2,1)S(1)}, u32[]{:S(2)}, u32[]{:S(2)}) collective-permute-start(bf16[2,64,768]{2,1,0:T(8,128)(2,1)S(1)} %pad_maximum_fusion.1), channel_id=1, source_target_pairs={{0,8},{8,0},{1,9},{9,1},{2,10},{10,2},{3,11},{11,3},{4,12},{12,4},... | collective-permute-start | bytes 589832 | tf_op jit(solution)/shard_map/ppermute | solution.py:1008
  112.0 8.2 %collective-permute-start.28 = (bf16[128,768]{1,0:T(8,128)(2,1)S(1)}, bf16[128,768]{1,0:T(8,128)(2,1)S(1)}, u32[]{:S(2)}, u32[]{:S(2)}) collective-permute-start(bf16[128,768]{1,0:T(8,128)(2,1)S(1)} %collective-permute-done.26.refs_3_), channel_id=1, source_target_pairs={{0,1},{1,0},{2,3},{3,2},{4,5},{5,4},{6,7},{7,6},{8,9},{9,8},{10,11... | collective-permute-start | bytes 589832 | tf_op jit(solution)/shard_map/ppermute | solution.py:1008
  114.6 11.3 %collective-permute-start.30 = (bf16[256,192]{1,0:T(8,128)(2,1)S(1)}, bf16[256,192]{1,0:T(8,128)(2,1)S(1)}, u32[]{:S(2)}, u32[]{:S(2)}) collective-permute-start(bf16[256,192]{1,0:T(8,128)(2,1)S(1)} %get-tuple-element.227), channel_id=1, source_target_pairs={{0,2},{2,0},{1,3},{3,1},{4,6},{6,4},{5,7},{7,5},{8,10},{10,8},{9,1... | collective-permute-start | bytes 294920 | tf_op jit(solution)/shard_map/ppermute | solution.py:1008
  125.2 14.9 %collective-permute-start.36 = (bf16[384,768]{1,0:T(8,128)(2,1)S(1)}, bf16[384,768]{1,0:T(8,128)(2,1)S(1)}, u32[]{:S(2)}, u32[]{:S(2)}) collective-permute-start(bf16[384,768]{1,0:T(8,128)(2,1)S(1)} %get-tuple-element.261), channel_id=1, source_target_pairs={{0,16},{16,0},{1,17},{17,1},{2,18},{18,2},{3,19},{19,3},{4,20},{20... | collective-permute-start | bytes 1769480 | tf_op jit(solution)/shard_map/ppermute | solution.py:1008
  125.9 14.6 %collective-permute-start.37 = (bf16[384,768]{1,0:T(8,128)(2,1)S(1)}, bf16[384,768]{1,0:T(8,128)(2,1)S(1)}, u32[]{:S(2)}, u32[]{:S(2)}) collective-permute-start(bf16[384,768]{1,0:T(8,128)(2,1)S(1)} %get-tuple-element.263), channel_id=1, source_target_pairs={{0,8},{8,0},{1,9},{9,1},{2,10},{10,2},{3,11},{11,3},{4,12},{12,4},... | collective-permute-start | bytes 1769480 | tf_op jit(solution)/shard_map/ppermute | solution.py:1008
  125.9 7.6 %collective-permute-start.31 = (bf16[80,768]{1,0:T(8,128)(2,1)S(1)}, bf16[80,768]{1,0:T(8,128)(2,1)S(1)}, u32[]{:S(2)}, u32[]{:S(2)}) collective-permute-start(bf16[80,768]{1,0:T(8,128)(2,1)S(1)} %get-tuple-element.243.refs_1_), channel_id=1, source_target_pairs={{0,2},{2,0},{1,3},{3,1},{4,6},{6,4},{5,7},{7,5},{8,10},{10,8},{9,1... | collective-permute-start | bytes 368648 | tf_op jit(solution)/shard_map/ppermute | solution.py:1008
  136.4 15.4 %collective-permute-start.35 = (bf16[3,128,768]{2,1,0:T(8,128)(2,1)S(1)}, bf16[3,128,768]{2,1,0:T(8,128)(2,1)S(1)}, u32[]{:S(2)}, u32[]{:S(2)}) collective-permute-start(bf16[3,128,768]{2,1,0:T(8,128)(2,1)S(1)} %get-tuple-element.251.refs_4_), channel_id=1, source_target_pairs={{0,1},{1,0},{2,3},{3,2},{4,5},{5,4},{6,7},{7,6},{8,9},{9,8},{10,11... | collective-permute-start | bytes 1769480 | tf_op jit(solution)/shard_map/ppermute | solution.py:1008
  141.3 13.7 %collective-permute-start.40 = (bf16[384,768]{1,0:T(8,128)(2,1)S(1)}, bf16[384,768]{1,0:T(8,128)(2,1)S(1)}, u32[]{:S(2)}, u32[]{:S(2)}) collective-permute-start(bf16[384,768]{1,0:T(8,128)(2,1)S(1)} %get-tuple-element.269.refs_2_), channel_id=1, source_target_pairs={{0,16},{16,0},{1,17},{17,1},{2,18},{18,2},{3,19},{19,3},{4,20},{20... | collective-permute-start | bytes 1769480 | tf_op jit(solution)/shard_map/ppermute | solution.py:1008
  142.8 13.4 %collective-permute-start.39 = (bf16[384,768]{1,0:T(8,128)(2,1)S(1)}, bf16[384,768]{1,0:T(8,128)(2,1)S(1)}, u32[]{:S(2)}, u32[]{:S(2)}) collective-permute-start(bf16[384,768]{1,0:T(8,128)(2,1)S(1)} %get-tuple-element.264.refs_2_.refs_0_), channel_id=1, source_target_pairs={{0,8},{8,0},{1,9},{9,1},{2,10},{10,2},{3,11},{11,3},{4,12},{12,4},... | collective-permute-start | bytes 1769480 | tf_op jit(solution)/shard_map/ppermute | solution.py:1008
  152.6 15.5 %collective-permute-start.38 = (bf16[3,64,768]{2,1,0:T(8,128)(2,1)S(1)}, bf16[3,64,768]{2,1,0:T(8,128)(2,1)S(1)}, u32[]{:S(2)}, u32[]{:S(2)}) collective-permute-start(bf16[3,64,768]{2,1,0:T(8,128)(2,1)S(1)} %get-tuple-element.268.refs_4_), channel_id=1, source_target_pairs={{0,2},{2,0},{1,3},{3,1},{4,6},{6,4},{5,7},{7,5},{8,10},{10,8},{9,1... | collective-permute-start | bytes 884744 | tf_op jit(solution)/shard_map/ppermute | solution.py:1008
  157.0 16.0 %collective-permute-start.47 = (bf16[384,768]{1,0:T(8,128)(2,1)S(1)}, bf16[384,768]{1,0:T(8,128)(2,1)S(1)}, u32[]{:S(2)}, u32[]{:S(2)}) collective-permute-start(bf16[384,768]{1,0:T(8,128)(2,1)S(1)} %get-tuple-element.281.refs_4_), channel_id=1, source_target_pairs={{0,8},{8,0},{1,9},{9,1},{2,10},{10,2},{3,11},{11,3},{4,12},{12,4},... | collective-permute-start | bytes 1769480 | tf_op jit(solution)/shard_map/ppermute | solution.py:1008
  157.7 15.3 %collective-permute-start.46 = (bf16[384,768]{1,0:T(8,128)(2,1)S(1)}, bf16[384,768]{1,0:T(8,128)(2,1)S(1)}, u32[]{:S(2)}, u32[]{:S(2)}) collective-permute-start(bf16[384,768]{1,0:T(8,128)(2,1)S(1)} %get-tuple-element.270.refs_2_.refs_0_), channel_id=1, source_target_pairs={{0,16},{16,0},{1,17},{17,1},{2,18},{18,2},{3,19},{19,3},{4,20},{20... | collective-permute-start | bytes 1769480 | tf_op jit(solution)/shard_map/ppermute | solution.py:1008
  158.3 12.5 %collective-permute-start.45 = (bf16[192,768]{1,0:T(8,128)(2,1)S(1)}, bf16[192,768]{1,0:T(8,128)(2,1)S(1)}, u32[]{:S(2)}, u32[]{:S(2)}) collective-permute-start(bf16[192,768]{1,0:T(8,128)(2,1)S(1)} %get-tuple-element.279), channel_id=1, source_target_pairs={{0,4},{4,0},{1,5},{5,1},{2,6},{6,2},{3,7},{7,3},{8,12},{12,8},{9,1... | collective-permute-start | bytes 884744 | tf_op jit(solution)/shard_map/ppermute | solution.py:1008
  158.3 12.0 %collective-permute-start.34 = (bf16[80,768]{1,0:T(8,128)(2,1)S(1)}, bf16[80,768]{1,0:T(8,128)(2,1)S(1)}, u32[]{:S(2)}, u32[]{:S(2)}) collective-permute-start(bf16[80,768]{1,0:T(8,128)(2,1)S(1)} %collective-permute-done.31.refs_2_), channel_id=1, source_target_pairs={{0,1},{1,0},{2,3},{3,2},{4,5},{5,4},{6,7},{7,6},{8,9},{9,8},{10,11... | collective-permute-start | bytes 368648 | tf_op jit(solution)/shard_map/ppermute | solution.py:1008
  170.7 19.3 %collective-permute-start.55 = (bf16[384,768]{1,0:T(8,128)(2,1)S(1)}, bf16[384,768]{1,0:T(8,128)(2,1)S(1)}, u32[]{:S(2)}, u32[]{:S(2)}) collective-permute-start(bf16[384,768]{1,0:T(8,128)(2,1)S(1)} %get-tuple-element.281.refs_4_), channel_id=1, source_target_pairs={{0,4},{4,0},{1,5},{5,1},{2,6},{6,2},{3,7},{7,3},{8,12},{12,8},{9,1... | collective-permute-start | bytes 1769480 | tf_op jit(solution)/shard_map/ppermute | solution.py:1008
  171.6 19.4 %collective-permute-start.53 = (bf16[384,768]{1,0:T(8,128)(2,1)S(1)}, bf16[384,768]{1,0:T(8,128)(2,1)S(1)}, u32[]{:S(2)}, u32[]{:S(2)}) collective-permute-start(bf16[384,768]{1,0:T(8,128)(2,1)S(1)} %get-tuple-element.270.refs_2_.refs_0_), channel_id=1, source_target_pairs={{0,4},{4,0},{1,5},{5,1},{2,6},{6,2},{3,7},{7,3},{8,12},{12,8},{9,1... | collective-permute-start | bytes 1769480 | tf_op jit(solution)/shard_map/ppermute | solution.py:1008
  177.8 11.0 %collective-permute-start.50 = (bf16[256,768]{1,0:T(8,128)(2,1)S(1)}, bf16[256,768]{1,0:T(8,128)(2,1)S(1)}, u32[]{:S(2)}, u32[]{:S(2)}) collective-permute-start(bf16[256,768]{1,0:T(8,128)(2,1)S(1)} %get-tuple-element.287), channel_id=1, source_target_pairs={{0,8},{8,0},{1,9},{9,1},{2,10},{10,2},{3,11},{11,3},{4,12},{12,4},... | collective-permute-start | bytes 1179656 | tf_op jit(solution)/shard_map/ppermute | solution.py:1008
  179.1 9.7 %collective-permute-start.49 = (bf16[240,768]{1,0:T(8,128)(2,1)S(1)}, bf16[240,768]{1,0:T(8,128)(2,1)S(1)}, u32[]{:S(2)}, u32[]{:S(2)}) collective-permute-start(bf16[240,768]{1,0:T(8,128)(2,1)S(1)} %get-tuple-element.285), channel_id=1, source_target_pairs={{0,16},{16,0},{1,17},{17,1},{2,18},{18,2},{3,19},{19,3},{4,20},{20... | collective-permute-start | bytes 1105928 | tf_op jit(solution)/shard_map/ppermute | solution.py:1008
  181.9 15.8 %collective-permute-start.57 = (bf16[2,3,32,768]{3,2,1,0:T(8,128)(2,1)S(1)}, bf16[2,3,32,768]{3,2,1,0:T(8,128)(2,1)S(1)}, u32[]{:S(2)}, u32[]{:S(2)}) collective-permute-start(bf16[2,3,32,768]{3,2,1,0:T(8,128)(2,1)S(1)} %pad_maximum_fusion.refs_4_), channel_id=1, source_target_pairs={{0,2},{2,0},{1,3},{3,1},{4,6},{6,4},{5,7},{7,5},{8,10},{10,8},{9,1... | collective-permute-start | bytes 884744 | tf_op jit(solution)/shard_map/ppermute | solution.py:1008
  188.8 9.0 %collective-permute-start.56 = (bf16[384,768]{1,0:T(8,128)(2,1)S(1)}, bf16[384,768]{1,0:T(8,128)(2,1)S(1)}, u32[]{:S(2)}, u32[]{:S(2)}) collective-permute-start(bf16[384,768]{1,0:T(8,128)(2,1)S(1)} %collective-permute-done.47.refs_14_.refs_5_), channel_id=1, source_target_pairs={{0,4},{4,0},{1,5},{5,1},{2,6},{6,2},{3,7},{7,3},{8,12},{12,8},{9,1... | collective-permute-start | bytes 1769480 | tf_op jit(solution)/shard_map/ppermute | solution.py:1008
  188.8 9.8 %collective-permute-start.54 = (bf16[384,768]{1,0:T(8,128)(2,1)S(1)}, bf16[384,768]{1,0:T(8,128)(2,1)S(1)}, u32[]{:S(2)}, u32[]{:S(2)}) collective-permute-start(bf16[384,768]{1,0:T(8,128)(2,1)S(1)} %collective-permute-done.46.refs_13_.refs_1_), channel_id=1, source_target_pairs={{0,4},{4,0},{1,5},{5,1},{2,6},{6,2},{3,7},{7,3},{8,12},{12,8},{9,1... | collective-permute-start | bytes 1769480 | tf_op jit(solution)/shard_map/ppermute | solution.py:1008
  190.0 17.5 %collective-permute-start.51 = (bf16[240,768]{1,0:T(8,128)(2,1)S(1)}, bf16[240,768]{1,0:T(8,128)(2,1)S(1)}, u32[]{:S(2)}, u32[]{:S(2)}) collective-permute-start(bf16[240,768]{1,0:T(8,128)(2,1)S(1)} %get-tuple-element.289.refs_8_.refs_0_), channel_id=1, source_target_pairs={{0,8},{8,0},{1,9},{9,1},{2,10},{10,2},{3,11},{11,3},{4,12},{12,4},... | collective-permute-start | bytes 1105928 | tf_op jit(solution)/shard_map/ppermute | solution.py:1008
  190.9 16.7 %collective-permute-start.52 = (bf16[256,768]{1,0:T(8,128)(2,1)S(1)}, bf16[256,768]{1,0:T(8,128)(2,1)S(1)}, u32[]{:S(2)}, u32[]{:S(2)}) collective-permute-start(bf16[256,768]{1,0:T(8,128)(2,1)S(1)} %get-tuple-element.290.refs_2_), channel_id=1, source_target_pairs={{0,16},{16,0},{1,17},{17,1},{2,18},{18,2},{3,19},{19,3},{4,20},{20... | collective-permute-start | bytes 1179656 | tf_op jit(solution)/shard_map/ppermute | solution.py:1008
  197.7 9.9 %collective-permute-start.58 = (bf16[2,3,32,768]{3,2,1,0:T(8,128)(2,1)S(1)}, bf16[2,3,32,768]{3,2,1,0:T(8,128)(2,1)S(1)}, u32[]{:S(2)}, u32[]{:S(2)}) collective-permute-start(bf16[2,3,32,768]{3,2,1,0:T(8,128)(2,1)S(1)} %collective-permute-done.57.refs_2_), channel_id=1, source_target_pairs={{0,1},{1,0},{2,3},{3,2},{4,5},{5,4},{6,7},{7,6},{8,9},{9,8},{10,11... | collective-permute-start | bytes 884744 | tf_op jit(solution)/shard_map/ppermute | solution.py:1008
  197.8 12.0 %collective-permute-start.42 = (bf16[2,64,768]{2,1,0:T(8,128)(2,1)S(1)}, bf16[2,64,768]{2,1,0:T(8,128)(2,1)S(1)}, u32[]{:S(2)}, u32[]{:S(2)}) collective-permute-start(bf16[2,64,768]{2,1,0:T(8,128)(2,1)S(1)} %pad_maximum_fusion.2), channel_id=1, source_target_pairs={{0,8},{8,0},{1,9},{9,1},{2,10},{10,2},{3,11},{11,3},{4,12},{12,4},... | collective-permute-start | bytes 589832 | tf_op jit(solution)/shard_map/ppermute | solution.py:1008
  198.6 14.3 %collective-permute-start.59 = (bf16[2,3,32,768]{3,2,1,0:T(8,128)(2,1)S(1)}, bf16[2,3,32,768]{3,2,1,0:T(8,128)(2,1)S(1)}, u32[]{:S(2)}, u32[]{:S(2)}) collective-permute-start(bf16[2,3,32,768]{3,2,1,0:T(8,128)(2,1)S(1)} %pad_maximum_fusion.refs_4_), channel_id=1, source_target_pairs={{0,1},{1,0},{2,3},{3,2},{4,5},{5,4},{6,7},{7,6},{8,9},{9,8},{10,11... | collective-permute-start | bytes 884744 | tf_op jit(solution)/shard_map/ppermute | solution.py:1008
  208.3 8.8 %collective-permute-start.60 = (bf16[240,768]{1,0:T(8,128)(2,1)S(1)}, bf16[240,768]{1,0:T(8,128)(2,1)S(1)}, u32[]{:S(2)}, u32[]{:S(2)}) collective-permute-start(bf16[240,768]{1,0:T(8,128)(2,1)S(1)} %get-tuple-element.292.refs_8_.refs_5_.refs_0_), channel_id=1, source_target_pairs={{0,16},{16,0},{1,17},{17,1},{2,18},{18,2},{3,19},{19,3},{4,20},{20... | collective-permute-start | bytes 1105928 | tf_op jit(solution)/shard_map/ppermute | solution.py:1008
  209.0 9.0 %collective-permute-start.61 = (bf16[256,768]{1,0:T(8,128)(2,1)S(1)}, bf16[256,768]{1,0:T(8,128)(2,1)S(1)}, u32[]{:S(2)}, u32[]{:S(2)}) collective-permute-start(bf16[256,768]{1,0:T(8,128)(2,1)S(1)} %get-tuple-element.296.refs_4_), channel_id=1, source_target_pairs={{0,8},{8,0},{1,9},{9,1},{2,10},{10,2},{3,11},{11,3},{4,12},{12,4},... | collective-permute-start | bytes 1179656 | tf_op jit(solution)/shard_map/ppermute | solution.py:1008
  209.8 10.5 %collective-permute-start.64 = (bf16[256,768]{1,0:T(8,128)(2,1)S(1)}, bf16[256,768]{1,0:T(8,128)(2,1)S(1)}, u32[]{:S(2)}, u32[]{:S(2)}) collective-permute-start(bf16[256,768]{1,0:T(8,128)(2,1)S(1)} %get-tuple-element.296.refs_4_), channel_id=1, source_target_pairs={{0,4},{4,0},{1,5},{5,1},{2,6},{6,2},{3,7},{7,3},{8,12},{12,8},{9,1... | collective-permute-start | bytes 1179656 | tf_op jit(solution)/shard_map/ppermute | solution.py:1008
  (37 other events, 211.3 us)

commit v6 on v5

--- a/solution.py
+++ b/solution.py
@@ -132,55 +132,46 @@
     return started
 
 
-def share_kernel(p_ref, exit_ref, up_ref, down_ref, bias_ref, ups_ref, downs_ref, biasv_ref, sems):
-    c = p_ref[0]
-    q = p_ref[1] * 2 + p_ref[2]
-    many = down_ref.shape[1] // 4
-    few = exit_ref.shape[1] // 4
-    started = copied(
-        [
-            (bias_ref, biasv_ref),
-            (up_ref.at[c, pl.ds(pl.multiple_of(q * many, 16), many)], ups_ref.at[pl.ds(0, many)]),
-            (
-                exit_ref.at[c, pl.ds(pl.multiple_of(q * few, 16), few)],
-                ups_ref.at[pl.ds(many + 16, few)],
-            ),
-            (down_ref.at[c, pl.ds(pl.multiple_of(q * many, 16), many)], downs_ref),
-        ],
-        sems,
-    )
-    started[0].wait()
-    left = biasv_ref[pl.ds(c, 1), :]
-    lines = []
-    for _ in range(3):
-        lines.append(left.astype(BF16).astype(F32))
-        left = left - lines[-1]
-    lines.append(jnp.zeros((13, left.shape[1]), F32))
-    ups_ref[many : many + 16, :] = jnp.concatenate(lines, axis=0).astype(BF16)
-    for copy in started[1:]:
-        copy.wait()
-
-
 def pack_kernel(
     p_ref,
     tok_ref,
     sp_ref,
     pos_ref,
     box_ref,
+    exit_ref,
+    up_ref,
+    down_ref,
+    bias_ref,
     far0_ref,
     far1_ref,
     far2_ref,
     near_ref,
     own_ref,
+    ups_ref,
+    downs_ref,
     posv_ref,
     boxv_ref,
+    biasv_ref,
     sems,
 ):
     c, y, zl, zh = p_ref[0], p_ref[2], p_ref[3], p_ref[4]
     block = zh * 2 + zl
     least = tok_ref.shape[3]
     rows = 4 * least
-    pairs = [(pos_ref, posv_ref), (box_ref, boxv_ref)]
+    q = p_ref[1] * 2 + y
+    many = down_ref.shape[1] // 4
+    few = exit_ref.shape[1] // 4
+    pairs = [
+        (pos_ref, posv_ref),
+        (box_ref, boxv_ref),
+        (bias_ref, biasv_ref),
+        (up_ref.at[c, pl.ds(pl.multiple_of(q * many, 16), many)], ups_ref.at[pl.ds(0, many)]),
+        (
+            exit_ref.at[c, pl.ds(pl.multiple_of(q * few, 16), few)],
+            ups_ref.at[pl.ds(many + 16, few)],
+        ),
+        (down_ref.at[c, pl.ds(pl.multiple_of(q * many, 16), many)], downs_ref),
+    ]
     for k in range(4):
         at = block ^ k
         to = pl.ds(k * least, least)
@@ -193,8 +184,15 @@
             (tok_ref.at[c, y, at], own_ref.at[to]),
         ]
     started = copied(pairs, sems)
-    for copy in started[:2]:
+    for copy in started[:3]:
         copy.wait()
+    left = biasv_ref[pl.ds(c, 1), :]
+    lines = []
+    for _ in range(3):
+        lines.append(left.astype(BF16).astype(F32))
+        left = left - lines[-1]
+    lines.append(jnp.zeros((13, left.shape[1]), F32))
+    ups_ref[many : many + 16, :] = jnp.concatenate(lines, axis=0).astype(BF16)
     lane = lax.broadcasted_iota(jnp.int32, (8, NBUCK), 1)
     width = far0_ref.shape[1]
     for page, ref, at in ((1 - y, far0_ref, rows), (y, near_ref, 2 * rows)):
@@ -214,7 +212,7 @@
         value = jnp.concatenate([value.astype(F32), jnp.zeros((8, NBUCK), F32)], axis=0)
         ref[at : at + 16, 0:NBUCK] = value.astype(BF16)
         ref[at : at + 16, NBUCK:] = jnp.zeros((16, width - NBUCK), BF16)
-    for copy in started[2:]:
+    for copy in started[3:]:
         copy.wait()
 
 
@@ -1065,26 +1063,17 @@
         return ((count, width), dtype)
 
     share = hidden // 4
-    up_part, down_part = run(
-        share_kernel,
-        [
-            (exit_matrix, "any"),
-            (up_weight, "any"),
-            (shrink_projection_array, "any"),
-            (hidden_bias, "any"),
-        ],
-        [rows_of(share + 16 + inner // 4), rows_of(share)],
-        scratch=[pltpu.VMEM(hidden_bias.shape, F32), pltpu.SemaphoreType.DMA((4,))],
-        vmem=PACK_VMEM,
-    )
-    up_part = swap(up_part, "zh")
-    far0, far1, far2, near, x00 = run(
+    far0, far1, far2, near, x00, up_part, down_part = run(
         pack_kernel,
         [
             (tokens.reshape(2, 2, 4, least, width), "any"),
             (spatial.reshape(2, 4, least, width), "any"),
             (positions, "any"),
             (boxes, "any"),
+            (exit_matrix, "any"),
+            (up_weight, "any"),
+            (shrink_projection_array, "any"),
+            (hidden_bias, "any"),
         ],
         [
             rows_of(rows + 16),
@@ -1092,16 +1081,18 @@
             rows_of(rows),
             rows_of(2 * rows + 16),
             rows_of(rows),
-        ],
-        us=30,
+            rows_of(share + 16 + inner // 4),
+            rows_of(share),
+        ],
         scratch=[
             pltpu.VMEM(positions.shape, jnp.int32),
             pltpu.VMEM(boxes.shape, jnp.int32),
-            pltpu.SemaphoreType.DMA((26,)),
+            pltpu.VMEM(hidden_bias.shape, F32),
+            pltpu.SemaphoreType.DMA((30,)),
         ],
         vmem=PACK_VMEM,
-        after=[down_part],
-    )
+    )
+    up_part = swap(up_part, "zh")
     i10, s10, x10 = swap(far0, "y"), swap(far1, "y"), swap(far2, "y")
     cot_far, cot_near, cot00 = run(
         cotangent_kernel,
@@ -1426,11 +1417,7 @@
     pages = jnp.stack([mine, got])
     pages_zh = swap(pages, "zh")
     pages_zl = swap(pages, "zl")
-    one_half, two_half = plus([(one_keep, one_recv), (two_keep, two_recv)], after=[pages])
-    one_other = swap(one_half, "y")
-    two_other = swap(two_half, "batch")
-    far_y = swap(jnp.stack([far_keep[1], far_core[1]]), "y")
-    halves = [up_half, up_far, down_half, down_far]
+    *halves, pages = join(up_half, up_far, down_half, down_far, pages)
     others = [swap(value, "core") for value in halves]
     grad_up, grad_down, spread_event = run(
         spread_kernel,
@@ -1440,12 +1427,19 @@
             ((2, 2, hidden // 2, width), F32),
             ((8, NBUCK), F32),
         ],
-        after=[one_half],
-    )
+        after=[pages],
+    )
+    one_half, two_half = plus(
+        [(one_keep, one_recv), (two_keep, two_recv)], after=[spread_event]
+    )
+    one_other = swap(one_half, "y")
+    two_other = swap(two_half, "batch")
+    far_y = swap(jnp.stack([far_keep[1], far_core[1]]), "y")
+    pages_zh, pages_zl = join(pages_zh, pages_zl)
     pages_zz = swap(pages_zh, "zl")
     one_half, two_half = plus(
         [(one_half, one_other), (two_half, two_other)],
-        after=[spread_event, pages_zz],
+        after=[pages_zz],
         over_batch=True,
     )
     one_far = swap(one_half, "batch")

time: 225 us -> 221 us (0.982)
  waiting for transfers between devices: 98.7 us -> 94.2 us
  starting transfers between devices: 49 us -> 52.4 us
    ppermute x64, waiting for transfers between devices: 98.3 us -> 93.7 us  [swap(): return lax.ppermute(value, axis, [(i, i ^ step) for i in range(size)])]
    ppermute x64, starting transfers between devices: 45 us -> 48.4 us  [swap(): return lax.ppermute(value, axis, [(i, i ^ step) for i in range(size)])]
    pallas_call x33 -> x32, Pallas kernels: 68.3 us -> 66.3 us  [kernel_call(): pl.pallas_call(kernel, out_shape=[jax.ShapeDtypeStruct(out[0], out[1]) fo...]
where the time goes in v6:
time: 221 us
  waiting for transfers between devices  94.2 us (43%)
  Pallas kernels  66.3 us (30%)
  starting transfers between devices  52.4 us (24%)
  local copies, waits for them, and re-layouts  6.8 us (3%)
    ppermute x64, waiting for transfers between devices, swap(): return lax.ppermute(value, axis, [(i, i ^ step) for i in range(size)])  93.7 us
    pallas_call x32, Pallas kernels, kernel_call(): pl.pallas_call(kernel, out_shape=[jax.ShapeDtypeStruct(out[0], out[1]) fo...  66.3 us
    ppermute x64, starting transfers between devices, swap(): return lax.ppermute(value, axis, [(i, i ^ step) for i in range(size)])  48.4 us
    unnamed x39, local copies, waits for them, and re-layouts  6.05 us
  transfers between devices with their start and end apart: 66, of which 36 were waited for; matrix products, arithmetic and copies ran while one was open for 0% of the time, Pallas kernels for 25%

profile of v6, /device:TPU:0, one launch (start us, length us, event | category | flops | bytes accessed | tf_op | source)
XLA Modules:
  0.0 221.0 jit_solution(7580035068573424807)
XLA Ops:
  1.3 4.0 %shard_map.246 = (bf16[144,768]{1,0:T(8,128)(2,1)}, bf16[128,768]{1,0:T(8,128)(2,1)}, bf16[128,768]{1,0:T(8,128)(2,1)}, bf16[272,768]{1,0:T(8,128)(2,1)}, bf16[1...) custom-call(s32[5]{0:T(128)} %stack.38.s_ref, bf16[2,2,4,32,768]{4,3,2,1,0:T(8,128)(2,1)} %bitcast.55, ...), custom_call_target="tpu_custom_call" | custom-call | flops 110000000 | bytes 350000 | tf_op jit(solution)/shard_map/pallas_call | solution.py:49
  5.8 3.7 %collective-permute-start.4 = (bf16[256,768]{1,0:T(8,128)(2,1)}, bf16[256,768]{1,0:T(8,128)(2,1)S(1)}, u32[]{:S(2)}, u32[]{:S(2)}) collective-permute-start(bf16[256,768]{1,0:T(8,128)(2,1)} %get-tuple-element.177), channel_id=1, source_target_pairs={{0,2},{2,0},{1,3},{3,1},{4,6},{6,4},{5,7},{7,5},{8,10},{10,8},{9,1... | collective-permute-start | bytes 1179656 | tf_op jit(solution)/shard_map/ppermute | solution.py:1006
  9.4 1.5 collective-permute-start
  11.4 1.5 collective-permute-start.2
  13.0 2.8 %shard_map.247 = (bf16[2,128,768]{2,1,0:T(8,128)(2,1)}, bf16[128,768]{1,0:T(8,128)(2,1)}, bf16[128,768]{1,0:T(8,128)(2,1)}) custom-call(s32[5]{0:T(128)} %stack.38.s_ref, bf16[2,2,4,32,768]{4,3,2,1,0:T(8,128)(2,1)} %bitcast.54, bf16[128,768]{1,0:T(8,128)(2,1)} %get-tuple-element.173.refs_1_.refs_0_), custom_call_target="tpu_custom_call" | custom-call | flops 110000000 | bytes 350000 | tf_op jit(solution)/shard_map/pallas_call | solution.py:49
  15.9 1.7 copy-done.1
  21.9 2.4 %shard_map.248 = (bf16[2,128,768]{2,1,0:T(8,128)(2,1)S(1)}, bf16[2,128,768]{2,1,0:T(8,128)(2,1)S(1)}, s32[8,256]{1,0:T(8,128)S(1)}, bf16[3,256,192]{2,1,0:T(8,12...) custom-call(s32[5]{0:T(128)S(1)} %copy-done.9, ...), custom_call_target="tpu_custom_call" | custom-call | flops 110000000 | bytes 350000 | tf_op jit(solution)/shard_map/pallas_call | solution.py:49
  25.7 2.1 collective-permute-done.4.refs_3_.refs_8_
  28.3 2.5 %collective-permute-start.10 = (bf16[256,768]{1,0:T(8,128)(2,1)S(1)}, bf16[256,768]{1,0:T(8,128)(2,1)S(1)}, u32[]{:S(2)}, u32[]{:S(2)}) collective-permute-start(bf16[256,768]{1,0:T(8,128)(2,1)S(1)} %collective-permute-done.4.refs_3_.refs_8_), channel_id=1, source_target_pairs={{0,24},{8,16},{16,8},{24,0},{1,25},{9,17},{17,9},{25,1},{2,26},{10... | collective-permute-start | bytes 1179656 | tf_op jit(solution)/shard_map/ppermute | solution.py:1011
  31.8 7.9 %shard_map.249 = (bf16[2,2,128,768]{3,2,1,0:T(8,128)(2,1)S(1)}, bf16[2,2,128,768]{3,2,1,0:T(8,128)(2,1)S(1)}, s32[512,8]{1,0:T(8,128)S(1)}, bf16[3,512,192]{2,1,...) custom-call(s32[5]{0:T(128)S(1)} %copy-done.9, ...), custom_call_target="tpu_custom_call" | custom-call | flops 32999999488 | bytes 105000000 | tf_op jit(solution)/shard_map/pallas_call | solution.py:49
  39.7 3.0 %collective-permute-start.11 = (bf16[256,192]{1,0:T(8,128)(2,1)S(1)}, bf16[256,192]{1,0:T(8,128)(2,1)S(1)}, u32[]{:S(2)}, u32[]{:S(2)}) collective-permute-start(bf16[256,192]{1,0:T(8,128)(2,1)S(1)} %get-tuple-element.192.refs_7_), channel_id=1, source_target_pairs={{0,2},{2,0},{1,3},{3,1},{4,6},{6,4},{5,7},{7,5},{8,10},{10,8},{9,1... | collective-permute-start | bytes 294920 | tf_op jit(solution)/shard_map/ppermute | solution.py:1006
  42.7 8.4 %collective-permute-done.7.refs_12_ = bf16[192,768]{1,0:T(8,128)(2,1)S(1)} collective-permute-done((bf16[192,768]{1,0:T(8,128)(2,1)S(1)}, bf16[192,768]{1,0:T(8,128)(2,1)S(1)}, u32[]{:S(2)}, u32[]{:S(2)}) %collective-permute-start.7) | collective-permute-done | bytes 294944 | tf_op jit(solution)/shard_map/ppermute | solution.py:1006
  51.1 1.6 collective-permute-start.14
  61.9 3.8 %collective-permute-done.15.refs_1_ = bf16[128,768]{1,0:T(8,128)(2,1)S(1)} collective-permute-done((bf16[128,768]{1,0:T(8,128)(2,1)S(1)}, bf16[128,768]{1,0:T(8,128)(2,1)S(1)}, u32[]{:S(2)}, u32[]{:S(2)}) %collective-permute-start.15) | collective-permute-done | bytes 196640 | tf_op jit(solution)/shard_map/ppermute | solution.py:1006
  66.3 1.8 collective-permute-start.19
  68.7 2.8 %shard_map.253 = (bf16[256,768]{1,0:T(8,128)(2,1)S(1)}, bf16[256,768]{1,0:T(8,128)(2,1)S(1)}, bf16[2,256,768]{2,1,0:T(8,128)(2,1)S(1)}, bf16[2,256,768]{2,1,0:T(...) custom-call(s32[5]{0:T(128)S(1)} %copy-done.9, ...), custom_call_target="tpu_custom_call" | custom-call | flops 110000000 | bytes 350000 | tf_op jit(solution)/shard_map/pallas_call | solution.py:49
  71.5 1.7 collective-permute-start.21
  74.5 4.4 %collective-permute-done.19.refs_1_ = bf16[128,768]{1,0:T(8,128)(2,1)S(1)} collective-permute-done((bf16[128,768]{1,0:T(8,128)(2,1)S(1)}, bf16[128,768]{1,0:T(8,128)(2,1)S(1)}, u32[]{:S(2)}, u32[]{:S(2)}) %collective-permute-start.19) | collective-permute-done | bytes 196640 | tf_op jit(solution)/shard_map/ppermute | solution.py:1006
  82.6 4.6 %collective-permute-done.18.refs_1_ = bf16[256,768]{1,0:T(8,128)(2,1)S(1)} collective-permute-done((bf16[256,768]{1,0:T(8,128)(2,1)S(1)}, bf16[256,768]{1,0:T(8,128)(2,1)S(1)}, u32[]{:S(2)}, u32[]{:S(2)}) %collective-permute-start.18) | collective-permute-done | bytes 393248 | tf_op jit(solution)/shard_map/ppermute | solution.py:1006
  88.7 1.6 shard_map.257
  90.4 2.3 %shard_map.258 = (bf16[256,768]{1,0:T(8,128)(2,1)S(1)}, bf16[256,768]{1,0:T(8,128)(2,1)S(1)}) custom-call(s32[5]{0:T(128)S(1)} %copy-done.9, bf16[256,768]{1,0:T(8,128)(2,1)S(1)} %get-tuple-element.219.refs_0_.refs_4_, bf16[768,768]{1,0:T(8,128)(2,1)S(1)} %get-tuple-element.204.refs_5_.refs_1_, ...), custom_call_target="tpu_custom_call" | custom-call | flops 110000000 | bytes 350000 | tf_op jit(solution)/shard_map/pallas_call | solution.py:49
  92.6 2.5 %collective-permute-start.25 = (bf16[256,768]{1,0:T(8,128)(2,1)S(1)}, bf16[256,768]{1,0:T(8,128)(2,1)S(1)}, u32[]{:S(2)}, u32[]{:S(2)}) collective-permute-start(bf16[256,768]{1,0:T(8,128)(2,1)S(1)} %get-tuple-element.223.refs_4_), channel_id=1, source_target_pairs={{0,1},{1,0},{2,3},{3,2},{4,5},{5,4},{6,7},{7,6},{8,9},{9,8},{10,11... | collective-permute-start | bytes 1179656 | tf_op jit(solution)/shard_map/ppermute | solution.py:1006
  96.2 3.7 %collective-permute-done.26.refs_3_ = bf16[128,768]{1,0:T(8,128)(2,1)S(1)} collective-permute-done((bf16[128,768]{1,0:T(8,128)(2,1)S(1)}, bf16[128,768]{1,0:T(8,128)(2,1)S(1)}, u32[]{:S(2)}, u32[]{:S(2)}) %collective-permute-start.26) | collective-permute-done | bytes 196640 | tf_op jit(solution)/shard_map/ppermute | solution.py:1006
  99.9 8.3 %collective-permute-done.25.refs_5_ = bf16[256,768]{1,0:T(8,128)(2,1)S(1)} collective-permute-done((bf16[256,768]{1,0:T(8,128)(2,1)S(1)}, bf16[256,768]{1,0:T(8,128)(2,1)S(1)}, u32[]{:S(2)}, u32[]{:S(2)}) %collective-permute-start.25) | collective-permute-done | bytes 393248 | tf_op jit(solution)/shard_map/ppermute | solution.py:1006
  109.7 1.6 collective-permute-done.29.refs_1_
  112.9 5.0 %collective-permute-done.28.refs_4_ = bf16[128,768]{1,0:T(8,128)(2,1)S(1)} collective-permute-done((bf16[128,768]{1,0:T(8,128)(2,1)S(1)}, bf16[128,768]{1,0:T(8,128)(2,1)S(1)}, u32[]{:S(2)}, u32[]{:S(2)}) %collective-permute-start.28) | collective-permute-done | bytes 196640 | tf_op jit(solution)/shard_map/ppermute | solution.py:1006
  117.9 2.4 %shard_map.261 = (bf16[2,64,768]{2,1,0:T(8,128)(2,1)S(1)}, bf16[2,64,768]{2,1,0:T(8,128)(2,1)S(1)}, f32[256,768]{1,0:T(8,128)}, bf16[256,768]{1,0:T(8,128)(2,1)S(1)}, f32[8,768]{1,0:T(8,128)}) custom-call(s32[5]{0:T(128)S(1)} %copy-done.9, bf16[2,2,128,768]{3,2,1,0:T(8,128)(2,1)S(1)} %get-tuple-element.187.refs_0_, ...), custom_call_target="tpu_custom_call" | custom-call | flops 110000000 | bytes 350000 | tf_op jit(solution)/shard_map/pallas_call | solution.py:49
  120.3 2.6 %shard_map.262 = (bf16[384,768]{1,0:T(8,128)(2,1)S(1)}, bf16[384,768]{1,0:T(8,128)(2,1)S(1)}, bf16[384,768]{1,0:T(8,128)(2,1)S(1)}, bf16[384,768]{1,0:T(8,128)(2,1)S(1)}, f32[8,768]{1,0:T(8,128)S(1)}) custom-call(s32[5]{0:T(128)S(1)} %copy-done.9, bf16[256,768]{1,0:T(8,128)(2,1)S(1)} %get-tuple-element.241.refs_0_, ...), custom_call_target="tpu_custom_call" | custom-call | flops 32999999488 | bytes 105000000 | tf_op jit(solution)/shard_map/pallas_call | solution.py:49
  123.7 5.3 %shard_map.263 = (bf16[3,512,512]{2,1,0:T(8,128)(2,1)S(1)}, bf16[3,512,192]{2,1,0:T(8,128)(2,1)S(1)}, bf16[2,512,192]{2,1,0:T(8,128)(2,1)S(1)}, bf16[128,768]{1,...) custom-call(s32[5]{0:T(128)S(1)} %copy-done.9, ...), custom_call_target="tpu_custom_call" | custom-call | flops 32999999488 | bytes 105000000 | tf_op jit(solution)/shard_map/pallas_call | solution.py:49
  129.1 2.1 collective-permute-done.31.refs_2_
  134.7 3.2 %collective-permute-done.36.refs_1_ = bf16[384,768]{1,0:T(8,128)(2,1)S(1)} collective-permute-done((bf16[384,768]{1,0:T(8,128)(2,1)S(1)}, bf16[384,768]{1,0:T(8,128)(2,1)S(1)}, u32[]{:S(2)}, u32[]{:S(2)}) %collective-permute-start.36) | collective-permute-done | bytes 589856 | tf_op jit(solution)/shard_map/ppermute | solution.py:1006
  141.8 5.9 %shard_map.267 = (bf16[240,768]{1,0:T(8,128)(2,1)S(1)}, bf16[240,768]{1,0:T(8,128)(2,1)S(1)}, bf16[96,768]{1,0:T(8,128)(2,1)S(1)}, f32[16,768]{1,0:T(8,128)S(1)}) custom-call(s32[5]{0:T(128)S(1)} %copy-done.9, bf16[2,2,128,768]{3,2,1,0:T(8,128)(2,1)S(1)} %get-tuple-element.187.refs_0_, bf16[3,512,512]{2,1,0:T(8,128)(2,1)S(1)} %get-tuple-element.262.refs_1_, ...), custom_call_target="tpu_custom_call" | custom-call | flops 110000000 | bytes 350000 | tf_op jit(solution)/shard_map/pallas_call | solution.py:49
  147.6 1.9 collective-permute-done.35.refs_1_
  150.2 2.5 %collective-permute-done.40.refs_3_ = bf16[384,768]{1,0:T(8,128)(2,1)S(1)} collective-permute-done((bf16[384,768]{1,0:T(8,128)(2,1)S(1)}, bf16[384,768]{1,0:T(8,128)(2,1)S(1)}, u32[]{:S(2)}, u32[]{:S(2)}) %collective-permute-start.40) | collective-permute-done | bytes 589856 | tf_op jit(solution)/shard_map/ppermute | solution.py:1006
  156.8 1.8 collective-permute-start.34
  158.6 10.7 %collective-permute-done.38.refs_1_ = bf16[3,64,768]{2,1,0:T(8,128)(2,1)S(1)} collective-permute-done((bf16[3,64,768]{2,1,0:T(8,128)(2,1)S(1)}, bf16[3,64,768]{2,1,0:T(8,128)(2,1)S(1)}, u32[]{:S(2)}, u32[]{:S(2)}) %collective-permute-start.38) | collective-permute-done | bytes 294944 | tf_op jit(solution)/shard_map/ppermute | solution.py:1006
  173.4 1.7 collective-permute-done.48.refs_1_
  178.8 3.0 %collective-permute-start.57 = (bf16[2,3,32,768]{3,2,1,0:T(8,128)(2,1)S(1)}, bf16[2,3,32,768]{3,2,1,0:T(8,128)(2,1)S(1)}, u32[]{:S(2)}, u32[]{:S(2)}) collective-permute-start(bf16[2,3,32,768]{3,2,1,0:T(8,128)(2,1)S(1)} %pad_maximum_fusion.refs_8_), channel_id=1, source_target_pairs={{0,2},{2,0},{1,3},{3,1},{4,6},{6,4},{5,7},{7,5},{8,10},{10,8},{9,1... | collective-permute-start | bytes 884744 | tf_op jit(solution)/shard_map/ppermute | solution.py:1006
  181.8 5.1 %shard_map.272 = (f32[2,2,384,768]{3,2,1,0:T(8,128)}, f32[2,2,384,768]{3,2,1,0:T(8,128)}, f32[8,128]{1,0:T(8,128)S(1)}) custom-call(s32[5]{0:T(128)S(1)} %copy-done.9, bf16[384,768]{1,0:T(8,128)(2,1)S(1)} %get-tuple-element.296.refs_2_.refs_0_, bf16[384,768]{1,0:T(8,128)(2,1)S(1)} %collective-permute-done.46.refs_13_.refs_1_, ...), custom_call_target="tpu_custom_call" | custom-call | flops 110000000 | bytes 350000 | tf_op jit(solution)/shard_map/pallas_call | solution.py:49
  191.0 1.7 collective-permute-done.58.refs_3_
  192.7 2.6 %collective-permute-done.57.refs_2_ = bf16[2,3,32,768]{3,2,1,0:T(8,128)(2,1)S(1)} collective-permute-done((bf16[2,3,32,768]{3,2,1,0:T(8,128)(2,1)S(1)}, bf16[2,3,32,768]{3,2,1,0:T(8,128)(2,1)S(1)}, u32[]{:S(2)}, u32[]{:S(2)}) %collective-permute-start.57) | collective-permute-done | bytes 294944 | tf_op jit(solution)/shard_map/ppermute | solution.py:1006
  196.4 5.6 %collective-permute-done.59.refs_4_ = bf16[2,3,32,768]{3,2,1,0:T(8,128)(2,1)S(1)} collective-permute-done((bf16[2,3,32,768]{3,2,1,0:T(8,128)(2,1)S(1)}, bf16[2,3,32,768]{3,2,1,0:T(8,128)(2,1)S(1)}, u32[]{:S(2)}, u32[]{:S(2)}) %collective-permute-start.59) | collective-permute-done | bytes 294944 | tf_op jit(solution)/shard_map/ppermute | solution.py:1006
  202.7 2.7 %collective-permute-start.60 = (bf16[240,768]{1,0:T(8,128)(2,1)S(1)}, bf16[240,768]{1,0:T(8,128)(2,1)S(1)}, u32[]{:S(2)}, u32[]{:S(2)}) collective-permute-start(bf16[240,768]{1,0:T(8,128)(2,1)S(1)} %get-tuple-element.305.refs_8_.refs_5_.refs_0_), channel_id=1, source_target_pairs={{0,16},{16,0},{1,17},{17,1},{2,18},{18,2},{3,19},{19,3},{4,20},{20... | collective-permute-start | bytes 1105928 | tf_op jit(solution)/shard_map/ppermute | solution.py:1006
  207.0 2.1 shard_map.276
  209.1 3.4 %collective-permute-done.60.refs_1_ = bf16[240,768]{1,0:T(8,128)(2,1)S(1)} collective-permute-done((bf16[240,768]{1,0:T(8,128)(2,1)S(1)}, bf16[240,768]{1,0:T(8,128)(2,1)S(1)}, u32[]{:S(2)}, u32[]{:S(2)}) %collective-permute-start.60) | collective-permute-done | bytes 368672 | tf_op jit(solution)/shard_map/ppermute | solution.py:1006
  212.5 2.0 collective-permute-done.61.refs_5_
  215.0 1.7 collective-permute-done.62.refs_2_
  217.3 3.7 %shard_map.277 = (f32[2,576,768]{2,1,0:T(8,128)}, f32[2,192,768]{2,1,0:T(8,128)}, f32[2,192,768]{2,1,0:T(8,128)}, f32[3,3,2,128]{3,2,1,0:T(2,128)}, f32[2,2,192]...) custom-call(s32[5]{0:T(128)S(1)} %copy-done.9, ...), custom_call_target="tpu_custom_call" | custom-call | flops 110000000 | bytes 350000 | tf_op jit(solution)/shard_map/pallas_call | solution.py:49
  (169 shorter events, 59.2 us)
Async XLA Ops:
  5.2 10.6 %collective-permute-start.3 = (bf16[272,768]{1,0:T(8,128)(2,1)}, bf16[272,768]{1,0:T(8,128)(2,1)}, u32[]{:S(2)}, u32[]{:S(2)}) collective-permute-start(bf16[272,768]{1,0:T(8,128)(2,1)} %get-tuple-element.174.refs_2_), channel_id=1, source_target_pairs={{0,4},{4,0},{1,5},{5,1},{2,6},{6,2},{3,7},{7,3},{8,12},{12,8},{9,1... | collective-permute-start | bytes 1253384 | tf_op jit(solution)/shard_map/ppermute | solution.py:1006
  5.8 22.0 %collective-permute-start.4 = (bf16[256,768]{1,0:T(8,128)(2,1)}, bf16[256,768]{1,0:T(8,128)(2,1)S(1)}, u32[]{:S(2)}, u32[]{:S(2)}) collective-permute-start(bf16[256,768]{1,0:T(8,128)(2,1)} %get-tuple-element.177), channel_id=1, source_target_pairs={{0,2},{2,0},{1,3},{3,1},{4,6},{6,4},{5,7},{7,5},{8,10},{10,8},{9,1... | collective-permute-start | bytes 1179656 | tf_op jit(solution)/shard_map/ppermute | solution.py:1006
  9.4 16.2 %collective-permute-start = (bf16[144,768]{1,0:T(8,128)(2,1)}, bf16[144,768]{1,0:T(8,128)(2,1)}, u32[]{:S(2)}, u32[]{:S(2)}) collective-permute-start(bf16[144,768]{1,0:T(8,128)(2,1)} %get-tuple-element.170), channel_id=1, source_target_pairs={{0,8},{8,0},{1,9},{9,1},{2,10},{10,2},{3,11},{11,3},{4,12},{12,4},... | collective-permute-start | bytes 663560 | tf_op jit(solution)/shard_map/ppermute | solution.py:1006
  11.0 13.3 %collective-permute-start.1 = (bf16[128,768]{1,0:T(8,128)(2,1)}, bf16[128,768]{1,0:T(8,128)(2,1)}, u32[]{:S(2)}, u32[]{:S(2)}) collective-permute-start(bf16[128,768]{1,0:T(8,128)(2,1)} %get-tuple-element.171), channel_id=1, source_target_pairs={{0,8},{8,0},{1,9},{9,1},{2,10},{10,2},{3,11},{11,3},{4,12},{12,4},... | collective-permute-start | bytes 589832 | tf_op jit(solution)/shard_map/ppermute | solution.py:1006
  11.4 14.2 %collective-permute-start.2 = (bf16[128,768]{1,0:T(8,128)(2,1)}, bf16[128,768]{1,0:T(8,128)(2,1)}, u32[]{:S(2)}, u32[]{:S(2)}) collective-permute-start(bf16[128,768]{1,0:T(8,128)(2,1)} %get-tuple-element.172), channel_id=1, source_target_pairs={{0,8},{8,0},{1,9},{9,1},{2,10},{10,2},{3,11},{11,3},{4,12},{12,4},... | collective-permute-start | bytes 589832 | tf_op jit(solution)/shard_map/ppermute | solution.py:1006
  28.3 22.8 %collective-permute-start.10 = (bf16[256,768]{1,0:T(8,128)(2,1)S(1)}, bf16[256,768]{1,0:T(8,128)(2,1)S(1)}, u32[]{:S(2)}, u32[]{:S(2)}) collective-permute-start(bf16[256,768]{1,0:T(8,128)(2,1)S(1)} %collective-permute-done.4.refs_3_.refs_8_), channel_id=1, source_target_pairs={{0,24},{8,16},{16,8},{24,0},{1,25},{9,17},{17,9},{25,1},{2,26},{10... | collective-permute-start | bytes 1179656 | tf_op jit(solution)/shard_map/ppermute | solution.py:1011
  30.8 20.3 %collective-permute-start.9 = (bf16[256,768]{1,0:T(8,128)(2,1)S(1)}, bf16[256,768]{1,0:T(8,128)(2,1)S(1)}, u32[]{:S(2)}, u32[]{:S(2)}) collective-permute-start(bf16[256,768]{1,0:T(8,128)(2,1)S(1)} %collective-permute-done.4.refs_3_.refs_8_), channel_id=1, source_target_pairs={{0,16},{16,0},{1,17},{17,1},{2,18},{18,2},{3,19},{19,3},{4,20},{20... | collective-permute-start | bytes 1179656 | tf_op jit(solution)/shard_map/ppermute | solution.py:1006
  31.3 19.7 %collective-permute-start.8 = (bf16[256,768]{1,0:T(8,128)(2,1)S(1)}, bf16[256,768]{1,0:T(8,128)(2,1)S(1)}, u32[]{:S(2)}, u32[]{:S(2)}) collective-permute-start(bf16[256,768]{1,0:T(8,128)(2,1)S(1)} %collective-permute-done.4.refs_3_.refs_8_), channel_id=1, source_target_pairs={{0,8},{8,0},{1,9},{9,1},{2,10},{10,2},{3,11},{11,3},{4,12},{12,4},... | collective-permute-start | bytes 1179656 | tf_op jit(solution)/shard_map/ppermute | solution.py:1006
  31.8 19.3 %collective-permute-start.7 = (bf16[192,768]{1,0:T(8,128)(2,1)S(1)}, bf16[192,768]{1,0:T(8,128)(2,1)S(1)}, u32[]{:S(2)}, u32[]{:S(2)}) collective-permute-start(bf16[192,768]{1,0:T(8,128)(2,1)S(1)} %copy-done.17), channel_id=1, source_target_pairs={{0,2},{2,0},{1,3},{3,1},{4,6},{6,4},{5,7},{7,5},{8,10},{10,8},{9,1... | collective-permute-start | bytes 884744 | tf_op jit(solution)/shard_map/ppermute | solution.py:1006
  39.7 14.4 %collective-permute-start.11 = (bf16[256,192]{1,0:T(8,128)(2,1)S(1)}, bf16[256,192]{1,0:T(8,128)(2,1)S(1)}, u32[]{:S(2)}, u32[]{:S(2)}) collective-permute-start(bf16[256,192]{1,0:T(8,128)(2,1)S(1)} %get-tuple-element.192.refs_7_), channel_id=1, source_target_pairs={{0,2},{2,0},{1,3},{3,1},{4,6},{6,4},{5,7},{7,5},{8,10},{10,8},{9,1... | collective-permute-start | bytes 294920 | tf_op jit(solution)/shard_map/ppermute | solution.py:1006
  51.1 6.8 %collective-permute-start.14 = (bf16[192,768]{1,0:T(8,128)(2,1)S(1)}, bf16[192,768]{1,0:T(8,128)(2,1)S(1)}, u32[]{:S(2)}, u32[]{:S(2)}) collective-permute-start(bf16[192,768]{1,0:T(8,128)(2,1)S(1)} %collective-permute-done.7.refs_12_), channel_id=1, source_target_pairs={{0,16},{16,0},{1,17},{17,1},{2,18},{18,2},{3,19},{19,3},{4,20},{20... | collective-permute-start | bytes 884744 | tf_op jit(solution)/shard_map/ppermute | solution.py:1006
  52.6 6.7 %collective-permute-start.13 = (bf16[192,768]{1,0:T(8,128)(2,1)S(1)}, bf16[192,768]{1,0:T(8,128)(2,1)S(1)}, u32[]{:S(2)}, u32[]{:S(2)}) collective-permute-start(bf16[192,768]{1,0:T(8,128)(2,1)S(1)} %collective-permute-done.7.refs_12_), channel_id=1, source_target_pairs={{0,8},{8,0},{1,9},{9,1},{2,10},{10,2},{3,11},{11,3},{4,12},{12,4},... | collective-permute-start | bytes 884744 | tf_op jit(solution)/shard_map/ppermute | solution.py:1006
  59.9 5.7 %collective-permute-start.15 = (bf16[128,768]{1,0:T(8,128)(2,1)S(1)}, bf16[128,768]{1,0:T(8,128)(2,1)S(1)}, u32[]{:S(2)}, u32[]{:S(2)}) collective-permute-start(bf16[128,768]{1,0:T(8,128)(2,1)S(1)} %shard_map.251.refs_0_), channel_id=1, source_target_pairs={{0,1},{1,0},{2,3},{3,2},{4,5},{5,4},{6,7},{7,6},{8,9},{9,8},{10,11... | collective-permute-start | bytes 589832 | tf_op jit(solution)/shard_map/ppermute | solution.py:1006
  60.4 8.3 %collective-permute-start.17 = (bf16[192,768]{1,0:T(8,128)(2,1)S(1)}, bf16[192,768]{1,0:T(8,128)(2,1)S(1)}, u32[]{:S(2)}, u32[]{:S(2)}) collective-permute-start(bf16[192,768]{1,0:T(8,128)(2,1)S(1)} %collective-permute-done.7.refs_12_), channel_id=1, source_target_pairs={{0,24},{8,16},{16,8},{24,0},{1,25},{9,17},{17,9},{25,1},{2,26},{10... | collective-permute-start | bytes 884744 | tf_op jit(solution)/shard_map/ppermute | solution.py:1011
  66.3 12.5 %collective-permute-start.19 = (bf16[128,768]{1,0:T(8,128)(2,1)S(1)}, bf16[128,768]{1,0:T(8,128)(2,1)S(1)}, u32[]{:S(2)}, u32[]{:S(2)}) collective-permute-start(bf16[128,768]{1,0:T(8,128)(2,1)S(1)} %shard_map.252.refs_1_), channel_id=1, source_target_pairs={{0,2},{2,0},{1,3},{3,1},{4,6},{6,4},{5,7},{7,5},{8,10},{10,8},{9,1... | collective-permute-start | bytes 589832 | tf_op jit(solution)/shard_map/ppermute | solution.py:1006
  71.5 10.9 %collective-permute-start.21 = (bf16[2,128,768]{2,1,0:T(8,128)(2,1)S(1)}, bf16[2,128,768]{2,1,0:T(8,128)(2,1)S(1)}, u32[]{:S(2)}, u32[]{:S(2)}) collective-permute-start(bf16[2,128,768]{2,1,0:T(8,128)(2,1)S(1)} %copy-done.16), channel_id=1, source_target_pairs={{0,8},{8,0},{1,9},{9,1},{2,10},{10,2},{3,11},{11,3},{4,12},{12,4},... | collective-permute-start | bytes 1179656 | tf_op jit(solution)/shard_map/ppermute | solution.py:1006
  73.2 14.0 %collective-permute-start.18 = (bf16[256,768]{1,0:T(8,128)(2,1)S(1)}, bf16[256,768]{1,0:T(8,128)(2,1)S(1)}, u32[]{:S(2)}, u32[]{:S(2)}) collective-permute-start(bf16[256,768]{1,0:T(8,128)(2,1)S(1)} %get-tuple-element.211.refs_5_.refs_0_), channel_id=1, source_target_pairs={{0,1},{1,0},{2,3},{3,2},{4,5},{5,4},{6,7},{7,6},{8,9},{9,8},{10,11... | collective-permute-start | bytes 1179656 | tf_op jit(solution)/shard_map/ppermute | solution.py:1006
  74.5 8.1 %collective-permute-start.22 = (bf16[128,768]{1,0:T(8,128)(2,1)S(1)}, bf16[128,768]{1,0:T(8,128)(2,1)S(1)}, u32[]{:S(2)}, u32[]{:S(2)}) collective-permute-start(bf16[128,768]{1,0:T(8,128)(2,1)S(1)} %copy-done.18), channel_id=1, source_target_pairs={{0,4},{4,0},{1,5},{5,1},{2,6},{6,2},{3,7},{7,3},{8,12},{12,8},{9,1... | collective-permute-start | bytes 589832 | tf_op jit(solution)/shard_map/ppermute | solution.py:1006
  82.4 6.3 %collective-permute-start.23 = (bf16[2,128,768]{2,1,0:T(8,128)(2,1)S(1)}, bf16[2,128,768]{2,1,0:T(8,128)(2,1)S(1)}, u32[]{:S(2)}, u32[]{:S(2)}) collective-permute-start(bf16[2,128,768]{2,1,0:T(8,128)(2,1)S(1)} %collective-permute-done.21), channel_id=1, source_target_pairs={{0,4},{4,0},{1,5},{5,1},{2,6},{6,2},{3,7},{7,3},{8,12},{12,8},{9,1... | collective-permute-start | bytes 1179656 | tf_op jit(solution)/shard_map/ppermute | solution.py:1006
  87.8 12.1 %collective-permute-start.26 = (bf16[128,768]{1,0:T(8,128)(2,1)S(1)}, bf16[128,768]{1,0:T(8,128)(2,1)S(1)}, u32[]{:S(2)}, u32[]{:S(2)}) collective-permute-start(bf16[128,768]{1,0:T(8,128)(2,1)S(1)} %get-tuple-element.213.refs_3_), channel_id=1, source_target_pairs={{0,2},{2,0},{1,3},{3,1},{4,6},{6,4},{5,7},{7,5},{8,10},{10,8},{9,1... | collective-permute-start | bytes 589832 | tf_op jit(solution)/shard_map/ppermute | solution.py:1006
  92.6 15.6 %collective-permute-start.25 = (bf16[256,768]{1,0:T(8,128)(2,1)S(1)}, bf16[256,768]{1,0:T(8,128)(2,1)S(1)}, u32[]{:S(2)}, u32[]{:S(2)}) collective-permute-start(bf16[256,768]{1,0:T(8,128)(2,1)S(1)} %get-tuple-element.223.refs_4_), channel_id=1, source_target_pairs={{0,1},{1,0},{2,3},{3,2},{4,5},{5,4},{6,7},{7,6},{8,9},{9,8},{10,11... | collective-permute-start | bytes 1179656 | tf_op jit(solution)/shard_map/ppermute | solution.py:1006
  95.3 13.0 %collective-permute-start.27 = (bf16[2,64,768]{2,1,0:T(8,128)(2,1)S(1)}, bf16[2,64,768]{2,1,0:T(8,128)(2,1)S(1)}, u32[]{:S(2)}, u32[]{:S(2)}) collective-permute-start(bf16[2,64,768]{2,1,0:T(8,128)(2,1)S(1)} %pad_maximum_fusion.1), channel_id=1, source_target_pairs={{0,8},{8,0},{1,9},{9,1},{2,10},{10,2},{3,11},{11,3},{4,12},{12,4},... | collective-permute-start | bytes 589832 | tf_op jit(solution)/shard_map/ppermute | solution.py:1006
  109.7 8.2 %collective-permute-start.28 = (bf16[128,768]{1,0:T(8,128)(2,1)S(1)}, bf16[128,768]{1,0:T(8,128)(2,1)S(1)}, u32[]{:S(2)}, u32[]{:S(2)}) collective-permute-start(bf16[128,768]{1,0:T(8,128)(2,1)S(1)} %collective-permute-done.26.refs_3_), channel_id=1, source_target_pairs={{0,1},{1,0},{2,3},{3,2},{4,5},{5,4},{6,7},{7,6},{8,9},{9,8},{10,11... | collective-permute-start | bytes 589832 | tf_op jit(solution)/shard_map/ppermute | solution.py:1006
  112.2 11.3 %collective-permute-start.30 = (bf16[256,192]{1,0:T(8,128)(2,1)S(1)}, bf16[256,192]{1,0:T(8,128)(2,1)S(1)}, u32[]{:S(2)}, u32[]{:S(2)}) collective-permute-start(bf16[256,192]{1,0:T(8,128)(2,1)S(1)} %get-tuple-element.234), channel_id=1, source_target_pairs={{0,2},{2,0},{1,3},{3,1},{4,6},{6,4},{5,7},{7,5},{8,10},{10,8},{9,1... | collective-permute-start | bytes 294920 | tf_op jit(solution)/shard_map/ppermute | solution.py:1006
  122.9 14.9 %collective-permute-start.36 = (bf16[384,768]{1,0:T(8,128)(2,1)S(1)}, bf16[384,768]{1,0:T(8,128)(2,1)S(1)}, u32[]{:S(2)}, u32[]{:S(2)}) collective-permute-start(bf16[384,768]{1,0:T(8,128)(2,1)S(1)} %get-tuple-element.268), channel_id=1, source_target_pairs={{0,16},{16,0},{1,17},{17,1},{2,18},{18,2},{3,19},{19,3},{4,20},{20... | collective-permute-start | bytes 1769480 | tf_op jit(solution)/shard_map/ppermute | solution.py:1006
  123.6 14.6 %collective-permute-start.37 = (bf16[384,768]{1,0:T(8,128)(2,1)S(1)}, bf16[384,768]{1,0:T(8,128)(2,1)S(1)}, u32[]{:S(2)}, u32[]{:S(2)}) collective-permute-start(bf16[384,768]{1,0:T(8,128)(2,1)S(1)} %get-tuple-element.270), channel_id=1, source_target_pairs={{0,8},{8,0},{1,9},{9,1},{2,10},{10,2},{3,11},{11,3},{4,12},{12,4},... | collective-permute-start | bytes 1769480 | tf_op jit(solution)/shard_map/ppermute | solution.py:1006
  123.6 7.6 %collective-permute-start.31 = (bf16[80,768]{1,0:T(8,128)(2,1)S(1)}, bf16[80,768]{1,0:T(8,128)(2,1)S(1)}, u32[]{:S(2)}, u32[]{:S(2)}) collective-permute-start(bf16[80,768]{1,0:T(8,128)(2,1)S(1)} %get-tuple-element.250.refs_1_), channel_id=1, source_target_pairs={{0,2},{2,0},{1,3},{3,1},{4,6},{6,4},{5,7},{7,5},{8,10},{10,8},{9,1... | collective-permute-start | bytes 368648 | tf_op jit(solution)/shard_map/ppermute | solution.py:1006
  134.1 15.4 %collective-permute-start.35 = (bf16[3,128,768]{2,1,0:T(8,128)(2,1)S(1)}, bf16[3,128,768]{2,1,0:T(8,128)(2,1)S(1)}, u32[]{:S(2)}, u32[]{:S(2)}) collective-permute-start(bf16[3,128,768]{2,1,0:T(8,128)(2,1)S(1)} %get-tuple-element.258.refs_4_), channel_id=1, source_target_pairs={{0,1},{1,0},{2,3},{3,2},{4,5},{5,4},{6,7},{7,6},{8,9},{9,8},{10,11... | collective-permute-start | bytes 1769480 | tf_op jit(solution)/shard_map/ppermute | solution.py:1006
  139.0 13.7 %collective-permute-start.40 = (bf16[384,768]{1,0:T(8,128)(2,1)S(1)}, bf16[384,768]{1,0:T(8,128)(2,1)S(1)}, u32[]{:S(2)}, u32[]{:S(2)}) collective-permute-start(bf16[384,768]{1,0:T(8,128)(2,1)S(1)} %get-tuple-element.276.refs_2_), channel_id=1, source_target_pairs={{0,16},{16,0},{1,17},{17,1},{2,18},{18,2},{3,19},{19,3},{4,20},{20... | collective-permute-start | bytes 1769480 | tf_op jit(solution)/shard_map/ppermute | solution.py:1006
  140.4 13.4 %collective-permute-start.39 = (bf16[384,768]{1,0:T(8,128)(2,1)S(1)}, bf16[384,768]{1,0:T(8,128)(2,1)S(1)}, u32[]{:S(2)}, u32[]{:S(2)}) collective-permute-start(bf16[384,768]{1,0:T(8,128)(2,1)S(1)} %get-tuple-element.271.refs_2_.refs_0_), channel_id=1, source_target_pairs={{0,8},{8,0},{1,9},{9,1},{2,10},{10,2},{3,11},{11,3},{4,12},{12,4},... | collective-permute-start | bytes 1769480 | tf_op jit(solution)/shard_map/ppermute | solution.py:1006
  154.6 17.7 %collective-permute-start.47 = (bf16[384,768]{1,0:T(8,128)(2,1)S(1)}, bf16[384,768]{1,0:T(8,128)(2,1)S(1)}, u32[]{:S(2)}, u32[]{:S(2)}) collective-permute-start(bf16[384,768]{1,0:T(8,128)(2,1)S(1)} %get-tuple-element.298.refs_4_), channel_id=1, source_target_pairs={{0,8},{8,0},{1,9},{9,1},{2,10},{10,2},{3,11},{11,3},{4,12},{12,4},... | collective-permute-start | bytes 1769480 | tf_op jit(solution)/shard_map/ppermute | solution.py:1006
  155.3 17.1 %collective-permute-start.46 = (bf16[384,768]{1,0:T(8,128)(2,1)S(1)}, bf16[384,768]{1,0:T(8,128)(2,1)S(1)}, u32[]{:S(2)}, u32[]{:S(2)}) collective-permute-start(bf16[384,768]{1,0:T(8,128)(2,1)S(1)} %get-tuple-element.296.refs_2_.refs_0_), channel_id=1, source_target_pairs={{0,16},{16,0},{1,17},{17,1},{2,18},{18,2},{3,19},{19,3},{4,20},{20... | collective-permute-start | bytes 1769480 | tf_op jit(solution)/shard_map/ppermute | solution.py:1006
  155.9 13.3 %collective-permute-start.38 = (bf16[3,64,768]{2,1,0:T(8,128)(2,1)S(1)}, bf16[3,64,768]{2,1,0:T(8,128)(2,1)S(1)}, u32[]{:S(2)}, u32[]{:S(2)}) collective-permute-start(bf16[3,64,768]{2,1,0:T(8,128)(2,1)S(1)} %get-tuple-element.275.refs_4_), channel_id=1, source_target_pairs={{0,2},{2,0},{1,3},{3,1},{4,6},{6,4},{5,7},{7,5},{8,10},{10,8},{9,1... | collective-permute-start | bytes 884744 | tf_op jit(solution)/shard_map/ppermute | solution.py:1006
  156.8 14.0 %collective-permute-start.45 = (bf16[192,768]{1,0:T(8,128)(2,1)S(1)}, bf16[192,768]{1,0:T(8,128)(2,1)S(1)}, u32[]{:S(2)}, u32[]{:S(2)}) collective-permute-start(bf16[192,768]{1,0:T(8,128)(2,1)S(1)} %get-tuple-element.286), channel_id=1, source_target_pairs={{0,4},{4,0},{1,5},{5,1},{2,6},{6,2},{3,7},{7,3},{8,12},{12,8},{9,1... | collective-permute-start | bytes 884744 | tf_op jit(solution)/shard_map/ppermute | solution.py:1006
  156.8 14.0 %collective-permute-start.34 = (bf16[80,768]{1,0:T(8,128)(2,1)S(1)}, bf16[80,768]{1,0:T(8,128)(2,1)S(1)}, u32[]{:S(2)}, u32[]{:S(2)}) collective-permute-start(bf16[80,768]{1,0:T(8,128)(2,1)S(1)} %collective-permute-done.31.refs_2_), channel_id=1, source_target_pairs={{0,1},{1,0},{2,3},{3,2},{4,5},{5,4},{6,7},{7,6},{8,9},{9,8},{10,11... | collective-permute-start | bytes 368648 | tf_op jit(solution)/shard_map/ppermute | solution.py:1006
  175.7 6.1 %collective-permute-start.54 = (bf16[384,768]{1,0:T(8,128)(2,1)S(1)}, bf16[384,768]{1,0:T(8,128)(2,1)S(1)}, u32[]{:S(2)}, u32[]{:S(2)}) collective-permute-start(bf16[384,768]{1,0:T(8,128)(2,1)S(1)} %collective-permute-done.47.refs_14_.refs_5_), channel_id=1, source_target_pairs={{0,4},{4,0},{1,5},{5,1},{2,6},{6,2},{3,7},{7,3},{8,12},{12,8},{9,1... | collective-permute-start | bytes 1769480 | tf_op jit(solution)/shard_map/ppermute | solution.py:1006
  176.2 11.6 %collective-permute-start.50 = (bf16[256,768]{1,0:T(8,128)(2,1)S(1)}, bf16[256,768]{1,0:T(8,128)(2,1)S(1)}, u32[]{:S(2)}, u32[]{:S(2)}) collective-permute-start(bf16[256,768]{1,0:T(8,128)(2,1)S(1)} %get-tuple-element.294), channel_id=1, source_target_pairs={{0,8},{8,0},{1,9},{9,1},{2,10},{10,2},{3,11},{11,3},{4,12},{12,4},... | collective-permute-start | bytes 1179656 | tf_op jit(solution)/shard_map/ppermute | solution.py:1006
  177.2 10.6 %collective-permute-start.49 = (bf16[240,768]{1,0:T(8,128)(2,1)S(1)}, bf16[240,768]{1,0:T(8,128)(2,1)S(1)}, u32[]{:S(2)}, u32[]{:S(2)}) collective-permute-start(bf16[240,768]{1,0:T(8,128)(2,1)S(1)} %get-tuple-element.292), channel_id=1, source_target_pairs={{0,16},{16,0},{1,17},{17,1},{2,18},{18,2},{3,19},{19,3},{4,20},{20... | collective-permute-start | bytes 1105928 | tf_op jit(solution)/shard_map/ppermute | solution.py:1006
  178.6 14.1 %collective-permute-start.58 = (bf16[2,3,32,768]{3,2,1,0:T(8,128)(2,1)S(1)}, bf16[2,3,32,768]{3,2,1,0:T(8,128)(2,1)S(1)}, u32[]{:S(2)}, u32[]{:S(2)}) collective-permute-start(bf16[2,3,32,768]{3,2,1,0:T(8,128)(2,1)S(1)} %pad_maximum_fusion.refs_8_), channel_id=1, source_target_pairs={{0,1},{1,0},{2,3},{3,2},{4,5},{5,4},{6,7},{7,6},{8,9},{9,8},{10,11... | collective-permute-start | bytes 884744 | tf_op jit(solution)/shard_map/ppermute | solution.py:1006
  178.8 16.4 %collective-permute-start.57 = (bf16[2,3,32,768]{3,2,1,0:T(8,128)(2,1)S(1)}, bf16[2,3,32,768]{3,2,1,0:T(8,128)(2,1)S(1)}, u32[]{:S(2)}, u32[]{:S(2)}) collective-permute-start(bf16[2,3,32,768]{3,2,1,0:T(8,128)(2,1)S(1)} %pad_maximum_fusion.refs_8_), channel_id=1, source_target_pairs={{0,2},{2,0},{1,3},{3,1},{4,6},{6,4},{5,7},{7,5},{8,10},{10,8},{9,1... | collective-permute-start | bytes 884744 | tf_op jit(solution)/shard_map/ppermute | solution.py:1006
  181.8 13.4 %collective-permute-start.41 = (bf16[2,64,768]{2,1,0:T(8,128)(2,1)S(1)}, bf16[2,64,768]{2,1,0:T(8,128)(2,1)S(1)}, u32[]{:S(2)}, u32[]{:S(2)}) collective-permute-start(bf16[2,64,768]{2,1,0:T(8,128)(2,1)S(1)} %get-tuple-element.279), channel_id=1, source_target_pairs={{0,4},{4,0},{1,5},{5,1},{2,6},{6,2},{3,7},{7,3},{8,12},{12,8},{9,1... | collective-permute-start | bytes 589832 | tf_op jit(solution)/shard_map/ppermute | solution.py:1006
  188.5 13.4 %collective-permute-start.55 = (bf16[240,768]{1,0:T(8,128)(2,1)S(1)}, bf16[240,768]{1,0:T(8,128)(2,1)S(1)}, u32[]{:S(2)}, u32[]{:S(2)}) collective-permute-start(bf16[240,768]{1,0:T(8,128)(2,1)S(1)} %get-tuple-element.302.refs_0_), channel_id=1, source_target_pairs={{0,8},{8,0},{1,9},{9,1},{2,10},{10,2},{3,11},{11,3},{4,12},{12,4},... | collective-permute-start | bytes 1105928 | tf_op jit(solution)/shard_map/ppermute | solution.py:1006
  189.6 12.4 %collective-permute-start.56 = (bf16[256,768]{1,0:T(8,128)(2,1)S(1)}, bf16[256,768]{1,0:T(8,128)(2,1)S(1)}, u32[]{:S(2)}, u32[]{:S(2)}) collective-permute-start(bf16[256,768]{1,0:T(8,128)(2,1)S(1)} %get-tuple-element.303.refs_2_), channel_id=1, source_target_pairs={{0,16},{16,0},{1,17},{17,1},{2,18},{18,2},{3,19},{19,3},{4,20},{20... | collective-permute-start | bytes 1179656 | tf_op jit(solution)/shard_map/ppermute | solution.py:1006
  195.2 6.7 %collective-permute-start.59 = (bf16[2,3,32,768]{3,2,1,0:T(8,128)(2,1)S(1)}, bf16[2,3,32,768]{3,2,1,0:T(8,128)(2,1)S(1)}, u32[]{:S(2)}, u32[]{:S(2)}) collective-permute-start(bf16[2,3,32,768]{3,2,1,0:T(8,128)(2,1)S(1)} %collective-permute-done.57.refs_2_), channel_id=1, source_target_pairs={{0,1},{1,0},{2,3},{3,2},{4,5},{5,4},{6,7},{7,6},{8,9},{9,8},{10,11... | collective-permute-start | bytes 884744 | tf_op jit(solution)/shard_map/ppermute | solution.py:1006
  195.3 10.1 %collective-permute-start.42 = (bf16[2,64,768]{2,1,0:T(8,128)(2,1)S(1)}, bf16[2,64,768]{2,1,0:T(8,128)(2,1)S(1)}, u32[]{:S(2)}, u32[]{:S(2)}) collective-permute-start(bf16[2,64,768]{2,1,0:T(8,128)(2,1)S(1)} %pad_maximum_fusion.2), channel_id=1, source_target_pairs={{0,8},{8,0},{1,9},{9,1},{2,10},{10,2},{3,11},{11,3},{4,12},{12,4},... | collective-permute-start | bytes 589832 | tf_op jit(solution)/shard_map/ppermute | solution.py:1006
  202.7 9.8 %collective-permute-start.60 = (bf16[240,768]{1,0:T(8,128)(2,1)S(1)}, bf16[240,768]{1,0:T(8,128)(2,1)S(1)}, u32[]{:S(2)}, u32[]{:S(2)}) collective-permute-start(bf16[240,768]{1,0:T(8,128)(2,1)S(1)} %get-tuple-element.305.refs_8_.refs_5_.refs_0_), channel_id=1, source_target_pairs={{0,16},{16,0},{1,17},{17,1},{2,18},{18,2},{3,19},{19,3},{4,20},{20... | collective-permute-start | bytes 1105928 | tf_op jit(solution)/shard_map/ppermute | solution.py:1006
  205.4 9.1 %collective-permute-start.61 = (bf16[256,768]{1,0:T(8,128)(2,1)S(1)}, bf16[256,768]{1,0:T(8,128)(2,1)S(1)}, u32[]{:S(2)}, u32[]{:S(2)}) collective-permute-start(bf16[256,768]{1,0:T(8,128)(2,1)S(1)} %get-tuple-element.310.refs_4_), channel_id=1, source_target_pairs={{0,8},{8,0},{1,9},{9,1},{2,10},{10,2},{3,11},{11,3},{4,12},{12,4},... | collective-permute-start | bytes 1179656 | tf_op jit(solution)/shard_map/ppermute | solution.py:1006
  205.4 11.3 %collective-permute-start.64 = (bf16[256,768]{1,0:T(8,128)(2,1)S(1)}, bf16[256,768]{1,0:T(8,128)(2,1)S(1)}, u32[]{:S(2)}, u32[]{:S(2)}) collective-permute-start(bf16[256,768]{1,0:T(8,128)(2,1)S(1)} %get-tuple-element.310.refs_4_), channel_id=1, source_target_pairs={{0,4},{4,0},{1,5},{5,1},{2,6},{6,2},{3,7},{7,3},{8,12},{12,8},{9,1... | collective-permute-start | bytes 1179656 | tf_op jit(solution)/shard_map/ppermute | solution.py:1006
  (37 other events, 207.2 us)

commit v7 on v6

--- a/solution.py
+++ b/solution.py
@@ -574,15 +574,22 @@
     hid_ref[...] = (total + mm(dup, upp_ref[...], NT)).astype(BF16)
 
 
+def ffn_own_kernel(p_ref, normed_ref, active_ref, dlow_ref, dup_ref, up_ref, down_ref, bias_ref):
+    dup = dup_ref[...]
+    up_ref[...] = mm(normed_ref[...], dup, TN)
+    down_ref[...] = mm(active_ref[...], dlow_ref[...], TN)
+    bias = jnp.sum(dup.astype(F32), axis=0, keepdims=True)
+    bias_ref[...] = jnp.broadcast_to(bias, bias_ref.shape)
+
+
 def ffn_grad_kernel(
     p_ref,
-    normed_ref,
+    upa_ref,
+    downa_ref,
+    biasa_ref,
     normedo_ref,
-    active_ref,
     activeo_ref,
-    dlow_ref,
     dlowo_ref,
-    dup_ref,
     slopeo_ref,
     down_ref,
     upk_ref,
@@ -594,16 +601,12 @@
 ):
     dlowo = dlowo_ref[...]
     dupo = (mm(dlowo, down_ref[...], NT) * slopeo_ref[...].astype(F32)).astype(BF16)
-    dup = dup_ref[...]
-    all_ref[...] = (mm(normed_ref[...], dup, TN) + mm(normedo_ref[...], dupo, TN)).astype(BF16)
+    all_ref[...] = (upa_ref[...] + mm(normedo_ref[...], dupo, TN)).astype(BF16)
     dealt(all_ref, p_ref[1], upk_ref, ups_ref)
-    all_ref[...] = (
-        mm(active_ref[...], dlow_ref[...], TN) + mm(activeo_ref[...], dlowo, TN)
-    ).astype(BF16)
+    all_ref[...] = (downa_ref[...] + mm(activeo_ref[...], dlowo, TN)).astype(BF16)
     dealt(all_ref, p_ref[2], downk_ref, downs_ref)
-    bias = jnp.sum(dup.astype(F32), axis=0, keepdims=True)
-    bias = bias + jnp.sum(dupo.astype(F32), axis=0, keepdims=True)
-    bias_ref[...] = jnp.broadcast_to(bias, bias_ref.shape)
+    bias = jnp.sum(dupo.astype(F32), axis=0, keepdims=True)
+    bias_ref[...] = biasa_ref[...] + jnp.broadcast_to(bias, bias_ref.shape)
 
 
 def first_kernel(
@@ -1208,7 +1211,7 @@
         ],
     )
     low_recv = swap(low, "zl")
-    cot_far, cot_near, low = join(cot_far, cot_near, low)
+    cot_far, cot_near, mixed0 = join(cot_far, cot_near, mixed0)
     cot10 = swap(cot_far, "y")
     cot01 = swap(cot_near, "core")
     mixed_far1 = swap(mixed_far0, "core")
@@ -1257,6 +1260,12 @@
         [rows_of(half), ((half, hidden), BF16)],
     )
     hid_recv = swap(hid, "zl")
+    up_own, down_own, bias_own = run(
+        ffn_own_kernel,
+        [normed, (active, (0, None, None)), dlow, dup],
+        [((width, hidden), F32), rows_of(hidden, F32), ((8, hidden), F32)],
+        after=[hid],
+    )
     out_core = swap(out_send, "core")
     out_y = swap(jnp.stack([out_keep[1], out_core[1]]), "y")
     hid_recv, far_low0, out_y = join(hid_recv, far_low0, out_y)
@@ -1265,6 +1274,7 @@
         first_kernel,
         [x_own, mixed0, mixed1, second, hid, hid_recv, gains],
         [rows_of(half, F32), rows_of(half), rows_of(8, F32)],
+        after=[bias_own],
     )
     dmix_core = swap(dmix, "core")
     datt, datt_send, dmix, pay = run(
@@ -1284,13 +1294,12 @@
     up_keep, up_send, down_keep, down_send, bias_grad = run(
         ffn_grad_kernel,
         [
-            normed,
+            up_own,
+            down_own,
+            bias_own,
             normed_far,
-            (active, (0, None, None)),
             active_far,
-            dlow,
             dlow_far,
-            dup,
             slope_far,
             down,
         ],

time: 221 us -> 220 us (level)
  waiting for transfers between devices: 94.2 us -> 90.9 us
    ppermute x64, waiting for transfers between devices: 93.7 us -> 86 us  [swap(): return lax.ppermute(value, axis, [(i, i ^ step) for i in range(size)])]
    ppermute x2, waiting for transfers between devices: 0.46 us -> 4.89 us  [swap_both(): lax.ppermute(value, ('batch', 'y'), [(i, i ^ 3) for i in range(size)])]
    pallas_call x32 -> x33, Pallas kernels: 66.3 us -> 67.1 us  [kernel_call(): pl.pallas_call(kernel, out_shape=[jax.ShapeDtypeStruct(out[0], out[1]) fo...]
    unnamed x39 -> x37, local copies, waits for them, and re-layouts: 6.05 us -> 6.05 us
  transfers between devices with their start and end apart: 66 -> 66, of which waited for: 36 -> 36; matrix products, arithmetic and copies ran while one was open for 0% -> 0% of each run, Pallas kernels for 25% -> 26%
where the time goes in v7:
time: 220 us; the launch traced here: 219 us
  waiting for transfers between devices  90.9 us (41%)
  Pallas kernels  67.1 us (30%)
  starting transfers between devices  53.4 us (24%)
  local copies, waits for them, and re-layouts  6.79 us (3%)
    ppermute x64, waiting for transfers between devices, swap(): return lax.ppermute(value, axis, [(i, i ^ step) for i in range(size)])  86 us
    pallas_call x33, Pallas kernels, kernel_call(): pl.pallas_call(kernel, out_shape=[jax.ShapeDtypeStruct(out[0], out[1]) fo...  67.1 us
    ppermute x64, starting transfers between devices, swap(): return lax.ppermute(value, axis, [(i, i ^ step) for i in range(size)])  50.4 us
    unnamed x37, local copies, waits for them, and re-layouts  6.05 us
    ppermute x2, waiting for transfers between devices, swap_both(): lax.ppermute(value, ('batch', 'y'), [(i, i ^ 3) for i in range(size)])  4.89 us
  transfers between devices with their start and end apart: 66, of which 36 were waited for; matrix products, arithmetic and copies ran while one was open for 0% of the time, Pallas kernels for 26%

profile of v7, /device:TPU:0, one launch (start us, length us, event | category | flops | bytes accessed | tf_op | source)
XLA Modules:
  0.0 219.4 jit_solution(13176894790445420048)
XLA Ops:
  1.3 4.0 %shard_map.246 = (bf16[144,768]{1,0:T(8,128)(2,1)}, bf16[128,768]{1,0:T(8,128)(2,1)}, bf16[128,768]{1,0:T(8,128)(2,1)}, bf16[272,768]{1,0:T(8,128)(2,1)}, bf16[1...) custom-call(s32[5]{0:T(128)} %stack.38.s_ref, bf16[2,2,4,32,768]{4,3,2,1,0:T(8,128)(2,1)} %bitcast.55, ...), custom_call_target="tpu_custom_call" | custom-call | flops 110000000 | bytes 350000 | tf_op jit(solution)/shard_map/pallas_call | solution.py:49
  5.8 3.7 %collective-permute-start.4 = (bf16[256,768]{1,0:T(8,128)(2,1)}, bf16[256,768]{1,0:T(8,128)(2,1)S(1)}, u32[]{:S(2)}, u32[]{:S(2)}) collective-permute-start(bf16[256,768]{1,0:T(8,128)(2,1)} %get-tuple-element.180), channel_id=1, source_target_pairs={{0,2},{2,0},{1,3},{3,1},{4,6},{6,4},{5,7},{7,5},{8,10},{10,8},{9,1... | collective-permute-start | bytes 1179656 | tf_op jit(solution)/shard_map/ppermute | solution.py:1009
  9.4 1.5 collective-permute-start
  11.4 1.5 collective-permute-start.2
  13.0 2.8 %shard_map.247 = (bf16[2,128,768]{2,1,0:T(8,128)(2,1)}, bf16[128,768]{1,0:T(8,128)(2,1)}, bf16[128,768]{1,0:T(8,128)(2,1)}) custom-call(s32[5]{0:T(128)} %stack.38.s_ref, bf16[2,2,4,32,768]{4,3,2,1,0:T(8,128)(2,1)} %bitcast.54, bf16[128,768]{1,0:T(8,128)(2,1)} %get-tuple-element.176.refs_1_.refs_0_), custom_call_target="tpu_custom_call" | custom-call | flops 110000000 | bytes 350000 | tf_op jit(solution)/shard_map/pallas_call | solution.py:49
  15.9 1.7 copy-done.1
  21.9 2.4 %shard_map.248 = (bf16[2,128,768]{2,1,0:T(8,128)(2,1)S(1)}, bf16[2,128,768]{2,1,0:T(8,128)(2,1)S(1)}, s32[8,256]{1,0:T(8,128)S(1)}, bf16[3,256,192]{2,1,0:T(8,12...) custom-call(s32[5]{0:T(128)S(1)} %copy-done.8, ...), custom_call_target="tpu_custom_call" | custom-call | flops 110000000 | bytes 350000 | tf_op jit(solution)/shard_map/pallas_call | solution.py:49
  25.7 2.1 collective-permute-done.4.refs_3_.refs_8_
  28.3 2.5 %collective-permute-start.10 = (bf16[256,768]{1,0:T(8,128)(2,1)S(1)}, bf16[256,768]{1,0:T(8,128)(2,1)S(1)}, u32[]{:S(2)}, u32[]{:S(2)}) collective-permute-start(bf16[256,768]{1,0:T(8,128)(2,1)S(1)} %collective-permute-done.4.refs_3_.refs_8_), channel_id=1, source_target_pairs={{0,24},{8,16},{16,8},{24,0},{1,25},{9,17},{17,9},{25,1},{2,26},{10... | collective-permute-start | bytes 1179656 | tf_op jit(solution)/shard_map/ppermute | solution.py:1014
  31.8 7.9 %shard_map.249 = (bf16[2,2,128,768]{3,2,1,0:T(8,128)(2,1)S(1)}, bf16[2,2,128,768]{3,2,1,0:T(8,128)(2,1)S(1)}, s32[512,8]{1,0:T(8,128)S(1)}, bf16[3,512,192]{2,1,...) custom-call(s32[5]{0:T(128)S(1)} %copy-done.8, ...), custom_call_target="tpu_custom_call" | custom-call | flops 32999999488 | bytes 105000000 | tf_op jit(solution)/shard_map/pallas_call | solution.py:49
  39.7 3.0 %collective-permute-start.11 = (bf16[256,192]{1,0:T(8,128)(2,1)S(1)}, bf16[256,192]{1,0:T(8,128)(2,1)S(1)}, u32[]{:S(2)}, u32[]{:S(2)}) collective-permute-start(bf16[256,192]{1,0:T(8,128)(2,1)S(1)} %get-tuple-element.197.refs_7_), channel_id=1, source_target_pairs={{0,2},{2,0},{1,3},{3,1},{4,6},{6,4},{5,7},{7,5},{8,10},{10,8},{9,1... | collective-permute-start | bytes 294920 | tf_op jit(solution)/shard_map/ppermute | solution.py:1009
  42.7 8.4 %collective-permute-done.7.refs_12_ = bf16[192,768]{1,0:T(8,128)(2,1)S(1)} collective-permute-done((bf16[192,768]{1,0:T(8,128)(2,1)S(1)}, bf16[192,768]{1,0:T(8,128)(2,1)S(1)}, u32[]{:S(2)}, u32[]{:S(2)}) %collective-permute-start.7) | collective-permute-done | bytes 294944 | tf_op jit(solution)/shard_map/ppermute | solution.py:1009
  51.1 1.6 collective-permute-start.14
  60.4 5.3 %collective-permute-done.15.refs_1_ = bf16[128,768]{1,0:T(8,128)(2,1)S(1)} collective-permute-done((bf16[128,768]{1,0:T(8,128)(2,1)S(1)}, bf16[128,768]{1,0:T(8,128)(2,1)S(1)}, u32[]{:S(2)}, u32[]{:S(2)}) %collective-permute-start.15) | collective-permute-done | bytes 196640 | tf_op jit(solution)/shard_map/ppermute | solution.py:1009
  66.3 1.6 collective-permute-start.21
  68.3 1.8 collective-permute-start.19
  70.7 4.9 %collective-permute-done.17.refs_15_ = bf16[192,768]{1,0:T(8,128)(2,1)S(1)} collective-permute-done((bf16[192,768]{1,0:T(8,128)(2,1)S(1)}, bf16[192,768]{1,0:T(8,128)(2,1)S(1)}, u32[]{:S(2)}, u32[]{:S(2)}) %collective-permute-start.17) | collective-permute-done | bytes 294944 | tf_op jit(solution)/shard_map/ppermute | solution.py:1014
  75.6 2.8 %shard_map.253 = (bf16[256,768]{1,0:T(8,128)(2,1)S(1)}, bf16[256,768]{1,0:T(8,128)(2,1)S(1)}, bf16[2,256,768]{2,1,0:T(8,128)(2,1)S(1)}, bf16[2,256,768]{2,1,0:T(...) custom-call(s32[5]{0:T(128)S(1)} %copy-done.8, ...), custom_call_target="tpu_custom_call" | custom-call | flops 110000000 | bytes 350000 | tf_op jit(solution)/shard_map/pallas_call | solution.py:49
  82.3 3.9 %collective-permute-done.18.refs_1_ = bf16[256,768]{1,0:T(8,128)(2,1)S(1)} collective-permute-done((bf16[256,768]{1,0:T(8,128)(2,1)S(1)}, bf16[256,768]{1,0:T(8,128)(2,1)S(1)}, u32[]{:S(2)}, u32[]{:S(2)}) %collective-permute-start.18) | collective-permute-done | bytes 393248 | tf_op jit(solution)/shard_map/ppermute | solution.py:1009
  86.9 2.3 %collective-permute-start.26 = (bf16[128,768]{1,0:T(8,128)(2,1)S(1)}, bf16[128,768]{1,0:T(8,128)(2,1)S(1)}, u32[]{:S(2)}, u32[]{:S(2)}) collective-permute-start(bf16[128,768]{1,0:T(8,128)(2,1)S(1)} %get-tuple-element.216.refs_3_), channel_id=1, source_target_pairs={{0,2},{2,0},{1,3},{3,1},{4,6},{6,4},{5,7},{7,5},{8,10},{10,8},{9,1... | collective-permute-start | bytes 589832 | tf_op jit(solution)/shard_map/ppermute | solution.py:1009
  89.2 1.6 shard_map.257
  90.8 2.3 %shard_map.258 = (bf16[256,768]{1,0:T(8,128)(2,1)S(1)}, bf16[256,768]{1,0:T(8,128)(2,1)S(1)}) custom-call(s32[5]{0:T(128)S(1)} %copy-done.8, bf16[256,768]{1,0:T(8,128)(2,1)S(1)} %get-tuple-element.222.refs_0_.refs_2_, bf16[768,768]{1,0:T(8,128)(2,1)S(1)} %get-tuple-element.208.refs_5_.refs_1_, bf16[768,768]{1,0:T(8,128)(2,1)S(1)} %get-tuple-element.209.refs_7_.refs_2_, ...), custom_call_target="tpu_custom_call" | custom-call | flops 110000000 | bytes 350000 | tf_op jit(solution)/shard_map/pallas_call | solution.py:49
  97.3 7.4 %collective-permute-done.25.refs_5_ = bf16[256,768]{1,0:T(8,128)(2,1)S(1)} collective-permute-done((bf16[256,768]{1,0:T(8,128)(2,1)S(1)}, bf16[256,768]{1,0:T(8,128)(2,1)S(1)}, u32[]{:S(2)}, u32[]{:S(2)}) %collective-permute-start.25) | collective-permute-done | bytes 393248 | tf_op jit(solution)/shard_map/ppermute | solution.py:1009
  108.7 2.3 %collective-permute-start.30 = (bf16[256,192]{1,0:T(8,128)(2,1)S(1)}, bf16[256,192]{1,0:T(8,128)(2,1)S(1)}, u32[]{:S(2)}, u32[]{:S(2)}) collective-permute-start(bf16[256,192]{1,0:T(8,128)(2,1)S(1)} %get-tuple-element.241), channel_id=1, source_target_pairs={{0,2},{2,0},{1,3},{3,1},{4,6},{6,4},{5,7},{7,5},{8,10},{10,8},{9,1... | collective-permute-start | bytes 294920 | tf_op jit(solution)/shard_map/ppermute | solution.py:1009
  111.0 4.9 %collective-permute-done.28.refs_4_ = bf16[128,768]{1,0:T(8,128)(2,1)S(1)} collective-permute-done((bf16[128,768]{1,0:T(8,128)(2,1)S(1)}, bf16[128,768]{1,0:T(8,128)(2,1)S(1)}, u32[]{:S(2)}, u32[]{:S(2)}) %collective-permute-start.28) | collective-permute-done | bytes 196640 | tf_op jit(solution)/shard_map/ppermute | solution.py:1009
  115.9 2.4 %shard_map.262 = (bf16[2,64,768]{2,1,0:T(8,128)(2,1)S(1)}, bf16[2,64,768]{2,1,0:T(8,128)(2,1)S(1)}, f32[256,768]{1,0:T(8,128)}, bf16[256,768]{1,0:T(8,128)(2,1)S(1)}, f32[8,768]{1,0:T(8,128)}) custom-call(s32[5]{0:T(128)S(1)} %copy-done.8, bf16[2,2,128,768]{3,2,1,0:T(8,128)(2,1)S(1)} %get-tuple-element.190.refs_0_, ...), custom_call_target="tpu_custom_call" | custom-call | flops 110000000 | bytes 350000 | tf_op jit(solution)/shard_map/pallas_call | solution.py:49
  118.3 2.0 shard_map.263
  121.0 1.8 collective-permute-start.37
  122.8 5.3 %shard_map.264 = (bf16[3,512,512]{2,1,0:T(8,128)(2,1)S(1)}, bf16[3,512,192]{2,1,0:T(8,128)(2,1)S(1)}, bf16[2,512,192]{2,1,0:T(8,128)(2,1)S(1)}, bf16[128,768]{1,...) custom-call(s32[5]{0:T(128)S(1)} %copy-done.8, ...), custom_call_target="tpu_custom_call" | custom-call | flops 32999999488 | bytes 105000000 | tf_op jit(solution)/shard_map/pallas_call | solution.py:49
  128.2 1.8 collective-permute-done.31.refs_2_
  133.8 1.6 collective-permute-done.36.refs_1_
  138.0 1.6 collective-permute-start.39
  140.6 5.8 %shard_map.268 = (bf16[240,768]{1,0:T(8,128)(2,1)S(1)}, bf16[240,768]{1,0:T(8,128)(2,1)S(1)}, bf16[96,768]{1,0:T(8,128)(2,1)S(1)}, f32[16,768]{1,0:T(8,128)S(1)}) custom-call(s32[5]{0:T(128)S(1)} %copy-done.8, bf16[2,2,128,768]{3,2,1,0:T(8,128)(2,1)S(1)} %get-tuple-element.190.refs_0_, bf16[3,512,512]{2,1,0:T(8,128)(2,1)S(1)} %get-tuple-element.268.refs_1_, ...), custom_call_target="tpu_custom_call" | custom-call | flops 110000000 | bytes 350000 | tf_op jit(solution)/shard_map/pallas_call | solution.py:49
  146.5 1.9 collective-permute-done.35.refs_1_
  152.2 1.7 collective-permute-start.47
  154.6 2.5 %collective-permute-start.34 = (bf16[80,768]{1,0:T(8,128)(2,1)S(1)}, bf16[80,768]{1,0:T(8,128)(2,1)S(1)}, u32[]{:S(2)}, u32[]{:S(2)}) collective-permute-start(bf16[80,768]{1,0:T(8,128)(2,1)S(1)} %collective-permute-done.31.refs_2_), channel_id=1, source_target_pairs={{0,1},{1,0},{2,3},{3,2},{4,5},{5,4},{6,7},{7,6},{8,9},{9,8},{10,11... | collective-permute-start | bytes 368648 | tf_op jit(solution)/shard_map/ppermute | solution.py:1009
  157.1 10.3 %collective-permute-done.38.refs_1_ = bf16[3,64,768]{2,1,0:T(8,128)(2,1)S(1)} collective-permute-done((bf16[3,64,768]{2,1,0:T(8,128)(2,1)S(1)}, bf16[3,64,768]{2,1,0:T(8,128)(2,1)S(1)}, u32[]{:S(2)}, u32[]{:S(2)}) %collective-permute-start.38) | collective-permute-done | bytes 294944 | tf_op jit(solution)/shard_map/ppermute | solution.py:1009
  171.0 2.5 %collective-permute-done.48.refs_1_ = bf16[3,32,768]{2,1,0:T(8,128)(2,1)S(1)} collective-permute-done((bf16[3,32,768]{2,1,0:T(8,128)(2,1)S(1)}, bf16[3,32,768]{2,1,0:T(8,128)(2,1)S(1)}, u32[]{:S(2)}, u32[]{:S(2)}) %collective-permute-start.48) | collective-permute-done | bytes 147488 | tf_op jit(solution)/shard_map/ppermute | solution.py:1009
  177.3 1.8 collective-permute-start.57
  179.1 5.1 %shard_map.273 = (f32[2,2,384,768]{3,2,1,0:T(8,128)}, f32[2,2,384,768]{3,2,1,0:T(8,128)}, f32[8,128]{1,0:T(8,128)S(1)}) custom-call(s32[5]{0:T(128)S(1)} %copy-done.8, bf16[384,768]{1,0:T(8,128)(2,1)S(1)} %get-tuple-element.302.refs_2_.refs_0_, bf16[384,768]{1,0:T(8,128)(2,1)S(1)} %collective-permute-done.46.refs_13_.refs_1_, ...), custom_call_target="tpu_custom_call" | custom-call | flops 110000000 | bytes 350000 | tf_op jit(solution)/shard_map/pallas_call | solution.py:49
  184.2 2.0 collective-permute-done.49.refs_1_
  188.9 1.6 collective-permute-done.58.refs_3_
  190.5 3.1 %collective-permute-done.57.refs_2_ = bf16[2,3,32,768]{3,2,1,0:T(8,128)(2,1)S(1)} collective-permute-done((bf16[2,3,32,768]{3,2,1,0:T(8,128)(2,1)S(1)}, bf16[2,3,32,768]{3,2,1,0:T(8,128)(2,1)S(1)}, u32[]{:S(2)}, u32[]{:S(2)}) %collective-permute-start.57) | collective-permute-done | bytes 294944 | tf_op jit(solution)/shard_map/ppermute | solution.py:1009
  194.0 7.8 %collective-permute-done.59.refs_4_ = bf16[2,3,32,768]{3,2,1,0:T(8,128)(2,1)S(1)} collective-permute-done((bf16[2,3,32,768]{3,2,1,0:T(8,128)(2,1)S(1)}, bf16[2,3,32,768]{3,2,1,0:T(8,128)(2,1)S(1)}, u32[]{:S(2)}, u32[]{:S(2)}) %collective-permute-start.59) | collective-permute-done | bytes 294944 | tf_op jit(solution)/shard_map/ppermute | solution.py:1009
  205.7 2.1 shard_map.277
  207.8 3.7 %collective-permute-done.60.refs_1_ = bf16[240,768]{1,0:T(8,128)(2,1)S(1)} collective-permute-done((bf16[240,768]{1,0:T(8,128)(2,1)S(1)}, bf16[240,768]{1,0:T(8,128)(2,1)S(1)}, u32[]{:S(2)}, u32[]{:S(2)}) %collective-permute-start.60) | collective-permute-done | bytes 368672 | tf_op jit(solution)/shard_map/ppermute | solution.py:1009
  213.4 1.7 collective-permute-done.62.refs_2_
  215.7 3.7 %shard_map.278 = (f32[2,576,768]{2,1,0:T(8,128)}, f32[2,192,768]{2,1,0:T(8,128)}, f32[2,192,768]{2,1,0:T(8,128)}, f32[3,3,2,128]{3,2,1,0:T(2,128)}, f32[2,2,192]...) custom-call(s32[5]{0:T(128)S(1)} %copy-done.8, ...), custom_call_target="tpu_custom_call" | custom-call | flops 110000000 | bytes 350000 | tf_op jit(solution)/shard_map/pallas_call | solution.py:49
  (168 shorter events, 60.0 us)
Async XLA Ops:
  5.2 10.6 %collective-permute-start.3 = (bf16[272,768]{1,0:T(8,128)(2,1)}, bf16[272,768]{1,0:T(8,128)(2,1)}, u32[]{:S(2)}, u32[]{:S(2)}) collective-permute-start(bf16[272,768]{1,0:T(8,128)(2,1)} %get-tuple-element.177.refs_2_), channel_id=1, source_target_pairs={{0,4},{4,0},{1,5},{5,1},{2,6},{6,2},{3,7},{7,3},{8,12},{12,8},{9,1... | collective-permute-start | bytes 1253384 | tf_op jit(solution)/shard_map/ppermute | solution.py:1009
  5.8 22.0 %collective-permute-start.4 = (bf16[256,768]{1,0:T(8,128)(2,1)}, bf16[256,768]{1,0:T(8,128)(2,1)S(1)}, u32[]{:S(2)}, u32[]{:S(2)}) collective-permute-start(bf16[256,768]{1,0:T(8,128)(2,1)} %get-tuple-element.180), channel_id=1, source_target_pairs={{0,2},{2,0},{1,3},{3,1},{4,6},{6,4},{5,7},{7,5},{8,10},{10,8},{9,1... | collective-permute-start | bytes 1179656 | tf_op jit(solution)/shard_map/ppermute | solution.py:1009
  9.4 16.2 %collective-permute-start = (bf16[144,768]{1,0:T(8,128)(2,1)}, bf16[144,768]{1,0:T(8,128)(2,1)}, u32[]{:S(2)}, u32[]{:S(2)}) collective-permute-start(bf16[144,768]{1,0:T(8,128)(2,1)} %get-tuple-element.173), channel_id=1, source_target_pairs={{0,8},{8,0},{1,9},{9,1},{2,10},{10,2},{3,11},{11,3},{4,12},{12,4},... | collective-permute-start | bytes 663560 | tf_op jit(solution)/shard_map/ppermute | solution.py:1009
  11.0 13.3 %collective-permute-start.1 = (bf16[128,768]{1,0:T(8,128)(2,1)}, bf16[128,768]{1,0:T(8,128)(2,1)}, u32[]{:S(2)}, u32[]{:S(2)}) collective-permute-start(bf16[128,768]{1,0:T(8,128)(2,1)} %get-tuple-element.174), channel_id=1, source_target_pairs={{0,8},{8,0},{1,9},{9,1},{2,10},{10,2},{3,11},{11,3},{4,12},{12,4},... | collective-permute-start | bytes 589832 | tf_op jit(solution)/shard_map/ppermute | solution.py:1009
  11.4 14.2 %collective-permute-start.2 = (bf16[128,768]{1,0:T(8,128)(2,1)}, bf16[128,768]{1,0:T(8,128)(2,1)}, u32[]{:S(2)}, u32[]{:S(2)}) collective-permute-start(bf16[128,768]{1,0:T(8,128)(2,1)} %get-tuple-element.175), channel_id=1, source_target_pairs={{0,8},{8,0},{1,9},{9,1},{2,10},{10,2},{3,11},{11,3},{4,12},{12,4},... | collective-permute-start | bytes 589832 | tf_op jit(solution)/shard_map/ppermute | solution.py:1009
  28.3 22.8 %collective-permute-start.10 = (bf16[256,768]{1,0:T(8,128)(2,1)S(1)}, bf16[256,768]{1,0:T(8,128)(2,1)S(1)}, u32[]{:S(2)}, u32[]{:S(2)}) collective-permute-start(bf16[256,768]{1,0:T(8,128)(2,1)S(1)} %collective-permute-done.4.refs_3_.refs_8_), channel_id=1, source_target_pairs={{0,24},{8,16},{16,8},{24,0},{1,25},{9,17},{17,9},{25,1},{2,26},{10... | collective-permute-start | bytes 1179656 | tf_op jit(solution)/shard_map/ppermute | solution.py:1014
  30.8 20.3 %collective-permute-start.9 = (bf16[256,768]{1,0:T(8,128)(2,1)S(1)}, bf16[256,768]{1,0:T(8,128)(2,1)S(1)}, u32[]{:S(2)}, u32[]{:S(2)}) collective-permute-start(bf16[256,768]{1,0:T(8,128)(2,1)S(1)} %collective-permute-done.4.refs_3_.refs_8_), channel_id=1, source_target_pairs={{0,16},{16,0},{1,17},{17,1},{2,18},{18,2},{3,19},{19,3},{4,20},{20... | collective-permute-start | bytes 1179656 | tf_op jit(solution)/shard_map/ppermute | solution.py:1009
  31.3 19.7 %collective-permute-start.8 = (bf16[256,768]{1,0:T(8,128)(2,1)S(1)}, bf16[256,768]{1,0:T(8,128)(2,1)S(1)}, u32[]{:S(2)}, u32[]{:S(2)}) collective-permute-start(bf16[256,768]{1,0:T(8,128)(2,1)S(1)} %collective-permute-done.4.refs_3_.refs_8_), channel_id=1, source_target_pairs={{0,8},{8,0},{1,9},{9,1},{2,10},{10,2},{3,11},{11,3},{4,12},{12,4},... | collective-permute-start | bytes 1179656 | tf_op jit(solution)/shard_map/ppermute | solution.py:1009
  31.8 19.3 %collective-permute-start.7 = (bf16[192,768]{1,0:T(8,128)(2,1)S(1)}, bf16[192,768]{1,0:T(8,128)(2,1)S(1)}, u32[]{:S(2)}, u32[]{:S(2)}) collective-permute-start(bf16[192,768]{1,0:T(8,128)(2,1)S(1)} %copy-done.16), channel_id=1, source_target_pairs={{0,2},{2,0},{1,3},{3,1},{4,6},{6,4},{5,7},{7,5},{8,10},{10,8},{9,1... | collective-permute-start | bytes 884744 | tf_op jit(solution)/shard_map/ppermute | solution.py:1009
  39.7 14.4 %collective-permute-start.11 = (bf16[256,192]{1,0:T(8,128)(2,1)S(1)}, bf16[256,192]{1,0:T(8,128)(2,1)S(1)}, u32[]{:S(2)}, u32[]{:S(2)}) collective-permute-start(bf16[256,192]{1,0:T(8,128)(2,1)S(1)} %get-tuple-element.197.refs_7_), channel_id=1, source_target_pairs={{0,2},{2,0},{1,3},{3,1},{4,6},{6,4},{5,7},{7,5},{8,10},{10,8},{9,1... | collective-permute-start | bytes 294920 | tf_op jit(solution)/shard_map/ppermute | solution.py:1009
  51.1 6.8 %collective-permute-start.14 = (bf16[192,768]{1,0:T(8,128)(2,1)S(1)}, bf16[192,768]{1,0:T(8,128)(2,1)S(1)}, u32[]{:S(2)}, u32[]{:S(2)}) collective-permute-start(bf16[192,768]{1,0:T(8,128)(2,1)S(1)} %collective-permute-done.7.refs_12_), channel_id=1, source_target_pairs={{0,16},{16,0},{1,17},{17,1},{2,18},{18,2},{3,19},{19,3},{4,20},{20... | collective-permute-start | bytes 884744 | tf_op jit(solution)/shard_map/ppermute | solution.py:1009
  52.6 6.7 %collective-permute-start.13 = (bf16[192,768]{1,0:T(8,128)(2,1)S(1)}, bf16[192,768]{1,0:T(8,128)(2,1)S(1)}, u32[]{:S(2)}, u32[]{:S(2)}) collective-permute-start(bf16[192,768]{1,0:T(8,128)(2,1)S(1)} %collective-permute-done.7.refs_12_), channel_id=1, source_target_pairs={{0,8},{8,0},{1,9},{9,1},{2,10},{10,2},{3,11},{11,3},{4,12},{12,4},... | collective-permute-start | bytes 884744 | tf_op jit(solution)/shard_map/ppermute | solution.py:1009
  59.9 5.7 %collective-permute-start.15 = (bf16[128,768]{1,0:T(8,128)(2,1)S(1)}, bf16[128,768]{1,0:T(8,128)(2,1)S(1)}, u32[]{:S(2)}, u32[]{:S(2)}) collective-permute-start(bf16[128,768]{1,0:T(8,128)(2,1)S(1)} %shard_map.251.refs_0_), channel_id=1, source_target_pairs={{0,1},{1,0},{2,3},{3,2},{4,5},{5,4},{6,7},{7,6},{8,9},{9,8},{10,11... | collective-permute-start | bytes 589832 | tf_op jit(solution)/shard_map/ppermute | solution.py:1009
  66.3 13.7 %collective-permute-start.21 = (bf16[2,128,768]{2,1,0:T(8,128)(2,1)S(1)}, bf16[2,128,768]{2,1,0:T(8,128)(2,1)S(1)}, u32[]{:S(2)}, u32[]{:S(2)}) collective-permute-start(bf16[2,128,768]{2,1,0:T(8,128)(2,1)S(1)} %copy-done.15), channel_id=1, source_target_pairs={{0,8},{8,0},{1,9},{9,1},{2,10},{10,2},{3,11},{11,3},{4,12},{12,4},... | collective-permute-start | bytes 1179656 | tf_op jit(solution)/shard_map/ppermute | solution.py:1009
  67.9 7.7 %collective-permute-start.17 = (bf16[192,768]{1,0:T(8,128)(2,1)S(1)}, bf16[192,768]{1,0:T(8,128)(2,1)S(1)}, u32[]{:S(2)}, u32[]{:S(2)}) collective-permute-start(bf16[192,768]{1,0:T(8,128)(2,1)S(1)} %collective-permute-done.7.refs_12_), channel_id=1, source_target_pairs={{0,24},{8,16},{16,8},{24,0},{1,25},{9,17},{17,9},{25,1},{2,26},{10... | collective-permute-start | bytes 884744 | tf_op jit(solution)/shard_map/ppermute | solution.py:1014
  68.3 10.4 %collective-permute-start.19 = (bf16[128,768]{1,0:T(8,128)(2,1)S(1)}, bf16[128,768]{1,0:T(8,128)(2,1)S(1)}, u32[]{:S(2)}, u32[]{:S(2)}) collective-permute-start(bf16[128,768]{1,0:T(8,128)(2,1)S(1)} %shard_map.252.refs_1_), channel_id=1, source_target_pairs={{0,2},{2,0},{1,3},{3,1},{4,6},{6,4},{5,7},{7,5},{8,10},{10,8},{9,1... | collective-permute-start | bytes 589832 | tf_op jit(solution)/shard_map/ppermute | solution.py:1009
  70.2 9.8 %collective-permute-start.22 = (bf16[128,768]{1,0:T(8,128)(2,1)S(1)}, bf16[128,768]{1,0:T(8,128)(2,1)S(1)}, u32[]{:S(2)}, u32[]{:S(2)}) collective-permute-start(bf16[128,768]{1,0:T(8,128)(2,1)S(1)} %copy-done.17), channel_id=1, source_target_pairs={{0,4},{4,0},{1,5},{5,1},{2,6},{6,2},{3,7},{7,3},{8,12},{12,8},{9,1... | collective-permute-start | bytes 589832 | tf_op jit(solution)/shard_map/ppermute | solution.py:1009
  78.4 7.8 %collective-permute-start.18 = (bf16[256,768]{1,0:T(8,128)(2,1)S(1)}, bf16[256,768]{1,0:T(8,128)(2,1)S(1)}, u32[]{:S(2)}, u32[]{:S(2)}) collective-permute-start(bf16[256,768]{1,0:T(8,128)(2,1)S(1)} %get-tuple-element.214.refs_5_.refs_0_), channel_id=1, source_target_pairs={{0,1},{1,0},{2,3},{3,2},{4,5},{5,4},{6,7},{7,6},{8,9},{9,8},{10,11... | collective-permute-start | bytes 1179656 | tf_op jit(solution)/shard_map/ppermute | solution.py:1009
  79.9 9.2 %collective-permute-start.23 = (bf16[2,128,768]{2,1,0:T(8,128)(2,1)S(1)}, bf16[2,128,768]{2,1,0:T(8,128)(2,1)S(1)}, u32[]{:S(2)}, u32[]{:S(2)}) collective-permute-start(bf16[2,128,768]{2,1,0:T(8,128)(2,1)S(1)} %collective-permute-done.21), channel_id=1, source_target_pairs={{0,4},{4,0},{1,5},{5,1},{2,6},{6,2},{3,7},{7,3},{8,12},{12,8},{9,1... | collective-permute-start | bytes 1179656 | tf_op jit(solution)/shard_map/ppermute | solution.py:1009
  86.9 10.4 %collective-permute-start.26 = (bf16[128,768]{1,0:T(8,128)(2,1)S(1)}, bf16[128,768]{1,0:T(8,128)(2,1)S(1)}, u32[]{:S(2)}, u32[]{:S(2)}) collective-permute-start(bf16[128,768]{1,0:T(8,128)(2,1)S(1)} %get-tuple-element.216.refs_3_), channel_id=1, source_target_pairs={{0,2},{2,0},{1,3},{3,1},{4,6},{6,4},{5,7},{7,5},{8,10},{10,8},{9,1... | collective-permute-start | bytes 589832 | tf_op jit(solution)/shard_map/ppermute | solution.py:1009
  93.1 11.6 %collective-permute-start.25 = (bf16[256,768]{1,0:T(8,128)(2,1)S(1)}, bf16[256,768]{1,0:T(8,128)(2,1)S(1)}, u32[]{:S(2)}, u32[]{:S(2)}) collective-permute-start(bf16[256,768]{1,0:T(8,128)(2,1)S(1)} %get-tuple-element.226.refs_4_), channel_id=1, source_target_pairs={{0,1},{1,0},{2,3},{3,2},{4,5},{5,4},{6,7},{7,6},{8,9},{9,8},{10,11... | collective-permute-start | bytes 1179656 | tf_op jit(solution)/shard_map/ppermute | solution.py:1009
  94.6 10.1 %collective-permute-start.27 = (bf16[2,64,768]{2,1,0:T(8,128)(2,1)S(1)}, bf16[2,64,768]{2,1,0:T(8,128)(2,1)S(1)}, u32[]{:S(2)}, u32[]{:S(2)}) collective-permute-start(bf16[2,64,768]{2,1,0:T(8,128)(2,1)S(1)} %pad_maximum_fusion.1), channel_id=1, source_target_pairs={{0,8},{8,0},{1,9},{9,1},{2,10},{10,2},{3,11},{11,3},{4,12},{12,4},... | collective-permute-start | bytes 589832 | tf_op jit(solution)/shard_map/ppermute | solution.py:1009
  106.0 9.9 %collective-permute-start.28 = (bf16[128,768]{1,0:T(8,128)(2,1)S(1)}, bf16[128,768]{1,0:T(8,128)(2,1)S(1)}, u32[]{:S(2)}, u32[]{:S(2)}) collective-permute-start(bf16[128,768]{1,0:T(8,128)(2,1)S(1)} %collective-permute-done.26.refs_3_), channel_id=1, source_target_pairs={{0,1},{1,0},{2,3},{3,2},{4,5},{5,4},{6,7},{7,6},{8,9},{9,8},{10,11... | collective-permute-start | bytes 589832 | tf_op jit(solution)/shard_map/ppermute | solution.py:1009
  108.7 14.1 %collective-permute-start.30 = (bf16[256,192]{1,0:T(8,128)(2,1)S(1)}, bf16[256,192]{1,0:T(8,128)(2,1)S(1)}, u32[]{:S(2)}, u32[]{:S(2)}) collective-permute-start(bf16[256,192]{1,0:T(8,128)(2,1)S(1)} %get-tuple-element.241), channel_id=1, source_target_pairs={{0,2},{2,0},{1,3},{3,1},{4,6},{6,4},{5,7},{7,5},{8,10},{10,8},{9,1... | collective-permute-start | bytes 294920 | tf_op jit(solution)/shard_map/ppermute | solution.py:1009
  120.4 15.0 %collective-permute-start.36 = (bf16[384,768]{1,0:T(8,128)(2,1)S(1)}, bf16[384,768]{1,0:T(8,128)(2,1)S(1)}, u32[]{:S(2)}, u32[]{:S(2)}) collective-permute-start(bf16[384,768]{1,0:T(8,128)(2,1)S(1)} %get-tuple-element.274), channel_id=1, source_target_pairs={{0,16},{16,0},{1,17},{17,1},{2,18},{18,2},{3,19},{19,3},{4,20},{20... | collective-permute-start | bytes 1769480 | tf_op jit(solution)/shard_map/ppermute | solution.py:1009
  121.0 14.6 %collective-permute-start.37 = (bf16[384,768]{1,0:T(8,128)(2,1)S(1)}, bf16[384,768]{1,0:T(8,128)(2,1)S(1)}, u32[]{:S(2)}, u32[]{:S(2)}) collective-permute-start(bf16[384,768]{1,0:T(8,128)(2,1)S(1)} %get-tuple-element.276), channel_id=1, source_target_pairs={{0,8},{8,0},{1,9},{9,1},{2,10},{10,2},{3,11},{11,3},{4,12},{12,4},... | collective-permute-start | bytes 1769480 | tf_op jit(solution)/shard_map/ppermute | solution.py:1009
  122.8 7.1 %collective-permute-start.31 = (bf16[80,768]{1,0:T(8,128)(2,1)S(1)}, bf16[80,768]{1,0:T(8,128)(2,1)S(1)}, u32[]{:S(2)}, u32[]{:S(2)}) collective-permute-start(bf16[80,768]{1,0:T(8,128)(2,1)S(1)} %get-tuple-element.256.refs_1_), channel_id=1, source_target_pairs={{0,2},{2,0},{1,3},{3,1},{4,6},{6,4},{5,7},{7,5},{8,10},{10,8},{9,1... | collective-permute-start | bytes 368648 | tf_op jit(solution)/shard_map/ppermute | solution.py:1009
  132.9 15.4 %collective-permute-start.35 = (bf16[3,128,768]{2,1,0:T(8,128)(2,1)S(1)}, bf16[3,128,768]{2,1,0:T(8,128)(2,1)S(1)}, u32[]{:S(2)}, u32[]{:S(2)}) collective-permute-start(bf16[3,128,768]{2,1,0:T(8,128)(2,1)S(1)} %get-tuple-element.264.refs_4_), channel_id=1, source_target_pairs={{0,1},{1,0},{2,3},{3,2},{4,5},{5,4},{6,7},{7,6},{8,9},{9,8},{10,11... | collective-permute-start | bytes 1769480 | tf_op jit(solution)/shard_map/ppermute | solution.py:1009
  136.5 13.8 %collective-permute-start.40 = (bf16[384,768]{1,0:T(8,128)(2,1)S(1)}, bf16[384,768]{1,0:T(8,128)(2,1)S(1)}, u32[]{:S(2)}, u32[]{:S(2)}) collective-permute-start(bf16[384,768]{1,0:T(8,128)(2,1)S(1)} %get-tuple-element.282.refs_2_), channel_id=1, source_target_pairs={{0,16},{16,0},{1,17},{17,1},{2,18},{18,2},{3,19},{19,3},{4,20},{20... | collective-permute-start | bytes 1769480 | tf_op jit(solution)/shard_map/ppermute | solution.py:1009
  138.0 13.4 %collective-permute-start.39 = (bf16[384,768]{1,0:T(8,128)(2,1)S(1)}, bf16[384,768]{1,0:T(8,128)(2,1)S(1)}, u32[]{:S(2)}, u32[]{:S(2)}) collective-permute-start(bf16[384,768]{1,0:T(8,128)(2,1)S(1)} %get-tuple-element.277.refs_2_.refs_0_), channel_id=1, source_target_pairs={{0,8},{8,0},{1,9},{9,1},{2,10},{10,2},{3,11},{11,3},{4,12},{12,4},... | collective-permute-start | bytes 1769480 | tf_op jit(solution)/shard_map/ppermute | solution.py:1009
  152.2 17.8 %collective-permute-start.47 = (bf16[384,768]{1,0:T(8,128)(2,1)S(1)}, bf16[384,768]{1,0:T(8,128)(2,1)S(1)}, u32[]{:S(2)}, u32[]{:S(2)}) collective-permute-start(bf16[384,768]{1,0:T(8,128)(2,1)S(1)} %get-tuple-element.304.refs_4_), channel_id=1, source_target_pairs={{0,8},{8,0},{1,9},{9,1},{2,10},{10,2},{3,11},{11,3},{4,12},{12,4},... | collective-permute-start | bytes 1769480 | tf_op jit(solution)/shard_map/ppermute | solution.py:1009
  153.9 16.1 %collective-permute-start.46 = (bf16[384,768]{1,0:T(8,128)(2,1)S(1)}, bf16[384,768]{1,0:T(8,128)(2,1)S(1)}, u32[]{:S(2)}, u32[]{:S(2)}) collective-permute-start(bf16[384,768]{1,0:T(8,128)(2,1)S(1)} %get-tuple-element.302.refs_2_.refs_0_), channel_id=1, source_target_pairs={{0,16},{16,0},{1,17},{17,1},{2,18},{18,2},{3,19},{19,3},{4,20},{20... | collective-permute-start | bytes 1769480 | tf_op jit(solution)/shard_map/ppermute | solution.py:1009
  154.6 12.8 %collective-permute-start.38 = (bf16[3,64,768]{2,1,0:T(8,128)(2,1)S(1)}, bf16[3,64,768]{2,1,0:T(8,128)(2,1)S(1)}, u32[]{:S(2)}, u32[]{:S(2)}) collective-permute-start(bf16[3,64,768]{2,1,0:T(8,128)(2,1)S(1)} %get-tuple-element.281.refs_4_), channel_id=1, source_target_pairs={{0,2},{2,0},{1,3},{3,1},{4,6},{6,4},{5,7},{7,5},{8,10},{10,8},{9,1... | collective-permute-start | bytes 884744 | tf_op jit(solution)/shard_map/ppermute | solution.py:1009
  154.6 13.9 %collective-permute-start.45 = (bf16[192,768]{1,0:T(8,128)(2,1)S(1)}, bf16[192,768]{1,0:T(8,128)(2,1)S(1)}, u32[]{:S(2)}, u32[]{:S(2)}) collective-permute-start(bf16[192,768]{1,0:T(8,128)(2,1)S(1)} %get-tuple-element.292), channel_id=1, source_target_pairs={{0,4},{4,0},{1,5},{5,1},{2,6},{6,2},{3,7},{7,3},{8,12},{12,8},{9,1... | collective-permute-start | bytes 884744 | tf_op jit(solution)/shard_map/ppermute | solution.py:1009
  154.6 13.8 %collective-permute-start.34 = (bf16[80,768]{1,0:T(8,128)(2,1)S(1)}, bf16[80,768]{1,0:T(8,128)(2,1)S(1)}, u32[]{:S(2)}, u32[]{:S(2)}) collective-permute-start(bf16[80,768]{1,0:T(8,128)(2,1)S(1)} %collective-permute-done.31.refs_2_), channel_id=1, source_target_pairs={{0,1},{1,0},{2,3},{3,2},{4,5},{5,4},{6,7},{7,6},{8,9},{9,8},{10,11... | collective-permute-start | bytes 368648 | tf_op jit(solution)/shard_map/ppermute | solution.py:1009
  168.0 5.5 %collective-permute-start.48 = (bf16[3,32,768]{2,1,0:T(8,128)(2,1)S(1)}, bf16[3,32,768]{2,1,0:T(8,128)(2,1)S(1)}, u32[]{:S(2)}, u32[]{:S(2)}) collective-permute-start(bf16[3,32,768]{2,1,0:T(8,128)(2,1)S(1)} %get-tuple-element.296), channel_id=1, source_target_pairs={{0,8},{8,0},{1,9},{9,1},{2,10},{10,2},{3,11},{11,3},{4,12},{12,4},... | collective-permute-start | bytes 442376 | tf_op jit(solution)/shard_map/ppermute | solution.py:1009
  174.6 11.6 %collective-permute-start.50 = (bf16[256,768]{1,0:T(8,128)(2,1)S(1)}, bf16[256,768]{1,0:T(8,128)(2,1)S(1)}, u32[]{:S(2)}, u32[]{:S(2)}) collective-permute-start(bf16[256,768]{1,0:T(8,128)(2,1)S(1)} %get-tuple-element.300), channel_id=1, source_target_pairs={{0,8},{8,0},{1,9},{9,1},{2,10},{10,2},{3,11},{11,3},{4,12},{12,4},... | collective-permute-start | bytes 1179656 | tf_op jit(solution)/shard_map/ppermute | solution.py:1009
  175.6 10.6 %collective-permute-start.49 = (bf16[240,768]{1,0:T(8,128)(2,1)S(1)}, bf16[240,768]{1,0:T(8,128)(2,1)S(1)}, u32[]{:S(2)}, u32[]{:S(2)}) collective-permute-start(bf16[240,768]{1,0:T(8,128)(2,1)S(1)} %get-tuple-element.298), channel_id=1, source_target_pairs={{0,16},{16,0},{1,17},{17,1},{2,18},{18,2},{3,19},{19,3},{4,20},{20... | collective-permute-start | bytes 1105928 | tf_op jit(solution)/shard_map/ppermute | solution.py:1009
  176.8 13.8 %collective-permute-start.58 = (bf16[2,3,32,768]{3,2,1,0:T(8,128)(2,1)S(1)}, bf16[2,3,32,768]{3,2,1,0:T(8,128)(2,1)S(1)}, u32[]{:S(2)}, u32[]{:S(2)}) collective-permute-start(bf16[2,3,32,768]{3,2,1,0:T(8,128)(2,1)S(1)} %pad_maximum_fusion.refs_8_), channel_id=1, source_target_pairs={{0,1},{1,0},{2,3},{3,2},{4,5},{5,4},{6,7},{7,6},{8,9},{9,8},{10,11... | collective-permute-start | bytes 884744 | tf_op jit(solution)/shard_map/ppermute | solution.py:1009
  177.3 16.3 %collective-permute-start.57 = (bf16[2,3,32,768]{3,2,1,0:T(8,128)(2,1)S(1)}, bf16[2,3,32,768]{3,2,1,0:T(8,128)(2,1)S(1)}, u32[]{:S(2)}, u32[]{:S(2)}) collective-permute-start(bf16[2,3,32,768]{3,2,1,0:T(8,128)(2,1)S(1)} %pad_maximum_fusion.refs_8_), channel_id=1, source_target_pairs={{0,2},{2,0},{1,3},{3,1},{4,6},{6,4},{5,7},{7,5},{8,10},{10,8},{9,1... | collective-permute-start | bytes 884744 | tf_op jit(solution)/shard_map/ppermute | solution.py:1009
  179.1 14.5 %collective-permute-start.41 = (bf16[2,64,768]{2,1,0:T(8,128)(2,1)S(1)}, bf16[2,64,768]{2,1,0:T(8,128)(2,1)S(1)}, u32[]{:S(2)}, u32[]{:S(2)}) collective-permute-start(bf16[2,64,768]{2,1,0:T(8,128)(2,1)S(1)} %get-tuple-element.285), channel_id=1, source_target_pairs={{0,4},{4,0},{1,5},{5,1},{2,6},{6,2},{3,7},{7,3},{8,12},{12,8},{9,1... | collective-permute-start | bytes 589832 | tf_op jit(solution)/shard_map/ppermute | solution.py:1009
  187.0 14.9 %collective-permute-start.55 = (bf16[240,768]{1,0:T(8,128)(2,1)S(1)}, bf16[240,768]{1,0:T(8,128)(2,1)S(1)}, u32[]{:S(2)}, u32[]{:S(2)}) collective-permute-start(bf16[240,768]{1,0:T(8,128)(2,1)S(1)} %get-tuple-element.308.refs_0_), channel_id=1, source_target_pairs={{0,8},{8,0},{1,9},{9,1},{2,10},{10,2},{3,11},{11,3},{4,12},{12,4},... | collective-permute-start | bytes 1105928 | tf_op jit(solution)/shard_map/ppermute | solution.py:1009
  187.8 14.1 %collective-permute-start.56 = (bf16[256,768]{1,0:T(8,128)(2,1)S(1)}, bf16[256,768]{1,0:T(8,128)(2,1)S(1)}, u32[]{:S(2)}, u32[]{:S(2)}) collective-permute-start(bf16[256,768]{1,0:T(8,128)(2,1)S(1)} %get-tuple-element.309.refs_2_), channel_id=1, source_target_pairs={{0,16},{16,0},{1,17},{17,1},{2,18},{18,2},{3,19},{19,3},{4,20},{20... | collective-permute-start | bytes 1179656 | tf_op jit(solution)/shard_map/ppermute | solution.py:1009
  193.6 8.2 %collective-permute-start.59 = (bf16[2,3,32,768]{3,2,1,0:T(8,128)(2,1)S(1)}, bf16[2,3,32,768]{3,2,1,0:T(8,128)(2,1)S(1)}, u32[]{:S(2)}, u32[]{:S(2)}) collective-permute-start(bf16[2,3,32,768]{3,2,1,0:T(8,128)(2,1)S(1)} %collective-permute-done.57.refs_2_), channel_id=1, source_target_pairs={{0,1},{1,0},{2,3},{3,2},{4,5},{5,4},{6,7},{7,6},{8,9},{9,8},{10,11... | collective-permute-start | bytes 884744 | tf_op jit(solution)/shard_map/ppermute | solution.py:1009
  193.7 10.4 %collective-permute-start.42 = (bf16[2,64,768]{2,1,0:T(8,128)(2,1)S(1)}, bf16[2,64,768]{2,1,0:T(8,128)(2,1)S(1)}, u32[]{:S(2)}, u32[]{:S(2)}) collective-permute-start(bf16[2,64,768]{2,1,0:T(8,128)(2,1)S(1)} %pad_maximum_fusion.2), channel_id=1, source_target_pairs={{0,8},{8,0},{1,9},{9,1},{2,10},{10,2},{3,11},{11,3},{4,12},{12,4},... | collective-permute-start | bytes 589832 | tf_op jit(solution)/shard_map/ppermute | solution.py:1009
  202.6 8.9 %collective-permute-start.60 = (bf16[240,768]{1,0:T(8,128)(2,1)S(1)}, bf16[240,768]{1,0:T(8,128)(2,1)S(1)}, u32[]{:S(2)}, u32[]{:S(2)}) collective-permute-start(bf16[240,768]{1,0:T(8,128)(2,1)S(1)} %get-tuple-element.311.refs_8_.refs_5_.refs_0_), channel_id=1, source_target_pairs={{0,16},{16,0},{1,17},{17,1},{2,18},{18,2},{3,19},{19,3},{4,20},{20... | collective-permute-start | bytes 1105928 | tf_op jit(solution)/shard_map/ppermute | solution.py:1009
  203.8 9.1 %collective-permute-start.61 = (bf16[256,768]{1,0:T(8,128)(2,1)S(1)}, bf16[256,768]{1,0:T(8,128)(2,1)S(1)}, u32[]{:S(2)}, u32[]{:S(2)}) collective-permute-start(bf16[256,768]{1,0:T(8,128)(2,1)S(1)} %get-tuple-element.316.refs_4_), channel_id=1, source_target_pairs={{0,8},{8,0},{1,9},{9,1},{2,10},{10,2},{3,11},{11,3},{4,12},{12,4},... | collective-permute-start | bytes 1179656 | tf_op jit(solution)/shard_map/ppermute | solution.py:1009
  204.1 11.0 %collective-permute-start.64 = (bf16[256,768]{1,0:T(8,128)(2,1)S(1)}, bf16[256,768]{1,0:T(8,128)(2,1)S(1)}, u32[]{:S(2)}, u32[]{:S(2)}) collective-permute-start(bf16[256,768]{1,0:T(8,128)(2,1)S(1)} %get-tuple-element.316.refs_4_), channel_id=1, source_target_pairs={{0,4},{4,0},{1,5},{5,1},{2,6},{6,2},{3,7},{7,3},{8,12},{12,8},{9,1... | collective-permute-start | bytes 1179656 | tf_op jit(solution)/shard_map/ppermute | solution.py:1009
  (36 other events, 240.6 us)

commit v8 on v7

--- a/solution.py
+++ b/solution.py
@@ -14,7 +14,11 @@
 F32 = jnp.float32
 BF16 = jnp.bfloat16
 VMEM_BYTES = 20 * 1024 * 1024
-TICK = 0.1
+TIMES = (
+    0.1, 2, 0.02, 30.0, 0.1, 0.1, 0.1, 0.1, 4, 0.1, 0.02,
+    0.1, 0.1, 0.1, 0.1, 0.1, 8, 30.0, 30.0, 0.1, 0.1, 30,
+    0.1, 0.1, 8, 0.1, 0.1, 0.1, 0.5, 0.1, 0.1, 0.1, 0.1,
+)
 PACK_VMEM = 60 * 1024 * 1024
 NN = (((1,), (0,)), ((), ()))
 NT = (((1,), (1,)), ((), ()))
@@ -1059,8 +1063,10 @@
     pair = lax.axis_index("batch") & 1
     place = jnp.stack([core, pair, page, zl, zh]).astype(jnp.int32)
 
-    def run(body, operands, outs, us=TICK, scratch=(), after=(), vmem=VMEM_BYTES):
-        return kernel_call(body, place, operands, outs, us, scratch, after, vmem)
+    times = iter(TIMES)
+
+    def run(body, operands, outs, scratch=(), after=(), vmem=VMEM_BYTES):
+        return kernel_call(body, place, operands, outs, next(times), scratch, after, vmem)
 
     def rows_of(count, dtype=BF16):
         return ((count, width), dtype)
@@ -1165,7 +1171,6 @@
             ((half, inner), BF16),
             ((half, inner), BF16),
         ],
-        us=30,
         scratch=[
             pltpu.VMEM((length, inner), BF16),
             pltpu.VMEM((3, length, inner), BF16),
@@ -1310,7 +1315,6 @@
             rows_of(hidden // 2),
             ((8, hidden), F32),
         ],
-        us=30,
         scratch=[pltpu.VMEM((width, hidden), BF16)],
         after=[datt],
     )
@@ -1333,7 +1337,6 @@
             piece,
             ((2, rows, width), BF16),
         ],
-        us=30,
         scratch=[pltpu.VMEM((heads, length, length), F32), pltpu.SemaphoreType.DMA((heads,))],
         after=[bias_grad],
     )
@@ -1396,7 +1399,7 @@
         after=[up_half],
     )
     got = swap(other, "y")
-    pay_recv, pay_zl, far_send, mine = join(pay_recv, pay_zl, far_send, mine)
+    pay_recv, pay_zl, far_send, send = join(pay_recv, pay_zl, far_send, send)
     pay_core, pay_zlcore = swap(pay_recv, "core"), swap(pay_zl, "core")
     far_core = swap(far_send, "core")
     base = few + 2 * inner + 32

time: 220 us -> 218 us (level)
  waiting for transfers between devices: 90.9 us -> 85.9 us
  starting transfers between devices: 53.4 us -> 56.6 us
    ppermute x2, waiting for transfers between devices: 4.89 us -> 0.01 us  [swap_both(): lax.ppermute(value, ('batch', 'y'), [(i, i ^ 3) for i in range(size)])]
    unnamed x37 -> x39, local copies, waits for them, and re-layouts: 6.05 us -> 6.06 us
  transfers between devices with their start and end apart: 66 -> 66, of which waited for: 36 -> 35; matrix products, arithmetic and copies ran while one was open for 0% -> 0% of each run, Pallas kernels for 26% -> 26%
where the time goes in v8:
time: 218 us
  waiting for transfers between devices  85.9 us (39%)
  Pallas kernels  67.2 us (31%)
  starting transfers between devices  56.6 us (26%)
  local copies, waits for them, and re-layouts  6.88 us (3%)
    ppermute x64, waiting for transfers between devices, swap(): return lax.ppermute(value, axis, [(i, i ^ step) for i in range(size)])  85.9 us
    pallas_call x33, Pallas kernels, kernel_call(): pl.pallas_call(kernel, out_shape=[jax.ShapeDtypeStruct(out[0], out[1]) fo...  67.2 us
    ppermute x64, starting transfers between devices, swap(): return lax.ppermute(value, axis, [(i, i ^ step) for i in range(size)])  52.6 us
    unnamed x39, local copies, waits for them, and re-layouts  6.06 us
  transfers between devices with their start and end apart: 66, of which 35 were waited for; matrix products, arithmetic and copies ran while one was open for 0% of the time, Pallas kernels for 26%

profile of v8, /device:TPU:0, one launch (start us, length us, event | category | flops | bytes accessed | tf_op | source)
XLA Modules:
  0.0 217.9 jit_solution(11350680971641789380)
XLA Ops:
  1.3 3.6 %shard_map.246 = (bf16[144,768]{1,0:T(8,128)(2,1)}, bf16[128,768]{1,0:T(8,128)(2,1)}, bf16[128,768]{1,0:T(8,128)(2,1)}, bf16[272,768]{1,0:T(8,128)(2,1)}, bf16[1...) custom-call(s32[5]{0:T(128)} %stack.38.s_ref, bf16[2,2,4,32,768]{4,3,2,1,0:T(8,128)(2,1)} %bitcast.54, ...), custom_call_target="tpu_custom_call" | custom-call | flops 110000000 | bytes 350000 | tf_op jit(solution)/shard_map/pallas_call | solution.py:53
  5.4 3.7 %collective-permute-start.4 = (bf16[256,768]{1,0:T(8,128)(2,1)}, bf16[256,768]{1,0:T(8,128)(2,1)S(1)}, u32[]{:S(2)}, u32[]{:S(2)}) collective-permute-start(bf16[256,768]{1,0:T(8,128)(2,1)} %get-tuple-element.179), channel_id=1, source_target_pairs={{0,2},{2,0},{1,3},{3,1},{4,6},{6,4},{5,7},{7,5},{8,10},{10,8},{9,1... | collective-permute-start | bytes 1179656 | tf_op jit(solution)/shard_map/ppermute | solution.py:1013
  9.1 1.5 collective-permute-start
  11.1 1.5 collective-permute-start.2
  12.7 3.2 %shard_map.247 = (bf16[2,128,768]{2,1,0:T(8,128)(2,1)}, bf16[128,768]{1,0:T(8,128)(2,1)}, bf16[128,768]{1,0:T(8,128)(2,1)}) custom-call(s32[5]{0:T(128)} %stack.38.s_ref, bf16[2,2,4,32,768]{4,3,2,1,0:T(8,128)(2,1)} %bitcast.61, bf16[128,768]{1,0:T(8,128)(2,1)} %get-tuple-element.175.refs_1_.refs_0_), custom_call_target="tpu_custom_call" | custom-call | flops 2200000000 | bytes 7000000 | tf_op jit(solution)/shard_map/pallas_call | solution.py:53
  15.9 1.7 copy-done.1
  21.9 2.4 %shard_map.248 = (bf16[2,128,768]{2,1,0:T(8,128)(2,1)S(1)}, bf16[2,128,768]{2,1,0:T(8,128)(2,1)S(1)}, s32[8,256]{1,0:T(8,128)S(1)}, bf16[3,256,192]{2,1,0:T(8,12...) custom-call(s32[5]{0:T(128)S(1)} %copy-done.9, ...), custom_call_target="tpu_custom_call" | custom-call | flops 22000000 | bytes 70000 | tf_op jit(solution)/shard_map/pallas_call | solution.py:53
  25.3 2.1 collective-permute-done.4.refs_3_.refs_8_
  28.0 2.5 %collective-permute-start.10 = (bf16[256,768]{1,0:T(8,128)(2,1)S(1)}, bf16[256,768]{1,0:T(8,128)(2,1)S(1)}, u32[]{:S(2)}, u32[]{:S(2)}) collective-permute-start(bf16[256,768]{1,0:T(8,128)(2,1)S(1)} %collective-permute-done.4.refs_3_.refs_8_), channel_id=1, source_target_pairs={{0,24},{8,16},{16,8},{24,0},{1,25},{9,17},{17,9},{25,1},{2,26},{10... | collective-permute-start | bytes 1179656 | tf_op jit(solution)/shard_map/ppermute | solution.py:1018
  31.5 7.9 %shard_map.249 = (bf16[2,2,128,768]{3,2,1,0:T(8,128)(2,1)S(1)}, bf16[2,2,128,768]{3,2,1,0:T(8,128)(2,1)S(1)}, s32[512,8]{1,0:T(8,128)S(1)}, bf16[3,512,192]{2,1,...) custom-call(s32[5]{0:T(128)S(1)} %copy-done.9, ...), custom_call_target="tpu_custom_call" | custom-call | flops 32999999488 | bytes 105000000 | tf_op jit(solution)/shard_map/pallas_call | solution.py:53
  39.4 3.0 %collective-permute-start.11 = (bf16[256,192]{1,0:T(8,128)(2,1)S(1)}, bf16[256,192]{1,0:T(8,128)(2,1)S(1)}, u32[]{:S(2)}, u32[]{:S(2)}) collective-permute-start(bf16[256,192]{1,0:T(8,128)(2,1)S(1)} %get-tuple-element.196.refs_7_), channel_id=1, source_target_pairs={{0,2},{2,0},{1,3},{3,1},{4,6},{6,4},{5,7},{7,5},{8,10},{10,8},{9,1... | collective-permute-start | bytes 294920 | tf_op jit(solution)/shard_map/ppermute | solution.py:1013
  42.4 8.4 %collective-permute-done.7.refs_12_ = bf16[192,768]{1,0:T(8,128)(2,1)S(1)} collective-permute-done((bf16[192,768]{1,0:T(8,128)(2,1)S(1)}, bf16[192,768]{1,0:T(8,128)(2,1)S(1)}, u32[]{:S(2)}, u32[]{:S(2)}) %collective-permute-start.7) | collective-permute-done | bytes 294944 | tf_op jit(solution)/shard_map/ppermute | solution.py:1013
  50.7 1.6 collective-permute-start.14
  61.5 3.8 %collective-permute-done.15.refs_1_ = bf16[128,768]{1,0:T(8,128)(2,1)S(1)} collective-permute-done((bf16[128,768]{1,0:T(8,128)(2,1)S(1)}, bf16[128,768]{1,0:T(8,128)(2,1)S(1)}, u32[]{:S(2)}, u32[]{:S(2)}) %collective-permute-start.15) | collective-permute-done | bytes 196640 | tf_op jit(solution)/shard_map/ppermute | solution.py:1013
  65.9 1.8 collective-permute-start.19
  68.3 1.6 collective-permute-start.21
  70.0 2.8 %shard_map.253 = (bf16[256,768]{1,0:T(8,128)(2,1)S(1)}, bf16[256,768]{1,0:T(8,128)(2,1)S(1)}, bf16[2,256,768]{2,1,0:T(8,128)(2,1)S(1)}, bf16[2,256,768]{2,1,0:T(...) custom-call(s32[5]{0:T(128)S(1)} %copy-done.9, ...), custom_call_target="tpu_custom_call" | custom-call | flops 110000000 | bytes 350000 | tf_op jit(solution)/shard_map/pallas_call | solution.py:53
  72.8 1.8 collective-permute-start.18
  75.2 4.2 %collective-permute-done.21 = bf16[2,128,768]{2,1,0:T(8,128)(2,1)S(1)} collective-permute-done((bf16[2,128,768]{2,1,0:T(8,128)(2,1)S(1)}, bf16[2,128,768]{2,1,0:T(8,128)(2,1)S(1)}, u32[]{:S(2)}, u32[]{:S(2)}) %collective-permute-start.21) | collective-permute-done | bytes 393248 | tf_op jit(solution)/shard_map/ppermute | solution.py:1013
  81.5 2.2 %collective-permute-done.18.refs_1_ = bf16[256,768]{1,0:T(8,128)(2,1)S(1)} collective-permute-done((bf16[256,768]{1,0:T(8,128)(2,1)S(1)}, bf16[256,768]{1,0:T(8,128)(2,1)S(1)}, u32[]{:S(2)}, u32[]{:S(2)}) %collective-permute-start.18) | collective-permute-done | bytes 393248 | tf_op jit(solution)/shard_map/ppermute | solution.py:1013
  85.8 1.6 shard_map.257
  87.5 2.3 %shard_map.258 = (bf16[256,768]{1,0:T(8,128)(2,1)S(1)}, bf16[256,768]{1,0:T(8,128)(2,1)S(1)}) custom-call(s32[5]{0:T(128)S(1)} %copy-done.9, bf16[256,768]{1,0:T(8,128)(2,1)S(1)} %get-tuple-element.221.refs_0_.refs_2_, bf16[768,768]{1,0:T(8,128)(2,1)S(1)} %get-tuple-element.207.refs_5_.refs_1_, bf16[768,768]{1,0:T(8,128)(2,1)S(1)} %get-tuple-element.208.refs_7_.refs_2_, ...), custom_call_target="tpu_custom_call" | custom-call | flops 110000000 | bytes 350000 | tf_op jit(solution)/shard_map/pallas_call | solution.py:53
  89.8 2.5 %collective-permute-start.25 = (bf16[256,768]{1,0:T(8,128)(2,1)S(1)}, bf16[256,768]{1,0:T(8,128)(2,1)S(1)}, u32[]{:S(2)}, u32[]{:S(2)}) collective-permute-start(bf16[256,768]{1,0:T(8,128)(2,1)S(1)} %get-tuple-element.225.refs_4_), channel_id=1, source_target_pairs={{0,1},{1,0},{2,3},{3,2},{4,5},{5,4},{6,7},{7,6},{8,9},{9,8},{10,11... | collective-permute-start | bytes 1179656 | tf_op jit(solution)/shard_map/ppermute | solution.py:1013
  92.4 1.7 collective-permute-start.27
  95.5 8.2 %collective-permute-done.25.refs_5_ = bf16[256,768]{1,0:T(8,128)(2,1)S(1)} collective-permute-done((bf16[256,768]{1,0:T(8,128)(2,1)S(1)}, bf16[256,768]{1,0:T(8,128)(2,1)S(1)}, u32[]{:S(2)}, u32[]{:S(2)}) %collective-permute-start.25) | collective-permute-done | bytes 393248 | tf_op jit(solution)/shard_map/ppermute | solution.py:1013
  107.6 2.4 %collective-permute-start.30 = (bf16[256,192]{1,0:T(8,128)(2,1)S(1)}, bf16[256,192]{1,0:T(8,128)(2,1)S(1)}, u32[]{:S(2)}, u32[]{:S(2)}) collective-permute-start(bf16[256,192]{1,0:T(8,128)(2,1)S(1)} %get-tuple-element.240), channel_id=1, source_target_pairs={{0,2},{2,0},{1,3},{3,1},{4,6},{6,4},{5,7},{7,5},{8,10},{10,8},{9,1... | collective-permute-start | bytes 294920 | tf_op jit(solution)/shard_map/ppermute | solution.py:1013
  110.0 5.0 %collective-permute-done.28.refs_4_ = bf16[128,768]{1,0:T(8,128)(2,1)S(1)} collective-permute-done((bf16[128,768]{1,0:T(8,128)(2,1)S(1)}, bf16[128,768]{1,0:T(8,128)(2,1)S(1)}, u32[]{:S(2)}, u32[]{:S(2)}) %collective-permute-start.28) | collective-permute-done | bytes 196640 | tf_op jit(solution)/shard_map/ppermute | solution.py:1013
  115.0 2.4 %shard_map.262 = (bf16[2,64,768]{2,1,0:T(8,128)(2,1)S(1)}, bf16[2,64,768]{2,1,0:T(8,128)(2,1)S(1)}, f32[256,768]{1,0:T(8,128)}, bf16[256,768]{1,0:T(8,128)(2,1)S(1)}, f32[8,768]{1,0:T(8,128)}) custom-call(s32[5]{0:T(128)S(1)} %copy-done.9, bf16[2,2,128,768]{3,2,1,0:T(8,128)(2,1)S(1)} %get-tuple-element.189.refs_0_, ...), custom_call_target="tpu_custom_call" | custom-call | flops 8800000000 | bytes 28000000 | tf_op jit(solution)/shard_map/pallas_call | solution.py:53
  117.4 2.1 shard_map.263
  120.1 1.6 collective-permute-start.37
  121.8 5.3 %shard_map.264 = (bf16[3,512,512]{2,1,0:T(8,128)(2,1)S(1)}, bf16[3,512,192]{2,1,0:T(8,128)(2,1)S(1)}, bf16[2,512,192]{2,1,0:T(8,128)(2,1)S(1)}, bf16[128,768]{1,...) custom-call(s32[5]{0:T(128)S(1)} %copy-done.9, ...), custom_call_target="tpu_custom_call" | custom-call | flops 32999999488 | bytes 105000000 | tf_op jit(solution)/shard_map/pallas_call | solution.py:53
  132.2 2.2 collective-permute-done.36.refs_1_
  137.0 1.6 collective-permute-start.44
  139.7 5.9 %shard_map.268 = (bf16[240,768]{1,0:T(8,128)(2,1)S(1)}, bf16[240,768]{1,0:T(8,128)(2,1)S(1)}, bf16[96,768]{1,0:T(8,128)(2,1)S(1)}, f32[16,768]{1,0:T(8,128)S(1)}) custom-call(s32[5]{0:T(128)S(1)} %copy-done.9, bf16[2,2,128,768]{3,2,1,0:T(8,128)(2,1)S(1)} %get-tuple-element.189.refs_0_, bf16[3,512,512]{2,1,0:T(8,128)(2,1)S(1)} %get-tuple-element.267.refs_1_, ...), custom_call_target="tpu_custom_call" | custom-call | flops 110000000 | bytes 350000 | tf_op jit(solution)/shard_map/pallas_call | solution.py:53
  147.5 1.8 collective-permute-done.45.refs_3_
  151.3 1.7 collective-permute-start.47
  153.6 2.0 collective-permute-start.34
  155.6 10.2 %collective-permute-done.43.refs_1_ = bf16[3,64,768]{2,1,0:T(8,128)(2,1)S(1)} collective-permute-done((bf16[3,64,768]{2,1,0:T(8,128)(2,1)S(1)}, bf16[3,64,768]{2,1,0:T(8,128)(2,1)S(1)}, u32[]{:S(2)}, u32[]{:S(2)}) %collective-permute-start.43) | collective-permute-done | bytes 294944 | tf_op jit(solution)/shard_map/ppermute | solution.py:1013
  170.0 2.1 collective-permute-done.48.refs_1_
  175.8 1.8 collective-permute-start.57
  177.7 5.1 %shard_map.273 = (f32[2,2,384,768]{3,2,1,0:T(8,128)}, f32[2,2,384,768]{3,2,1,0:T(8,128)}, f32[8,128]{1,0:T(8,128)S(1)}) custom-call(s32[5]{0:T(128)S(1)} %copy-done.9, bf16[384,768]{1,0:T(8,128)(2,1)S(1)} %get-tuple-element.300.refs_2_.refs_0_, bf16[384,768]{1,0:T(8,128)(2,1)S(1)} %collective-permute-done.46.refs_13_.refs_1_, ...), custom_call_target="tpu_custom_call" | custom-call | flops 110000000 | bytes 350000 | tf_op jit(solution)/shard_map/pallas_call | solution.py:53
  182.7 2.0 collective-permute-done.49.refs_1_
  188.7 3.4 %collective-permute-done.57.refs_2_ = bf16[2,3,32,768]{3,2,1,0:T(8,128)(2,1)S(1)} collective-permute-done((bf16[2,3,32,768]{3,2,1,0:T(8,128)(2,1)S(1)}, bf16[2,3,32,768]{3,2,1,0:T(8,128)(2,1)S(1)}, u32[]{:S(2)}, u32[]{:S(2)}) %collective-permute-start.57) | collective-permute-done | bytes 294944 | tf_op jit(solution)/shard_map/ppermute | solution.py:1013
  192.8 7.6 %collective-permute-done.59.refs_4_ = bf16[2,3,32,768]{3,2,1,0:T(8,128)(2,1)S(1)} collective-permute-done((bf16[2,3,32,768]{3,2,1,0:T(8,128)(2,1)S(1)}, bf16[2,3,32,768]{3,2,1,0:T(8,128)(2,1)S(1)}, u32[]{:S(2)}, u32[]{:S(2)}) %collective-permute-start.59) | collective-permute-done | bytes 294944 | tf_op jit(solution)/shard_map/ppermute | solution.py:1013
  204.8 2.1 shard_map.277
  206.9 3.2 %collective-permute-done.60.refs_1_ = bf16[240,768]{1,0:T(8,128)(2,1)S(1)} collective-permute-done((bf16[240,768]{1,0:T(8,128)(2,1)S(1)}, bf16[240,768]{1,0:T(8,128)(2,1)S(1)}, u32[]{:S(2)}, u32[]{:S(2)}) %collective-permute-start.60) | collective-permute-done | bytes 368672 | tf_op jit(solution)/shard_map/ppermute | solution.py:1013
  211.9 1.7 collective-permute-done.62.refs_2_
  214.1 3.7 %shard_map.278 = (f32[2,576,768]{2,1,0:T(8,128)}, f32[2,192,768]{2,1,0:T(8,128)}, f32[2,192,768]{2,1,0:T(8,128)}, f32[3,3,2,128]{3,2,1,0:T(2,128)}, f32[2,2,192]...) custom-call(s32[5]{0:T(128)S(1)} %copy-done.9, ...), custom_call_target="tpu_custom_call" | custom-call | flops 110000000 | bytes 350000 | tf_op jit(solution)/shard_map/pallas_call | solution.py:53
  (170 shorter events, 62.2 us)
Async XLA Ops:
  4.9 11.0 %collective-permute-start.3 = (bf16[272,768]{1,0:T(8,128)(2,1)}, bf16[272,768]{1,0:T(8,128)(2,1)}, u32[]{:S(2)}, u32[]{:S(2)}) collective-permute-start(bf16[272,768]{1,0:T(8,128)(2,1)} %get-tuple-element.176.refs_2_), channel_id=1, source_target_pairs={{0,4},{4,0},{1,5},{5,1},{2,6},{6,2},{3,7},{7,3},{8,12},{12,8},{9,1... | collective-permute-start | bytes 1253384 | tf_op jit(solution)/shard_map/ppermute | solution.py:1013
  5.4 22.0 %collective-permute-start.4 = (bf16[256,768]{1,0:T(8,128)(2,1)}, bf16[256,768]{1,0:T(8,128)(2,1)S(1)}, u32[]{:S(2)}, u32[]{:S(2)}) collective-permute-start(bf16[256,768]{1,0:T(8,128)(2,1)} %get-tuple-element.179), channel_id=1, source_target_pairs={{0,2},{2,0},{1,3},{3,1},{4,6},{6,4},{5,7},{7,5},{8,10},{10,8},{9,1... | collective-permute-start | bytes 1179656 | tf_op jit(solution)/shard_map/ppermute | solution.py:1013
  9.1 16.2 %collective-permute-start = (bf16[144,768]{1,0:T(8,128)(2,1)}, bf16[144,768]{1,0:T(8,128)(2,1)}, u32[]{:S(2)}, u32[]{:S(2)}) collective-permute-start(bf16[144,768]{1,0:T(8,128)(2,1)} %get-tuple-element.172), channel_id=1, source_target_pairs={{0,8},{8,0},{1,9},{9,1},{2,10},{10,2},{3,11},{11,3},{4,12},{12,4},... | collective-permute-start | bytes 663560 | tf_op jit(solution)/shard_map/ppermute | solution.py:1013
  10.6 13.7 %collective-permute-start.1 = (bf16[128,768]{1,0:T(8,128)(2,1)}, bf16[128,768]{1,0:T(8,128)(2,1)}, u32[]{:S(2)}, u32[]{:S(2)}) collective-permute-start(bf16[128,768]{1,0:T(8,128)(2,1)} %get-tuple-element.173), channel_id=1, source_target_pairs={{0,8},{8,0},{1,9},{9,1},{2,10},{10,2},{3,11},{11,3},{4,12},{12,4},... | collective-permute-start | bytes 589832 | tf_op jit(solution)/shard_map/ppermute | solution.py:1013
  11.1 14.2 %collective-permute-start.2 = (bf16[128,768]{1,0:T(8,128)(2,1)}, bf16[128,768]{1,0:T(8,128)(2,1)}, u32[]{:S(2)}, u32[]{:S(2)}) collective-permute-start(bf16[128,768]{1,0:T(8,128)(2,1)} %get-tuple-element.174), channel_id=1, source_target_pairs={{0,8},{8,0},{1,9},{9,1},{2,10},{10,2},{3,11},{11,3},{4,12},{12,4},... | collective-permute-start | bytes 589832 | tf_op jit(solution)/shard_map/ppermute | solution.py:1013
  28.0 22.8 %collective-permute-start.10 = (bf16[256,768]{1,0:T(8,128)(2,1)S(1)}, bf16[256,768]{1,0:T(8,128)(2,1)S(1)}, u32[]{:S(2)}, u32[]{:S(2)}) collective-permute-start(bf16[256,768]{1,0:T(8,128)(2,1)S(1)} %collective-permute-done.4.refs_3_.refs_8_), channel_id=1, source_target_pairs={{0,24},{8,16},{16,8},{24,0},{1,25},{9,17},{17,9},{25,1},{2,26},{10... | collective-permute-start | bytes 1179656 | tf_op jit(solution)/shard_map/ppermute | solution.py:1018
  30.5 20.3 %collective-permute-start.9 = (bf16[256,768]{1,0:T(8,128)(2,1)S(1)}, bf16[256,768]{1,0:T(8,128)(2,1)S(1)}, u32[]{:S(2)}, u32[]{:S(2)}) collective-permute-start(bf16[256,768]{1,0:T(8,128)(2,1)S(1)} %collective-permute-done.4.refs_3_.refs_8_), channel_id=1, source_target_pairs={{0,16},{16,0},{1,17},{17,1},{2,18},{18,2},{3,19},{19,3},{4,20},{20... | collective-permute-start | bytes 1179656 | tf_op jit(solution)/shard_map/ppermute | solution.py:1013
  31.0 19.7 %collective-permute-start.8 = (bf16[256,768]{1,0:T(8,128)(2,1)S(1)}, bf16[256,768]{1,0:T(8,128)(2,1)S(1)}, u32[]{:S(2)}, u32[]{:S(2)}) collective-permute-start(bf16[256,768]{1,0:T(8,128)(2,1)S(1)} %collective-permute-done.4.refs_3_.refs_8_), channel_id=1, source_target_pairs={{0,8},{8,0},{1,9},{9,1},{2,10},{10,2},{3,11},{11,3},{4,12},{12,4},... | collective-permute-start | bytes 1179656 | tf_op jit(solution)/shard_map/ppermute | solution.py:1013
  31.5 19.3 %collective-permute-start.7 = (bf16[192,768]{1,0:T(8,128)(2,1)S(1)}, bf16[192,768]{1,0:T(8,128)(2,1)S(1)}, u32[]{:S(2)}, u32[]{:S(2)}) collective-permute-start(bf16[192,768]{1,0:T(8,128)(2,1)S(1)} %copy-done.17), channel_id=1, source_target_pairs={{0,2},{2,0},{1,3},{3,1},{4,6},{6,4},{5,7},{7,5},{8,10},{10,8},{9,1... | collective-permute-start | bytes 884744 | tf_op jit(solution)/shard_map/ppermute | solution.py:1013
  39.4 14.4 %collective-permute-start.11 = (bf16[256,192]{1,0:T(8,128)(2,1)S(1)}, bf16[256,192]{1,0:T(8,128)(2,1)S(1)}, u32[]{:S(2)}, u32[]{:S(2)}) collective-permute-start(bf16[256,192]{1,0:T(8,128)(2,1)S(1)} %get-tuple-element.196.refs_7_), channel_id=1, source_target_pairs={{0,2},{2,0},{1,3},{3,1},{4,6},{6,4},{5,7},{7,5},{8,10},{10,8},{9,1... | collective-permute-start | bytes 294920 | tf_op jit(solution)/shard_map/ppermute | solution.py:1013
  50.7 6.8 %collective-permute-start.14 = (bf16[192,768]{1,0:T(8,128)(2,1)S(1)}, bf16[192,768]{1,0:T(8,128)(2,1)S(1)}, u32[]{:S(2)}, u32[]{:S(2)}) collective-permute-start(bf16[192,768]{1,0:T(8,128)(2,1)S(1)} %collective-permute-done.7.refs_12_), channel_id=1, source_target_pairs={{0,16},{16,0},{1,17},{17,1},{2,18},{18,2},{3,19},{19,3},{4,20},{20... | collective-permute-start | bytes 884744 | tf_op jit(solution)/shard_map/ppermute | solution.py:1013
  52.3 6.7 %collective-permute-start.13 = (bf16[192,768]{1,0:T(8,128)(2,1)S(1)}, bf16[192,768]{1,0:T(8,128)(2,1)S(1)}, u32[]{:S(2)}, u32[]{:S(2)}) collective-permute-start(bf16[192,768]{1,0:T(8,128)(2,1)S(1)} %collective-permute-done.7.refs_12_), channel_id=1, source_target_pairs={{0,8},{8,0},{1,9},{9,1},{2,10},{10,2},{3,11},{11,3},{4,12},{12,4},... | collective-permute-start | bytes 884744 | tf_op jit(solution)/shard_map/ppermute | solution.py:1013
  59.6 5.7 %collective-permute-start.15 = (bf16[128,768]{1,0:T(8,128)(2,1)S(1)}, bf16[128,768]{1,0:T(8,128)(2,1)S(1)}, u32[]{:S(2)}, u32[]{:S(2)}) collective-permute-start(bf16[128,768]{1,0:T(8,128)(2,1)S(1)} %shard_map.251.refs_0_), channel_id=1, source_target_pairs={{0,1},{1,0},{2,3},{3,2},{4,5},{5,4},{6,7},{7,6},{8,9},{9,8},{10,11... | collective-permute-start | bytes 589832 | tf_op jit(solution)/shard_map/ppermute | solution.py:1013
  60.0 9.9 %collective-permute-start.17 = (bf16[192,768]{1,0:T(8,128)(2,1)S(1)}, bf16[192,768]{1,0:T(8,128)(2,1)S(1)}, u32[]{:S(2)}, u32[]{:S(2)}) collective-permute-start(bf16[192,768]{1,0:T(8,128)(2,1)S(1)} %collective-permute-done.7.refs_12_), channel_id=1, source_target_pairs={{0,24},{8,16},{16,8},{24,0},{1,25},{9,17},{17,9},{25,1},{2,26},{10... | collective-permute-start | bytes 884744 | tf_op jit(solution)/shard_map/ppermute | solution.py:1018
  65.9 9.2 %collective-permute-start.19 = (bf16[128,768]{1,0:T(8,128)(2,1)S(1)}, bf16[128,768]{1,0:T(8,128)(2,1)S(1)}, u32[]{:S(2)}, u32[]{:S(2)}) collective-permute-start(bf16[128,768]{1,0:T(8,128)(2,1)S(1)} %shard_map.252.refs_1_), channel_id=1, source_target_pairs={{0,2},{2,0},{1,3},{3,1},{4,6},{6,4},{5,7},{7,5},{8,10},{10,8},{9,1... | collective-permute-start | bytes 589832 | tf_op jit(solution)/shard_map/ppermute | solution.py:1013
  67.8 7.4 %collective-permute-start.22 = (bf16[128,768]{1,0:T(8,128)(2,1)S(1)}, bf16[128,768]{1,0:T(8,128)(2,1)S(1)}, u32[]{:S(2)}, u32[]{:S(2)}) collective-permute-start(bf16[128,768]{1,0:T(8,128)(2,1)S(1)} %copy-done.18), channel_id=1, source_target_pairs={{0,4},{4,0},{1,5},{5,1},{2,6},{6,2},{3,7},{7,3},{8,12},{12,8},{9,1... | collective-permute-start | bytes 589832 | tf_op jit(solution)/shard_map/ppermute | solution.py:1013
  68.3 11.1 %collective-permute-start.21 = (bf16[2,128,768]{2,1,0:T(8,128)(2,1)S(1)}, bf16[2,128,768]{2,1,0:T(8,128)(2,1)S(1)}, u32[]{:S(2)}, u32[]{:S(2)}) collective-permute-start(bf16[2,128,768]{2,1,0:T(8,128)(2,1)S(1)} %copy-done.16), channel_id=1, source_target_pairs={{0,8},{8,0},{1,9},{9,1},{2,10},{10,2},{3,11},{11,3},{4,12},{12,4},... | collective-permute-start | bytes 1179656 | tf_op jit(solution)/shard_map/ppermute | solution.py:1013
  72.8 10.9 %collective-permute-start.18 = (bf16[256,768]{1,0:T(8,128)(2,1)S(1)}, bf16[256,768]{1,0:T(8,128)(2,1)S(1)}, u32[]{:S(2)}, u32[]{:S(2)}) collective-permute-start(bf16[256,768]{1,0:T(8,128)(2,1)S(1)} %get-tuple-element.213.refs_5_.refs_0_), channel_id=1, source_target_pairs={{0,1},{1,0},{2,3},{3,2},{4,5},{5,4},{6,7},{7,6},{8,9},{9,8},{10,11... | collective-permute-start | bytes 1179656 | tf_op jit(solution)/shard_map/ppermute | solution.py:1013
  79.4 6.4 %collective-permute-start.23 = (bf16[2,128,768]{2,1,0:T(8,128)(2,1)S(1)}, bf16[2,128,768]{2,1,0:T(8,128)(2,1)S(1)}, u32[]{:S(2)}, u32[]{:S(2)}) collective-permute-start(bf16[2,128,768]{2,1,0:T(8,128)(2,1)S(1)} %collective-permute-done.21), channel_id=1, source_target_pairs={{0,4},{4,0},{1,5},{5,1},{2,6},{6,2},{3,7},{7,3},{8,12},{12,8},{9,1... | collective-permute-start | bytes 1179656 | tf_op jit(solution)/shard_map/ppermute | solution.py:1013
  84.3 11.1 %collective-permute-start.26 = (bf16[128,768]{1,0:T(8,128)(2,1)S(1)}, bf16[128,768]{1,0:T(8,128)(2,1)S(1)}, u32[]{:S(2)}, u32[]{:S(2)}) collective-permute-start(bf16[128,768]{1,0:T(8,128)(2,1)S(1)} %get-tuple-element.215.refs_3_), channel_id=1, source_target_pairs={{0,2},{2,0},{1,3},{3,1},{4,6},{6,4},{5,7},{7,5},{8,10},{10,8},{9,1... | collective-permute-start | bytes 589832 | tf_op jit(solution)/shard_map/ppermute | solution.py:1013
  89.8 13.9 %collective-permute-start.25 = (bf16[256,768]{1,0:T(8,128)(2,1)S(1)}, bf16[256,768]{1,0:T(8,128)(2,1)S(1)}, u32[]{:S(2)}, u32[]{:S(2)}) collective-permute-start(bf16[256,768]{1,0:T(8,128)(2,1)S(1)} %get-tuple-element.225.refs_4_), channel_id=1, source_target_pairs={{0,1},{1,0},{2,3},{3,2},{4,5},{5,4},{6,7},{7,6},{8,9},{9,8},{10,11... | collective-permute-start | bytes 1179656 | tf_op jit(solution)/shard_map/ppermute | solution.py:1013
  92.4 11.3 %collective-permute-start.27 = (bf16[2,64,768]{2,1,0:T(8,128)(2,1)S(1)}, bf16[2,64,768]{2,1,0:T(8,128)(2,1)S(1)}, u32[]{:S(2)}, u32[]{:S(2)}) collective-permute-start(bf16[2,64,768]{2,1,0:T(8,128)(2,1)S(1)} %pad_maximum_fusion.1), channel_id=1, source_target_pairs={{0,8},{8,0},{1,9},{9,1},{2,10},{10,2},{3,11},{11,3},{4,12},{12,4},... | collective-permute-start | bytes 589832 | tf_op jit(solution)/shard_map/ppermute | solution.py:1013
  105.1 9.9 %collective-permute-start.28 = (bf16[128,768]{1,0:T(8,128)(2,1)S(1)}, bf16[128,768]{1,0:T(8,128)(2,1)S(1)}, u32[]{:S(2)}, u32[]{:S(2)}) collective-permute-start(bf16[128,768]{1,0:T(8,128)(2,1)S(1)} %collective-permute-done.26.refs_3_), channel_id=1, source_target_pairs={{0,1},{1,0},{2,3},{3,2},{4,5},{5,4},{6,7},{7,6},{8,9},{9,8},{10,11... | collective-permute-start | bytes 589832 | tf_op jit(solution)/shard_map/ppermute | solution.py:1013
  107.6 14.1 %collective-permute-start.30 = (bf16[256,192]{1,0:T(8,128)(2,1)S(1)}, bf16[256,192]{1,0:T(8,128)(2,1)S(1)}, u32[]{:S(2)}, u32[]{:S(2)}) collective-permute-start(bf16[256,192]{1,0:T(8,128)(2,1)S(1)} %get-tuple-element.240), channel_id=1, source_target_pairs={{0,2},{2,0},{1,3},{3,1},{4,6},{6,4},{5,7},{7,5},{8,10},{10,8},{9,1... | collective-permute-start | bytes 294920 | tf_op jit(solution)/shard_map/ppermute | solution.py:1013
  119.5 14.9 %collective-permute-start.36 = (bf16[384,768]{1,0:T(8,128)(2,1)S(1)}, bf16[384,768]{1,0:T(8,128)(2,1)S(1)}, u32[]{:S(2)}, u32[]{:S(2)}) collective-permute-start(bf16[384,768]{1,0:T(8,128)(2,1)S(1)} %get-tuple-element.273), channel_id=1, source_target_pairs={{0,16},{16,0},{1,17},{17,1},{2,18},{18,2},{3,19},{19,3},{4,20},{20... | collective-permute-start | bytes 1769480 | tf_op jit(solution)/shard_map/ppermute | solution.py:1013
  120.1 14.6 %collective-permute-start.37 = (bf16[384,768]{1,0:T(8,128)(2,1)S(1)}, bf16[384,768]{1,0:T(8,128)(2,1)S(1)}, u32[]{:S(2)}, u32[]{:S(2)}) collective-permute-start(bf16[384,768]{1,0:T(8,128)(2,1)S(1)} %get-tuple-element.275), channel_id=1, source_target_pairs={{0,8},{8,0},{1,9},{9,1},{2,10},{10,2},{3,11},{11,3},{4,12},{12,4},... | collective-permute-start | bytes 1769480 | tf_op jit(solution)/shard_map/ppermute | solution.py:1013
  121.8 6.6 %collective-permute-start.31 = (bf16[80,768]{1,0:T(8,128)(2,1)S(1)}, bf16[80,768]{1,0:T(8,128)(2,1)S(1)}, u32[]{:S(2)}, u32[]{:S(2)}) collective-permute-start(bf16[80,768]{1,0:T(8,128)(2,1)S(1)} %get-tuple-element.255.refs_1_), channel_id=1, source_target_pairs={{0,2},{2,0},{1,3},{3,1},{4,6},{6,4},{5,7},{7,5},{8,10},{10,8},{9,1... | collective-permute-start | bytes 368648 | tf_op jit(solution)/shard_map/ppermute | solution.py:1013
  131.4 15.4 %collective-permute-start.35 = (bf16[3,128,768]{2,1,0:T(8,128)(2,1)S(1)}, bf16[3,128,768]{2,1,0:T(8,128)(2,1)S(1)}, u32[]{:S(2)}, u32[]{:S(2)}) collective-permute-start(bf16[3,128,768]{2,1,0:T(8,128)(2,1)S(1)} %get-tuple-element.263.refs_4_), channel_id=1, source_target_pairs={{0,1},{1,0},{2,3},{3,2},{4,5},{5,4},{6,7},{7,6},{8,9},{9,8},{10,11... | collective-permute-start | bytes 1769480 | tf_op jit(solution)/shard_map/ppermute | solution.py:1013
  135.5 13.7 %collective-permute-start.45 = (bf16[384,768]{1,0:T(8,128)(2,1)S(1)}, bf16[384,768]{1,0:T(8,128)(2,1)S(1)}, u32[]{:S(2)}, u32[]{:S(2)}) collective-permute-start(bf16[384,768]{1,0:T(8,128)(2,1)S(1)} %get-tuple-element.289.refs_2_), channel_id=1, source_target_pairs={{0,16},{16,0},{1,17},{17,1},{2,18},{18,2},{3,19},{19,3},{4,20},{20... | collective-permute-start | bytes 1769480 | tf_op jit(solution)/shard_map/ppermute | solution.py:1013
  137.0 13.4 %collective-permute-start.44 = (bf16[384,768]{1,0:T(8,128)(2,1)S(1)}, bf16[384,768]{1,0:T(8,128)(2,1)S(1)}, u32[]{:S(2)}, u32[]{:S(2)}) collective-permute-start(bf16[384,768]{1,0:T(8,128)(2,1)S(1)} %get-tuple-element.276.refs_2_.refs_0_), channel_id=1, source_target_pairs={{0,8},{8,0},{1,9},{9,1},{2,10},{10,2},{3,11},{11,3},{4,12},{12,4},... | collective-permute-start | bytes 1769480 | tf_op jit(solution)/shard_map/ppermute | solution.py:1013
  151.3 17.7 %collective-permute-start.47 = (bf16[384,768]{1,0:T(8,128)(2,1)S(1)}, bf16[384,768]{1,0:T(8,128)(2,1)S(1)}, u32[]{:S(2)}, u32[]{:S(2)}) collective-permute-start(bf16[384,768]{1,0:T(8,128)(2,1)S(1)} %get-tuple-element.302.refs_4_), channel_id=1, source_target_pairs={{0,8},{8,0},{1,9},{9,1},{2,10},{10,2},{3,11},{11,3},{4,12},{12,4},... | collective-permute-start | bytes 1769480 | tf_op jit(solution)/shard_map/ppermute | solution.py:1013
  153.0 16.0 %collective-permute-start.46 = (bf16[384,768]{1,0:T(8,128)(2,1)S(1)}, bf16[384,768]{1,0:T(8,128)(2,1)S(1)}, u32[]{:S(2)}, u32[]{:S(2)}) collective-permute-start(bf16[384,768]{1,0:T(8,128)(2,1)S(1)} %get-tuple-element.300.refs_2_.refs_0_), channel_id=1, source_target_pairs={{0,16},{16,0},{1,17},{17,1},{2,18},{18,2},{3,19},{19,3},{4,20},{20... | collective-permute-start | bytes 1769480 | tf_op jit(solution)/shard_map/ppermute | solution.py:1013
  153.6 12.2 %collective-permute-start.43 = (bf16[3,64,768]{2,1,0:T(8,128)(2,1)S(1)}, bf16[3,64,768]{2,1,0:T(8,128)(2,1)S(1)}, u32[]{:S(2)}, u32[]{:S(2)}) collective-permute-start(bf16[3,64,768]{2,1,0:T(8,128)(2,1)S(1)} %get-tuple-element.279.refs_4_), channel_id=1, source_target_pairs={{0,2},{2,0},{1,3},{3,1},{4,6},{6,4},{5,7},{7,5},{8,10},{10,8},{9,1... | collective-permute-start | bytes 884744 | tf_op jit(solution)/shard_map/ppermute | solution.py:1013
  153.6 13.9 %collective-permute-start.42 = (bf16[192,768]{1,0:T(8,128)(2,1)S(1)}, bf16[192,768]{1,0:T(8,128)(2,1)S(1)}, u32[]{:S(2)}, u32[]{:S(2)}) collective-permute-start(bf16[192,768]{1,0:T(8,128)(2,1)S(1)} %get-tuple-element.287), channel_id=1, source_target_pairs={{0,4},{4,0},{1,5},{5,1},{2,6},{6,2},{3,7},{7,3},{8,12},{12,8},{9,1... | collective-permute-start | bytes 884744 | tf_op jit(solution)/shard_map/ppermute | solution.py:1013
  153.6 13.9 %collective-permute-start.34 = (bf16[80,768]{1,0:T(8,128)(2,1)S(1)}, bf16[80,768]{1,0:T(8,128)(2,1)S(1)}, u32[]{:S(2)}, u32[]{:S(2)}) collective-permute-start(bf16[80,768]{1,0:T(8,128)(2,1)S(1)} %collective-permute-done.31.refs_2_), channel_id=1, source_target_pairs={{0,1},{1,0},{2,3},{3,2},{4,5},{5,4},{6,7},{7,6},{8,9},{9,8},{10,11... | collective-permute-start | bytes 368648 | tf_op jit(solution)/shard_map/ppermute | solution.py:1013
  166.4 5.7 %collective-permute-start.48 = (bf16[3,32,768]{2,1,0:T(8,128)(2,1)S(1)}, bf16[3,32,768]{2,1,0:T(8,128)(2,1)S(1)}, u32[]{:S(2)}, u32[]{:S(2)}) collective-permute-start(bf16[3,32,768]{2,1,0:T(8,128)(2,1)S(1)} %get-tuple-element.294), channel_id=1, source_target_pairs={{0,8},{8,0},{1,9},{9,1},{2,10},{10,2},{3,11},{11,3},{4,12},{12,4},... | collective-permute-start | bytes 442376 | tf_op jit(solution)/shard_map/ppermute | solution.py:1013
  173.2 11.6 %collective-permute-start.50 = (bf16[256,768]{1,0:T(8,128)(2,1)S(1)}, bf16[256,768]{1,0:T(8,128)(2,1)S(1)}, u32[]{:S(2)}, u32[]{:S(2)}) collective-permute-start(bf16[256,768]{1,0:T(8,128)(2,1)S(1)} %get-tuple-element.298), channel_id=1, source_target_pairs={{0,8},{8,0},{1,9},{9,1},{2,10},{10,2},{3,11},{11,3},{4,12},{12,4},... | collective-permute-start | bytes 1179656 | tf_op jit(solution)/shard_map/ppermute | solution.py:1013
  174.1 10.6 %collective-permute-start.49 = (bf16[240,768]{1,0:T(8,128)(2,1)S(1)}, bf16[240,768]{1,0:T(8,128)(2,1)S(1)}, u32[]{:S(2)}, u32[]{:S(2)}) collective-permute-start(bf16[240,768]{1,0:T(8,128)(2,1)S(1)} %get-tuple-element.296), channel_id=1, source_target_pairs={{0,16},{16,0},{1,17},{17,1},{2,18},{18,2},{3,19},{19,3},{4,20},{20... | collective-permute-start | bytes 1105928 | tf_op jit(solution)/shard_map/ppermute | solution.py:1013
  175.2 13.5 %collective-permute-start.58 = (bf16[2,3,32,768]{3,2,1,0:T(8,128)(2,1)S(1)}, bf16[2,3,32,768]{3,2,1,0:T(8,128)(2,1)S(1)}, u32[]{:S(2)}, u32[]{:S(2)}) collective-permute-start(bf16[2,3,32,768]{3,2,1,0:T(8,128)(2,1)S(1)} %pad_maximum_fusion.refs_8_), channel_id=1, source_target_pairs={{0,1},{1,0},{2,3},{3,2},{4,5},{5,4},{6,7},{7,6},{8,9},{9,8},{10,11... | collective-permute-start | bytes 884744 | tf_op jit(solution)/shard_map/ppermute | solution.py:1013
  175.8 16.3 %collective-permute-start.57 = (bf16[2,3,32,768]{3,2,1,0:T(8,128)(2,1)S(1)}, bf16[2,3,32,768]{3,2,1,0:T(8,128)(2,1)S(1)}, u32[]{:S(2)}, u32[]{:S(2)}) collective-permute-start(bf16[2,3,32,768]{3,2,1,0:T(8,128)(2,1)S(1)} %pad_maximum_fusion.refs_8_), channel_id=1, source_target_pairs={{0,2},{2,0},{1,3},{3,1},{4,6},{6,4},{5,7},{7,5},{8,10},{10,8},{9,1... | collective-permute-start | bytes 884744 | tf_op jit(solution)/shard_map/ppermute | solution.py:1013
  177.7 14.5 %collective-permute-start.38 = (bf16[2,64,768]{2,1,0:T(8,128)(2,1)S(1)}, bf16[2,64,768]{2,1,0:T(8,128)(2,1)S(1)}, u32[]{:S(2)}, u32[]{:S(2)}) collective-permute-start(bf16[2,64,768]{2,1,0:T(8,128)(2,1)S(1)} %get-tuple-element.280), channel_id=1, source_target_pairs={{0,4},{4,0},{1,5},{5,1},{2,6},{6,2},{3,7},{7,3},{8,12},{12,8},{9,1... | collective-permute-start | bytes 589832 | tf_op jit(solution)/shard_map/ppermute | solution.py:1013
  185.5 14.9 %collective-permute-start.55 = (bf16[240,768]{1,0:T(8,128)(2,1)S(1)}, bf16[240,768]{1,0:T(8,128)(2,1)S(1)}, u32[]{:S(2)}, u32[]{:S(2)}) collective-permute-start(bf16[240,768]{1,0:T(8,128)(2,1)S(1)} %get-tuple-element.306.refs_0_), channel_id=1, source_target_pairs={{0,8},{8,0},{1,9},{9,1},{2,10},{10,2},{3,11},{11,3},{4,12},{12,4},... | collective-permute-start | bytes 1105928 | tf_op jit(solution)/shard_map/ppermute | solution.py:1013
  186.3 14.1 %collective-permute-start.56 = (bf16[256,768]{1,0:T(8,128)(2,1)S(1)}, bf16[256,768]{1,0:T(8,128)(2,1)S(1)}, u32[]{:S(2)}, u32[]{:S(2)}) collective-permute-start(bf16[256,768]{1,0:T(8,128)(2,1)S(1)} %get-tuple-element.307.refs_2_), channel_id=1, source_target_pairs={{0,16},{16,0},{1,17},{17,1},{2,18},{18,2},{3,19},{19,3},{4,20},{20... | collective-permute-start | bytes 1179656 | tf_op jit(solution)/shard_map/ppermute | solution.py:1013
  192.1 8.2 %collective-permute-start.59 = (bf16[2,3,32,768]{3,2,1,0:T(8,128)(2,1)S(1)}, bf16[2,3,32,768]{3,2,1,0:T(8,128)(2,1)S(1)}, u32[]{:S(2)}, u32[]{:S(2)}) collective-permute-start(bf16[2,3,32,768]{3,2,1,0:T(8,128)(2,1)S(1)} %collective-permute-done.57.refs_2_), channel_id=1, source_target_pairs={{0,1},{1,0},{2,3},{3,2},{4,5},{5,4},{6,7},{7,6},{8,9},{9,8},{10,11... | collective-permute-start | bytes 884744 | tf_op jit(solution)/shard_map/ppermute | solution.py:1013
  192.2 11.0 %collective-permute-start.39 = (bf16[2,64,768]{2,1,0:T(8,128)(2,1)S(1)}, bf16[2,64,768]{2,1,0:T(8,128)(2,1)S(1)}, u32[]{:S(2)}, u32[]{:S(2)}) collective-permute-start(bf16[2,64,768]{2,1,0:T(8,128)(2,1)S(1)} %pad_maximum_fusion.2), channel_id=1, source_target_pairs={{0,8},{8,0},{1,9},{9,1},{2,10},{10,2},{3,11},{11,3},{4,12},{12,4},... | collective-permute-start | bytes 589832 | tf_op jit(solution)/shard_map/ppermute | solution.py:1013
  201.1 8.9 %collective-permute-start.60 = (bf16[240,768]{1,0:T(8,128)(2,1)S(1)}, bf16[240,768]{1,0:T(8,128)(2,1)S(1)}, u32[]{:S(2)}, u32[]{:S(2)}) collective-permute-start(bf16[240,768]{1,0:T(8,128)(2,1)S(1)} %get-tuple-element.309.refs_8_.refs_5_.refs_0_), channel_id=1, source_target_pairs={{0,16},{16,0},{1,17},{17,1},{2,18},{18,2},{3,19},{19,3},{4,20},{20... | collective-permute-start | bytes 1105928 | tf_op jit(solution)/shard_map/ppermute | solution.py:1013
  202.2 9.1 %collective-permute-start.61 = (bf16[256,768]{1,0:T(8,128)(2,1)S(1)}, bf16[256,768]{1,0:T(8,128)(2,1)S(1)}, u32[]{:S(2)}, u32[]{:S(2)}) collective-permute-start(bf16[256,768]{1,0:T(8,128)(2,1)S(1)} %get-tuple-element.314.refs_4_), channel_id=1, source_target_pairs={{0,8},{8,0},{1,9},{9,1},{2,10},{10,2},{3,11},{11,3},{4,12},{12,4},... | collective-permute-start | bytes 1179656 | tf_op jit(solution)/shard_map/ppermute | solution.py:1013
  203.2 10.4 %collective-permute-start.64 = (bf16[256,768]{1,0:T(8,128)(2,1)S(1)}, bf16[256,768]{1,0:T(8,128)(2,1)S(1)}, u32[]{:S(2)}, u32[]{:S(2)}) collective-permute-start(bf16[256,768]{1,0:T(8,128)(2,1)S(1)} %get-tuple-element.314.refs_4_), channel_id=1, source_target_pairs={{0,4},{4,0},{1,5},{5,1},{2,6},{6,2},{3,7},{7,3},{8,12},{12,8},{9,1... | collective-permute-start | bytes 1179656 | tf_op jit(solution)/shard_map/ppermute | solution.py:1013
  (37 other events, 192.6 us)

commit v9 on v8

--- a/solution.py
+++ b/solution.py
@@ -15,7 +15,7 @@
 BF16 = jnp.bfloat16
 VMEM_BYTES = 20 * 1024 * 1024
 TIMES = (
-    0.1, 2, 0.02, 30.0, 0.1, 0.1, 0.1, 0.1, 4, 0.1, 0.02,
+    0.1, 2, 0.02, 30.0, 0.1, 0.1, 0.1, 0.1, 8, 0.1, 0.02,
     0.1, 0.1, 0.1, 0.1, 0.1, 8, 30.0, 30.0, 0.1, 0.1, 30,
     0.1, 0.1, 8, 0.1, 0.1, 0.1, 0.5, 0.1, 0.1, 0.1, 0.1,
 )

time: 218 us -> 218 us (level)
  no operation moved by 1% of the time
where the time goes in v9:
time: 218 us
  waiting for transfers between devices  85.9 us (39%)
  Pallas kernels  67.2 us (31%)
  starting transfers between devices  56.6 us (26%)
  local copies, waits for them, and re-layouts  6.88 us (3%)
    ppermute x64, waiting for transfers between devices, swap(): return lax.ppermute(value, axis, [(i, i ^ step) for i in range(size)])  85.9 us
    pallas_call x33, Pallas kernels, kernel_call(): pl.pallas_call(kernel, out_shape=[jax.ShapeDtypeStruct(out[0], out[1]) fo...  67.2 us
    ppermute x64, starting transfers between devices, swap(): return lax.ppermute(value, axis, [(i, i ^ step) for i in range(size)])  52.6 us
    unnamed x39, local copies, waits for them, and re-layouts  6.06 us
  transfers between devices with their start and end apart: 66, of which 35 were waited for; matrix products, arithmetic and copies ran while one was open for 0% of the time, Pallas kernels for 26%

profile of v9, /device:TPU:0, one launch (start us, length us, event | category | flops | bytes accessed | tf_op | source)
XLA Modules:
  0.0 217.9 jit_solution(11350680971641789380)
XLA Ops:
  1.3 3.6 %shard_map.246 = (bf16[144,768]{1,0:T(8,128)(2,1)}, bf16[128,768]{1,0:T(8,128)(2,1)}, bf16[128,768]{1,0:T(8,128)(2,1)}, bf16[272,768]{1,0:T(8,128)(2,1)}, bf16[1...) custom-call(s32[5]{0:T(128)} %stack.38.s_ref, bf16[2,2,4,32,768]{4,3,2,1,0:T(8,128)(2,1)} %bitcast.54, ...), custom_call_target="tpu_custom_call" | custom-call | flops 110000000 | bytes 350000 | tf_op jit(solution)/shard_map/pallas_call | solution.py:53
  5.4 3.7 %collective-permute-start.4 = (bf16[256,768]{1,0:T(8,128)(2,1)}, bf16[256,768]{1,0:T(8,128)(2,1)S(1)}, u32[]{:S(2)}, u32[]{:S(2)}) collective-permute-start(bf16[256,768]{1,0:T(8,128)(2,1)} %get-tuple-element.179), channel_id=1, source_target_pairs={{0,2},{2,0},{1,3},{3,1},{4,6},{6,4},{5,7},{7,5},{8,10},{10,8},{9,1... | collective-permute-start | bytes 1179656 | tf_op jit(solution)/shard_map/ppermute | solution.py:1013
  9.1 1.5 collective-permute-start
  11.1 1.5 collective-permute-start.2
  12.7 3.2 %shard_map.247 = (bf16[2,128,768]{2,1,0:T(8,128)(2,1)}, bf16[128,768]{1,0:T(8,128)(2,1)}, bf16[128,768]{1,0:T(8,128)(2,1)}) custom-call(s32[5]{0:T(128)} %stack.38.s_ref, bf16[2,2,4,32,768]{4,3,2,1,0:T(8,128)(2,1)} %bitcast.61, bf16[128,768]{1,0:T(8,128)(2,1)} %get-tuple-element.175.refs_1_.refs_0_), custom_call_target="tpu_custom_call" | custom-call | flops 2200000000 | bytes 7000000 | tf_op jit(solution)/shard_map/pallas_call | solution.py:53
  15.9 1.7 copy-done.1
  21.9 2.4 %shard_map.248 = (bf16[2,128,768]{2,1,0:T(8,128)(2,1)S(1)}, bf16[2,128,768]{2,1,0:T(8,128)(2,1)S(1)}, s32[8,256]{1,0:T(8,128)S(1)}, bf16[3,256,192]{2,1,0:T(8,12...) custom-call(s32[5]{0:T(128)S(1)} %copy-done.9, ...), custom_call_target="tpu_custom_call" | custom-call | flops 22000000 | bytes 70000 | tf_op jit(solution)/shard_map/pallas_call | solution.py:53
  25.3 2.1 collective-permute-done.4.refs_3_.refs_8_
  28.0 2.5 %collective-permute-start.10 = (bf16[256,768]{1,0:T(8,128)(2,1)S(1)}, bf16[256,768]{1,0:T(8,128)(2,1)S(1)}, u32[]{:S(2)}, u32[]{:S(2)}) collective-permute-start(bf16[256,768]{1,0:T(8,128)(2,1)S(1)} %collective-permute-done.4.refs_3_.refs_8_), channel_id=1, source_target_pairs={{0,24},{8,16},{16,8},{24,0},{1,25},{9,17},{17,9},{25,1},{2,26},{10... | collective-permute-start | bytes 1179656 | tf_op jit(solution)/shard_map/ppermute | solution.py:1018
  31.5 7.9 %shard_map.249 = (bf16[2,2,128,768]{3,2,1,0:T(8,128)(2,1)S(1)}, bf16[2,2,128,768]{3,2,1,0:T(8,128)(2,1)S(1)}, s32[512,8]{1,0:T(8,128)S(1)}, bf16[3,512,192]{2,1,...) custom-call(s32[5]{0:T(128)S(1)} %copy-done.9, ...), custom_call_target="tpu_custom_call" | custom-call | flops 32999999488 | bytes 105000000 | tf_op jit(solution)/shard_map/pallas_call | solution.py:53
  39.4 3.0 %collective-permute-start.11 = (bf16[256,192]{1,0:T(8,128)(2,1)S(1)}, bf16[256,192]{1,0:T(8,128)(2,1)S(1)}, u32[]{:S(2)}, u32[]{:S(2)}) collective-permute-start(bf16[256,192]{1,0:T(8,128)(2,1)S(1)} %get-tuple-element.196.refs_7_), channel_id=1, source_target_pairs={{0,2},{2,0},{1,3},{3,1},{4,6},{6,4},{5,7},{7,5},{8,10},{10,8},{9,1... | collective-permute-start | bytes 294920 | tf_op jit(solution)/shard_map/ppermute | solution.py:1013
  42.4 8.4 %collective-permute-done.7.refs_12_ = bf16[192,768]{1,0:T(8,128)(2,1)S(1)} collective-permute-done((bf16[192,768]{1,0:T(8,128)(2,1)S(1)}, bf16[192,768]{1,0:T(8,128)(2,1)S(1)}, u32[]{:S(2)}, u32[]{:S(2)}) %collective-permute-start.7) | collective-permute-done | bytes 294944 | tf_op jit(solution)/shard_map/ppermute | solution.py:1013
  50.7 1.6 collective-permute-start.14
  61.5 3.8 %collective-permute-done.15.refs_1_ = bf16[128,768]{1,0:T(8,128)(2,1)S(1)} collective-permute-done((bf16[128,768]{1,0:T(8,128)(2,1)S(1)}, bf16[128,768]{1,0:T(8,128)(2,1)S(1)}, u32[]{:S(2)}, u32[]{:S(2)}) %collective-permute-start.15) | collective-permute-done | bytes 196640 | tf_op jit(solution)/shard_map/ppermute | solution.py:1013
  65.9 1.8 collective-permute-start.19
  68.3 1.6 collective-permute-start.21
  70.0 2.8 %shard_map.253 = (bf16[256,768]{1,0:T(8,128)(2,1)S(1)}, bf16[256,768]{1,0:T(8,128)(2,1)S(1)}, bf16[2,256,768]{2,1,0:T(8,128)(2,1)S(1)}, bf16[2,256,768]{2,1,0:T(...) custom-call(s32[5]{0:T(128)S(1)} %copy-done.9, ...), custom_call_target="tpu_custom_call" | custom-call | flops 110000000 | bytes 350000 | tf_op jit(solution)/shard_map/pallas_call | solution.py:53
  72.8 1.8 collective-permute-start.18
  75.2 4.2 %collective-permute-done.21 = bf16[2,128,768]{2,1,0:T(8,128)(2,1)S(1)} collective-permute-done((bf16[2,128,768]{2,1,0:T(8,128)(2,1)S(1)}, bf16[2,128,768]{2,1,0:T(8,128)(2,1)S(1)}, u32[]{:S(2)}, u32[]{:S(2)}) %collective-permute-start.21) | collective-permute-done | bytes 393248 | tf_op jit(solution)/shard_map/ppermute | solution.py:1013
  81.5 2.2 %collective-permute-done.18.refs_1_ = bf16[256,768]{1,0:T(8,128)(2,1)S(1)} collective-permute-done((bf16[256,768]{1,0:T(8,128)(2,1)S(1)}, bf16[256,768]{1,0:T(8,128)(2,1)S(1)}, u32[]{:S(2)}, u32[]{:S(2)}) %collective-permute-start.18) | collective-permute-done | bytes 393248 | tf_op jit(solution)/shard_map/ppermute | solution.py:1013
  85.8 1.6 shard_map.257
  87.5 2.3 %shard_map.258 = (bf16[256,768]{1,0:T(8,128)(2,1)S(1)}, bf16[256,768]{1,0:T(8,128)(2,1)S(1)}) custom-call(s32[5]{0:T(128)S(1)} %copy-done.9, bf16[256,768]{1,0:T(8,128)(2,1)S(1)} %get-tuple-element.221.refs_0_.refs_2_, bf16[768,768]{1,0:T(8,128)(2,1)S(1)} %get-tuple-element.207.refs_5_.refs_1_, bf16[768,768]{1,0:T(8,128)(2,1)S(1)} %get-tuple-element.208.refs_7_.refs_2_, ...), custom_call_target="tpu_custom_call" | custom-call | flops 110000000 | bytes 350000 | tf_op jit(solution)/shard_map/pallas_call | solution.py:53
  89.8 2.5 %collective-permute-start.25 = (bf16[256,768]{1,0:T(8,128)(2,1)S(1)}, bf16[256,768]{1,0:T(8,128)(2,1)S(1)}, u32[]{:S(2)}, u32[]{:S(2)}) collective-permute-start(bf16[256,768]{1,0:T(8,128)(2,1)S(1)} %get-tuple-element.225.refs_4_), channel_id=1, source_target_pairs={{0,1},{1,0},{2,3},{3,2},{4,5},{5,4},{6,7},{7,6},{8,9},{9,8},{10,11... | collective-permute-start | bytes 1179656 | tf_op jit(solution)/shard_map/ppermute | solution.py:1013
  92.4 1.7 collective-permute-start.27
  95.5 8.2 %collective-permute-done.25.refs_5_ = bf16[256,768]{1,0:T(8,128)(2,1)S(1)} collective-permute-done((bf16[256,768]{1,0:T(8,128)(2,1)S(1)}, bf16[256,768]{1,0:T(8,128)(2,1)S(1)}, u32[]{:S(2)}, u32[]{:S(2)}) %collective-permute-start.25) | collective-permute-done | bytes 393248 | tf_op jit(solution)/shard_map/ppermute | solution.py:1013
  107.6 2.4 %collective-permute-start.30 = (bf16[256,192]{1,0:T(8,128)(2,1)S(1)}, bf16[256,192]{1,0:T(8,128)(2,1)S(1)}, u32[]{:S(2)}, u32[]{:S(2)}) collective-permute-start(bf16[256,192]{1,0:T(8,128)(2,1)S(1)} %get-tuple-element.240), channel_id=1, source_target_pairs={{0,2},{2,0},{1,3},{3,1},{4,6},{6,4},{5,7},{7,5},{8,10},{10,8},{9,1... | collective-permute-start | bytes 294920 | tf_op jit(solution)/shard_map/ppermute | solution.py:1013
  110.0 5.0 %collective-permute-done.28.refs_4_ = bf16[128,768]{1,0:T(8,128)(2,1)S(1)} collective-permute-done((bf16[128,768]{1,0:T(8,128)(2,1)S(1)}, bf16[128,768]{1,0:T(8,128)(2,1)S(1)}, u32[]{:S(2)}, u32[]{:S(2)}) %collective-permute-start.28) | collective-permute-done | bytes 196640 | tf_op jit(solution)/shard_map/ppermute | solution.py:1013
  115.0 2.4 %shard_map.262 = (bf16[2,64,768]{2,1,0:T(8,128)(2,1)S(1)}, bf16[2,64,768]{2,1,0:T(8,128)(2,1)S(1)}, f32[256,768]{1,0:T(8,128)}, bf16[256,768]{1,0:T(8,128)(2,1)S(1)}, f32[8,768]{1,0:T(8,128)}) custom-call(s32[5]{0:T(128)S(1)} %copy-done.9, bf16[2,2,128,768]{3,2,1,0:T(8,128)(2,1)S(1)} %get-tuple-element.189.refs_0_, ...), custom_call_target="tpu_custom_call" | custom-call | flops 8800000000 | bytes 28000000 | tf_op jit(solution)/shard_map/pallas_call | solution.py:53
  117.4 2.1 shard_map.263
  120.1 1.6 collective-permute-start.37
  121.8 5.3 %shard_map.264 = (bf16[3,512,512]{2,1,0:T(8,128)(2,1)S(1)}, bf16[3,512,192]{2,1,0:T(8,128)(2,1)S(1)}, bf16[2,512,192]{2,1,0:T(8,128)(2,1)S(1)}, bf16[128,768]{1,...) custom-call(s32[5]{0:T(128)S(1)} %copy-done.9, ...), custom_call_target="tpu_custom_call" | custom-call | flops 32999999488 | bytes 105000000 | tf_op jit(solution)/shard_map/pallas_call | solution.py:53
  132.2 2.2 collective-permute-done.36.refs_1_
  137.0 1.6 collective-permute-start.44
  139.7 5.9 %shard_map.268 = (bf16[240,768]{1,0:T(8,128)(2,1)S(1)}, bf16[240,768]{1,0:T(8,128)(2,1)S(1)}, bf16[96,768]{1,0:T(8,128)(2,1)S(1)}, f32[16,768]{1,0:T(8,128)S(1)}) custom-call(s32[5]{0:T(128)S(1)} %copy-done.9, bf16[2,2,128,768]{3,2,1,0:T(8,128)(2,1)S(1)} %get-tuple-element.189.refs_0_, bf16[3,512,512]{2,1,0:T(8,128)(2,1)S(1)} %get-tuple-element.267.refs_1_, ...), custom_call_target="tpu_custom_call" | custom-call | flops 110000000 | bytes 350000 | tf_op jit(solution)/shard_map/pallas_call | solution.py:53
  147.5 1.8 collective-permute-done.45.refs_3_
  151.3 1.7 collective-permute-start.47
  153.6 2.0 collective-permute-start.34
  155.6 10.2 %collective-permute-done.43.refs_1_ = bf16[3,64,768]{2,1,0:T(8,128)(2,1)S(1)} collective-permute-done((bf16[3,64,768]{2,1,0:T(8,128)(2,1)S(1)}, bf16[3,64,768]{2,1,0:T(8,128)(2,1)S(1)}, u32[]{:S(2)}, u32[]{:S(2)}) %collective-permute-start.43) | collective-permute-done | bytes 294944 | tf_op jit(solution)/shard_map/ppermute | solution.py:1013
  170.0 2.1 collective-permute-done.48.refs_1_
  175.8 1.8 collective-permute-start.57
  177.7 5.1 %shard_map.273 = (f32[2,2,384,768]{3,2,1,0:T(8,128)}, f32[2,2,384,768]{3,2,1,0:T(8,128)}, f32[8,128]{1,0:T(8,128)S(1)}) custom-call(s32[5]{0:T(128)S(1)} %copy-done.9, bf16[384,768]{1,0:T(8,128)(2,1)S(1)} %get-tuple-element.300.refs_2_.refs_0_, bf16[384,768]{1,0:T(8,128)(2,1)S(1)} %collective-permute-done.46.refs_13_.refs_1_, ...), custom_call_target="tpu_custom_call" | custom-call | flops 110000000 | bytes 350000 | tf_op jit(solution)/shard_map/pallas_call | solution.py:53
  182.7 2.0 collective-permute-done.49.refs_1_
  188.7 3.4 %collective-permute-done.57.refs_2_ = bf16[2,3,32,768]{3,2,1,0:T(8,128)(2,1)S(1)} collective-permute-done((bf16[2,3,32,768]{3,2,1,0:T(8,128)(2,1)S(1)}, bf16[2,3,32,768]{3,2,1,0:T(8,128)(2,1)S(1)}, u32[]{:S(2)}, u32[]{:S(2)}) %collective-permute-start.57) | collective-permute-done | bytes 294944 | tf_op jit(solution)/shard_map/ppermute | solution.py:1013
  192.8 7.6 %collective-permute-done.59.refs_4_ = bf16[2,3,32,768]{3,2,1,0:T(8,128)(2,1)S(1)} collective-permute-done((bf16[2,3,32,768]{3,2,1,0:T(8,128)(2,1)S(1)}, bf16[2,3,32,768]{3,2,1,0:T(8,128)(2,1)S(1)}, u32[]{:S(2)}, u32[]{:S(2)}) %collective-permute-start.59) | collective-permute-done | bytes 294944 | tf_op jit(solution)/shard_map/ppermute | solution.py:1013
  204.8 2.1 shard_map.277
  206.9 3.2 %collective-permute-done.60.refs_1_ = bf16[240,768]{1,0:T(8,128)(2,1)S(1)} collective-permute-done((bf16[240,768]{1,0:T(8,128)(2,1)S(1)}, bf16[240,768]{1,0:T(8,128)(2,1)S(1)}, u32[]{:S(2)}, u32[]{:S(2)}) %collective-permute-start.60) | collective-permute-done | bytes 368672 | tf_op jit(solution)/shard_map/ppermute | solution.py:1013
  211.9 1.7 collective-permute-done.62.refs_2_
  214.1 3.7 %shard_map.278 = (f32[2,576,768]{2,1,0:T(8,128)}, f32[2,192,768]{2,1,0:T(8,128)}, f32[2,192,768]{2,1,0:T(8,128)}, f32[3,3,2,128]{3,2,1,0:T(2,128)}, f32[2,2,192]...) custom-call(s32[5]{0:T(128)S(1)} %copy-done.9, ...), custom_call_target="tpu_custom_call" | custom-call | flops 110000000 | bytes 350000 | tf_op jit(solution)/shard_map/pallas_call | solution.py:53
  (170 shorter events, 62.2 us)
Async XLA Ops:
  4.9 11.0 %collective-permute-start.3 = (bf16[272,768]{1,0:T(8,128)(2,1)}, bf16[272,768]{1,0:T(8,128)(2,1)}, u32[]{:S(2)}, u32[]{:S(2)}) collective-permute-start(bf16[272,768]{1,0:T(8,128)(2,1)} %get-tuple-element.176.refs_2_), channel_id=1, source_target_pairs={{0,4},{4,0},{1,5},{5,1},{2,6},{6,2},{3,7},{7,3},{8,12},{12,8},{9,1... | collective-permute-start | bytes 1253384 | tf_op jit(solution)/shard_map/ppermute | solution.py:1013
  5.4 22.0 %collective-permute-start.4 = (bf16[256,768]{1,0:T(8,128)(2,1)}, bf16[256,768]{1,0:T(8,128)(2,1)S(1)}, u32[]{:S(2)}, u32[]{:S(2)}) collective-permute-start(bf16[256,768]{1,0:T(8,128)(2,1)} %get-tuple-element.179), channel_id=1, source_target_pairs={{0,2},{2,0},{1,3},{3,1},{4,6},{6,4},{5,7},{7,5},{8,10},{10,8},{9,1... | collective-permute-start | bytes 1179656 | tf_op jit(solution)/shard_map/ppermute | solution.py:1013
  9.1 16.2 %collective-permute-start = (bf16[144,768]{1,0:T(8,128)(2,1)}, bf16[144,768]{1,0:T(8,128)(2,1)}, u32[]{:S(2)}, u32[]{:S(2)}) collective-permute-start(bf16[144,768]{1,0:T(8,128)(2,1)} %get-tuple-element.172), channel_id=1, source_target_pairs={{0,8},{8,0},{1,9},{9,1},{2,10},{10,2},{3,11},{11,3},{4,12},{12,4},... | collective-permute-start | bytes 663560 | tf_op jit(solution)/shard_map/ppermute | solution.py:1013
  10.6 13.7 %collective-permute-start.1 = (bf16[128,768]{1,0:T(8,128)(2,1)}, bf16[128,768]{1,0:T(8,128)(2,1)}, u32[]{:S(2)}, u32[]{:S(2)}) collective-permute-start(bf16[128,768]{1,0:T(8,128)(2,1)} %get-tuple-element.173), channel_id=1, source_target_pairs={{0,8},{8,0},{1,9},{9,1},{2,10},{10,2},{3,11},{11,3},{4,12},{12,4},... | collective-permute-start | bytes 589832 | tf_op jit(solution)/shard_map/ppermute | solution.py:1013
  11.1 14.2 %collective-permute-start.2 = (bf16[128,768]{1,0:T(8,128)(2,1)}, bf16[128,768]{1,0:T(8,128)(2,1)}, u32[]{:S(2)}, u32[]{:S(2)}) collective-permute-start(bf16[128,768]{1,0:T(8,128)(2,1)} %get-tuple-element.174), channel_id=1, source_target_pairs={{0,8},{8,0},{1,9},{9,1},{2,10},{10,2},{3,11},{11,3},{4,12},{12,4},... | collective-permute-start | bytes 589832 | tf_op jit(solution)/shard_map/ppermute | solution.py:1013
  28.0 22.8 %collective-permute-start.10 = (bf16[256,768]{1,0:T(8,128)(2,1)S(1)}, bf16[256,768]{1,0:T(8,128)(2,1)S(1)}, u32[]{:S(2)}, u32[]{:S(2)}) collective-permute-start(bf16[256,768]{1,0:T(8,128)(2,1)S(1)} %collective-permute-done.4.refs_3_.refs_8_), channel_id=1, source_target_pairs={{0,24},{8,16},{16,8},{24,0},{1,25},{9,17},{17,9},{25,1},{2,26},{10... | collective-permute-start | bytes 1179656 | tf_op jit(solution)/shard_map/ppermute | solution.py:1018
  30.5 20.3 %collective-permute-start.9 = (bf16[256,768]{1,0:T(8,128)(2,1)S(1)}, bf16[256,768]{1,0:T(8,128)(2,1)S(1)}, u32[]{:S(2)}, u32[]{:S(2)}) collective-permute-start(bf16[256,768]{1,0:T(8,128)(2,1)S(1)} %collective-permute-done.4.refs_3_.refs_8_), channel_id=1, source_target_pairs={{0,16},{16,0},{1,17},{17,1},{2,18},{18,2},{3,19},{19,3},{4,20},{20... | collective-permute-start | bytes 1179656 | tf_op jit(solution)/shard_map/ppermute | solution.py:1013
  31.0 19.7 %collective-permute-start.8 = (bf16[256,768]{1,0:T(8,128)(2,1)S(1)}, bf16[256,768]{1,0:T(8,128)(2,1)S(1)}, u32[]{:S(2)}, u32[]{:S(2)}) collective-permute-start(bf16[256,768]{1,0:T(8,128)(2,1)S(1)} %collective-permute-done.4.refs_3_.refs_8_), channel_id=1, source_target_pairs={{0,8},{8,0},{1,9},{9,1},{2,10},{10,2},{3,11},{11,3},{4,12},{12,4},... | collective-permute-start | bytes 1179656 | tf_op jit(solution)/shard_map/ppermute | solution.py:1013
  31.5 19.3 %collective-permute-start.7 = (bf16[192,768]{1,0:T(8,128)(2,1)S(1)}, bf16[192,768]{1,0:T(8,128)(2,1)S(1)}, u32[]{:S(2)}, u32[]{:S(2)}) collective-permute-start(bf16[192,768]{1,0:T(8,128)(2,1)S(1)} %copy-done.17), channel_id=1, source_target_pairs={{0,2},{2,0},{1,3},{3,1},{4,6},{6,4},{5,7},{7,5},{8,10},{10,8},{9,1... | collective-permute-start | bytes 884744 | tf_op jit(solution)/shard_map/ppermute | solution.py:1013
  39.4 14.4 %collective-permute-start.11 = (bf16[256,192]{1,0:T(8,128)(2,1)S(1)}, bf16[256,192]{1,0:T(8,128)(2,1)S(1)}, u32[]{:S(2)}, u32[]{:S(2)}) collective-permute-start(bf16[256,192]{1,0:T(8,128)(2,1)S(1)} %get-tuple-element.196.refs_7_), channel_id=1, source_target_pairs={{0,2},{2,0},{1,3},{3,1},{4,6},{6,4},{5,7},{7,5},{8,10},{10,8},{9,1... | collective-permute-start | bytes 294920 | tf_op jit(solution)/shard_map/ppermute | solution.py:1013
  50.7 6.8 %collective-permute-start.14 = (bf16[192,768]{1,0:T(8,128)(2,1)S(1)}, bf16[192,768]{1,0:T(8,128)(2,1)S(1)}, u32[]{:S(2)}, u32[]{:S(2)}) collective-permute-start(bf16[192,768]{1,0:T(8,128)(2,1)S(1)} %collective-permute-done.7.refs_12_), channel_id=1, source_target_pairs={{0,16},{16,0},{1,17},{17,1},{2,18},{18,2},{3,19},{19,3},{4,20},{20... | collective-permute-start | bytes 884744 | tf_op jit(solution)/shard_map/ppermute | solution.py:1013
  52.3 6.7 %collective-permute-start.13 = (bf16[192,768]{1,0:T(8,128)(2,1)S(1)}, bf16[192,768]{1,0:T(8,128)(2,1)S(1)}, u32[]{:S(2)}, u32[]{:S(2)}) collective-permute-start(bf16[192,768]{1,0:T(8,128)(2,1)S(1)} %collective-permute-done.7.refs_12_), channel_id=1, source_target_pairs={{0,8},{8,0},{1,9},{9,1},{2,10},{10,2},{3,11},{11,3},{4,12},{12,4},... | collective-permute-start | bytes 884744 | tf_op jit(solution)/shard_map/ppermute | solution.py:1013
  59.6 5.7 %collective-permute-start.15 = (bf16[128,768]{1,0:T(8,128)(2,1)S(1)}, bf16[128,768]{1,0:T(8,128)(2,1)S(1)}, u32[]{:S(2)}, u32[]{:S(2)}) collective-permute-start(bf16[128,768]{1,0:T(8,128)(2,1)S(1)} %shard_map.251.refs_0_), channel_id=1, source_target_pairs={{0,1},{1,0},{2,3},{3,2},{4,5},{5,4},{6,7},{7,6},{8,9},{9,8},{10,11... | collective-permute-start | bytes 589832 | tf_op jit(solution)/shard_map/ppermute | solution.py:1013
  60.0 9.9 %collective-permute-start.17 = (bf16[192,768]{1,0:T(8,128)(2,1)S(1)}, bf16[192,768]{1,0:T(8,128)(2,1)S(1)}, u32[]{:S(2)}, u32[]{:S(2)}) collective-permute-start(bf16[192,768]{1,0:T(8,128)(2,1)S(1)} %collective-permute-done.7.refs_12_), channel_id=1, source_target_pairs={{0,24},{8,16},{16,8},{24,0},{1,25},{9,17},{17,9},{25,1},{2,26},{10... | collective-permute-start | bytes 884744 | tf_op jit(solution)/shard_map/ppermute | solution.py:1018
  65.9 9.2 %collective-permute-start.19 = (bf16[128,768]{1,0:T(8,128)(2,1)S(1)}, bf16[128,768]{1,0:T(8,128)(2,1)S(1)}, u32[]{:S(2)}, u32[]{:S(2)}) collective-permute-start(bf16[128,768]{1,0:T(8,128)(2,1)S(1)} %shard_map.252.refs_1_), channel_id=1, source_target_pairs={{0,2},{2,0},{1,3},{3,1},{4,6},{6,4},{5,7},{7,5},{8,10},{10,8},{9,1... | collective-permute-start | bytes 589832 | tf_op jit(solution)/shard_map/ppermute | solution.py:1013
  67.8 7.4 %collective-permute-start.22 = (bf16[128,768]{1,0:T(8,128)(2,1)S(1)}, bf16[128,768]{1,0:T(8,128)(2,1)S(1)}, u32[]{:S(2)}, u32[]{:S(2)}) collective-permute-start(bf16[128,768]{1,0:T(8,128)(2,1)S(1)} %copy-done.18), channel_id=1, source_target_pairs={{0,4},{4,0},{1,5},{5,1},{2,6},{6,2},{3,7},{7,3},{8,12},{12,8},{9,1... | collective-permute-start | bytes 589832 | tf_op jit(solution)/shard_map/ppermute | solution.py:1013
  68.3 11.1 %collective-permute-start.21 = (bf16[2,128,768]{2,1,0:T(8,128)(2,1)S(1)}, bf16[2,128,768]{2,1,0:T(8,128)(2,1)S(1)}, u32[]{:S(2)}, u32[]{:S(2)}) collective-permute-start(bf16[2,128,768]{2,1,0:T(8,128)(2,1)S(1)} %copy-done.16), channel_id=1, source_target_pairs={{0,8},{8,0},{1,9},{9,1},{2,10},{10,2},{3,11},{11,3},{4,12},{12,4},... | collective-permute-start | bytes 1179656 | tf_op jit(solution)/shard_map/ppermute | solution.py:1013
  72.8 10.9 %collective-permute-start.18 = (bf16[256,768]{1,0:T(8,128)(2,1)S(1)}, bf16[256,768]{1,0:T(8,128)(2,1)S(1)}, u32[]{:S(2)}, u32[]{:S(2)}) collective-permute-start(bf16[256,768]{1,0:T(8,128)(2,1)S(1)} %get-tuple-element.213.refs_5_.refs_0_), channel_id=1, source_target_pairs={{0,1},{1,0},{2,3},{3,2},{4,5},{5,4},{6,7},{7,6},{8,9},{9,8},{10,11... | collective-permute-start | bytes 1179656 | tf_op jit(solution)/shard_map/ppermute | solution.py:1013
  79.4 6.4 %collective-permute-start.23 = (bf16[2,128,768]{2,1,0:T(8,128)(2,1)S(1)}, bf16[2,128,768]{2,1,0:T(8,128)(2,1)S(1)}, u32[]{:S(2)}, u32[]{:S(2)}) collective-permute-start(bf16[2,128,768]{2,1,0:T(8,128)(2,1)S(1)} %collective-permute-done.21), channel_id=1, source_target_pairs={{0,4},{4,0},{1,5},{5,1},{2,6},{6,2},{3,7},{7,3},{8,12},{12,8},{9,1... | collective-permute-start | bytes 1179656 | tf_op jit(solution)/shard_map/ppermute | solution.py:1013
  84.3 11.1 %collective-permute-start.26 = (bf16[128,768]{1,0:T(8,128)(2,1)S(1)}, bf16[128,768]{1,0:T(8,128)(2,1)S(1)}, u32[]{:S(2)}, u32[]{:S(2)}) collective-permute-start(bf16[128,768]{1,0:T(8,128)(2,1)S(1)} %get-tuple-element.215.refs_3_), channel_id=1, source_target_pairs={{0,2},{2,0},{1,3},{3,1},{4,6},{6,4},{5,7},{7,5},{8,10},{10,8},{9,1... | collective-permute-start | bytes 589832 | tf_op jit(solution)/shard_map/ppermute | solution.py:1013
  89.8 13.9 %collective-permute-start.25 = (bf16[256,768]{1,0:T(8,128)(2,1)S(1)}, bf16[256,768]{1,0:T(8,128)(2,1)S(1)}, u32[]{:S(2)}, u32[]{:S(2)}) collective-permute-start(bf16[256,768]{1,0:T(8,128)(2,1)S(1)} %get-tuple-element.225.refs_4_), channel_id=1, source_target_pairs={{0,1},{1,0},{2,3},{3,2},{4,5},{5,4},{6,7},{7,6},{8,9},{9,8},{10,11... | collective-permute-start | bytes 1179656 | tf_op jit(solution)/shard_map/ppermute | solution.py:1013
  92.4 11.3 %collective-permute-start.27 = (bf16[2,64,768]{2,1,0:T(8,128)(2,1)S(1)}, bf16[2,64,768]{2,1,0:T(8,128)(2,1)S(1)}, u32[]{:S(2)}, u32[]{:S(2)}) collective-permute-start(bf16[2,64,768]{2,1,0:T(8,128)(2,1)S(1)} %pad_maximum_fusion.1), channel_id=1, source_target_pairs={{0,8},{8,0},{1,9},{9,1},{2,10},{10,2},{3,11},{11,3},{4,12},{12,4},... | collective-permute-start | bytes 589832 | tf_op jit(solution)/shard_map/ppermute | solution.py:1013
  105.1 9.9 %collective-permute-start.28 = (bf16[128,768]{1,0:T(8,128)(2,1)S(1)}, bf16[128,768]{1,0:T(8,128)(2,1)S(1)}, u32[]{:S(2)}, u32[]{:S(2)}) collective-permute-start(bf16[128,768]{1,0:T(8,128)(2,1)S(1)} %collective-permute-done.26.refs_3_), channel_id=1, source_target_pairs={{0,1},{1,0},{2,3},{3,2},{4,5},{5,4},{6,7},{7,6},{8,9},{9,8},{10,11... | collective-permute-start | bytes 589832 | tf_op jit(solution)/shard_map/ppermute | solution.py:1013
  107.6 14.1 %collective-permute-start.30 = (bf16[256,192]{1,0:T(8,128)(2,1)S(1)}, bf16[256,192]{1,0:T(8,128)(2,1)S(1)}, u32[]{:S(2)}, u32[]{:S(2)}) collective-permute-start(bf16[256,192]{1,0:T(8,128)(2,1)S(1)} %get-tuple-element.240), channel_id=1, source_target_pairs={{0,2},{2,0},{1,3},{3,1},{4,6},{6,4},{5,7},{7,5},{8,10},{10,8},{9,1... | collective-permute-start | bytes 294920 | tf_op jit(solution)/shard_map/ppermute | solution.py:1013
  119.5 14.9 %collective-permute-start.36 = (bf16[384,768]{1,0:T(8,128)(2,1)S(1)}, bf16[384,768]{1,0:T(8,128)(2,1)S(1)}, u32[]{:S(2)}, u32[]{:S(2)}) collective-permute-start(bf16[384,768]{1,0:T(8,128)(2,1)S(1)} %get-tuple-element.273), channel_id=1, source_target_pairs={{0,16},{16,0},{1,17},{17,1},{2,18},{18,2},{3,19},{19,3},{4,20},{20... | collective-permute-start | bytes 1769480 | tf_op jit(solution)/shard_map/ppermute | solution.py:1013
  120.1 14.6 %collective-permute-start.37 = (bf16[384,768]{1,0:T(8,128)(2,1)S(1)}, bf16[384,768]{1,0:T(8,128)(2,1)S(1)}, u32[]{:S(2)}, u32[]{:S(2)}) collective-permute-start(bf16[384,768]{1,0:T(8,128)(2,1)S(1)} %get-tuple-element.275), channel_id=1, source_target_pairs={{0,8},{8,0},{1,9},{9,1},{2,10},{10,2},{3,11},{11,3},{4,12},{12,4},... | collective-permute-start | bytes 1769480 | tf_op jit(solution)/shard_map/ppermute | solution.py:1013
  121.8 6.6 %collective-permute-start.31 = (bf16[80,768]{1,0:T(8,128)(2,1)S(1)}, bf16[80,768]{1,0:T(8,128)(2,1)S(1)}, u32[]{:S(2)}, u32[]{:S(2)}) collective-permute-start(bf16[80,768]{1,0:T(8,128)(2,1)S(1)} %get-tuple-element.255.refs_1_), channel_id=1, source_target_pairs={{0,2},{2,0},{1,3},{3,1},{4,6},{6,4},{5,7},{7,5},{8,10},{10,8},{9,1... | collective-permute-start | bytes 368648 | tf_op jit(solution)/shard_map/ppermute | solution.py:1013
  131.4 15.4 %collective-permute-start.35 = (bf16[3,128,768]{2,1,0:T(8,128)(2,1)S(1)}, bf16[3,128,768]{2,1,0:T(8,128)(2,1)S(1)}, u32[]{:S(2)}, u32[]{:S(2)}) collective-permute-start(bf16[3,128,768]{2,1,0:T(8,128)(2,1)S(1)} %get-tuple-element.263.refs_4_), channel_id=1, source_target_pairs={{0,1},{1,0},{2,3},{3,2},{4,5},{5,4},{6,7},{7,6},{8,9},{9,8},{10,11... | collective-permute-start | bytes 1769480 | tf_op jit(solution)/shard_map/ppermute | solution.py:1013
  135.5 13.7 %collective-permute-start.45 = (bf16[384,768]{1,0:T(8,128)(2,1)S(1)}, bf16[384,768]{1,0:T(8,128)(2,1)S(1)}, u32[]{:S(2)}, u32[]{:S(2)}) collective-permute-start(bf16[384,768]{1,0:T(8,128)(2,1)S(1)} %get-tuple-element.289.refs_2_), channel_id=1, source_target_pairs={{0,16},{16,0},{1,17},{17,1},{2,18},{18,2},{3,19},{19,3},{4,20},{20... | collective-permute-start | bytes 1769480 | tf_op jit(solution)/shard_map/ppermute | solution.py:1013
  137.0 13.4 %collective-permute-start.44 = (bf16[384,768]{1,0:T(8,128)(2,1)S(1)}, bf16[384,768]{1,0:T(8,128)(2,1)S(1)}, u32[]{:S(2)}, u32[]{:S(2)}) collective-permute-start(bf16[384,768]{1,0:T(8,128)(2,1)S(1)} %get-tuple-element.276.refs_2_.refs_0_), channel_id=1, source_target_pairs={{0,8},{8,0},{1,9},{9,1},{2,10},{10,2},{3,11},{11,3},{4,12},{12,4},... | collective-permute-start | bytes 1769480 | tf_op jit(solution)/shard_map/ppermute | solution.py:1013
  151.3 17.7 %collective-permute-start.47 = (bf16[384,768]{1,0:T(8,128)(2,1)S(1)}, bf16[384,768]{1,0:T(8,128)(2,1)S(1)}, u32[]{:S(2)}, u32[]{:S(2)}) collective-permute-start(bf16[384,768]{1,0:T(8,128)(2,1)S(1)} %get-tuple-element.302.refs_4_), channel_id=1, source_target_pairs={{0,8},{8,0},{1,9},{9,1},{2,10},{10,2},{3,11},{11,3},{4,12},{12,4},... | collective-permute-start | bytes 1769480 | tf_op jit(solution)/shard_map/ppermute | solution.py:1013
  153.0 16.0 %collective-permute-start.46 = (bf16[384,768]{1,0:T(8,128)(2,1)S(1)}, bf16[384,768]{1,0:T(8,128)(2,1)S(1)}, u32[]{:S(2)}, u32[]{:S(2)}) collective-permute-start(bf16[384,768]{1,0:T(8,128)(2,1)S(1)} %get-tuple-element.300.refs_2_.refs_0_), channel_id=1, source_target_pairs={{0,16},{16,0},{1,17},{17,1},{2,18},{18,2},{3,19},{19,3},{4,20},{20... | collective-permute-start | bytes 1769480 | tf_op jit(solution)/shard_map/ppermute | solution.py:1013
  153.6 12.2 %collective-permute-start.43 = (bf16[3,64,768]{2,1,0:T(8,128)(2,1)S(1)}, bf16[3,64,768]{2,1,0:T(8,128)(2,1)S(1)}, u32[]{:S(2)}, u32[]{:S(2)}) collective-permute-start(bf16[3,64,768]{2,1,0:T(8,128)(2,1)S(1)} %get-tuple-element.279.refs_4_), channel_id=1, source_target_pairs={{0,2},{2,0},{1,3},{3,1},{4,6},{6,4},{5,7},{7,5},{8,10},{10,8},{9,1... | collective-permute-start | bytes 884744 | tf_op jit(solution)/shard_map/ppermute | solution.py:1013
  153.6 13.9 %collective-permute-start.42 = (bf16[192,768]{1,0:T(8,128)(2,1)S(1)}, bf16[192,768]{1,0:T(8,128)(2,1)S(1)}, u32[]{:S(2)}, u32[]{:S(2)}) collective-permute-start(bf16[192,768]{1,0:T(8,128)(2,1)S(1)} %get-tuple-element.287), channel_id=1, source_target_pairs={{0,4},{4,0},{1,5},{5,1},{2,6},{6,2},{3,7},{7,3},{8,12},{12,8},{9,1... | collective-permute-start | bytes 884744 | tf_op jit(solution)/shard_map/ppermute | solution.py:1013
  153.6 13.9 %collective-permute-start.34 = (bf16[80,768]{1,0:T(8,128)(2,1)S(1)}, bf16[80,768]{1,0:T(8,128)(2,1)S(1)}, u32[]{:S(2)}, u32[]{:S(2)}) collective-permute-start(bf16[80,768]{1,0:T(8,128)(2,1)S(1)} %collective-permute-done.31.refs_2_), channel_id=1, source_target_pairs={{0,1},{1,0},{2,3},{3,2},{4,5},{5,4},{6,7},{7,6},{8,9},{9,8},{10,11... | collective-permute-start | bytes 368648 | tf_op jit(solution)/shard_map/ppermute | solution.py:1013
  166.4 5.7 %collective-permute-start.48 = (bf16[3,32,768]{2,1,0:T(8,128)(2,1)S(1)}, bf16[3,32,768]{2,1,0:T(8,128)(2,1)S(1)}, u32[]{:S(2)}, u32[]{:S(2)}) collective-permute-start(bf16[3,32,768]{2,1,0:T(8,128)(2,1)S(1)} %get-tuple-element.294), channel_id=1, source_target_pairs={{0,8},{8,0},{1,9},{9,1},{2,10},{10,2},{3,11},{11,3},{4,12},{12,4},... | collective-permute-start | bytes 442376 | tf_op jit(solution)/shard_map/ppermute | solution.py:1013
  173.2 11.6 %collective-permute-start.50 = (bf16[256,768]{1,0:T(8,128)(2,1)S(1)}, bf16[256,768]{1,0:T(8,128)(2,1)S(1)}, u32[]{:S(2)}, u32[]{:S(2)}) collective-permute-start(bf16[256,768]{1,0:T(8,128)(2,1)S(1)} %get-tuple-element.298), channel_id=1, source_target_pairs={{0,8},{8,0},{1,9},{9,1},{2,10},{10,2},{3,11},{11,3},{4,12},{12,4},... | collective-permute-start | bytes 1179656 | tf_op jit(solution)/shard_map/ppermute | solution.py:1013
  174.1 10.6 %collective-permute-start.49 = (bf16[240,768]{1,0:T(8,128)(2,1)S(1)}, bf16[240,768]{1,0:T(8,128)(2,1)S(1)}, u32[]{:S(2)}, u32[]{:S(2)}) collective-permute-start(bf16[240,768]{1,0:T(8,128)(2,1)S(1)} %get-tuple-element.296), channel_id=1, source_target_pairs={{0,16},{16,0},{1,17},{17,1},{2,18},{18,2},{3,19},{19,3},{4,20},{20... | collective-permute-start | bytes 1105928 | tf_op jit(solution)/shard_map/ppermute | solution.py:1013
  175.2 13.5 %collective-permute-start.58 = (bf16[2,3,32,768]{3,2,1,0:T(8,128)(2,1)S(1)}, bf16[2,3,32,768]{3,2,1,0:T(8,128)(2,1)S(1)}, u32[]{:S(2)}, u32[]{:S(2)}) collective-permute-start(bf16[2,3,32,768]{3,2,1,0:T(8,128)(2,1)S(1)} %pad_maximum_fusion.refs_8_), channel_id=1, source_target_pairs={{0,1},{1,0},{2,3},{3,2},{4,5},{5,4},{6,7},{7,6},{8,9},{9,8},{10,11... | collective-permute-start | bytes 884744 | tf_op jit(solution)/shard_map/ppermute | solution.py:1013
  175.8 16.3 %collective-permute-start.57 = (bf16[2,3,32,768]{3,2,1,0:T(8,128)(2,1)S(1)}, bf16[2,3,32,768]{3,2,1,0:T(8,128)(2,1)S(1)}, u32[]{:S(2)}, u32[]{:S(2)}) collective-permute-start(bf16[2,3,32,768]{3,2,1,0:T(8,128)(2,1)S(1)} %pad_maximum_fusion.refs_8_), channel_id=1, source_target_pairs={{0,2},{2,0},{1,3},{3,1},{4,6},{6,4},{5,7},{7,5},{8,10},{10,8},{9,1... | collective-permute-start | bytes 884744 | tf_op jit(solution)/shard_map/ppermute | solution.py:1013
  177.7 14.5 %collective-permute-start.38 = (bf16[2,64,768]{2,1,0:T(8,128)(2,1)S(1)}, bf16[2,64,768]{2,1,0:T(8,128)(2,1)S(1)}, u32[]{:S(2)}, u32[]{:S(2)}) collective-permute-start(bf16[2,64,768]{2,1,0:T(8,128)(2,1)S(1)} %get-tuple-element.280), channel_id=1, source_target_pairs={{0,4},{4,0},{1,5},{5,1},{2,6},{6,2},{3,7},{7,3},{8,12},{12,8},{9,1... | collective-permute-start | bytes 589832 | tf_op jit(solution)/shard_map/ppermute | solution.py:1013
  185.5 14.9 %collective-permute-start.55 = (bf16[240,768]{1,0:T(8,128)(2,1)S(1)}, bf16[240,768]{1,0:T(8,128)(2,1)S(1)}, u32[]{:S(2)}, u32[]{:S(2)}) collective-permute-start(bf16[240,768]{1,0:T(8,128)(2,1)S(1)} %get-tuple-element.306.refs_0_), channel_id=1, source_target_pairs={{0,8},{8,0},{1,9},{9,1},{2,10},{10,2},{3,11},{11,3},{4,12},{12,4},... | collective-permute-start | bytes 1105928 | tf_op jit(solution)/shard_map/ppermute | solution.py:1013
  186.3 14.1 %collective-permute-start.56 = (bf16[256,768]{1,0:T(8,128)(2,1)S(1)}, bf16[256,768]{1,0:T(8,128)(2,1)S(1)}, u32[]{:S(2)}, u32[]{:S(2)}) collective-permute-start(bf16[256,768]{1,0:T(8,128)(2,1)S(1)} %get-tuple-element.307.refs_2_), channel_id=1, source_target_pairs={{0,16},{16,0},{1,17},{17,1},{2,18},{18,2},{3,19},{19,3},{4,20},{20... | collective-permute-start | bytes 1179656 | tf_op jit(solution)/shard_map/ppermute | solution.py:1013
  192.1 8.2 %collective-permute-start.59 = (bf16[2,3,32,768]{3,2,1,0:T(8,128)(2,1)S(1)}, bf16[2,3,32,768]{3,2,1,0:T(8,128)(2,1)S(1)}, u32[]{:S(2)}, u32[]{:S(2)}) collective-permute-start(bf16[2,3,32,768]{3,2,1,0:T(8,128)(2,1)S(1)} %collective-permute-done.57.refs_2_), channel_id=1, source_target_pairs={{0,1},{1,0},{2,3},{3,2},{4,5},{5,4},{6,7},{7,6},{8,9},{9,8},{10,11... | collective-permute-start | bytes 884744 | tf_op jit(solution)/shard_map/ppermute | solution.py:1013
  192.2 11.0 %collective-permute-start.39 = (bf16[2,64,768]{2,1,0:T(8,128)(2,1)S(1)}, bf16[2,64,768]{2,1,0:T(8,128)(2,1)S(1)}, u32[]{:S(2)}, u32[]{:S(2)}) collective-permute-start(bf16[2,64,768]{2,1,0:T(8,128)(2,1)S(1)} %pad_maximum_fusion.2), channel_id=1, source_target_pairs={{0,8},{8,0},{1,9},{9,1},{2,10},{10,2},{3,11},{11,3},{4,12},{12,4},... | collective-permute-start | bytes 589832 | tf_op jit(solution)/shard_map/ppermute | solution.py:1013
  201.1 8.9 %collective-permute-start.60 = (bf16[240,768]{1,0:T(8,128)(2,1)S(1)}, bf16[240,768]{1,0:T(8,128)(2,1)S(1)}, u32[]{:S(2)}, u32[]{:S(2)}) collective-permute-start(bf16[240,768]{1,0:T(8,128)(2,1)S(1)} %get-tuple-element.309.refs_8_.refs_5_.refs_0_), channel_id=1, source_target_pairs={{0,16},{16,0},{1,17},{17,1},{2,18},{18,2},{3,19},{19,3},{4,20},{20... | collective-permute-start | bytes 1105928 | tf_op jit(solution)/shard_map/ppermute | solution.py:1013
  202.2 9.1 %collective-permute-start.61 = (bf16[256,768]{1,0:T(8,128)(2,1)S(1)}, bf16[256,768]{1,0:T(8,128)(2,1)S(1)}, u32[]{:S(2)}, u32[]{:S(2)}) collective-permute-start(bf16[256,768]{1,0:T(8,128)(2,1)S(1)} %get-tuple-element.314.refs_4_), channel_id=1, source_target_pairs={{0,8},{8,0},{1,9},{9,1},{2,10},{10,2},{3,11},{11,3},{4,12},{12,4},... | collective-permute-start | bytes 1179656 | tf_op jit(solution)/shard_map/ppermute | solution.py:1013
  203.2 10.4 %collective-permute-start.64 = (bf16[256,768]{1,0:T(8,128)(2,1)S(1)}, bf16[256,768]{1,0:T(8,128)(2,1)S(1)}, u32[]{:S(2)}, u32[]{:S(2)}) collective-permute-start(bf16[256,768]{1,0:T(8,128)(2,1)S(1)} %get-tuple-element.314.refs_4_), channel_id=1, source_target_pairs={{0,4},{4,0},{1,5},{5,1},{2,6},{6,2},{3,7},{7,3},{8,12},{12,8},{9,1... | collective-permute-start | bytes 1179656 | tf_op jit(solution)/shard_map/ppermute | solution.py:1013
  (37 other events, 192.6 us)
